TPU v7x, 32 devices: a whole 2x2x4 slice. The times are simulated.
32 devices in a mesh: scen: 8 (over z, core), col: 4 (over y, x).
Axes of the slice: x: 2, y: 2, z: 4, core: 2. Of those that a mesh axis runs over, the one named last changes fastest.
Arguments:
- inverse_factor: bfloat16 [32, 512, 512], P(('scen', 'col')), as said below
- true_orders: int32 [32], P(('scen', 'col')), may hold values from 64 to 512, as said below
- slab_border: bfloat16 [32, 256, 512], P(('scen', 'col')), may hold values from -0.25 to 0.25
- slab_columns: int32 [32, 256], P('scen'), may hold values from 0 to 511
- panel_border: bfloat16 [4, 32, 48, 512], P('col', 'scen'), may hold values from -6 to 6
- panel_rows: int32 [4, 32, 48], P('col', 'scen'), may hold values from 0 to 1919
- barrier_diag: float32 [512], replicated, may hold values from 20 to 400
Outputs:
- diag_factor: float32 [512, 512], P('col')
- panel_factor: float32 [7680, 512], P(('scen', 'col'))
Inputs may be any that keep to these rules, and one draw needn't show every extreme that they name: `inverse_factor`: symmetric; its leading block of each scenario's true order is positive definite. `true_orders`: scenario 0 has the full padded order.
All inputs are finite; a program needn't handle non-finite values.
Results may differ from a plain program's by a relative error of at most 0.0003.
The roundings to bfloat16 on the way count: a program that leaves them out, or rounds other values in their place, can miss the bound.
Values may be sent and summed in bfloat16 or wider, within the bound.
No kernel may reach another device: no remote copies, remote signals or barrier semaphores. Data moves between devices by JAX's collectives and lax.ppermute only.
A program may use at most 64 MiB of HBM per device.

v0:
```python
import jax
import jax.numpy as jnp
from jax import lax
from jax.sharding import PartitionSpec as P

NF = 8192
DIAG = 512


highest = lax.Precision.HIGHEST


def masked_product(factor, order_value, border):
    positions = jnp.arange(factor.shape[0], dtype=jnp.int32)
    inside = positions < order_value
    masked = jnp.where(inside[:, None] & inside[None, :], factor, jnp.zeros((), jnp.bfloat16))
    return jnp.dot(border, masked, preferred_element_type=jnp.float32)


def spread_map(index, width):
    return (index[:, None] == jnp.arange(width, dtype=jnp.int32)[None, :]).astype(jnp.float32)


def place_panel(running, coupling, row_index, columns):
    widened = jnp.dot(coupling, spread_map(columns, running.shape[1]), precision=highest)
    row_map = spread_map(row_index, running.shape[0])
    return running + jnp.einsum("br,bd->rd", row_map, widened, precision=highest)


def diag_step(running, operands):
    border, moved_rows, columns = operands
    terms = jnp.einsum("ap,bp->ab", border, moved_rows, preferred_element_type=jnp.float32)
    col_map = spread_map(columns, running.shape[0])
    widened = jnp.dot(terms, col_map, precision=highest)
    return (running + jnp.einsum("ad,ae->de", col_map, widened, precision=highest), None)


def panel_step(running, operands):
    border_values, moved_rows, row_index, columns = operands
    coupling = jnp.einsum(
        "bp,jp->bj", border_values, moved_rows, preferred_element_type=jnp.float32
    )
    return (place_panel(running, coupling, row_index, columns), None)


def shards(
    inverse_factor, true_orders, slab_border, slab_columns, panel_border, panel_rows, barrier_diag
):
    local_count = inverse_factor.shape[0]
    col_count = lax.axis_size("col")
    col_place = lax.axis_index("col")
    product = masked_product(inverse_factor[0], true_orders[0], slab_border[0])
    results = [product.astype(jnp.bfloat16)]
    transformed = jnp.stack(results)
    own_columns = lax.dynamic_slice_in_dim(slab_columns, col_place * local_count, local_count, 0)
    zero_diag = jnp.zeros((DIAG, DIAG), jnp.float32)
    diag_partial, _ = lax.scan(diag_step, zero_diag, (slab_border, transformed, own_columns))
    half = DIAG // 2
    symmetric = 0.5 * (diag_partial + diag_partial.T)
    upper_left = symmetric[:half, :half]
    lower_left = symmetric[half:, :half]
    lower_right = symmetric[half:, half:]
    zero_row = jnp.zeros((1, half), jnp.float32)
    shifted = jnp.concatenate([zero_row, upper_left], 0)
    flipped = jnp.concatenate([lower_right.T, zero_row], 0)
    row_ids = jnp.arange(half + 1, dtype=jnp.int32)[:, None]
    col_ids = jnp.arange(half, dtype=jnp.int32)[None, :]
    packed = jnp.where(row_ids > col_ids, shifted, flipped)
    packed_sum, lower_sum = lax.psum((packed, lower_left), ("scen", "col"))
    first_block = jnp.tril(packed_sum[1:])
    first_block = first_block + jnp.tril(first_block, -1).T
    second_block = jnp.triu(packed_sum[:half]).T
    second_block = second_block + jnp.tril(second_block, -1).T
    top_rows = jnp.concatenate([first_block, lower_sum.T], 1)
    bottom_rows = jnp.concatenate([lower_sum, second_block], 1)
    schur_diag = jnp.concatenate([top_rows, bottom_rows], 0) + jnp.diag(barrier_diag)
    factor_full = jnp.linalg.cholesky(schur_diag)
    rows_panel = (NF - DIAG) // col_count
    zero_panel = jnp.zeros((rows_panel, DIAG), jnp.float32)
    group_border = panel_border[0]
    group_rows = panel_rows[0]
    total, _ = lax.scan(
        panel_step,
        zero_panel,
        (
            group_border,
            lax.all_gather(transformed, "col", axis=0, tiled=True),
            group_rows,
            slab_columns,
        ),
    )
    own_rows = lax.psum_scatter(total, "scen", scatter_dimension=0, tiled=True)
    solved = lax.linalg.triangular_solve(
        factor_full, own_rows, left_side=False, lower=True, transpose_a=True
    )
    diag_rows = DIAG // col_count
    return (lax.dynamic_slice_in_dim(factor_full, col_place * diag_rows, diag_rows, 0), solved)


def solution(mesh):
    in_specs = (
        P(("scen", "col"), None, None),
        P(("scen", "col")),
        P(("scen", "col"), None, None),
        P("scen", None),
        P("col", "scen", None, None),
        P("col", "scen", None),
        P(),
    )
    out_specs = (P("col", None), P(("scen", "col"), None))
    return jax.shard_map(shards, mesh=mesh, in_specs=in_specs, out_specs=out_specs, check_vma=False)
```

profile of v0, /device:TPU:0, one launch (start us, length us, event | category | flops | bytes accessed | tf_op | source)
XLA Modules:
  0.0 311.1 jit_solution(11754066118302753529)
XLA Ops:
  9.0 2.2 convolution_convert_fusion
  16.7 24.1 %all-gather.3.cloned.1.call-done = bf16[1024,512]{0,1:T(8,128)(2,1)} async-done(((bf16[256,512]{0,1:T(8,128)(2,1)}), bf16[1024,512]{0,1:T(8,128)(2,1)}) %all-gather.3.cloned.1.call-update) | async-done | bytes 1048592 | tf_op jit(solution)/shard_map/all_gather | solution.py:87
  40.8 1.5 copy.20
  42.3 32.6 %while.17 = (s32[]{:T(128)}, f32[1920,512]{1,0:T(8,128)}, s32[4,48]{1,0:T(4,128)}, bf16[4,48,512]{2,1,0:T(8,128)(2,1)}, bf16[4,256,512]{2,1,0:T(8,128)(2,1)S(1)}, /*index=5*/s32[4,256]{1,0:T(4,128)}, s32[]{:T(128)}, s32[]{:T(128)}) while((s32[]{:T(128)}, f32[1920,512]{1,0:T(8,128)}, s32[4,48]{1,0:T(4,128)}, ...), condition=%wide.region_11.12_spmd.clone, body=%wide.region_10.11_spmd.clone.sunk | while | flops 656500736 | bytes 8475311 | solution.py:82
  45.1 3.8 %select_add_fusion.2 = f32[1920,512]{1,0:T(8,128)} fusion(f32[1920,512]{1,0:T(8,128)} %get-tuple-element.205, f32[48,512]{1,0:T(8,128)S(1)} %fusion.81, pred[]{:T(512)S(6)} %compare.47, s32[48]{0:T(128)S(1)} %fusion.82), kind=kOutput, calls=%fused_computation.2.clone.1 | convolution fusion | flops 568289280 | bytes 7962817 | tf_op jit(solution)/shard_map/while/body/eval_jaxpr/br,bd->rd/dot_general | solution.py:27
  51.7 5.9 %select_add_fusion.2 = f32[1920,512]{1,0:T(8,128)} fusion(f32[1920,512]{1,0:T(8,128)} %get-tuple-element.205, f32[48,512]{1,0:T(8,128)S(1)} %fusion.81, pred[]{:T(512)S(6)} %compare.47, s32[48]{0:T(128)S(1)} %fusion.82), kind=kOutput, calls=%fused_computation.2.clone.1 | convolution fusion | flops 568289280 | bytes 7962817 | tf_op jit(solution)/shard_map/while/body/eval_jaxpr/br,bd->rd/dot_general | solution.py:27
  60.4 5.9 %select_add_fusion.2 = f32[1920,512]{1,0:T(8,128)} fusion(f32[1920,512]{1,0:T(8,128)} %get-tuple-element.205, f32[48,512]{1,0:T(8,128)S(1)} %fusion.81, pred[]{:T(512)S(6)} %compare.47, s32[48]{0:T(128)S(1)} %fusion.82), kind=kOutput, calls=%fused_computation.2.clone.1 | convolution fusion | flops 568289280 | bytes 7962817 | tf_op jit(solution)/shard_map/while/body/eval_jaxpr/br,bd->rd/dot_general | solution.py:27
  69.0 5.9 %select_add_fusion.2 = f32[1920,512]{1,0:T(8,128)} fusion(f32[1920,512]{1,0:T(8,128)} %get-tuple-element.205, f32[48,512]{1,0:T(8,128)S(1)} %fusion.81, pred[]{:T(512)S(6)} %compare.47, s32[48]{0:T(128)S(1)} %fusion.82), kind=kOutput, calls=%fused_computation.2.clone.1 | convolution fusion | flops 568289280 | bytes 7962817 | tf_op jit(solution)/shard_map/while/body/eval_jaxpr/br,bd->rd/dot_general | solution.py:27
  75.3 81.7 %all-reduce.6.cloned.1.call-done = (f32[257,256]{1,0:T(8,128)}, f32[256,256]{1,0:T(8,128)}) async-done(((f32[257,256]{1,0:T(8,128)}, f32[256,256]{1,0:T(8,128)}), (f32[257,256]{1,0:T(8,128)}, f32[256,256]{1,0:T(8,128)})) %all-reduce.6.cloned.1.call-update) | async-done | bytes 525328 | tf_op jit(solution)/shard_map/psum | solution.py:69
  161.6 11.7 %cholesky.103 = f32[128,128]{1,0:T(8,128)S(1)} custom-call(f32[128,128]{1,0:T(8,128)S(1)} %cholesky.263), custom_call_target="Cholesky" | custom-call | tf_op jit(solution)/shard_map/jit(cholesky)/cholesky | solution.py:77
  173.5 9.8 %custom-call.30 = f32[1,128,128]{1,2,0:T(8,128)S(1)} custom-call(f32[1,128,128]{2,1,0:T(8,128)S(1)} %get-tuple-element.125), custom_call_target="InvertDiagBlocksLowerTriangular" | custom-call | tf_op jit(solution)/shard_map/jit(cholesky)/cholesky | solution.py:77
  184.0 11.7 %cholesky.215 = f32[128,128]{1,0:T(8,128)S(1)} custom-call(f32[128,128]{1,0:T(8,128)S(1)} %cholesky.267), custom_call_target="Cholesky" | custom-call | tf_op jit(solution)/shard_map/jit(cholesky)/cholesky | solution.py:77
  195.7 9.9 %custom-call.31 = f32[1,128,128]{1,2,0:T(8,128)S(1)} custom-call(f32[1,128,128]{2,1,0:T(8,128)S(1)} %get-tuple-element.122), custom_call_target="InvertDiagBlocksLowerTriangular" | custom-call | tf_op jit(solution)/shard_map/jit(cholesky)/cholesky | solution.py:77
  206.3 11.7 %cholesky.236 = f32[128,128]{1,0:T(8,128)S(1)} custom-call(f32[128,128]{1,0:T(8,128)S(1)} %cholesky.272), custom_call_target="Cholesky" | custom-call | tf_op jit(solution)/shard_map/jit(cholesky)/cholesky | solution.py:77
  218.1 9.8 %custom-call.32 = f32[1,128,128]{1,2,0:T(8,128)S(1)} custom-call(f32[1,128,128]{2,1,0:T(8,128)S(1)} %get-tuple-element.119), custom_call_target="InvertDiagBlocksLowerTriangular" | custom-call | tf_op jit(solution)/shard_map/jit(cholesky)/cholesky | solution.py:77
  228.5 11.9 %cholesky.253 = f32[128,128]{1,0:T(8,128)S(1)} custom-call(f32[128,128]{1,0:T(8,128)S(1)} %convolution_subtract_fusion.5), custom_call_target="Cholesky" | custom-call | tf_op jit(solution)/shard_map/jit(cholesky)/cholesky | solution.py:77
  245.4 10.8 %while.16 = (s32[]{:T(128)}, f32[512,512]{1,0:T(8,128)S(1)}, s32[4,2]{0,1:T(2,128)S(1)}, f32[4,128,128]{2,1,0:T(8,128)}, s32[]{:T(128)}) while((s32[]{:T(128)}, f32[512,512]{1,0:T(8,128)S(1)}, s32[4,2]{0,1:T(2,128)S(1)}, f32[4,128,128]{2,1,0:T(8,128)}, s32[]{:T(128)}) %tuple.58), condition=%wide.while_cond, body=%wide.while_body.sunk | while | flops 2 | bytes 132205 | solution.py:93
  246.0 2.0 bitcast_dynamic-update-slice_fusion.2
  248.7 2.0 bitcast_dynamic-update-slice_fusion.2
  251.4 2.0 bitcast_dynamic-update-slice_fusion.2
  254.1 2.0 bitcast_dynamic-update-slice_fusion.2
  256.2 40.1 %custom-call.33 = f32[4,128,128]{1,2,0:T(8,128)S(1)} custom-call(f32[4,128,128]{2,1,0:T(8,128)} %get-tuple-element.57), custom_call_target="InvertDiagBlocksLowerTriangular" | custom-call | tf_op jit(solution)/shard_map/triangular_solve | solution.py:93
  299.7 1.3 convolution_subtract_fusion.3
  301.2 1.4 convolution_subtract_fusion.4
  (89 shorter events, 33.1 us)
Async XLA Ops:
  8.0 1.0 copy-start
  8.0 32.8 %all-gather.3.cloned.1.call-start = ((), (), s32[]{:S(2)}) async-start(), calls=%async_computation.2 | async-start | bytes 1310720 | tf_op jit(solution)/shard_map/all_gather | solution.py:87
  11.2 145.8 %all-reduce.6.cloned.1.call-start = ((), (), s32[]{:S(2)}) async-start(), calls=%async_computation.3 | async-start | bytes 1064960 | tf_op jit(solution)/shard_map/psum | solution.py:69
  16.6 280.4 %reduce-scatter.2.cloned.1.call-start = ((), (), s32[]{:S(2)}) async-start(), calls=%async_computation.1 | async-start | bytes 4423680 | tf_op jit(solution)/shard_map/reduce_scatter | solution.py:92
  74.9 85.9 %copy-start.2 = (f32[512]{0:T(512)S(1)}, f32[512]{0:T(512)}, u32[]{:S(2)}) copy-start(f32[512]{0:T(512)} %param.15) | copy-start | bytes 6148
  157.0 3.7 %copy-start.1 = (f32[256,256]{1,0:T(8,128)S(1)}, f32[256,256]{1,0:T(8,128)}, u32[]{:S(2)}) copy-start(f32[256,256]{1,0:T(8,128)} %get-tuple-element.106) | copy-start | bytes 786436
Sparse Core Ops, SparseCore 0:
  11.4 29.4 all-gather.2
  75.1 48.2 reduce-scatter.1
Sparse Core Ops, SparseCore 1:
  17.6 139.4 all-reduce.5
where the time goes:
time: 313 us; the launch traced here: 311 us
  other arithmetic  125 us (40%)
  waiting for transfers between devices  106 us (34%)
  matrix products  39.2 us (13%)
  local copies, waits for them, and re-layouts  21.9 us (7%)
  between operations  19.2 us (6%)
    psum x1, waiting for transfers between devices, shards(): packed_sum, lower_sum = lax.psum((packed, lower_left), ('scen', 'col'))  81.7 us
    another operation x14, other arithmetic, shards(): factor_full = jnp.linalg.cholesky(schur_diag)  78.7 us
    another operation x4, other arithmetic, shards(): lax.linalg.triangular_solve(factor_full, own_rows, left_side=False, lower...  41.2 us
    all_gather x1, waiting for transfers between devices, shards(): lax.all_gather(transformed, 'col', axis=0, tiled=True)  24.1 us
    dot_general x4, matrix products, place_panel(): jnp.einsum('br,bd->rd', row_map, widened, precision=highest)  21.5 us
    another operation x12, local copies, waits for them, and re-layouts  10.8 us
  transfers between devices with their start and end apart: 3, of which 2 were waited for; matrix products, arithmetic and copies ran while one was open for 57% of the time, Pallas kernels for 0%

commit v1 on v0

v1 whole, which is shorter than its diff:
```python
import functools

import jax
import jax.numpy as jnp
from jax import lax
from jax.experimental import pallas as pl
from jax.experimental.pallas import tpu as pltpu
from jax.sharding import PartitionSpec as P

NF = 8192
BLOCK = 128
HIGHEST = lax.Precision.HIGHEST
VMEM = pl.BlockSpec(memory_space=pltpu.VMEM)
SMEM = pl.BlockSpec(memory_space=pltpu.SMEM)
PARAMS = pltpu.CompilerParams(vmem_limit_bytes=40 * 2**20)


def split_two(value):
    high = value.astype(jnp.bfloat16)
    low = (value - high.astype(jnp.float32)).astype(jnp.bfloat16)
    return high, low


def matmul(left, right):
    return jnp.dot(left, right, preferred_element_type=jnp.float32)


def matmul_nt(left, right):
    return lax.dot_general(
        left, right, (((1,), (1,)), ((), ())), preferred_element_type=jnp.float32
    )


def exact_tn(left, right):
    return lax.dot_general(
        left,
        right,
        (((0,), (0,)), ((), ())),
        precision=HIGHEST,
        preferred_element_type=jnp.float32,
    )


def exact(left, right):
    return jnp.dot(left, right, precision=HIGHEST, preferred_element_type=jnp.float32)


def exact_nt(left, right):
    return lax.dot_general(
        left,
        right,
        (((1,), (1,)), ((), ())),
        precision=HIGHEST,
        preferred_element_type=jnp.float32,
    )


def upper_blocks(width):
    count = width // BLOCK
    return [(i, j) for i in range(count) for j in range(i, count)]


def front_kernel(
    order_ref, factor_ref, border_ref, columns_ref, moved_ref, keep_ref, send_ref, packed_ref, *, width
):
    count = factor_ref.shape[0]
    core = lax.rem(lax.axis_index("scen"), 2)
    place = lax.axis_index("col")
    order = order_ref[0]
    border = border_ref[0]
    within = lax.broadcasted_iota(jnp.int32, border.shape, 1) < order
    inside = jnp.where(within, border.astype(jnp.float32), 0.0).astype(jnp.bfloat16)
    product = matmul(inside, factor_ref[0])
    moved = jnp.where(within, product, 0.0).astype(jnp.bfloat16)
    moved_ref[...] = moved
    terms = 0.5 * (matmul_nt(border, moved) + matmul_nt(moved, border))
    columns = columns_ref[pl.ds(place * count, 1), :]
    spread = (
        lax.broadcasted_iota(jnp.int32, (width, columns.shape[1]), 0) == columns
    ).astype(jnp.bfloat16)
    high, low = split_two(terms)
    half_spread = matmul_nt(high, spread) + matmul_nt(low, spread)
    high, low = split_two(half_spread)
    row = 0
    for i in range(width // BLOCK):
        rows = spread[i * BLOCK : (i + 1) * BLOCK]
        part = matmul(rows, high[:, i * BLOCK :]) + matmul(rows, low[:, i * BLOCK :])
        for j in range(i, width // BLOCK):
            packed_ref[row : row + BLOCK, :] = part[:, (j - i) * BLOCK : (j - i + 1) * BLOCK]
            row += BLOCK
    half = keep_ref.shape[0]
    keep_ref[...] = packed_ref[pl.ds(pl.multiple_of(core * half, 8), half), :]
    send_ref[...] = packed_ref[pl.ds(pl.multiple_of((1 - core) * half, 8), half), :]


def front(order, factor, border, columns, width):
    total = len(upper_blocks(width)) * BLOCK
    half = jax.ShapeDtypeStruct((total // 2, BLOCK), jnp.float32)
    return pl.pallas_call(
        functools.partial(front_kernel, width=width),
        out_shape=[jax.ShapeDtypeStruct(border.shape[1:], jnp.bfloat16), half, half],
        in_specs=[SMEM, VMEM, VMEM, VMEM],
        out_specs=[VMEM, VMEM, VMEM],
        scratch_shapes=[pltpu.VMEM((total, BLOCK), jnp.float32)],
        compiler_params=PARAMS,
        name="front",
    )(order, factor, border, columns)


def quarter_kernel(keep_ref, got_ref, *out_refs):
    place = lax.axis_index("col")
    rows = out_refs[0].shape[0]
    for m, out_ref in enumerate(out_refs):
        at = pl.ds(pl.multiple_of((place ^ m) * rows, 8), rows)
        out_ref[...] = keep_ref[at, :] + got_ref[at, :]


def quarters(keep, got, col_count):
    piece = jax.ShapeDtypeStruct((keep.shape[0] // col_count, BLOCK), jnp.float32)
    return pl.pallas_call(
        quarter_kernel,
        out_shape=[piece] * col_count,
        in_specs=[VMEM, VMEM],
        out_specs=[VMEM] * col_count,
        compiler_params=PARAMS,
        name="quarters",
    )(keep, got)


def swap(value, axis, step):
    count = lax.axis_size(axis)
    return lax.ppermute(value, axis, [(i, i ^ step) for i in range(count)])


def tree_sum(values):
    while len(values) > 1:
        values = [values[i] + values[i + 1] for i in range(0, len(values), 2)]
    return values[0]


def row_of(tile, i):
    return jnp.broadcast_to(tile[i : i + 1, :], tile.shape)


def column_of(tile, j):
    return jnp.broadcast_to(tile[:, j : j + 1], (tile.shape[0], BLOCK))


def factor_block(block):
    groups = BLOCK // 8
    sub = lax.broadcasted_iota(jnp.int32, (8, BLOCK), 0)
    lane = lax.broadcasted_iota(jnp.int32, (8, BLOCK), 1)
    left = [block[8 * t : 8 * t + 8, :] for t in range(groups)]
    right = [(lane == sub + 8 * t).astype(jnp.float32) for t in range(groups)]
    upper = []
    inverse = []
    for g in range(groups):
        a, b = left[g], right[g]
        near = [column_of(a, 8 * g + m) for m in range(8)]
        out_a, out_b = a, b
        for i in range(8):
            pivot = row_of(near[i], i)
            recip = 1.0 / pivot
            root = lax.rsqrt(pivot)
            factor = jnp.where(sub == i, 1.0 - recip, near[i] * recip)
            row_a, row_b = row_of(a, i), row_of(b, i)
            out_a = jnp.where(sub == i, row_a * root, out_a)
            out_b = jnp.where(sub == i, row_b * root, out_b)
            for m in range(i + 1, 8):
                near[m] = near[m] - factor * row_of(near[m], i)
            a = a - factor * row_a
            b = b - factor * row_b
        upper.append(jnp.where(lane >= sub + 8 * g, out_a, 0.0))
        inverse.append(out_b)
        if g + 1 < groups:
            rows_a = [row_of(a, i) for i in range(8)]
            rows_b = [row_of(b, i) for i in range(8)]
            for t in range(g + 1, groups):
                weights = [column_of(left[t], 8 * g + i) for i in range(8)]
                sum_a = weights[0] * rows_a[0]
                sum_b = weights[0] * rows_b[0]
                for i in range(1, 8):
                    sum_a = sum_a + weights[i] * rows_a[i]
                    sum_b = sum_b + weights[i] * rows_b[i]
                left[t] = left[t] - sum_a
                right[t] = right[t] - sum_b
    return jnp.concatenate(upper, 0), jnp.concatenate(inverse, 0)


def cholesky_kernel(*refs, col_count):
    pieces = refs[: 2 * col_count]
    barrier_ref, upper_ref, inverse_ref, slice_ref, packed_ref, lower_ref = refs[2 * col_count :]
    width = barrier_ref.shape[1]
    count = width // BLOCK
    rows = pieces[0].shape[0]
    core = lax.rem(lax.axis_index("scen"), 2)
    place = lax.axis_index("col")
    for side in range(2):
        owner = core if side == 0 else 1 - core
        for m in range(col_count):
            at = (owner * col_count + (place ^ m)) * rows
            packed_ref[pl.ds(pl.multiple_of(at, 8), rows), :] = pieces[side * col_count + m][...]
    diagonal = lax.broadcasted_iota(jnp.int32, (BLOCK, BLOCK), 0) == lax.broadcasted_iota(
        jnp.int32, (BLOCK, BLOCK), 1
    )
    blocks = {}
    for n, (i, j) in enumerate(upper_blocks(width)):
        blocks[i, j] = packed_ref[n * BLOCK : (n + 1) * BLOCK, :]
        if i == j:
            extra = barrier_ref[:, i * BLOCK : (i + 1) * BLOCK]
            blocks[i, j] = blocks[i, j] + jnp.where(diagonal, extra, 0.0)
    panels = [jnp.concatenate([blocks[i, j] for j in range(i, count)], 1) for i in range(count)]
    lower_ref[...] = jnp.zeros(lower_ref.shape, jnp.float32)
    for i in range(count):
        here = slice(i * BLOCK, (i + 1) * BLOCK)
        own, inverse = factor_block(panels[i][:, :BLOCK])
        upper_ref[here, here] = own
        inverse_ref[i] = inverse
        lower_ref[here, here] = own.T
        if i + 1 < count:
            rest = exact(inverse, panels[i][:, BLOCK:])
            upper_ref[here, (i + 1) * BLOCK :] = rest
            for j in range(i + 1, count):
                first = (j - i - 1) * BLOCK
                block = rest[:, first : first + BLOCK]
                lower_ref[j * BLOCK : (j + 1) * BLOCK, here] = block.T
                panels[j] = panels[j] - exact_tn(block, rest[:, first:])
    slice_rows = slice_ref.shape[0]
    slice_ref[...] = lower_ref[pl.ds(pl.multiple_of(place * slice_rows, 8), slice_rows), :]


def cholesky(pieces, barrier):
    width = barrier.shape[0]
    col_count = len(pieces) // 2
    return pl.pallas_call(
        functools.partial(cholesky_kernel, col_count=col_count),
        out_shape=[
            jax.ShapeDtypeStruct((width, width), jnp.float32),
            jax.ShapeDtypeStruct((width // BLOCK, BLOCK, BLOCK), jnp.float32),
            jax.ShapeDtypeStruct((width // col_count, width), jnp.float32),
        ],
        in_specs=[VMEM] * (len(pieces) + 1),
        out_specs=[VMEM] * 3,
        scratch_shapes=[
            pltpu.VMEM((len(upper_blocks(width)) * BLOCK, BLOCK), jnp.float32),
            pltpu.VMEM((width, width), jnp.float32),
        ],
        compiler_params=PARAMS,
        cost_estimate=pl.CostEstimate(
            flops=2 * width**3, bytes_accessed=12 * width**2, transcendentals=width
        ),
        name="cholesky",
    )(*pieces, barrier[None])


def coupling_kernel(moved_ref, *refs):
    count = len(refs) // 2
    moved = moved_ref[...]
    for border_ref, out_ref in zip(refs[:count], refs[count:]):
        out_ref[...] = matmul_nt(border_ref[...], moved)


def couplings(moved, borders):
    shape = jax.ShapeDtypeStruct((borders[0].shape[0], moved.shape[0]), jnp.float32)
    return pl.pallas_call(
        coupling_kernel,
        out_shape=[shape] * len(borders),
        in_specs=[VMEM] * (len(borders) + 1),
        out_specs=[VMEM] * len(borders),
        compiler_params=PARAMS,
        name="couplings",
    )(moved, *borders)


def solve_rows(rows, upper, inverse, out_ref):
    width = rows.shape[1]
    solved = []
    for k in range(width // BLOCK):
        here = slice(k * BLOCK, (k + 1) * BLOCK)
        left = rows[:, here]
        if k > 0:
            left = left - exact(jnp.concatenate(solved, 1), upper[: k * BLOCK, here])
        solved.append(exact_nt(left, inverse[k]))
        out_ref[:, here] = solved[-1]


def panel_kernel(*refs, group):
    groups = refs[:-3]
    upper_ref, inverse_ref, out_ref = refs[-3:]
    rows_here, width = out_ref.shape
    first = lax.axis_index("scen") * rows_here
    total = jnp.zeros((rows_here, width), jnp.float32)
    for group_ref in groups:
        wide = group_ref.shape[1]
        size = (group_ref.shape[0] - 8) // group
        index = group_ref[group * size :, :]
        spreads = []
        for i in range(group):
            columns = index[i : i + 1, :].astype(jnp.int32)
            spread = lax.broadcasted_iota(jnp.int32, (width, wide), 0) == columns
            high, low = split_two(group_ref[i * size : (i + 1) * size, :])
            both = matmul_nt(
                jnp.concatenate([high, low], 0), spread.astype(jnp.bfloat16)
            )
            spreads.append(both[:size] + both[size:])
        widened = jnp.concatenate(spreads, 0)
        row_index = index[group : group + 1, : group * size].astype(jnp.int32) - first
        row_map = (
            lax.broadcasted_iota(jnp.int32, (rows_here, group * size), 0) == row_index
        ).astype(jnp.bfloat16)
        high, low = split_two(widened)
        total = total + (matmul(row_map, high) + matmul(row_map, low))
    solve_rows(total, upper_ref[...], inverse_ref[...], out_ref)


def panel_rows_of(groups, group, upper, inverse, rows_here):
    return pl.pallas_call(
        functools.partial(panel_kernel, group=group),
        out_shape=jax.ShapeDtypeStruct((rows_here, upper.shape[1]), jnp.float32),
        in_specs=[VMEM] * (len(groups) + 2),
        out_specs=VMEM,
        compiler_params=PARAMS,
        name="panel",
    )(*groups, upper, inverse)


def dense_panel(couplings_here, rows, columns, rows_panel, width):
    def step(running, operands):
        coupling, row_index, column_index = operands
        column_map = (column_index[:, None] == jnp.arange(width)[None, :]).astype(jnp.float32)
        row_map = (row_index[:, None] == jnp.arange(rows_panel)[None, :]).astype(jnp.float32)
        widened = jnp.dot(coupling, column_map, precision=HIGHEST)
        return running + jnp.einsum("br,bd->rd", row_map, widened, precision=HIGHEST), None

    zero = jnp.zeros((rows_panel, width), jnp.float32)
    total, _ = lax.scan(step, zero, (couplings_here, rows, columns))
    return lax.psum_scatter(total, "scen", scatter_dimension=0, tiled=True)


def dense_solve(rows, upper, inverse):
    width = rows.shape[1]
    solved = []
    for k in range(width // BLOCK):
        here = slice(k * BLOCK, (k + 1) * BLOCK)
        left = rows[:, here]
        if k > 0:
            left = left - jnp.dot(
                jnp.concatenate(solved, 1), upper[: k * BLOCK, here], precision=HIGHEST
            )
        solved.append(jnp.dot(left, inverse[k].T, precision=HIGHEST))
    return jnp.concatenate(solved, 1)


def shards(
    rows_here,
    inverse_factor,
    true_orders,
    slab_border,
    slab_columns,
    panel_border,
    panel_rows,
    barrier_diag,
):
    scen_count = lax.axis_size("scen")
    col_count = lax.axis_size("col")
    place = lax.axis_index("col")
    width = barrier_diag.shape[0]
    group, size, depth = panel_border.shape[1:]
    wide = slab_columns.shape[1]

    order = [place ^ m for m in range(col_count)]
    own_borders = [
        lax.dynamic_index_in_dim(panel_border[0], order[m], 0, keepdims=False)
        for m in range(col_count)
    ]
    borders = [own_borders[0]] + [swap(own_borders[m], "col", m) for m in range(1, col_count)]

    moved, keep, send = front(true_orders, inverse_factor, slab_border, slab_columns, width)
    got = swap(send, "scen", 1)
    parts = quarters(keep, got, col_count)
    part = tree_sum([parts[0]] + [swap(parts[m], "col", m) for m in range(1, col_count)])
    part = tree_sum([part] + [swap(part, "scen", 2 * m) for m in range(1, scen_count // 2)])
    pieces = [part] + [swap(part, "col", m) for m in range(1, col_count)]
    pieces = pieces + [swap(piece, "scen", 1) for piece in pieces]
    upper, inverse, factor_rows = cholesky(pieces, barrier_diag)

    partial = couplings(moved, borders)
    mine = [partial[0]] + [swap(partial[m], "col", m) for m in range(1, col_count)]
    rows_panel = rows_here * scen_count
    fits = group < 8 and group * size <= wide
    if fits and scen_count * group * size * wide < rows_panel * width:
        order = jnp.stack(order)
        rows_index = panel_rows[0][order].reshape(1, group * size)
        rows_index = jnp.pad(rows_index, ((0, 0), (0, wide - group * size)))
        index = jnp.concatenate([slab_columns[order], rows_index], 0).astype(jnp.float32)
        index = jnp.pad(index, ((0, 7 - group), (0, 0)))
        own = jnp.concatenate(mine + [index], 0)
        near = [own] + [swap(own, "scen", 2 * m) for m in range(1, scen_count // 2)]
        groups = near + [swap(value, "scen", 1) for value in near]
        solved = panel_rows_of(groups, group, upper, inverse, rows_here)
    else:
        rows = dense_panel(
            jnp.stack(mine), panel_rows[0][jnp.stack(order)], slab_columns[jnp.stack(order)], rows_panel, width
        )
        solved = dense_solve(rows, upper, inverse)
    return factor_rows, solved


def solution(mesh):
    in_specs = (
        P(("scen", "col"), None, None),
        P(("scen", "col")),
        P(("scen", "col"), None, None),
        P("scen", None),
        P("col", "scen", None, None),
        P("col", "scen", None),
        P(),
    )
    out_specs = (P("col", None), P(("scen", "col"), None))

    def whole(*args):
        devices = mesh.shape["scen"] * mesh.shape["col"]
        first_section = NF - args[-1].shape[0]
        body = functools.partial(shards, first_section // devices)
        return jax.shard_map(
            body, mesh=mesh, in_specs=in_specs, out_specs=out_specs, check_vma=False
        )(*args)

    return whole
```

time: 313 us -> 84.1 us (0.27)
  other arithmetic: 125 us -> 0.14 us
  waiting for transfers between devices: 106 us -> 14.3 us
  matrix products: 39.2 us -> 0 us
  starting transfers between devices: 0.12 us -> 32.6 us
  Pallas kernels: 0 us -> 30.8 us
  between operations: 19.2 us -> 1.4 us
  local copies, waits for them, and re-layouts: 21.9 us -> 4.53 us
    another operation x18 -> x0, other arithmetic: 120 us -> none  [the longest x14 78.7 us: shards(): factor_full = jnp.linalg.cholesky(schur_diag)]
    psum x1 -> x0, waiting for transfers between devices: 81.7 us -> none  [shards(): packed_sum, lower_sum = lax.psum((packed, lower_left), ('scen', 'col'))]
    ppermute x0 -> x27, starting transfers between devices: none -> 32.6 us  [swap(): return lax.ppermute(value, axis, [(i, i ^ step) for i in range(count)])]
    dot_general x16 -> x0, matrix products: 31.6 us -> none  [the longest x4 21.5 us: place_panel(): jnp.einsum('br,bd->rd', row_map, widened, precision=highest)]
    pallas_call x0 -> x5, Pallas kernels: none -> 30.8 us  [the longest x1 21.6 us: cholesky(): pl.pallas_call(functools.partial(cholesky_kernel, col_count=col_count), o...]
    all_gather x1 -> x0, waiting for transfers between devices: 24.1 us -> none  [shards(): lax.all_gather(transformed, 'col', axis=0, tiled=True)]
    ppermute x0 -> x27, waiting for transfers between devices: none -> 14.3 us  [swap(): return lax.ppermute(value, axis, [(i, i ^ step) for i in range(count)])]
    another operation x17 -> x0, local copies, waits for them, and re-layouts: 11 us -> none
  transfers between devices with their start and end apart: 3 -> 27, of which waited for: 2 -> 11; matrix products, arithmetic and copies ran while one was open for 57% -> 2% of each run, Pallas kernels for 0% -> 26%
where the time goes in v1:
time: 84.1 us; the launch traced here: 83.8 us
  starting transfers between devices  32.6 us (39%)
  Pallas kernels  30.8 us (37%)
  waiting for transfers between devices  14.3 us (17%)
  local copies, waits for them, and re-layouts  4.53 us (5%)
  between operations  1.4 us (2%)
    ppermute x27, starting transfers between devices, swap(): return lax.ppermute(value, axis, [(i, i ^ step) for i in range(count)])  32.6 us
    pallas_call x1, Pallas kernels, cholesky(): pl.pallas_call(functools.partial(cholesky_kernel, col_count=col_count), o...  21.6 us
    ppermute x27, waiting for transfers between devices, swap(): return lax.ppermute(value, axis, [(i, i ^ step) for i in range(count)])  14.3 us
    pallas_call x1, Pallas kernels, panel_rows_of(): pl.pallas_call(functools.partial(panel_kernel, group=group), out_shape=ja...  7.38 us
    unnamed x18, local copies, waits for them, and re-layouts  3.31 us
  transfers between devices with their start and end apart: 27, of which 11 were waited for; matrix products, arithmetic and copies ran while one was open for 2% of the time, Pallas kernels for 26%

profile of v1, /device:TPU:0, one launch (start us, length us, event | category | flops | bytes accessed | tf_op | source)
XLA Modules:
  0.0 83.8 jit_solution(1509635022335652258)
XLA Ops:
  1.3 1.0 %copy-done.1 = bf16[1,512,512]{2,1,0:T(8,128)(2,1)S(1)} copy-done((bf16[1,512,512]{2,1,0:T(8,128)(2,1)S(1)}, bf16[1,512,512]{2,1,0:T(8,128)(2,1)}, u32[]{:S(2)}) %copy-start.1) | copy-done | bytes 524312
  3.0 0.9 %copy-done.4 = bf16[1,256,512]{2,1,0:T(8,128)(2,1)S(1)} copy-done((bf16[1,256,512]{2,1,0:T(8,128)(2,1)S(1)}, bf16[1,256,512]{2,1,0:T(8,128)(2,1)}, u32[]{:S(2)}) %copy-start.4) | copy-done | bytes 262168
  4.0 1.4 %front.1 = (bf16[256,512]{1,0:T(8,128)(2,1)S(1)}, f32[640,128]{1,0:T(8,128)S(1)}, f32[640,128]{1,0:T(8,128)S(1)}) custom-call(s32[1]{0:T(128)S(6)} %copy.13.order_ref, bf16[1,512,512]{2,1,0:T(8,128)(2,1)S(1)} %copy-done.1, bf16[1,256,512]{2,1,0:T(8,128)(2,1)S(1)} %copy-done.4, s32[4,256]{1,0:T(4,128)S(1)} %copy-done.2), custom_call_target="tpu_custom_call" | custom-call | tf_op jit(solution)/shard_map/front/pallas_call | solution.py:99
  5.9 2.6 %collective-permute-start.14 = (bf16[48,512]{1,0:T(8,128)(2,1)S(1)}, bf16[48,512]{1,0:T(8,128)(2,1)S(1)}, u32[]{:S(2)}, u32[]{:S(2)}) collective-permute-start(bf16[48,512]{1,0:T(8,128)(2,1)S(1)} %get-tuple-element.31), channel_id=1, source_target_pairs={{0,1},{1,0},{2,3},{3,2},{4,5},{5,4},{6,7},{7,6},{8,9},{9,8},{10,11... | collective-permute-start | bytes 147464 | tf_op jit(solution)/shard_map/ppermute | solution.py:132
  8.5 1.5 %collective-permute-start.15 = (bf16[48,512]{1,0:T(8,128)(2,1)S(1)}, bf16[48,512]{1,0:T(8,128)(2,1)S(1)}, u32[]{:S(2)}, u32[]{:S(2)}) collective-permute-start(bf16[48,512]{1,0:T(8,128)(2,1)S(1)} %get-tuple-element.33), channel_id=1, source_target_pairs={{0,2},{1,3},{2,0},{3,1},{4,6},{5,7},{6,4},{7,5},{8,10},{9,11},{10,... | collective-permute-start | bytes 147464 | tf_op jit(solution)/shard_map/ppermute | solution.py:132
  12.6 2.4 %collective-permute-done.16.refs_3_ = bf16[48,512]{1,0:T(8,128)(2,1)S(1)} collective-permute-done((bf16[48,512]{1,0:T(8,128)(2,1)S(1)}, bf16[48,512]{1,0:T(8,128)(2,1)S(1)}, u32[]{:S(2)}, u32[]{:S(2)}) %collective-permute-start.16) | collective-permute-done | bytes 49184 | tf_op jit(solution)/shard_map/ppermute | solution.py:132
  16.1 2.8 %collective-permute-start.19 = (f32[48,256]{1,0:T(8,128)S(1)}, f32[48,256]{1,0:T(8,128)S(1)}, u32[]{:S(2)}, u32[]{:S(2)}) collective-permute-start(f32[48,256]{1,0:T(8,128)S(1)} %get-tuple-element.27), channel_id=1, source_target_pairs={{0,3},{1,2},{2,1},{3,0},{4,7},{5,6},{6,5},{7,4},{8,11},{9,10},{10,... | collective-permute-start | bytes 147464 | tf_op jit(solution)/shard_map/ppermute | solution.py:132
  20.1 0.7 collective-permute-start.2
  20.8 2.3 %collective-permute-start.3 = (f32[160,128]{1,0:T(8,128)S(1)}, f32[160,128]{1,0:T(8,128)S(1)}, u32[]{:S(2)}, u32[]{:S(2)}) collective-permute-start(f32[160,128]{1,0:T(8,128)S(1)} %get-tuple-element.21), channel_id=1, source_target_pairs={{0,3},{1,2},{2,1},{3,0},{4,7},{5,6},{6,5},{7,4},{8,11},{9,10},{10,... | collective-permute-start | bytes 245768 | tf_op jit(solution)/shard_map/ppermute | solution.py:132
  23.7 0.9 %collective-permute-done.2 = f32[160,128]{1,0:T(8,128)S(1)} collective-permute-done((f32[160,128]{1,0:T(8,128)S(1)}, f32[160,128]{1,0:T(8,128)S(1)}, u32[]{:S(2)}, u32[]{:S(2)}) %collective-permute-start.2) | collective-permute-done | bytes 81952 | tf_op jit(solution)/shard_map/ppermute | solution.py:132
  24.6 1.6 %collective-permute-done.3 = f32[160,128]{1,0:T(8,128)S(1)} collective-permute-done((f32[160,128]{1,0:T(8,128)S(1)}, f32[160,128]{1,0:T(8,128)S(1)}, u32[]{:S(2)}, u32[]{:S(2)}) %collective-permute-start.3) | collective-permute-done | bytes 81952 | tf_op jit(solution)/shard_map/ppermute | solution.py:132
  26.2 1.4 %collective-permute-done.1 = f32[160,128]{1,0:T(8,128)S(1)} collective-permute-done((f32[160,128]{1,0:T(8,128)S(1)}, f32[160,128]{1,0:T(8,128)S(1)}, u32[]{:S(2)}, u32[]{:S(2)}) %collective-permute-start.1) | collective-permute-done | bytes 81952 | tf_op jit(solution)/shard_map/ppermute | solution.py:132
  27.6 2.7 %collective-permute-start.5 = (f32[160,128]{1,0:T(8,128)S(1)}, f32[160,128]{1,0:T(8,128)S(1)}, u32[]{:S(2)}, u32[]{:S(2)}) collective-permute-start(f32[160,128]{1,0:T(8,128)S(1)} %add_add_fusion.1), channel_id=1, source_target_pairs={{0,16},{4,20},{8,24},{12,28},{16,0},{20,4},{24,8},{28,12},{1,17},{... | collective-permute-start | bytes 245768 | tf_op jit(solution)/shard_map/ppermute | solution.py:132
  30.3 1.3 %collective-permute-start.6 = (f32[160,128]{1,0:T(8,128)S(1)}, f32[160,128]{1,0:T(8,128)S(1)}, u32[]{:S(2)}, u32[]{:S(2)}) collective-permute-start(f32[160,128]{1,0:T(8,128)S(1)} %add_add_fusion.1), channel_id=1, source_target_pairs={{0,24},{4,28},{8,16},{12,20},{16,8},{20,12},{24,0},{28,4},{1,25},{... | collective-permute-start | bytes 245768 | tf_op jit(solution)/shard_map/ppermute | solution.py:132
  31.8 1.8 %collective-permute-start.20 = (f32[200,256]{1,0:T(8,128)S(1)}, f32[200,256]{1,0:T(8,128)S(1)}, u32[]{:S(2)}, u32[]{:S(2)}) collective-permute-start(f32[200,256]{1,0:T(8,128)S(1)} %constant_dynamic-update-slice_fusion.refs_0_), channel_id=1, source_target_pairs={{0,8},{4,12},{8,0},{12,4},{16,24},{20,28},{24,16},{28,20},{1,9},{5... | collective-permute-start | bytes 614408 | tf_op jit(solution)/shard_map/ppermute | solution.py:132
  33.6 1.7 %collective-permute-start.21 = (f32[200,256]{1,0:T(8,128)S(1)}, f32[200,256]{1,0:T(8,128)S(1)}, u32[]{:S(2)}, u32[]{:S(2)}) collective-permute-start(f32[200,256]{1,0:T(8,128)S(1)} %constant_dynamic-update-slice_fusion.refs_0_), channel_id=1, source_target_pairs={{0,16},{4,20},{8,24},{12,28},{16,0},{20,4},{24,8},{28,12},{1,17},{... | collective-permute-start | bytes 614408 | tf_op jit(solution)/shard_map/ppermute | solution.py:132
  35.3 7.8 %collective-permute-start.22 = (f32[200,256]{1,0:T(8,128)S(1)}, f32[200,256]{1,0:T(8,128)S(1)}, u32[]{:S(2)}, u32[]{:S(2)}) collective-permute-start(f32[200,256]{1,0:T(8,128)S(1)} %constant_dynamic-update-slice_fusion.refs_0_), channel_id=1, source_target_pairs={{0,24},{4,28},{8,16},{12,20},{16,8},{20,12},{24,0},{28,4},{1,25},{... | collective-permute-start | bytes 614408 | tf_op jit(solution)/shard_map/ppermute | solution.py:132
  43.6 1.6 %collective-permute-start.8 = (f32[160,128]{1,0:T(8,128)S(1)}, f32[160,128]{1,0:T(8,128)S(1)}, u32[]{:S(2)}, u32[]{:S(2)}) collective-permute-start(f32[160,128]{1,0:T(8,128)S(1)} %add_add_fusion.refs_0_), channel_id=1, source_target_pairs={{0,2},{1,3},{2,0},{3,1},{4,6},{5,7},{6,4},{7,5},{8,10},{9,11},{10,... | collective-permute-start | bytes 245768 | tf_op jit(solution)/shard_map/ppermute | solution.py:132
  45.1 1.6 %collective-permute-start.9 = (f32[160,128]{1,0:T(8,128)S(1)}, f32[160,128]{1,0:T(8,128)S(1)}, u32[]{:S(2)}, u32[]{:S(2)}) collective-permute-start(f32[160,128]{1,0:T(8,128)S(1)} %add_add_fusion.refs_0_), channel_id=1, source_target_pairs={{0,3},{1,2},{2,1},{3,0},{4,7},{5,6},{6,5},{7,4},{8,11},{9,10},{10,... | collective-permute-start | bytes 245768 | tf_op jit(solution)/shard_map/ppermute | solution.py:132
  46.7 3.8 %collective-permute-done.21.refs_2_ = f32[200,256]{1,0:T(8,128)S(1)} collective-permute-done((f32[200,256]{1,0:T(8,128)S(1)}, f32[200,256]{1,0:T(8,128)S(1)}, u32[]{:S(2)}, u32[]{:S(2)}) %collective-permute-start.21) | collective-permute-done | bytes 204832 | tf_op jit(solution)/shard_map/ppermute | solution.py:132
  52.3 1.2 %collective-permute-done.12.refs_6_ = f32[160,128]{1,0:T(8,128)S(1)} collective-permute-done((f32[160,128]{1,0:T(8,128)S(1)}, f32[160,128]{1,0:T(8,128)S(1)}, u32[]{:S(2)}, u32[]{:S(2)}) %collective-permute-start.12) | collective-permute-done | bytes 81952 | tf_op jit(solution)/shard_map/ppermute | solution.py:132
  53.7 1.1 %collective-permute-done.13.refs_7_ = f32[160,128]{1,0:T(8,128)S(1)} collective-permute-done((f32[160,128]{1,0:T(8,128)S(1)}, f32[160,128]{1,0:T(8,128)S(1)}, u32[]{:S(2)}, u32[]{:S(2)}) %collective-permute-start.13) | collective-permute-done | bytes 81952 | tf_op jit(solution)/shard_map/ppermute | solution.py:132
  54.8 21.6 %cholesky.1 = (f32[512,512]{1,0:T(8,128)S(1)}, f32[4,128,128]{2,1,0:T(8,128)S(1)}, f32[128,512]{1,0:T(8,128)}) custom-call(f32[160,128]{1,0:T(8,128)S(1)} %add_add_fusion.refs_0_, f32[160,128]{1,0:T(8,128)S(1)} %collective-permute-done.7.refs_1_, f32[160,128]{1,0:T(8,128)S(1)} %collective-permute-done.8.refs_2_, ...), custom_call_target="tpu_custom_call" | custom-call | flops 268435456 | bytes 3145728 | tf_op jit(solution)/shard_map/cholesky/pallas_call | solution.py:235
  76.5 7.4 %panel.1 = f32[240,512]{1,0:T(8,128)} custom-call(f32[200,256]{1,0:T(8,128)S(1)} %constant_dynamic-update-slice_fusion.refs_0_, f32[200,256]{1,0:T(8,128)S(1)} %collective-permute-done.20.refs_1_, f32[200,256]{1,0:T(8,128)S(1)} %collective-permute-done.21.refs_2_, f32[200,256]{1,0:T(8,128)S(1)} %collective-permute-done.22.refs_3_, ...), custom_call_target="tpu_custom_call" | custom-call | tf_op jit(solution)/shard_map/panel/pallas_call | solution.py:317
  (63 shorter events, 9.4 us)
Async XLA Ops:
  5.3 14.7 %collective-permute-start = (f32[640,128]{1,0:T(8,128)S(1)}, f32[640,128]{1,0:T(8,128)S(1)}, u32[]{:S(2)}, u32[]{:S(2)}) collective-permute-start(f32[640,128]{1,0:T(8,128)S(1)} %get-tuple-element.17), channel_id=1, source_target_pairs={{0,4},{4,0},{8,12},{12,8},{16,20},{20,16},{24,28},{28,24},{1,5},{5... | collective-permute-start | bytes 983048 | tf_op jit(solution)/shard_map/ppermute | solution.py:132
  5.9 6.1 %collective-permute-start.14 = (bf16[48,512]{1,0:T(8,128)(2,1)S(1)}, bf16[48,512]{1,0:T(8,128)(2,1)S(1)}, u32[]{:S(2)}, u32[]{:S(2)}) collective-permute-start(bf16[48,512]{1,0:T(8,128)(2,1)S(1)} %get-tuple-element.31), channel_id=1, source_target_pairs={{0,1},{1,0},{2,3},{3,2},{4,5},{5,4},{6,7},{7,6},{8,9},{9,8},{10,11... | collective-permute-start | bytes 147464 | tf_op jit(solution)/shard_map/ppermute | solution.py:132
  8.5 4.1 %collective-permute-start.15 = (bf16[48,512]{1,0:T(8,128)(2,1)S(1)}, bf16[48,512]{1,0:T(8,128)(2,1)S(1)}, u32[]{:S(2)}, u32[]{:S(2)}) collective-permute-start(bf16[48,512]{1,0:T(8,128)(2,1)S(1)} %get-tuple-element.33), channel_id=1, source_target_pairs={{0,2},{1,3},{2,0},{3,1},{4,6},{5,7},{6,4},{7,5},{8,10},{9,11},{10,... | collective-permute-start | bytes 147464 | tf_op jit(solution)/shard_map/ppermute | solution.py:132
  10.0 5.0 %collective-permute-start.16 = (bf16[48,512]{1,0:T(8,128)(2,1)S(1)}, bf16[48,512]{1,0:T(8,128)(2,1)S(1)}, u32[]{:S(2)}, u32[]{:S(2)}) collective-permute-start(bf16[48,512]{1,0:T(8,128)(2,1)S(1)} %get-tuple-element.30), channel_id=1, source_target_pairs={{0,3},{1,2},{2,1},{3,0},{4,7},{5,6},{6,5},{7,4},{8,11},{9,10},{10,... | collective-permute-start | bytes 147464 | tf_op jit(solution)/shard_map/ppermute | solution.py:132
  15.4 4.1 %collective-permute-start.17 = (f32[48,256]{1,0:T(8,128)S(1)}, f32[48,256]{1,0:T(8,128)S(1)}, u32[]{:S(2)}, u32[]{:S(2)}) collective-permute-start(f32[48,256]{1,0:T(8,128)S(1)} %get-tuple-element.25), channel_id=1, source_target_pairs={{0,1},{1,0},{2,3},{3,2},{4,5},{5,4},{6,7},{7,6},{8,9},{9,8},{10,11... | collective-permute-start | bytes 147464 | tf_op jit(solution)/shard_map/ppermute | solution.py:132
  16.0 4.1 %collective-permute-start.18 = (f32[48,256]{1,0:T(8,128)S(1)}, f32[48,256]{1,0:T(8,128)S(1)}, u32[]{:S(2)}, u32[]{:S(2)}) collective-permute-start(f32[48,256]{1,0:T(8,128)S(1)} %get-tuple-element.26), channel_id=1, source_target_pairs={{0,2},{1,3},{2,0},{3,1},{4,6},{5,7},{6,4},{7,5},{8,10},{9,11},{10,... | collective-permute-start | bytes 147464 | tf_op jit(solution)/shard_map/ppermute | solution.py:132
  16.1 7.6 %collective-permute-start.19 = (f32[48,256]{1,0:T(8,128)S(1)}, f32[48,256]{1,0:T(8,128)S(1)}, u32[]{:S(2)}, u32[]{:S(2)}) collective-permute-start(f32[48,256]{1,0:T(8,128)S(1)} %get-tuple-element.27), channel_id=1, source_target_pairs={{0,3},{1,2},{2,1},{3,0},{4,7},{5,6},{6,5},{7,4},{8,11},{9,10},{10,... | collective-permute-start | bytes 147464 | tf_op jit(solution)/shard_map/ppermute | solution.py:132
  20.1 4.5 %collective-permute-start.2 = (f32[160,128]{1,0:T(8,128)S(1)}, f32[160,128]{1,0:T(8,128)S(1)}, u32[]{:S(2)}, u32[]{:S(2)}) collective-permute-start(f32[160,128]{1,0:T(8,128)S(1)} %get-tuple-element.20), channel_id=1, source_target_pairs={{0,2},{1,3},{2,0},{3,1},{4,6},{5,7},{6,4},{7,5},{8,10},{9,11},{10,... | collective-permute-start | bytes 245768 | tf_op jit(solution)/shard_map/ppermute | solution.py:132
  20.8 5.3 %collective-permute-start.3 = (f32[160,128]{1,0:T(8,128)S(1)}, f32[160,128]{1,0:T(8,128)S(1)}, u32[]{:S(2)}, u32[]{:S(2)}) collective-permute-start(f32[160,128]{1,0:T(8,128)S(1)} %get-tuple-element.21), channel_id=1, source_target_pairs={{0,3},{1,2},{2,1},{3,0},{4,7},{5,6},{6,5},{7,4},{8,11},{9,10},{10,... | collective-permute-start | bytes 245768 | tf_op jit(solution)/shard_map/ppermute | solution.py:132
  23.1 4.4 %collective-permute-start.1 = (f32[160,128]{1,0:T(8,128)S(1)}, f32[160,128]{1,0:T(8,128)S(1)}, u32[]{:S(2)}, u32[]{:S(2)}) collective-permute-start(f32[160,128]{1,0:T(8,128)S(1)} %get-tuple-element.19), channel_id=1, source_target_pairs={{0,1},{1,0},{2,3},{3,2},{4,5},{5,4},{6,7},{7,6},{8,9},{9,8},{10,11... | collective-permute-start | bytes 245768 | tf_op jit(solution)/shard_map/ppermute | solution.py:132
  27.6 7.7 %collective-permute-start.5 = (f32[160,128]{1,0:T(8,128)S(1)}, f32[160,128]{1,0:T(8,128)S(1)}, u32[]{:S(2)}, u32[]{:S(2)}) collective-permute-start(f32[160,128]{1,0:T(8,128)S(1)} %add_add_fusion.1), channel_id=1, source_target_pairs={{0,16},{4,20},{8,24},{12,28},{16,0},{20,4},{24,8},{28,12},{1,17},{... | collective-permute-start | bytes 245768 | tf_op jit(solution)/shard_map/ppermute | solution.py:132
  30.3 12.9 %collective-permute-start.6 = (f32[160,128]{1,0:T(8,128)S(1)}, f32[160,128]{1,0:T(8,128)S(1)}, u32[]{:S(2)}, u32[]{:S(2)}) collective-permute-start(f32[160,128]{1,0:T(8,128)S(1)} %add_add_fusion.1), channel_id=1, source_target_pairs={{0,24},{4,28},{8,16},{12,20},{16,8},{20,12},{24,0},{28,4},{1,25},{... | collective-permute-start | bytes 245768 | tf_op jit(solution)/shard_map/ppermute | solution.py:132
  31.6 11.5 %collective-permute-start.4 = (f32[160,128]{1,0:T(8,128)S(1)}, f32[160,128]{1,0:T(8,128)S(1)}, u32[]{:S(2)}, u32[]{:S(2)}) collective-permute-start(f32[160,128]{1,0:T(8,128)S(1)} %add_add_fusion.1), channel_id=1, source_target_pairs={{0,8},{4,12},{8,0},{12,4},{16,24},{20,28},{24,16},{28,20},{1,9},{5... | collective-permute-start | bytes 245768 | tf_op jit(solution)/shard_map/ppermute | solution.py:132
  31.8 13.3 %collective-permute-start.20 = (f32[200,256]{1,0:T(8,128)S(1)}, f32[200,256]{1,0:T(8,128)S(1)}, u32[]{:S(2)}, u32[]{:S(2)}) collective-permute-start(f32[200,256]{1,0:T(8,128)S(1)} %constant_dynamic-update-slice_fusion.refs_0_), channel_id=1, source_target_pairs={{0,8},{4,12},{8,0},{12,4},{16,24},{20,28},{24,16},{28,20},{1,9},{5... | collective-permute-start | bytes 614408 | tf_op jit(solution)/shard_map/ppermute | solution.py:132
  33.6 16.9 %collective-permute-start.21 = (f32[200,256]{1,0:T(8,128)S(1)}, f32[200,256]{1,0:T(8,128)S(1)}, u32[]{:S(2)}, u32[]{:S(2)}) collective-permute-start(f32[200,256]{1,0:T(8,128)S(1)} %constant_dynamic-update-slice_fusion.refs_0_), channel_id=1, source_target_pairs={{0,16},{4,20},{8,24},{12,28},{16,0},{20,4},{24,8},{28,12},{1,17},{... | collective-permute-start | bytes 614408 | tf_op jit(solution)/shard_map/ppermute | solution.py:132
  35.3 15.7 %collective-permute-start.22 = (f32[200,256]{1,0:T(8,128)S(1)}, f32[200,256]{1,0:T(8,128)S(1)}, u32[]{:S(2)}, u32[]{:S(2)}) collective-permute-start(f32[200,256]{1,0:T(8,128)S(1)} %constant_dynamic-update-slice_fusion.refs_0_), channel_id=1, source_target_pairs={{0,24},{4,28},{8,16},{12,20},{16,8},{20,12},{24,0},{28,4},{1,25},{... | collective-permute-start | bytes 614408 | tf_op jit(solution)/shard_map/ppermute | solution.py:132
  43.2 7.4 %collective-permute-start.7 = (f32[160,128]{1,0:T(8,128)S(1)}, f32[160,128]{1,0:T(8,128)S(1)}, u32[]{:S(2)}, u32[]{:S(2)}) collective-permute-start(f32[160,128]{1,0:T(8,128)S(1)} %add_add_fusion.refs_0_), channel_id=1, source_target_pairs={{0,1},{1,0},{2,3},{3,2},{4,5},{5,4},{6,7},{7,6},{8,9},{9,8},{10,11... | collective-permute-start | bytes 245768 | tf_op jit(solution)/shard_map/ppermute | solution.py:132
  43.6 7.6 %collective-permute-start.8 = (f32[160,128]{1,0:T(8,128)S(1)}, f32[160,128]{1,0:T(8,128)S(1)}, u32[]{:S(2)}, u32[]{:S(2)}) collective-permute-start(f32[160,128]{1,0:T(8,128)S(1)} %add_add_fusion.refs_0_), channel_id=1, source_target_pairs={{0,2},{1,3},{2,0},{3,1},{4,6},{5,7},{6,4},{7,5},{8,10},{9,11},{10,... | collective-permute-start | bytes 245768 | tf_op jit(solution)/shard_map/ppermute | solution.py:132
  45.1 6.5 %collective-permute-start.9 = (f32[160,128]{1,0:T(8,128)S(1)}, f32[160,128]{1,0:T(8,128)S(1)}, u32[]{:S(2)}, u32[]{:S(2)}) collective-permute-start(f32[160,128]{1,0:T(8,128)S(1)} %add_add_fusion.refs_0_), channel_id=1, source_target_pairs={{0,3},{1,2},{2,1},{3,0},{4,7},{5,6},{6,5},{7,4},{8,11},{9,10},{10,... | collective-permute-start | bytes 245768 | tf_op jit(solution)/shard_map/ppermute | solution.py:132
  50.6 1.5 %collective-permute-start.11 = (f32[160,128]{1,0:T(8,128)S(1)}, f32[160,128]{1,0:T(8,128)S(1)}, u32[]{:S(2)}, u32[]{:S(2)}) collective-permute-start(f32[160,128]{1,0:T(8,128)S(1)} %collective-permute-done.7.refs_1_), channel_id=1, source_target_pairs={{0,4},{4,0},{8,12},{12,8},{16,20},{20,16},{24,28},{28,24},{1,5},{5... | collective-permute-start | bytes 245768 | tf_op jit(solution)/shard_map/ppermute | solution.py:132
  51.1 25.4 %collective-permute-start.23 = (f32[200,256]{1,0:T(8,128)S(1)}, f32[200,256]{1,0:T(8,128)S(1)}, u32[]{:S(2)}, u32[]{:S(2)}) collective-permute-start(f32[200,256]{1,0:T(8,128)S(1)} %constant_dynamic-update-slice_fusion.refs_0_), channel_id=1, source_target_pairs={{0,4},{4,0},{8,12},{12,8},{16,20},{20,16},{24,28},{28,24},{1,5},{5... | collective-permute-start | bytes 614408 | tf_op jit(solution)/shard_map/ppermute | solution.py:132
  51.1 25.3 %collective-permute-start.24 = (f32[200,256]{1,0:T(8,128)S(1)}, f32[200,256]{1,0:T(8,128)S(1)}, u32[]{:S(2)}, u32[]{:S(2)}) collective-permute-start(f32[200,256]{1,0:T(8,128)S(1)} %collective-permute-done.20.refs_1_), channel_id=1, source_target_pairs={{0,4},{4,0},{8,12},{12,8},{16,20},{20,16},{24,28},{28,24},{1,5},{5... | collective-permute-start | bytes 614408 | tf_op jit(solution)/shard_map/ppermute | solution.py:132
  51.6 24.9 %collective-permute-start.25 = (f32[200,256]{1,0:T(8,128)S(1)}, f32[200,256]{1,0:T(8,128)S(1)}, u32[]{:S(2)}, u32[]{:S(2)}) collective-permute-start(f32[200,256]{1,0:T(8,128)S(1)} %collective-permute-done.21.refs_2_), channel_id=1, source_target_pairs={{0,4},{4,0},{8,12},{12,8},{16,20},{20,16},{24,28},{28,24},{1,5},{5... | collective-permute-start | bytes 614408 | tf_op jit(solution)/shard_map/ppermute | solution.py:132
  51.8 24.6 %collective-permute-start.26 = (f32[200,256]{1,0:T(8,128)S(1)}, f32[200,256]{1,0:T(8,128)S(1)}, u32[]{:S(2)}, u32[]{:S(2)}) collective-permute-start(f32[200,256]{1,0:T(8,128)S(1)} %collective-permute-done.22.refs_3_), channel_id=1, source_target_pairs={{0,4},{4,0},{8,12},{12,8},{16,20},{20,16},{24,28},{28,24},{1,5},{5... | collective-permute-start | bytes 614408 | tf_op jit(solution)/shard_map/ppermute | solution.py:132
  (10 other events, 42.8 us)

commit v2 on v1

--- a/solution.py
+++ b/solution.py
@@ -12,7 +12,12 @@
 HIGHEST = lax.Precision.HIGHEST
 VMEM = pl.BlockSpec(memory_space=pltpu.VMEM)
 SMEM = pl.BlockSpec(memory_space=pltpu.SMEM)
+ANY = pl.BlockSpec(memory_space=pl.ANY)
 PARAMS = pltpu.CompilerParams(vmem_limit_bytes=40 * 2**20)
+
+
+def long_cost(micros):
+    return pl.CostEstimate(flops=micros * 10**9, bytes_accessed=2**20, transcendentals=0)
 
 
 def split_two(value):
@@ -103,6 +108,7 @@
         out_specs=[VMEM, VMEM, VMEM],
         scratch_shapes=[pltpu.VMEM((total, BLOCK), jnp.float32)],
         compiler_params=PARAMS,
+        cost_estimate=long_cost(20),
         name="front",
     )(order, factor, border, columns)
 
@@ -187,9 +193,26 @@
     return jnp.concatenate(upper, 0), jnp.concatenate(inverse, 0)
 
 
-def cholesky_kernel(*refs, col_count):
+def eliminate(panels, first, last, upper_ref, inverse_ref):
+    count = len(panels)
+    for i in range(first, last):
+        here = slice((i - first) * BLOCK, (i - first + 1) * BLOCK)
+        own, inverse = factor_block(panels[i][:, :BLOCK])
+        if i > 0:
+            upper_ref[here, : i * BLOCK] = jnp.zeros((BLOCK, i * BLOCK), jnp.float32)
+        upper_ref[here, i * BLOCK : (i + 1) * BLOCK] = own
+        inverse_ref[i - first] = inverse
+        if i + 1 < count:
+            rest = exact(inverse, panels[i][:, BLOCK:])
+            upper_ref[here, (i + 1) * BLOCK :] = rest
+            for j in range(i + 1, count):
+                at = (j - i - 1) * BLOCK
+                panels[j] = panels[j] - exact_tn(rest[:, at : at + BLOCK], rest[:, at:])
+
+
+def early_kernel(*refs, col_count):
     pieces = refs[: 2 * col_count]
-    barrier_ref, upper_ref, inverse_ref, slice_ref, packed_ref, lower_ref = refs[2 * col_count :]
+    barrier_ref, upper_ref, inverse_ref, rest_ref, packed_ref = refs[2 * col_count :]
     width = barrier_ref.shape[1]
     count = width // BLOCK
     rows = pieces[0].shape[0]
@@ -210,83 +233,139 @@
             extra = barrier_ref[:, i * BLOCK : (i + 1) * BLOCK]
             blocks[i, j] = blocks[i, j] + jnp.where(diagonal, extra, 0.0)
     panels = [jnp.concatenate([blocks[i, j] for j in range(i, count)], 1) for i in range(count)]
-    lower_ref[...] = jnp.zeros(lower_ref.shape, jnp.float32)
-    for i in range(count):
-        here = slice(i * BLOCK, (i + 1) * BLOCK)
-        own, inverse = factor_block(panels[i][:, :BLOCK])
-        upper_ref[here, here] = own
-        inverse_ref[i] = inverse
-        lower_ref[here, here] = own.T
-        if i + 1 < count:
-            rest = exact(inverse, panels[i][:, BLOCK:])
-            upper_ref[here, (i + 1) * BLOCK :] = rest
-            for j in range(i + 1, count):
-                first = (j - i - 1) * BLOCK
-                block = rest[:, first : first + BLOCK]
-                lower_ref[j * BLOCK : (j + 1) * BLOCK, here] = block.T
-                panels[j] = panels[j] - exact_tn(block, rest[:, first:])
-    slice_rows = slice_ref.shape[0]
-    slice_ref[...] = lower_ref[pl.ds(pl.multiple_of(place * slice_rows, 8), slice_rows), :]
-
-
-def cholesky(pieces, barrier):
+    done = inverse_ref.shape[0]
+    eliminate(panels, 0, done, upper_ref, inverse_ref)
+    for i in range(done, count):
+        rest_ref[(i - done) * BLOCK : (i - done + 1) * BLOCK, (i - done) * BLOCK :] = panels[i]
+
+
+def early_cholesky(pieces, barrier):
     width = barrier.shape[0]
+    half = width // 2
     col_count = len(pieces) // 2
     return pl.pallas_call(
-        functools.partial(cholesky_kernel, col_count=col_count),
+        functools.partial(early_kernel, col_count=col_count),
         out_shape=[
-            jax.ShapeDtypeStruct((width, width), jnp.float32),
-            jax.ShapeDtypeStruct((width // BLOCK, BLOCK, BLOCK), jnp.float32),
-            jax.ShapeDtypeStruct((width // col_count, width), jnp.float32),
+            jax.ShapeDtypeStruct((half, width), jnp.float32),
+            jax.ShapeDtypeStruct((half // BLOCK, BLOCK, BLOCK), jnp.float32),
+            jax.ShapeDtypeStruct((half, half), jnp.float32),
         ],
         in_specs=[VMEM] * (len(pieces) + 1),
         out_specs=[VMEM] * 3,
-        scratch_shapes=[
-            pltpu.VMEM((len(upper_blocks(width)) * BLOCK, BLOCK), jnp.float32),
-            pltpu.VMEM((width, width), jnp.float32),
+        scratch_shapes=[pltpu.VMEM((len(upper_blocks(width)) * BLOCK, BLOCK), jnp.float32)],
+        compiler_params=PARAMS,
+        cost_estimate=long_cost(20),
+        name="early",
+    )(*pieces, barrier[None])
+
+
+def late_kernel(*refs):
+    early_ref, rest_ref = refs[:2]
+    upper_ref, inverse_ref, slice_ref, turned_ref = refs[-4:]
+    width = early_ref.shape[1]
+    count = width // BLOCK
+    done = count // 2
+    half = done * BLOCK
+    place = lax.axis_index("col")
+    panels = [None] * done + [
+        rest_ref[i * BLOCK : (i + 1) * BLOCK, i * BLOCK :] for i in range(count - done)
+    ]
+    eliminate(panels, done, count, upper_ref, inverse_ref)
+    slice_rows = slice_ref.shape[0]
+    start = place * slice_rows
+    block = pl.ds(pl.multiple_of(start // BLOCK * BLOCK, BLOCK), BLOCK)
+    turned_ref[:, :half] = early_ref[:, block].T
+    turned_ref[:, half:] = upper_ref[:, block].T
+    slice_ref[...] = turned_ref[pl.ds(pl.multiple_of(lax.rem(start, BLOCK), 8), slice_rows), :]
+
+
+def late_cholesky(early, rest, col_count, waits):
+    half, width = early.shape
+    return pl.pallas_call(
+        late_kernel,
+        out_shape=[
+            jax.ShapeDtypeStruct((half, width), jnp.float32),
+            jax.ShapeDtypeStruct((half // BLOCK, BLOCK, BLOCK), jnp.float32),
+            jax.ShapeDtypeStruct((width // col_count, width), jnp.float32),
         ],
-        compiler_params=PARAMS,
-        cost_estimate=pl.CostEstimate(
-            flops=2 * width**3, bytes_accessed=12 * width**2, transcendentals=width
-        ),
-        name="cholesky",
-    )(*pieces, barrier[None])
-
-
-def coupling_kernel(moved_ref, *refs):
-    count = len(refs) // 2
+        in_specs=[VMEM, VMEM] + [ANY] * len(waits),
+        out_specs=[VMEM] * 3,
+        scratch_shapes=[pltpu.VMEM((BLOCK, width), jnp.float32)],
+        compiler_params=PARAMS,
+        cost_estimate=long_cost(20),
+        name="late",
+    )(early, rest, *waits)
+
+
+def coupling_kernel(moved_ref, *refs, parts):
+    count = (len(refs) - parts - 1) // 2
+    refs[parts + count][...] = tree_sum([ref[...] for ref in refs[:parts]])
     moved = moved_ref[...]
-    for border_ref, out_ref in zip(refs[:count], refs[count:]):
+    for border_ref, out_ref in zip(refs[parts:], refs[parts + count + 1 :]):
         out_ref[...] = matmul_nt(border_ref[...], moved)
 
 
-def couplings(moved, borders):
+def sum_and_couplings(parts, moved, borders):
     shape = jax.ShapeDtypeStruct((borders[0].shape[0], moved.shape[0]), jnp.float32)
+    total, *partial = pl.pallas_call(
+        functools.partial(coupling_kernel, parts=len(parts)),
+        out_shape=[jax.ShapeDtypeStruct(parts[0].shape, jnp.float32)] + [shape] * len(borders),
+        in_specs=[VMEM] * (len(parts) + len(borders) + 1),
+        out_specs=[VMEM] * (len(borders) + 1),
+        compiler_params=PARAMS,
+        name="couplings",
+    )(moved, *parts, *borders)
+    return total, partial
+
+
+def assemble_kernel(columns_ref, rows_ref, *refs, parts):
+    refs[-2][...] = tree_sum([ref[...] for ref in refs[:parts]])
+    pieces, out_ref = refs[parts:-2], refs[-1]
+    place = lax.axis_index("col")
+    size, wide = pieces[0].shape
+    count = len(pieces)
+    for m, piece in enumerate(pieces):
+        out_ref[pl.ds(pl.multiple_of((place ^ m) * size, 8), size), :] = piece[...]
+    out_ref[count * size :, :] = jnp.zeros((out_ref.shape[0] - count * size, wide), jnp.float32)
+    out_ref[count * size : count * size + count, :] = columns_ref[...].astype(jnp.float32)
+    for i in range(count):
+        at = count * size + count
+        out_ref[at : at + 1, i * size : (i + 1) * size] = rows_ref[0, i : i + 1, :].astype(
+            jnp.float32
+        )
+
+
+def sum_and_assemble(parts, pieces, columns, rows):
+    size, wide = pieces[0].shape
     return pl.pallas_call(
-        coupling_kernel,
-        out_shape=[shape] * len(borders),
-        in_specs=[VMEM] * (len(borders) + 1),
-        out_specs=[VMEM] * len(borders),
-        compiler_params=PARAMS,
-        name="couplings",
-    )(moved, *borders)
-
-
-def solve_rows(rows, upper, inverse, out_ref):
-    width = rows.shape[1]
-    solved = []
-    for k in range(width // BLOCK):
-        here = slice(k * BLOCK, (k + 1) * BLOCK)
-        left = rows[:, here]
-        if k > 0:
-            left = left - exact(jnp.concatenate(solved, 1), upper[: k * BLOCK, here])
-        solved.append(exact_nt(left, inverse[k]))
-        out_ref[:, here] = solved[-1]
+        functools.partial(assemble_kernel, parts=len(parts)),
+        out_shape=[
+            jax.ShapeDtypeStruct(parts[0].shape, jnp.float32),
+            jax.ShapeDtypeStruct((len(pieces) * size + 8, wide), jnp.float32),
+        ],
+        in_specs=[VMEM] * (len(parts) + len(pieces) + 2),
+        out_specs=[VMEM] * 2,
+        compiler_params=PARAMS,
+        name="assemble",
+    )(columns, rows, *parts, *pieces)
+
+
+def solve_rows(rows, uppers, inverses, out_ref):
+    count = rows.shape[1] // BLOCK
+    done = count // 2
+    here = [slice(k * BLOCK, (k + 1) * BLOCK) for k in range(count)]
+    left = [rows[:, h] for h in here]
+    for k in range(count):
+        solved = exact_nt(left[k], inverses[k // done][k % done])
+        out_ref[:, here[k]] = solved
+        for j in range(k + 1, count):
+            left[j] = left[j] - exact(solved, uppers[k // done][here[k % done], here[j]])
 
 
 def panel_kernel(*refs, group):
-    groups = refs[:-3]
-    upper_ref, inverse_ref, out_ref = refs[-3:]
+    groups = refs[:-5]
+    out_ref = refs[-1]
+    uppers, inverses = refs[-5:-3], refs[-3:-1]
     rows_here, width = out_ref.shape
     first = lax.axis_index("scen") * rows_here
     total = jnp.zeros((rows_here, width), jnp.float32)
@@ -310,18 +389,18 @@
         ).astype(jnp.bfloat16)
         high, low = split_two(widened)
         total = total + (matmul(row_map, high) + matmul(row_map, low))
-    solve_rows(total, upper_ref[...], inverse_ref[...], out_ref)
-
-
-def panel_rows_of(groups, group, upper, inverse, rows_here):
+    solve_rows(total, uppers, inverses, out_ref)
+
+
+def panel_rows_of(groups, group, uppers, inverses, rows_here):
     return pl.pallas_call(
         functools.partial(panel_kernel, group=group),
-        out_shape=jax.ShapeDtypeStruct((rows_here, upper.shape[1]), jnp.float32),
-        in_specs=[VMEM] * (len(groups) + 2),
+        out_shape=jax.ShapeDtypeStruct((rows_here, uppers[0].shape[1]), jnp.float32),
+        in_specs=[VMEM] * (len(groups) + 4),
         out_specs=VMEM,
         compiler_params=PARAMS,
         name="panel",
-    )(*groups, upper, inverse)
+    )(*groups, *uppers, *inverses)
 
 
 def dense_panel(couplings_here, rows, columns, rows_panel, width):
@@ -378,31 +457,39 @@
     moved, keep, send = front(true_orders, inverse_factor, slab_border, slab_columns, width)
     got = swap(send, "scen", 1)
     parts = quarters(keep, got, col_count)
-    part = tree_sum([parts[0]] + [swap(parts[m], "col", m) for m in range(1, col_count)])
-    part = tree_sum([part] + [swap(part, "scen", 2 * m) for m in range(1, scen_count // 2)])
+    parts = [parts[0]] + [swap(parts[m], "col", m) for m in range(1, col_count)]
+    part, partial = sum_and_couplings(parts, moved, borders)
+    mine = [partial[0]] + [swap(partial[m], "col", m) for m in range(1, col_count)]
+    parts = [part] + [swap(part, "scen", 2 * m) for m in range(1, scen_count // 2)]
+    rows_panel = rows_here * scen_count
+    fits = group < 8 and group == col_count and group * size <= wide
+    sparse = fits and scen_count * group * size * wide < rows_panel * width
+    if sparse:
+        part, own = sum_and_assemble(parts, mine, slab_columns, panel_rows)
+    else:
+        part = tree_sum(parts)
     pieces = [part] + [swap(part, "col", m) for m in range(1, col_count)]
     pieces = pieces + [swap(piece, "scen", 1) for piece in pieces]
-    upper, inverse, factor_rows = cholesky(pieces, barrier_diag)
-
-    partial = couplings(moved, borders)
-    mine = [partial[0]] + [swap(partial[m], "col", m) for m in range(1, col_count)]
-    rows_panel = rows_here * scen_count
-    fits = group < 8 and group * size <= wide
-    if fits and scen_count * group * size * wide < rows_panel * width:
+    early, early_inverse, rest = early_cholesky(pieces, barrier_diag)
+
+    if sparse:
+        near = [own] + [swap(own, "scen", 2 * m) for m in range(1, scen_count // 2)]
+        late, late_inverse, factor_rows = late_cholesky(early, rest, col_count, near[1:])
+        groups = near + [swap(value, "scen", 1) for value in near]
+        solved = panel_rows_of(
+            groups, group, (early, late), (early_inverse, late_inverse), rows_here
+        )
+    else:
         order = jnp.stack(order)
-        rows_index = panel_rows[0][order].reshape(1, group * size)
-        rows_index = jnp.pad(rows_index, ((0, 0), (0, wide - group * size)))
-        index = jnp.concatenate([slab_columns[order], rows_index], 0).astype(jnp.float32)
-        index = jnp.pad(index, ((0, 7 - group), (0, 0)))
-        own = jnp.concatenate(mine + [index], 0)
-        near = [own] + [swap(own, "scen", 2 * m) for m in range(1, scen_count // 2)]
-        groups = near + [swap(value, "scen", 1) for value in near]
-        solved = panel_rows_of(groups, group, upper, inverse, rows_here)
-    else:
         rows = dense_panel(
-            jnp.stack(mine), panel_rows[0][jnp.stack(order)], slab_columns[jnp.stack(order)], rows_panel, width
+            jnp.stack(mine), panel_rows[0][order], slab_columns[order], rows_panel, width
         )
-        solved = dense_solve(rows, upper, inverse)
+        late, late_inverse, factor_rows = late_cholesky(early, rest, col_count, [])
+        solved = dense_solve(
+            rows,
+            jnp.concatenate([early, late], 0),
+            jnp.concatenate([early_inverse, late_inverse], 0),
+        )
     return factor_rows, solved
 
 

time: 84.1 us -> 77.9 us (0.926)
  the two profiles are of different devices: /device:TPU:0 before, /device:TPU:11 now
where the time goes in v2:
time: 77.9 us; the launch traced here: 77.7 us
  Pallas kernels  30.8 us (40%)
  starting transfers between devices  28.9 us (37%)
  waiting for transfers between devices  13.8 us (18%)
  local copies, waits for them, and re-layouts  2.71 us (3%)
  between operations  1.38 us (2%)
    ppermute x27, starting transfers between devices, swap(): return lax.ppermute(value, axis, [(i, i ^ step) for i in range(count)])  28.9 us
    ppermute x27, waiting for transfers between devices, swap(): return lax.ppermute(value, axis, [(i, i ^ step) for i in range(count)])  13.8 us
    pallas_call x1, Pallas kernels, early_cholesky(): pl.pallas_call(functools.partial(early_kernel, col_count=col_count), out_...  10.9 us
    pallas_call x1, Pallas kernels, late_cholesky(): pl.pallas_call(late_kernel, out_shape=[jax.ShapeDtypeStruct((half, width)...  10.7 us
    pallas_call x1, Pallas kernels, panel_rows_of(): pl.pallas_call(functools.partial(panel_kernel, group=group), out_shape=ja...  7.33 us
    unnamed x14, local copies, waits for them, and re-layouts  2.7 us
  transfers between devices with their start and end apart: 27, of which 7 were waited for; matrix products, arithmetic and copies ran while one was open for 0% of the time, Pallas kernels for 28%

profile of v2, /device:TPU:11, one launch (start us, length us, event | category | flops | bytes accessed | tf_op | source)
XLA Modules:
  0.0 77.7 jit_solution(2516543007756802494)
XLA Ops:
  2.0 1.0 %copy-done.3 = bf16[1,512,512]{2,1,0:T(8,128)(2,1)S(1)} copy-done((bf16[1,512,512]{2,1,0:T(8,128)(2,1)S(1)}, bf16[1,512,512]{2,1,0:T(8,128)(2,1)}, u32[]{:S(2)}) %copy-start.3) | copy-done | bytes 524312
  3.0 0.9 %copy-done.4 = bf16[1,256,512]{2,1,0:T(8,128)(2,1)S(1)} copy-done((bf16[1,256,512]{2,1,0:T(8,128)(2,1)S(1)}, bf16[1,256,512]{2,1,0:T(8,128)(2,1)}, u32[]{:S(2)}) %copy-start.4) | copy-done | bytes 262168
  4.0 1.4 %front.1 = (bf16[256,512]{1,0:T(8,128)(2,1)S(1)}, f32[640,128]{1,0:T(8,128)S(1)}, f32[640,128]{1,0:T(8,128)S(1)}) custom-call(s32[1]{0:T(128)S(6)} %copy.9.order_ref, bf16[1,512,512]{2,1,0:T(8,128)(2,1)S(1)} %copy-done.3, bf16[1,256,512]{2,1,0:T(8,128)(2,1)S(1)} %copy-done.4, s32[4,256]{1,0:T(4,128)S(1)} %copy-done), custom_call_target="tpu_custom_call" | custom-call | flops 20000000000 | bytes 1048576 | tf_op jit(solution)/shard_map/front/pallas_call | solution.py:104
  6.4 0.9 %collective-permute-done.got_ref = f32[640,128]{1,0:T(8,128)S(1)} collective-permute-done((f32[640,128]{1,0:T(8,128)S(1)}, f32[640,128]{1,0:T(8,128)S(1)}, u32[]{:S(2)}, u32[]{:S(2)}) %collective-permute-start) | collective-permute-done | bytes 327712 | tf_op jit(solution)/shard_map/ppermute | solution.py:138
  7.7 1.2 %collective-permute-start.2 = (f32[160,128]{1,0:T(8,128)S(1)}, f32[160,128]{1,0:T(8,128)S(1)}, u32[]{:S(2)}, u32[]{:S(2)}) collective-permute-start(f32[160,128]{1,0:T(8,128)S(1)} %get-tuple-element.27), channel_id=1, source_target_pairs={{0,2},{1,3},{2,0},{3,1},{4,6},{5,7},{6,4},{7,5},{8,10},{9,11},{10,... | collective-permute-start | bytes 245768 | tf_op jit(solution)/shard_map/ppermute | solution.py:138
  9.0 1.1 %collective-permute-start.3 = (f32[160,128]{1,0:T(8,128)S(1)}, f32[160,128]{1,0:T(8,128)S(1)}, u32[]{:S(2)}, u32[]{:S(2)}) collective-permute-start(f32[160,128]{1,0:T(8,128)S(1)} %get-tuple-element.28), channel_id=1, source_target_pairs={{0,3},{1,2},{2,1},{3,0},{4,7},{5,6},{6,5},{7,4},{8,11},{9,10},{10,... | collective-permute-start | bytes 245768 | tf_op jit(solution)/shard_map/ppermute | solution.py:138
  10.1 1.2 %collective-permute-start.5 = (bf16[48,512]{1,0:T(8,128)(2,1)S(1)}, bf16[48,512]{1,0:T(8,128)(2,1)S(1)}, u32[]{:S(2)}, u32[]{:S(2)}) collective-permute-start(bf16[48,512]{1,0:T(8,128)(2,1)S(1)} %get-tuple-element.45), channel_id=1, source_target_pairs={{0,2},{1,3},{2,0},{3,1},{4,6},{5,7},{6,4},{7,5},{8,10},{9,11},{10,... | collective-permute-start | bytes 147464 | tf_op jit(solution)/shard_map/ppermute | solution.py:138
  11.6 3.6 %collective-permute-done.5.refs_6_ = bf16[48,512]{1,0:T(8,128)(2,1)S(1)} collective-permute-done((bf16[48,512]{1,0:T(8,128)(2,1)S(1)}, bf16[48,512]{1,0:T(8,128)(2,1)S(1)}, u32[]{:S(2)}, u32[]{:S(2)}) %collective-permute-start.5) | collective-permute-done | bytes 49184 | tf_op jit(solution)/shard_map/ppermute | solution.py:138
  15.7 1.1 %collective-permute-start.10 = (f32[48,256]{1,0:T(8,128)S(1)}, f32[48,256]{1,0:T(8,128)S(1)}, u32[]{:S(2)}, u32[]{:S(2)}) collective-permute-start(f32[48,256]{1,0:T(8,128)S(1)} %get-tuple-element.31), channel_id=1, source_target_pairs={{0,1},{1,0},{2,3},{3,2},{4,5},{5,4},{6,7},{7,6},{8,9},{9,8},{10,11... | collective-permute-start | bytes 147464 | tf_op jit(solution)/shard_map/ppermute | solution.py:138
  17.0 2.3 %collective-permute-start.8 = (f32[160,128]{1,0:T(8,128)S(1)}, f32[160,128]{1,0:T(8,128)S(1)}, u32[]{:S(2)}, u32[]{:S(2)}) collective-permute-start(f32[160,128]{1,0:T(8,128)S(1)} %get-tuple-element.29.refs_0_), channel_id=1, source_target_pairs={{0,16},{4,20},{8,24},{12,28},{16,0},{20,4},{24,8},{28,12},{1,17},{... | collective-permute-start | bytes 245768 | tf_op jit(solution)/shard_map/ppermute | solution.py:138
  19.4 1.1 %collective-permute-start.11 = (f32[48,256]{1,0:T(8,128)S(1)}, f32[48,256]{1,0:T(8,128)S(1)}, u32[]{:S(2)}, u32[]{:S(2)}) collective-permute-start(f32[48,256]{1,0:T(8,128)S(1)} %get-tuple-element.32), channel_id=1, source_target_pairs={{0,2},{1,3},{2,0},{3,1},{4,6},{5,7},{6,4},{7,5},{8,10},{9,11},{10,... | collective-permute-start | bytes 147464 | tf_op jit(solution)/shard_map/ppermute | solution.py:138
  21.0 1.6 %collective-permute-done.11.refs_6_ = f32[48,256]{1,0:T(8,128)S(1)} collective-permute-done((f32[48,256]{1,0:T(8,128)S(1)}, f32[48,256]{1,0:T(8,128)S(1)}, u32[]{:S(2)}, u32[]{:S(2)}) %collective-permute-start.11) | collective-permute-done | bytes 49184 | tf_op jit(solution)/shard_map/ppermute | solution.py:138
  22.7 2.0 %collective-permute-done.12.refs_7_ = f32[48,256]{1,0:T(8,128)S(1)} collective-permute-done((f32[48,256]{1,0:T(8,128)S(1)}, f32[48,256]{1,0:T(8,128)S(1)}, u32[]{:S(2)}, u32[]{:S(2)}) %collective-permute-start.12) | collective-permute-done | bytes 49184 | tf_op jit(solution)/shard_map/ppermute | solution.py:138
  25.6 1.9 %collective-permute-start.15 = (f32[160,128]{1,0:T(8,128)S(1)}, f32[160,128]{1,0:T(8,128)S(1)}, u32[]{:S(2)}, u32[]{:S(2)}) collective-permute-start(f32[160,128]{1,0:T(8,128)S(1)} %get-tuple-element.34.refs_0_), channel_id=1, source_target_pairs={{0,3},{1,2},{2,1},{3,0},{4,7},{5,6},{6,5},{7,4},{8,11},{9,10},{10,... | collective-permute-start | bytes 245768 | tf_op jit(solution)/shard_map/ppermute | solution.py:138
  27.5 5.3 %collective-permute-start.16 = (f32[160,128]{1,0:T(8,128)S(1)}, f32[160,128]{1,0:T(8,128)S(1)}, u32[]{:S(2)}, u32[]{:S(2)}) collective-permute-start(f32[160,128]{1,0:T(8,128)S(1)} %get-tuple-element.34.refs_0_), channel_id=1, source_target_pairs={{0,4},{4,0},{8,12},{12,8},{16,20},{20,16},{24,28},{28,24},{1,5},{5... | collective-permute-start | bytes 245768 | tf_op jit(solution)/shard_map/ppermute | solution.py:138
  32.8 0.9 %collective-permute-start.17 = (f32[160,128]{1,0:T(8,128)S(1)}, f32[160,128]{1,0:T(8,128)S(1)}, u32[]{:S(2)}, u32[]{:S(2)}) collective-permute-start(f32[160,128]{1,0:T(8,128)S(1)} %collective-permute-done.13.refs_1_), channel_id=1, source_target_pairs={{0,4},{4,0},{8,12},{12,8},{16,20},{20,16},{24,28},{28,24},{1,5},{5... | collective-permute-start | bytes 245768 | tf_op jit(solution)/shard_map/ppermute | solution.py:138
  34.5 2.4 %collective-permute-start.19 = (f32[160,128]{1,0:T(8,128)S(1)}, f32[160,128]{1,0:T(8,128)S(1)}, u32[]{:S(2)}, u32[]{:S(2)}) collective-permute-start(f32[160,128]{1,0:T(8,128)S(1)} %collective-permute-done.15.refs_3_), channel_id=1, source_target_pairs={{0,4},{4,0},{8,12},{12,8},{16,20},{20,16},{24,28},{28,24},{1,5},{5... | collective-permute-start | bytes 245768 | tf_op jit(solution)/shard_map/ppermute | solution.py:138
  37.4 2.7 %collective-permute-start.21 = (f32[200,256]{1,0:T(8,128)S(1)}, f32[200,256]{1,0:T(8,128)S(1)}, u32[]{:S(2)}, u32[]{:S(2)}) collective-permute-start(f32[200,256]{1,0:T(8,128)S(1)} %get-tuple-element.37.refs_0_), channel_id=1, source_target_pairs={{0,16},{4,20},{8,24},{12,28},{16,0},{20,4},{24,8},{28,12},{1,17},{... | collective-permute-start | bytes 614408 | tf_op jit(solution)/shard_map/ppermute | solution.py:138
  41.0 10.9 %early.1 = (f32[256,512]{1,0:T(8,128)S(1)}, f32[2,128,128]{2,1,0:T(8,128)S(1)}, f32[256,256]{1,0:T(8,128)S(1)}) custom-call(f32[160,128]{1,0:T(8,128)S(1)} %get-tuple-element.34.refs_0_, f32[160,128]{1,0:T(8,128)S(1)} %collective-permute-done.13.refs_1_, f32[160,128]{1,0:T(8,128)S(1)} %collective-permute-done.14.refs_2_, ...), custom_call_target="tpu_custom_call" | custom-call | flops 20000000000 | bytes 1048576 | tf_op jit(solution)/shard_map/early/pallas_call | solution.py:246
  52.0 1.3 %collective-permute-done.21.refs_3_.refs_2_ = f32[200,256]{1,0:T(8,128)S(1)} collective-permute-done((f32[200,256]{1,0:T(8,128)S(1)}, f32[200,256]{1,0:T(8,128)S(1)}, u32[]{:S(2)}, u32[]{:S(2)}) %collective-permute-start.21) | collective-permute-done | bytes 204832 | tf_op jit(solution)/shard_map/ppermute | solution.py:138
  53.3 1.3 %collective-permute-start.25 = (f32[200,256]{1,0:T(8,128)S(1)}, f32[200,256]{1,0:T(8,128)S(1)}, u32[]{:S(2)}, u32[]{:S(2)}) collective-permute-start(f32[200,256]{1,0:T(8,128)S(1)} %collective-permute-done.21.refs_3_.refs_2_), channel_id=1, source_target_pairs={{0,4},{4,0},{8,12},{12,8},{16,20},{20,16},{24,28},{28,24},{1,5},{5... | collective-permute-start | bytes 614408 | tf_op jit(solution)/shard_map/ppermute | solution.py:138
  54.7 4.2 %collective-permute-done.22.refs_4_.refs_3_ = f32[200,256]{1,0:T(8,128)S(1)} collective-permute-done((f32[200,256]{1,0:T(8,128)S(1)}, f32[200,256]{1,0:T(8,128)S(1)}, u32[]{:S(2)}, u32[]{:S(2)}) %collective-permute-start.22) | collective-permute-done | bytes 204832 | tf_op jit(solution)/shard_map/ppermute | solution.py:138
  59.6 10.7 %late.1 = (f32[256,512]{1,0:T(8,128)S(1)}, f32[2,128,128]{2,1,0:T(8,128)S(1)}, f32[128,512]{1,0:T(8,128)}) custom-call(f32[256,512]{1,0:T(8,128)S(1)} %get-tuple-element.35.refs_0_.refs_8_, f32[256,256]{1,0:T(8,128)S(1)} %get-tuple-element.36.refs_1_, f32[200,256]{1,0:T(8,128)S(1)} %collective-permute-done.20.refs_2_.refs_1_, ...), custom_call_target="tpu_custom_call" | custom-call | flops 20000000000 | bytes 1048576 | tf_op jit(solution)/shard_map/late/pallas_call | solution.py:284
  70.4 7.3 %panel.1 = f32[240,512]{1,0:T(8,128)} custom-call(f32[200,256]{1,0:T(8,128)S(1)} %get-tuple-element.37.refs_0_, f32[200,256]{1,0:T(8,128)S(1)} %collective-permute-done.20.refs_2_.refs_1_, f32[200,256]{1,0:T(8,128)S(1)} %collective-permute-done.21.refs_3_.refs_2_, f32[200,256]{1,0:T(8,128)S(1)} %collective-permute-done.22.refs_4_.refs_3_, ...), custom_call_target="tpu_custom_call" | custom-call | tf_op jit(solution)/shard_map/panel/pallas_call | solution.py:396
  (52 shorter events, 7.6 us)
Async XLA Ops:
  6.1 5.2 %collective-permute-start.4 = (bf16[48,512]{1,0:T(8,128)(2,1)S(1)}, bf16[48,512]{1,0:T(8,128)(2,1)S(1)}, u32[]{:S(2)}, u32[]{:S(2)}) collective-permute-start(bf16[48,512]{1,0:T(8,128)(2,1)S(1)} %get-tuple-element.43), channel_id=1, source_target_pairs={{0,1},{1,0},{2,3},{3,2},{4,5},{5,4},{6,7},{7,6},{8,9},{9,8},{10,11... | collective-permute-start | bytes 147464 | tf_op jit(solution)/shard_map/ppermute | solution.py:138
  7.4 7.9 %collective-permute-start.1 = (f32[160,128]{1,0:T(8,128)S(1)}, f32[160,128]{1,0:T(8,128)S(1)}, u32[]{:S(2)}, u32[]{:S(2)}) collective-permute-start(f32[160,128]{1,0:T(8,128)S(1)} %get-tuple-element.26), channel_id=1, source_target_pairs={{0,1},{1,0},{2,3},{3,2},{4,5},{5,4},{6,7},{7,6},{8,9},{9,8},{10,11... | collective-permute-start | bytes 245768 | tf_op jit(solution)/shard_map/ppermute | solution.py:138
  7.7 7.5 %collective-permute-start.2 = (f32[160,128]{1,0:T(8,128)S(1)}, f32[160,128]{1,0:T(8,128)S(1)}, u32[]{:S(2)}, u32[]{:S(2)}) collective-permute-start(f32[160,128]{1,0:T(8,128)S(1)} %get-tuple-element.27), channel_id=1, source_target_pairs={{0,2},{1,3},{2,0},{3,1},{4,6},{5,7},{6,4},{7,5},{8,10},{9,11},{10,... | collective-permute-start | bytes 245768 | tf_op jit(solution)/shard_map/ppermute | solution.py:138
  9.0 6.3 %collective-permute-start.3 = (f32[160,128]{1,0:T(8,128)S(1)}, f32[160,128]{1,0:T(8,128)S(1)}, u32[]{:S(2)}, u32[]{:S(2)}) collective-permute-start(f32[160,128]{1,0:T(8,128)S(1)} %get-tuple-element.28), channel_id=1, source_target_pairs={{0,3},{1,2},{2,1},{3,0},{4,7},{5,6},{6,5},{7,4},{8,11},{9,10},{10,... | collective-permute-start | bytes 245768 | tf_op jit(solution)/shard_map/ppermute | solution.py:138
  10.1 5.1 %collective-permute-start.5 = (bf16[48,512]{1,0:T(8,128)(2,1)S(1)}, bf16[48,512]{1,0:T(8,128)(2,1)S(1)}, u32[]{:S(2)}, u32[]{:S(2)}) collective-permute-start(bf16[48,512]{1,0:T(8,128)(2,1)S(1)} %get-tuple-element.45), channel_id=1, source_target_pairs={{0,2},{1,3},{2,0},{3,1},{4,6},{5,7},{6,4},{7,5},{8,10},{9,11},{10,... | collective-permute-start | bytes 147464 | tf_op jit(solution)/shard_map/ppermute | solution.py:138
  15.7 4.9 %collective-permute-start.10 = (f32[48,256]{1,0:T(8,128)S(1)}, f32[48,256]{1,0:T(8,128)S(1)}, u32[]{:S(2)}, u32[]{:S(2)}) collective-permute-start(f32[48,256]{1,0:T(8,128)S(1)} %get-tuple-element.31), channel_id=1, source_target_pairs={{0,1},{1,0},{2,3},{3,2},{4,5},{5,4},{6,7},{7,6},{8,9},{9,8},{10,11... | collective-permute-start | bytes 147464 | tf_op jit(solution)/shard_map/ppermute | solution.py:138
  16.8 7.9 %collective-permute-start.7 = (f32[160,128]{1,0:T(8,128)S(1)}, f32[160,128]{1,0:T(8,128)S(1)}, u32[]{:S(2)}, u32[]{:S(2)}) collective-permute-start(f32[160,128]{1,0:T(8,128)S(1)} %get-tuple-element.29.refs_0_), channel_id=1, source_target_pairs={{0,8},{4,12},{8,0},{12,4},{16,24},{20,28},{24,16},{28,20},{1,9},{5... | collective-permute-start | bytes 245768 | tf_op jit(solution)/shard_map/ppermute | solution.py:138
  17.0 7.8 %collective-permute-start.8 = (f32[160,128]{1,0:T(8,128)S(1)}, f32[160,128]{1,0:T(8,128)S(1)}, u32[]{:S(2)}, u32[]{:S(2)}) collective-permute-start(f32[160,128]{1,0:T(8,128)S(1)} %get-tuple-element.29.refs_0_), channel_id=1, source_target_pairs={{0,16},{4,20},{8,24},{12,28},{16,0},{20,4},{24,8},{28,12},{1,17},{... | collective-permute-start | bytes 245768 | tf_op jit(solution)/shard_map/ppermute | solution.py:138
  19.3 5.5 %collective-permute-start.9 = (f32[160,128]{1,0:T(8,128)S(1)}, f32[160,128]{1,0:T(8,128)S(1)}, u32[]{:S(2)}, u32[]{:S(2)}) collective-permute-start(f32[160,128]{1,0:T(8,128)S(1)} %get-tuple-element.29.refs_0_), channel_id=1, source_target_pairs={{0,24},{4,28},{8,16},{12,20},{16,8},{20,12},{24,0},{28,4},{1,25},{... | collective-permute-start | bytes 245768 | tf_op jit(solution)/shard_map/ppermute | solution.py:138
  20.6 4.1 %collective-permute-start.12 = (f32[48,256]{1,0:T(8,128)S(1)}, f32[48,256]{1,0:T(8,128)S(1)}, u32[]{:S(2)}, u32[]{:S(2)}) collective-permute-start(f32[48,256]{1,0:T(8,128)S(1)} %get-tuple-element.33), channel_id=1, source_target_pairs={{0,3},{1,2},{2,1},{3,0},{4,7},{5,6},{6,5},{7,4},{8,11},{9,10},{10,... | collective-permute-start | bytes 147464 | tf_op jit(solution)/shard_map/ppermute | solution.py:138
  24.8 8.0 %collective-permute-start.13 = (f32[160,128]{1,0:T(8,128)S(1)}, f32[160,128]{1,0:T(8,128)S(1)}, u32[]{:S(2)}, u32[]{:S(2)}) collective-permute-start(f32[160,128]{1,0:T(8,128)S(1)} %get-tuple-element.34.refs_0_), channel_id=1, source_target_pairs={{0,1},{1,0},{2,3},{3,2},{4,5},{5,4},{6,7},{7,6},{8,9},{9,8},{10,11... | collective-permute-start | bytes 245768 | tf_op jit(solution)/shard_map/ppermute | solution.py:138
  25.2 8.6 %collective-permute-start.14 = (f32[160,128]{1,0:T(8,128)S(1)}, f32[160,128]{1,0:T(8,128)S(1)}, u32[]{:S(2)}, u32[]{:S(2)}) collective-permute-start(f32[160,128]{1,0:T(8,128)S(1)} %get-tuple-element.34.refs_0_), channel_id=1, source_target_pairs={{0,2},{1,3},{2,0},{3,1},{4,6},{5,7},{6,4},{7,5},{8,10},{9,11},{10,... | collective-permute-start | bytes 245768 | tf_op jit(solution)/shard_map/ppermute | solution.py:138
  25.6 8.8 %collective-permute-start.15 = (f32[160,128]{1,0:T(8,128)S(1)}, f32[160,128]{1,0:T(8,128)S(1)}, u32[]{:S(2)}, u32[]{:S(2)}) collective-permute-start(f32[160,128]{1,0:T(8,128)S(1)} %get-tuple-element.34.refs_0_), channel_id=1, source_target_pairs={{0,3},{1,2},{2,1},{3,0},{4,7},{5,6},{6,5},{7,4},{8,11},{9,10},{10,... | collective-permute-start | bytes 245768 | tf_op jit(solution)/shard_map/ppermute | solution.py:138
  27.5 9.9 %collective-permute-start.16 = (f32[160,128]{1,0:T(8,128)S(1)}, f32[160,128]{1,0:T(8,128)S(1)}, u32[]{:S(2)}, u32[]{:S(2)}) collective-permute-start(f32[160,128]{1,0:T(8,128)S(1)} %get-tuple-element.34.refs_0_), channel_id=1, source_target_pairs={{0,4},{4,0},{8,12},{12,8},{16,20},{20,16},{24,28},{28,24},{1,5},{5... | collective-permute-start | bytes 245768 | tf_op jit(solution)/shard_map/ppermute | solution.py:138
  32.8 7.3 %collective-permute-start.17 = (f32[160,128]{1,0:T(8,128)S(1)}, f32[160,128]{1,0:T(8,128)S(1)}, u32[]{:S(2)}, u32[]{:S(2)}) collective-permute-start(f32[160,128]{1,0:T(8,128)S(1)} %collective-permute-done.13.refs_1_), channel_id=1, source_target_pairs={{0,4},{4,0},{8,12},{12,8},{16,20},{20,16},{24,28},{28,24},{1,5},{5... | collective-permute-start | bytes 245768 | tf_op jit(solution)/shard_map/ppermute | solution.py:138
  33.8 6.7 %collective-permute-start.18 = (f32[160,128]{1,0:T(8,128)S(1)}, f32[160,128]{1,0:T(8,128)S(1)}, u32[]{:S(2)}, u32[]{:S(2)}) collective-permute-start(f32[160,128]{1,0:T(8,128)S(1)} %collective-permute-done.14.refs_2_), channel_id=1, source_target_pairs={{0,4},{4,0},{8,12},{12,8},{16,20},{20,16},{24,28},{28,24},{1,5},{5... | collective-permute-start | bytes 245768 | tf_op jit(solution)/shard_map/ppermute | solution.py:138
  34.5 6.6 %collective-permute-start.19 = (f32[160,128]{1,0:T(8,128)S(1)}, f32[160,128]{1,0:T(8,128)S(1)}, u32[]{:S(2)}, u32[]{:S(2)}) collective-permute-start(f32[160,128]{1,0:T(8,128)S(1)} %collective-permute-done.15.refs_3_), channel_id=1, source_target_pairs={{0,4},{4,0},{8,12},{12,8},{16,20},{20,16},{24,28},{28,24},{1,5},{5... | collective-permute-start | bytes 245768 | tf_op jit(solution)/shard_map/ppermute | solution.py:138
  36.9 15.0 %collective-permute-start.20 = (f32[200,256]{1,0:T(8,128)S(1)}, f32[200,256]{1,0:T(8,128)S(1)}, u32[]{:S(2)}, u32[]{:S(2)}) collective-permute-start(f32[200,256]{1,0:T(8,128)S(1)} %get-tuple-element.37.refs_0_), channel_id=1, source_target_pairs={{0,8},{4,12},{8,0},{12,4},{16,24},{20,28},{24,16},{28,20},{1,9},{5... | collective-permute-start | bytes 614408 | tf_op jit(solution)/shard_map/ppermute | solution.py:138
  37.4 15.9 %collective-permute-start.21 = (f32[200,256]{1,0:T(8,128)S(1)}, f32[200,256]{1,0:T(8,128)S(1)}, u32[]{:S(2)}, u32[]{:S(2)}) collective-permute-start(f32[200,256]{1,0:T(8,128)S(1)} %get-tuple-element.37.refs_0_), channel_id=1, source_target_pairs={{0,16},{4,20},{8,24},{12,28},{16,0},{20,4},{24,8},{28,12},{1,17},{... | collective-permute-start | bytes 614408 | tf_op jit(solution)/shard_map/ppermute | solution.py:138
  40.1 18.7 %collective-permute-start.22 = (f32[200,256]{1,0:T(8,128)S(1)}, f32[200,256]{1,0:T(8,128)S(1)}, u32[]{:S(2)}, u32[]{:S(2)}) collective-permute-start(f32[200,256]{1,0:T(8,128)S(1)} %get-tuple-element.37.refs_0_), channel_id=1, source_target_pairs={{0,24},{4,28},{8,16},{12,20},{16,8},{20,12},{24,0},{28,4},{1,25},{... | collective-permute-start | bytes 614408 | tf_op jit(solution)/shard_map/ppermute | solution.py:138
  40.4 29.9 %collective-permute-start.23 = (f32[200,256]{1,0:T(8,128)S(1)}, f32[200,256]{1,0:T(8,128)S(1)}, u32[]{:S(2)}, u32[]{:S(2)}) collective-permute-start(f32[200,256]{1,0:T(8,128)S(1)} %get-tuple-element.37.refs_0_), channel_id=1, source_target_pairs={{0,4},{4,0},{8,12},{12,8},{16,20},{20,16},{24,28},{28,24},{1,5},{5... | collective-permute-start | bytes 614408 | tf_op jit(solution)/shard_map/ppermute | solution.py:138
  51.9 18.4 %collective-permute-start.24 = (f32[200,256]{1,0:T(8,128)S(1)}, f32[200,256]{1,0:T(8,128)S(1)}, u32[]{:S(2)}, u32[]{:S(2)}) collective-permute-start(f32[200,256]{1,0:T(8,128)S(1)} %collective-permute-done.20.refs_2_.refs_1_), channel_id=1, source_target_pairs={{0,4},{4,0},{8,12},{12,8},{16,20},{20,16},{24,28},{28,24},{1,5},{5... | collective-permute-start | bytes 614408 | tf_op jit(solution)/shard_map/ppermute | solution.py:138
  53.3 17.0 %collective-permute-start.25 = (f32[200,256]{1,0:T(8,128)S(1)}, f32[200,256]{1,0:T(8,128)S(1)}, u32[]{:S(2)}, u32[]{:S(2)}) collective-permute-start(f32[200,256]{1,0:T(8,128)S(1)} %collective-permute-done.21.refs_3_.refs_2_), channel_id=1, source_target_pairs={{0,4},{4,0},{8,12},{12,8},{16,20},{20,16},{24,28},{28,24},{1,5},{5... | collective-permute-start | bytes 614408 | tf_op jit(solution)/shard_map/ppermute | solution.py:138
  58.8 11.5 %collective-permute-start.26 = (f32[200,256]{1,0:T(8,128)S(1)}, f32[200,256]{1,0:T(8,128)S(1)}, u32[]{:S(2)}, u32[]{:S(2)}) collective-permute-start(f32[200,256]{1,0:T(8,128)S(1)} %collective-permute-done.22.refs_4_.refs_3_), channel_id=1, source_target_pairs={{0,4},{4,0},{8,12},{12,8},{16,20},{20,16},{24,28},{28,24},{1,5},{5... | collective-permute-start | bytes 614408 | tf_op jit(solution)/shard_map/ppermute | solution.py:138
  (10 other events, 44.5 us)

commit v3 on v1

--- a/solution.py
+++ b/solution.py
@@ -12,7 +12,16 @@
 HIGHEST = lax.Precision.HIGHEST
 VMEM = pl.BlockSpec(memory_space=pltpu.VMEM)
 SMEM = pl.BlockSpec(memory_space=pltpu.SMEM)
+HBM = pl.BlockSpec(memory_space=pltpu.HBM)
 PARAMS = pltpu.CompilerParams(vmem_limit_bytes=40 * 2**20)
+
+
+def long_cost(micros):
+    return pl.CostEstimate(flops=micros * 10**9, bytes_accessed=2**20, transcendentals=0)
+
+
+def in_hbm(value):
+    return pltpu.with_memory_space_constraint(value, pltpu.HBM)
 
 
 def split_two(value):
@@ -61,23 +70,53 @@
 
 
 def front_kernel(
-    order_ref, factor_ref, border_ref, columns_ref, moved_ref, keep_ref, send_ref, packed_ref, *, width
+    order_ref,
+    columns_ref,
+    factor_ref,
+    border_ref,
+    wait_ref,
+    moved_ref,
+    keep_ref,
+    send_ref,
+    packed_ref,
+    factor_here,
+    border_here,
+    columns_here,
+    sems,
+    *,
+    width,
 ):
-    count = factor_ref.shape[0]
+    depth = factor_here.shape[0]
+    chunk = depth // 4
+    chunks = [slice(k * chunk, (k + 1) * chunk) for k in range(4)]
+    loads = [pltpu.make_async_copy(border_ref.at[0], border_here, sems.at[0])]
+    columns_load = pltpu.make_async_copy(columns_ref, columns_here, sems.at[5])
+    columns_load.start()
+    for k, at in enumerate(chunks):
+        loads.append(
+            pltpu.make_async_copy(factor_ref.at[0, at], factor_here.at[at], sems.at[k + 1])
+        )
+    for load in loads:
+        load.start()
     core = lax.rem(lax.axis_index("scen"), 2)
     place = lax.axis_index("col")
     order = order_ref[0]
-    border = border_ref[0]
+    columns_load.wait()
+    columns = columns_here[pl.ds(place, 1), :]
+    spread = (
+        lax.broadcasted_iota(jnp.int32, (width, columns.shape[1]), 0) == columns
+    ).astype(jnp.bfloat16)
+    loads[0].wait()
+    border = border_here[...]
     within = lax.broadcasted_iota(jnp.int32, border.shape, 1) < order
     inside = jnp.where(within, border.astype(jnp.float32), 0.0).astype(jnp.bfloat16)
-    product = matmul(inside, factor_ref[0])
+    product = jnp.zeros(border.shape, jnp.float32)
+    for k, at in enumerate(chunks):
+        loads[k + 1].wait()
+        product = product + matmul(inside[:, at], factor_here[at])
     moved = jnp.where(within, product, 0.0).astype(jnp.bfloat16)
     moved_ref[...] = moved
     terms = 0.5 * (matmul_nt(border, moved) + matmul_nt(moved, border))
-    columns = columns_ref[pl.ds(place * count, 1), :]
-    spread = (
-        lax.broadcasted_iota(jnp.int32, (width, columns.shape[1]), 0) == columns
-    ).astype(jnp.bfloat16)
     high, low = split_two(terms)
     half_spread = matmul_nt(high, spread) + matmul_nt(low, spread)
     high, low = split_two(half_spread)
@@ -93,38 +132,93 @@
     send_ref[...] = packed_ref[pl.ds(pl.multiple_of((1 - core) * half, 8), half), :]
 
 
-def front(order, factor, border, columns, width):
+def front(order, columns, factor, border, width, wait):
     total = len(upper_blocks(width)) * BLOCK
     half = jax.ShapeDtypeStruct((total // 2, BLOCK), jnp.float32)
     return pl.pallas_call(
         functools.partial(front_kernel, width=width),
         out_shape=[jax.ShapeDtypeStruct(border.shape[1:], jnp.bfloat16), half, half],
-        in_specs=[SMEM, VMEM, VMEM, VMEM],
+        in_specs=[SMEM, HBM, HBM, HBM, VMEM],
         out_specs=[VMEM, VMEM, VMEM],
-        scratch_shapes=[pltpu.VMEM((total, BLOCK), jnp.float32)],
+        scratch_shapes=[
+            pltpu.VMEM((total, BLOCK), jnp.float32),
+            pltpu.VMEM(factor.shape[1:], factor.dtype),
+            pltpu.VMEM(border.shape[1:], border.dtype),
+            pltpu.VMEM(columns.shape, columns.dtype),
+            pltpu.SemaphoreType.DMA((6,)),
+        ],
         compiler_params=PARAMS,
+        cost_estimate=long_cost(20),
         name="front",
-    )(order, factor, border, columns)
-
-
-def quarter_kernel(keep_ref, got_ref, *out_refs):
+    )(order, in_hbm(columns), in_hbm(factor), in_hbm(border), wait)
+
+
+def deal_kernel(border_ref, *refs):
+    out_refs, sems = refs[:-1], refs[-1]
+    place = lax.axis_index("col")
+    loads = [
+        pltpu.make_async_copy(border_ref.at[0, place ^ m], out_ref, sems.at[m])
+        for m, out_ref in enumerate(out_refs)
+    ]
+    for load in loads:
+        load.start()
+    for load in loads:
+        load.wait()
+
+
+def deal(border):
+    count = border.shape[1]
+    return pl.pallas_call(
+        deal_kernel,
+        out_shape=[jax.ShapeDtypeStruct(border.shape[2:], border.dtype)] * count,
+        in_specs=[HBM],
+        out_specs=[VMEM] * count,
+        scratch_shapes=[pltpu.SemaphoreType.DMA((count,))],
+        compiler_params=PARAMS,
+        name="deal",
+    )(in_hbm(border))
+
+
+def quarter_kernel(keep_ref, got_ref, moved_ref, *refs):
+    count = (len(refs) - 1) // 2
+    borders, own_ref, out_refs = refs[:count], refs[count], refs[count + 1 :]
     place = lax.axis_index("col")
     rows = out_refs[0].shape[0]
-    for m, out_ref in enumerate(out_refs):
+    size, wide = own_ref.shape
+    moved = moved_ref[...]
+    for m, (border_ref, out_ref) in enumerate(zip(borders, out_refs)):
         at = pl.ds(pl.multiple_of((place ^ m) * rows, 8), rows)
-        out_ref[...] = keep_ref[at, :] + got_ref[at, :]
-
-
-def quarters(keep, got, col_count):
-    piece = jax.ShapeDtypeStruct((keep.shape[0] // col_count, BLOCK), jnp.float32)
-    return pl.pallas_call(
+        if m > 0:
+            rows = out_ref.shape[0] - wide // BLOCK * size
+            at = pl.ds(pl.multiple_of((place ^ m) * rows, 8), rows)
+        coupling = matmul_nt(border_ref[...], moved)
+        out_ref[:rows, :] = keep_ref[at, :] + got_ref[at, :]
+        if m == 0:
+            own_ref[...] = coupling
+            continue
+        for n in range(wide // BLOCK):
+            out_ref[rows + n * size : rows + (n + 1) * size, :] = coupling[
+                :, n * BLOCK : (n + 1) * BLOCK
+            ]
+
+
+def quarters(keep, got, moved, borders):
+    count = len(borders)
+    rows = keep.shape[0] // count
+    size, wide = borders[0].shape[0], moved.shape[0]
+    rider = wide // BLOCK * size
+    out_shape = [jax.ShapeDtypeStruct((size, wide), jnp.float32)]
+    out_shape += [jax.ShapeDtypeStruct((rows, BLOCK), jnp.float32)]
+    out_shape += [jax.ShapeDtypeStruct((rows + rider, BLOCK), jnp.float32)] * (count - 1)
+    own, *parts = pl.pallas_call(
         quarter_kernel,
-        out_shape=[piece] * col_count,
-        in_specs=[VMEM, VMEM],
-        out_specs=[VMEM] * col_count,
+        out_shape=out_shape,
+        in_specs=[VMEM] * (3 + count),
+        out_specs=[VMEM] * (1 + count),
         compiler_params=PARAMS,
         name="quarters",
-    )(keep, got)
+    )(keep, got, moved, *borders)
+    return own, parts
 
 
 def swap(value, axis, step):
@@ -187,9 +281,26 @@
     return jnp.concatenate(upper, 0), jnp.concatenate(inverse, 0)
 
 
+def eliminate(panels, first, last, upper_ref, inverse_ref):
+    count = len(panels)
+    for i in range(first, last):
+        here = slice((i - first) * BLOCK, (i - first + 1) * BLOCK)
+        own, inverse = factor_block(panels[i][:, :BLOCK])
+        if i > 0:
+            upper_ref[here, : i * BLOCK] = jnp.zeros((BLOCK, i * BLOCK), jnp.float32)
+        upper_ref[here, i * BLOCK : (i + 1) * BLOCK] = own
+        inverse_ref[i - first] = inverse
+        if i + 1 < count:
+            rest = exact(inverse, panels[i][:, BLOCK:])
+            upper_ref[here, (i + 1) * BLOCK :] = rest
+            for j in range(i + 1, count):
+                at = (j - i - 1) * BLOCK
+                panels[j] = panels[j] - exact_tn(rest[:, at : at + BLOCK], rest[:, at:])
+
+
 def cholesky_kernel(*refs, col_count):
     pieces = refs[: 2 * col_count]
-    barrier_ref, upper_ref, inverse_ref, slice_ref, packed_ref, lower_ref = refs[2 * col_count :]
+    barrier_ref, upper_ref, inverse_ref, slice_ref, packed_ref, turned_ref = refs[2 * col_count :]
     width = barrier_ref.shape[1]
     count = width // BLOCK
     rows = pieces[0].shape[0]
@@ -210,23 +321,12 @@
             extra = barrier_ref[:, i * BLOCK : (i + 1) * BLOCK]
             blocks[i, j] = blocks[i, j] + jnp.where(diagonal, extra, 0.0)
     panels = [jnp.concatenate([blocks[i, j] for j in range(i, count)], 1) for i in range(count)]
-    lower_ref[...] = jnp.zeros(lower_ref.shape, jnp.float32)
-    for i in range(count):
-        here = slice(i * BLOCK, (i + 1) * BLOCK)
-        own, inverse = factor_block(panels[i][:, :BLOCK])
-        upper_ref[here, here] = own
-        inverse_ref[i] = inverse
-        lower_ref[here, here] = own.T
-        if i + 1 < count:
-            rest = exact(inverse, panels[i][:, BLOCK:])
-            upper_ref[here, (i + 1) * BLOCK :] = rest
-            for j in range(i + 1, count):
-                first = (j - i - 1) * BLOCK
-                block = rest[:, first : first + BLOCK]
-                lower_ref[j * BLOCK : (j + 1) * BLOCK, here] = block.T
-                panels[j] = panels[j] - exact_tn(block, rest[:, first:])
+    eliminate(panels, 0, count, upper_ref, inverse_ref)
     slice_rows = slice_ref.shape[0]
-    slice_ref[...] = lower_ref[pl.ds(pl.multiple_of(place * slice_rows, 8), slice_rows), :]
+    start = place * slice_rows
+    block = pl.ds(pl.multiple_of(start // BLOCK * BLOCK, BLOCK), BLOCK)
+    turned_ref[...] = upper_ref[:, block].T
+    slice_ref[...] = turned_ref[pl.ds(pl.multiple_of(lax.rem(start, BLOCK), 8), slice_rows), :]
 
 
 def cholesky(pieces, barrier):
@@ -243,85 +343,108 @@
         out_specs=[VMEM] * 3,
         scratch_shapes=[
             pltpu.VMEM((len(upper_blocks(width)) * BLOCK, BLOCK), jnp.float32),
-            pltpu.VMEM((width, width), jnp.float32),
+            pltpu.VMEM((BLOCK, width), jnp.float32),
         ],
         compiler_params=PARAMS,
-        cost_estimate=pl.CostEstimate(
-            flops=2 * width**3, bytes_accessed=12 * width**2, transcendentals=width
-        ),
+        cost_estimate=long_cost(40),
         name="cholesky",
     )(*pieces, barrier[None])
 
 
-def coupling_kernel(moved_ref, *refs):
-    count = len(refs) // 2
-    moved = moved_ref[...]
-    for border_ref, out_ref in zip(refs[:count], refs[count:]):
-        out_ref[...] = matmul_nt(border_ref[...], moved)
-
-
-def couplings(moved, borders):
-    shape = jax.ShapeDtypeStruct((borders[0].shape[0], moved.shape[0]), jnp.float32)
+def assemble_kernel(columns_ref, rows_ref, own_ref, *refs):
+    parts, total_ref, out_ref = refs[:-2], refs[-2], refs[-1]
+    rows = total_ref.shape[0]
+    total_ref[...] = tree_sum([part[:rows, :] for part in parts])
+    place = lax.axis_index("col")
+    size, wide = own_ref.shape
+    count = len(parts)
+    out_ref[pl.ds(pl.multiple_of(place * size, 8), size), :] = own_ref[...]
+    for m in range(1, count):
+        at = pl.ds(pl.multiple_of((place ^ m) * size, 8), size)
+        for n in range(wide // BLOCK):
+            out_ref[at, n * BLOCK : (n + 1) * BLOCK] = parts[m][
+                rows + n * size : rows + (n + 1) * size, :
+            ]
+    out_ref[count * size :, :] = jnp.zeros((out_ref.shape[0] - count * size, wide), jnp.float32)
+    out_ref[count * size : count * size + count, :] = columns_ref[...].astype(jnp.float32)
+    at = count * size + count
+    out_ref[at : at + count, :size] = rows_ref[0].astype(jnp.float32)
+
+
+def sum_and_assemble(parts, own, columns, rows):
+    size, wide = own.shape
     return pl.pallas_call(
-        coupling_kernel,
-        out_shape=[shape] * len(borders),
-        in_specs=[VMEM] * (len(borders) + 1),
-        out_specs=[VMEM] * len(borders),
+        assemble_kernel,
+        out_shape=[
+            jax.ShapeDtypeStruct(parts[0].shape, jnp.float32),
+            jax.ShapeDtypeStruct((len(parts) * size + -(-len(parts) // 4) * 8, wide), jnp.float32),
+        ],
+        in_specs=[VMEM] * (len(parts) + 3),
+        out_specs=[VMEM] * 2,
         compiler_params=PARAMS,
-        name="couplings",
-    )(moved, *borders)
+        name="assemble",
+    )(columns, rows, own, *parts)
 
 
 def solve_rows(rows, upper, inverse, out_ref):
-    width = rows.shape[1]
-    solved = []
-    for k in range(width // BLOCK):
-        here = slice(k * BLOCK, (k + 1) * BLOCK)
-        left = rows[:, here]
-        if k > 0:
-            left = left - exact(jnp.concatenate(solved, 1), upper[: k * BLOCK, here])
-        solved.append(exact_nt(left, inverse[k]))
-        out_ref[:, here] = solved[-1]
-
-
-def panel_kernel(*refs, group):
-    groups = refs[:-3]
-    upper_ref, inverse_ref, out_ref = refs[-3:]
+    count = rows.shape[1] // BLOCK
+    here = [slice(k * BLOCK, (k + 1) * BLOCK) for k in range(count)]
+    left = [rows[:, h] for h in here]
+    for k in range(count):
+        solved = exact_nt(left[k], inverse[k])
+        out_ref[:, here[k]] = solved
+        for j in range(k + 1, count):
+            left[j] = left[j] - exact(solved, upper[here[k], here[j]])
+
+
+def panel_kernel(source_ref, upper_ref, inverse_ref, out_ref, groups_ref, sems, *, group):
+    loads = [
+        pltpu.make_async_copy(source_ref.at[s], groups_ref.at[s], sems.at[s])
+        for s in range(source_ref.shape[0])
+    ]
+    for load in loads:
+        load.start()
     rows_here, width = out_ref.shape
     first = lax.axis_index("scen") * rows_here
     total = jnp.zeros((rows_here, width), jnp.float32)
-    for group_ref in groups:
-        wide = group_ref.shape[1]
-        size = (group_ref.shape[0] - 8) // group
-        index = group_ref[group * size :, :]
+    size = (groups_ref.shape[1] - 2 * group) // group
+    wide = groups_ref.shape[2]
+    for s in range(groups_ref.shape[0]):
+        loads[s].wait()
+        index = groups_ref[s, group * size :, :]
         spreads = []
         for i in range(group):
             columns = index[i : i + 1, :].astype(jnp.int32)
             spread = lax.broadcasted_iota(jnp.int32, (width, wide), 0) == columns
-            high, low = split_two(group_ref[i * size : (i + 1) * size, :])
-            both = matmul_nt(
-                jnp.concatenate([high, low], 0), spread.astype(jnp.bfloat16)
-            )
+            high, low = split_two(groups_ref[s, i * size : (i + 1) * size, :])
+            both = matmul_nt(jnp.concatenate([high, low], 0), spread.astype(jnp.bfloat16))
             spreads.append(both[:size] + both[size:])
         widened = jnp.concatenate(spreads, 0)
-        row_index = index[group : group + 1, : group * size].astype(jnp.int32) - first
+        row_index = jnp.concatenate(
+            [index[group + i : group + i + 1, :size] for i in range(group)], 1
+        )
+        row_index = row_index.astype(jnp.int32) - first
         row_map = (
             lax.broadcasted_iota(jnp.int32, (rows_here, group * size), 0) == row_index
         ).astype(jnp.bfloat16)
         high, low = split_two(widened)
         total = total + (matmul(row_map, high) + matmul(row_map, low))
-    solve_rows(total, upper_ref[...], inverse_ref[...], out_ref)
+    solve_rows(total, upper_ref, inverse_ref, out_ref)
 
 
 def panel_rows_of(groups, group, upper, inverse, rows_here):
     return pl.pallas_call(
         functools.partial(panel_kernel, group=group),
         out_shape=jax.ShapeDtypeStruct((rows_here, upper.shape[1]), jnp.float32),
-        in_specs=[VMEM] * (len(groups) + 2),
+        in_specs=[HBM, VMEM, VMEM],
         out_specs=VMEM,
+        scratch_shapes=[
+            pltpu.VMEM(groups.shape, groups.dtype),
+            pltpu.SemaphoreType.DMA((groups.shape[0],)),
+        ],
         compiler_params=PARAMS,
         name="panel",
-    )(*groups, upper, inverse)
+    )(in_hbm(groups), upper, inverse)
 
 
 def dense_panel(couplings_here, rows, columns, rows_panel, width):
@@ -363,45 +486,32 @@
 ):
     scen_count = lax.axis_size("scen")
     col_count = lax.axis_size("col")
-    place = lax.axis_index("col")
     width = barrier_diag.shape[0]
-    group, size, depth = panel_border.shape[1:]
+    group, size = panel_border.shape[1:3]
     wide = slab_columns.shape[1]
 
-    order = [place ^ m for m in range(col_count)]
-    own_borders = [
-        lax.dynamic_index_in_dim(panel_border[0], order[m], 0, keepdims=False)
-        for m in range(col_count)
-    ]
-    borders = [own_borders[0]] + [swap(own_borders[m], "col", m) for m in range(1, col_count)]
-
-    moved, keep, send = front(true_orders, inverse_factor, slab_border, slab_columns, width)
+    dealt = deal(panel_border)
+    borders = [dealt[0]] + [swap(dealt[m], "col", m) for m in range(1, col_count)]
+    moved, keep, send = front(
+        true_orders, slab_columns, inverse_factor, slab_border, width, dealt[0]
+    )
     got = swap(send, "scen", 1)
-    parts = quarters(keep, got, col_count)
-    part = tree_sum([parts[0]] + [swap(parts[m], "col", m) for m in range(1, col_count)])
+    own, parts = quarters(keep, got, moved, borders)
+    parts = [parts[0]] + [swap(parts[m], "col", m) for m in range(1, col_count)]
+    part, own = sum_and_assemble(parts, own, slab_columns, panel_rows)
+    rows_panel = rows_here * scen_count
+    sparse = scen_count * group * size * wide < rows_panel * width
+    if sparse:
+        groups = lax.all_gather(own, "scen")
     part = tree_sum([part] + [swap(part, "scen", 2 * m) for m in range(1, scen_count // 2)])
     pieces = [part] + [swap(part, "col", m) for m in range(1, col_count)]
     pieces = pieces + [swap(piece, "scen", 1) for piece in pieces]
     upper, inverse, factor_rows = cholesky(pieces, barrier_diag)
-
-    partial = couplings(moved, borders)
-    mine = [partial[0]] + [swap(partial[m], "col", m) for m in range(1, col_count)]
-    rows_panel = rows_here * scen_count
-    fits = group < 8 and group * size <= wide
-    if fits and scen_count * group * size * wide < rows_panel * width:
-        order = jnp.stack(order)
-        rows_index = panel_rows[0][order].reshape(1, group * size)
-        rows_index = jnp.pad(rows_index, ((0, 0), (0, wide - group * size)))
-        index = jnp.concatenate([slab_columns[order], rows_index], 0).astype(jnp.float32)
-        index = jnp.pad(index, ((0, 7 - group), (0, 0)))
-        own = jnp.concatenate(mine + [index], 0)
-        near = [own] + [swap(own, "scen", 2 * m) for m in range(1, scen_count // 2)]
-        groups = near + [swap(value, "scen", 1) for value in near]
+    if sparse:
         solved = panel_rows_of(groups, group, upper, inverse, rows_here)
     else:
-        rows = dense_panel(
-            jnp.stack(mine), panel_rows[0][jnp.stack(order)], slab_columns[jnp.stack(order)], rows_panel, width
-        )
+        local = own[: group * size].reshape(group, size, wide)
+        rows = dense_panel(local, panel_rows[0], slab_columns, rows_panel, width)
         solved = dense_solve(rows, upper, inverse)
     return factor_rows, solved
 

time: 84.1 us -> 87.4 us (1.039)
  starting transfers between devices: 32.6 us -> 16 us
  between operations: 1.4 us -> 14.8 us
  waiting for transfers between devices: 14.3 us -> 21.2 us
  local copies, waits for them, and re-layouts: 4.53 us -> 0.02 us
  Pallas kernels: 30.8 us -> 35.2 us
    ppermute x27 -> x17, starting transfers between devices: 32.6 us -> 15.9 us  [swap(): return lax.ppermute(value, axis, [(i, i ^ step) for i in range(count)])]
    ppermute x27 -> x17, waiting for transfers between devices: 14.3 us -> 19.8 us  [swap(): return lax.ppermute(value, axis, [(i, i ^ step) for i in range(count)])]
    unnamed x18 -> x6, local copies, waits for them, and re-layouts: 3.31 us -> 0.02 us
    pallas_call x2 -> x3, Pallas kernels: 0.44 us -> 2.05 us  [the longest x1 0.91 us: deal(): pl.pallas_call(deal_kernel, out_shape=[jax.ShapeDtypeStruct(border.shape[...]
    pallas_call x1, Pallas kernels: 7.38 us -> 8.9 us  [panel_rows_of(): pl.pallas_call(functools.partial(panel_kernel, group=group), out_shape=ja...]
    all_gather x0 -> x1, waiting for transfers between devices: none -> 1.46 us  [shards(): groups = lax.all_gather(own, 'scen')]
    pallas_call x1, Pallas kernels: 1.36 us -> 2.65 us  [front(): pl.pallas_call(functools.partial(front_kernel, width=width), out_shape=[j...]
    gather x2 -> x0, local copies, waits for them, and re-layouts: 1.12 us -> none  [the longest x1 0.56 us: shards(): slab_columns[order]]
  transfers between devices with their start and end apart: 27 -> 18, of which waited for: 11 -> 13; matrix products, arithmetic and copies ran while one was open for 2% -> 0% of each run, Pallas kernels for 26% -> 25%
where the time goes in v3:
time: 87.4 us; the launch traced here: 87.2 us
  Pallas kernels  35.2 us (40%)
  waiting for transfers between devices  21.2 us (24%)
  starting transfers between devices  16 us (18%)
  between operations  14.8 us (17%)
    pallas_call x1, Pallas kernels, cholesky(): pl.pallas_call(functools.partial(cholesky_kernel, col_count=col_count), o...  21.6 us
    ppermute x17, waiting for transfers between devices, swap(): return lax.ppermute(value, axis, [(i, i ^ step) for i in range(count)])  19.8 us
    ppermute x17, starting transfers between devices, swap(): return lax.ppermute(value, axis, [(i, i ^ step) for i in range(count)])  15.9 us
    pallas_call x1, Pallas kernels, panel_rows_of(): pl.pallas_call(functools.partial(panel_kernel, group=group), out_shape=ja...  8.9 us
    pallas_call x1, Pallas kernels, front(): pl.pallas_call(functools.partial(front_kernel, width=width), out_shape=[j...  2.65 us
  transfers between devices with their start and end apart: 18, of which 13 were waited for; matrix products, arithmetic and copies ran while one was open for 0% of the time, Pallas kernels for 25%

profile of v3, /device:TPU:0, one launch (start us, length us, event | category | flops | bytes accessed | tf_op | source)
XLA Modules:
  0.0 87.2 jit_solution(16399209409168599291)
XLA Ops:
  7.9 0.9 %deal.1 = (bf16[48,512]{1,0:T(8,128)(2,1)S(1)}, bf16[48,512]{1,0:T(8,128)(2,1)S(1)}, bf16[48,512]{1,0:T(8,128)(2,1)S(1)}, bf16[48,512]{1,0:T(8,128)(2,1)S(1)}) custom-call(bf16[1,4,48,512]{3,2,1,0:T(8,128)(2,1)} %border_ref.2), custom_call_target="tpu_custom_call" | custom-call | tf_op jit(solution)/shard_map/deal/pallas_call | solution.py:171
  8.8 2.7 %front.1 = (bf16[256,512]{1,0:T(8,128)(2,1)S(1)}, f32[640,128]{1,0:T(8,128)S(1)}, f32[640,128]{1,0:T(8,128)S(1)}) custom-call(s32[1]{0:T(128)S(6)} %copy.9.order_ref, s32[4,256]{1,0:T(4,128)} %columns_ref.3, bf16[1,512,512]{2,1,0:T(8,128)(2,1)} %factor_ref.1, bf16[1,256,512]{2,1,0:T(8,128)(2,1)} %border_ref.3, ...), custom_call_target="tpu_custom_call" | custom-call | flops 20000000000 | bytes 1048576 | tf_op jit(solution)/shard_map/front/pallas_call | solution.py:138
  12.0 2.6 %collective-permute-start.1 = (bf16[48,512]{1,0:T(8,128)(2,1)S(1)}, bf16[48,512]{1,0:T(8,128)(2,1)S(1)}, u32[]{:S(2)}, u32[]{:S(2)}) collective-permute-start(bf16[48,512]{1,0:T(8,128)(2,1)S(1)} %get-tuple-element.23), channel_id=1, source_target_pairs={{0,1},{1,0},{2,3},{3,2},{4,5},{5,4},{6,7},{7,6},{8,9},{9,8},{10,11... | collective-permute-start | bytes 147464 | tf_op jit(solution)/shard_map/ppermute | solution.py:226
  14.6 1.5 %collective-permute-start.2 = (bf16[48,512]{1,0:T(8,128)(2,1)S(1)}, bf16[48,512]{1,0:T(8,128)(2,1)S(1)}, u32[]{:S(2)}, u32[]{:S(2)}) collective-permute-start(bf16[48,512]{1,0:T(8,128)(2,1)S(1)} %get-tuple-element.24), channel_id=1, source_target_pairs={{0,2},{1,3},{2,0},{3,1},{4,6},{5,7},{6,4},{7,5},{8,10},{9,11},{10,... | collective-permute-start | bytes 147464 | tf_op jit(solution)/shard_map/ppermute | solution.py:226
  16.1 0.8 collective-permute-done.1.refs_1_
  16.9 1.8 %collective-permute-done.2.refs_2_ = bf16[48,512]{1,0:T(8,128)(2,1)S(1)} collective-permute-done((bf16[48,512]{1,0:T(8,128)(2,1)S(1)}, bf16[48,512]{1,0:T(8,128)(2,1)S(1)}, u32[]{:S(2)}, u32[]{:S(2)}) %collective-permute-start.2) | collective-permute-done | bytes 49184 | tf_op jit(solution)/shard_map/ppermute | solution.py:226
  18.6 2.4 %collective-permute-done.3.refs_3_ = bf16[48,512]{1,0:T(8,128)(2,1)S(1)} collective-permute-done((bf16[48,512]{1,0:T(8,128)(2,1)S(1)}, bf16[48,512]{1,0:T(8,128)(2,1)S(1)}, u32[]{:S(2)}, u32[]{:S(2)}) %collective-permute-start.3) | collective-permute-done | bytes 49184 | tf_op jit(solution)/shard_map/ppermute | solution.py:226
  22.2 2.8 %collective-permute-start.6 = (f32[256,128]{1,0:T(8,128)S(1)}, f32[256,128]{1,0:T(8,128)S(1)}, u32[]{:S(2)}, u32[]{:S(2)}) collective-permute-start(f32[256,128]{1,0:T(8,128)S(1)} %get-tuple-element.30), channel_id=1, source_target_pairs={{0,3},{1,2},{2,1},{3,0},{4,7},{5,6},{6,5},{7,4},{8,11},{9,10},{10,... | collective-permute-start | bytes 393224 | tf_op jit(solution)/shard_map/ppermute | solution.py:226
  25.0 2.1 %collective-permute-done.4.refs_1_ = f32[256,128]{1,0:T(8,128)S(1)} collective-permute-done((f32[256,128]{1,0:T(8,128)S(1)}, f32[256,128]{1,0:T(8,128)S(1)}, u32[]{:S(2)}, u32[]{:S(2)}) %collective-permute-start.4) | collective-permute-done | bytes 131104 | tf_op jit(solution)/shard_map/ppermute | solution.py:226
  27.1 1.7 %collective-permute-done.5.refs_2_ = f32[256,128]{1,0:T(8,128)S(1)} collective-permute-done((f32[256,128]{1,0:T(8,128)S(1)}, f32[256,128]{1,0:T(8,128)S(1)}, u32[]{:S(2)}, u32[]{:S(2)}) %collective-permute-start.5) | collective-permute-done | bytes 131104 | tf_op jit(solution)/shard_map/ppermute | solution.py:226
  28.8 0.7 assemble.1
  29.5 2.7 %collective-permute-start.8 = (f32[160,128]{1,0:T(8,128)S(1)}, f32[160,128]{1,0:T(8,128)S(1)}, u32[]{:S(2)}, u32[]{:S(2)}) collective-permute-start(f32[160,128]{1,0:T(8,128)S(1)} %get-tuple-element.31), channel_id=1, source_target_pairs={{0,16},{4,20},{8,24},{12,28},{16,0},{20,4},{24,8},{28,12},{1,17},{... | collective-permute-start | bytes 245768 | tf_op jit(solution)/shard_map/ppermute | solution.py:226
  32.2 1.3 %collective-permute-start.9 = (f32[160,128]{1,0:T(8,128)S(1)}, f32[160,128]{1,0:T(8,128)S(1)}, u32[]{:S(2)}, u32[]{:S(2)}) collective-permute-start(f32[160,128]{1,0:T(8,128)S(1)} %get-tuple-element.31), channel_id=1, source_target_pairs={{0,24},{4,28},{8,16},{12,20},{16,8},{20,12},{24,0},{28,4},{1,25},{... | collective-permute-start | bytes 245768 | tf_op jit(solution)/shard_map/ppermute | solution.py:226
  33.7 2.7 %collective-permute-done.8 = f32[160,128]{1,0:T(8,128)S(1)} collective-permute-done((f32[160,128]{1,0:T(8,128)S(1)}, f32[160,128]{1,0:T(8,128)S(1)}, u32[]{:S(2)}, u32[]{:S(2)}) %collective-permute-start.8) | collective-permute-done | bytes 81952 | tf_op jit(solution)/shard_map/ppermute | solution.py:226
  36.4 2.1 %collective-permute-done.9 = f32[160,128]{1,0:T(8,128)S(1)} collective-permute-done((f32[160,128]{1,0:T(8,128)S(1)}, f32[160,128]{1,0:T(8,128)S(1)}, u32[]{:S(2)}, u32[]{:S(2)}) %collective-permute-start.9) | collective-permute-done | bytes 81952 | tf_op jit(solution)/shard_map/ppermute | solution.py:226
  38.9 1.9 %collective-permute-start.10 = (f32[160,128]{1,0:T(8,128)S(1)}, f32[160,128]{1,0:T(8,128)S(1)}, u32[]{:S(2)}, u32[]{:S(2)}) collective-permute-start(f32[160,128]{1,0:T(8,128)S(1)} %add_add_fusion.refs_0_), channel_id=1, source_target_pairs={{0,1},{1,0},{2,3},{3,2},{4,5},{5,4},{6,7},{7,6},{8,9},{9,8},{10,11... | collective-permute-start | bytes 245768 | tf_op jit(solution)/shard_map/ppermute | solution.py:226
  40.7 1.1 %collective-permute-start.11 = (f32[160,128]{1,0:T(8,128)S(1)}, f32[160,128]{1,0:T(8,128)S(1)}, u32[]{:S(2)}, u32[]{:S(2)}) collective-permute-start(f32[160,128]{1,0:T(8,128)S(1)} %add_add_fusion.refs_0_), channel_id=1, source_target_pairs={{0,2},{1,3},{2,0},{3,1},{4,6},{5,7},{6,4},{7,5},{8,10},{9,11},{10,... | collective-permute-start | bytes 245768 | tf_op jit(solution)/shard_map/ppermute | solution.py:226
  42.4 0.9 %collective-permute-done.10.refs_1_ = f32[160,128]{1,0:T(8,128)S(1)} collective-permute-done((f32[160,128]{1,0:T(8,128)S(1)}, f32[160,128]{1,0:T(8,128)S(1)}, u32[]{:S(2)}, u32[]{:S(2)}) %collective-permute-start.10) | collective-permute-done | bytes 81952 | tf_op jit(solution)/shard_map/ppermute | solution.py:226
  43.4 1.8 %collective-permute-done.11.refs_2_ = f32[160,128]{1,0:T(8,128)S(1)} collective-permute-done((f32[160,128]{1,0:T(8,128)S(1)}, f32[160,128]{1,0:T(8,128)S(1)}, u32[]{:S(2)}, u32[]{:S(2)}) %collective-permute-start.11) | collective-permute-done | bytes 81952 | tf_op jit(solution)/shard_map/ppermute | solution.py:226
  45.2 2.0 %collective-permute-done.12.refs_3_ = f32[160,128]{1,0:T(8,128)S(1)} collective-permute-done((f32[160,128]{1,0:T(8,128)S(1)}, f32[160,128]{1,0:T(8,128)S(1)}, u32[]{:S(2)}, u32[]{:S(2)}) %collective-permute-start.12) | collective-permute-done | bytes 81952 | tf_op jit(solution)/shard_map/ppermute | solution.py:226
  47.2 1.2 %collective-permute-done.16.refs_7_ = f32[160,128]{1,0:T(8,128)S(1)} collective-permute-done((f32[160,128]{1,0:T(8,128)S(1)}, f32[160,128]{1,0:T(8,128)S(1)}, u32[]{:S(2)}, u32[]{:S(2)}) %collective-permute-start.16) | collective-permute-done | bytes 81952 | tf_op jit(solution)/shard_map/ppermute | solution.py:226
  48.4 21.6 %cholesky.1 = (f32[512,512]{1,0:T(8,128)S(1)}, f32[4,128,128]{2,1,0:T(8,128)S(1)}, f32[128,512]{1,0:T(8,128)}) custom-call(f32[160,128]{1,0:T(8,128)S(1)} %add_add_fusion.refs_0_, f32[160,128]{1,0:T(8,128)S(1)} %collective-permute-done.10.refs_1_, f32[160,128]{1,0:T(8,128)S(1)} %collective-permute-done.11.refs_2_, ...), custom_call_target="tpu_custom_call" | custom-call | flops 40000000000 | bytes 1048576 | tf_op jit(solution)/shard_map/cholesky/pallas_call | solution.py:335
  70.0 1.5 %all-gather.3.cloned.1.call-done = f32[1600,256]{1,0:T(8,128)} async-done(((f32[200,256]{1,0:T(8,128)}), f32[1600,256]{1,0:T(8,128)}) %all-gather.3.cloned.1.call-update) | async-done | bytes 1638416 | tf_op jit(solution)/shard_map/all_gather | solution.py:505
  71.4 8.9 %panel.1 = f32[240,512]{1,0:T(8,128)} custom-call(f32[8,200,256]{2,1,0:T(8,128)} %bitcast.3, f32[512,512]{1,0:T(8,128)S(1)} %get-tuple-element.34.upper_ref, f32[4,128,128]{2,1,0:T(8,128)S(1)} %get-tuple-element.35.inverse_ref), custom_call_target="tpu_custom_call" | custom-call | tf_op jit(solution)/shard_map/panel/pallas_call | solution.py:436
  (26 shorter events, 2.9 us)
Async XLA Ops:
  7.2 64.3 %all-gather.3.cloned.1.call-start = ((), (), s32[]{:S(2)}) async-start(), calls=%async_computation | async-start | bytes 1843200 | tf_op jit(solution)/shard_map/all_gather | solution.py:505
  8.8 20.0 %copy-start = (s32[4,256]{1,0:T(4,128)S(1)}, s32[4,256]{1,0:T(4,128)}, u32[]{:S(2)}) copy-start(s32[4,256]{1,0:T(4,128)} %columns_ref.3) | copy-start | bytes 12292
  8.8 20.0 %copy-start.1 = (s32[1,4,48]{2,1,0:T(4,128)S(1)}, s32[1,4,48]{2,1,0:T(4,128)}, u32[]{:S(2)}) copy-start(s32[1,4,48]{2,1,0:T(4,128)} %rows_ref.1) | copy-start | bytes 2308
  11.5 36.9 %copy-start.2 = (f32[512]{0:T(512)S(1)}, f32[512]{0:T(512)}, u32[]{:S(2)}) copy-start(f32[512]{0:T(512)} %param.13) | copy-start | bytes 6148
  11.5 9.6 %collective-permute-start = (f32[640,128]{1,0:T(8,128)S(1)}, f32[640,128]{1,0:T(8,128)S(1)}, u32[]{:S(2)}, u32[]{:S(2)}) collective-permute-start(f32[640,128]{1,0:T(8,128)S(1)} %get-tuple-element.21), channel_id=1, source_target_pairs={{0,4},{4,0},{8,12},{12,8},{16,20},{20,16},{24,28},{28,24},{1,5},{5... | collective-permute-start | bytes 983048 | tf_op jit(solution)/shard_map/ppermute | solution.py:226
  12.0 4.9 %collective-permute-start.1 = (bf16[48,512]{1,0:T(8,128)(2,1)S(1)}, bf16[48,512]{1,0:T(8,128)(2,1)S(1)}, u32[]{:S(2)}, u32[]{:S(2)}) collective-permute-start(bf16[48,512]{1,0:T(8,128)(2,1)S(1)} %get-tuple-element.23), channel_id=1, source_target_pairs={{0,1},{1,0},{2,3},{3,2},{4,5},{5,4},{6,7},{7,6},{8,9},{9,8},{10,11... | collective-permute-start | bytes 147464 | tf_op jit(solution)/shard_map/ppermute | solution.py:226
  14.6 4.1 %collective-permute-start.2 = (bf16[48,512]{1,0:T(8,128)(2,1)S(1)}, bf16[48,512]{1,0:T(8,128)(2,1)S(1)}, u32[]{:S(2)}, u32[]{:S(2)}) collective-permute-start(bf16[48,512]{1,0:T(8,128)(2,1)S(1)} %get-tuple-element.24), channel_id=1, source_target_pairs={{0,2},{1,3},{2,0},{3,1},{4,6},{5,7},{6,4},{7,5},{8,10},{9,11},{10,... | collective-permute-start | bytes 147464 | tf_op jit(solution)/shard_map/ppermute | solution.py:226
  16.1 5.0 %collective-permute-start.3 = (bf16[48,512]{1,0:T(8,128)(2,1)S(1)}, bf16[48,512]{1,0:T(8,128)(2,1)S(1)}, u32[]{:S(2)}, u32[]{:S(2)}) collective-permute-start(bf16[48,512]{1,0:T(8,128)(2,1)S(1)} %get-tuple-element.25), channel_id=1, source_target_pairs={{0,3},{1,2},{2,1},{3,0},{4,7},{5,6},{6,5},{7,4},{8,11},{9,10},{10,... | collective-permute-start | bytes 147464 | tf_op jit(solution)/shard_map/ppermute | solution.py:226
  21.5 5.6 %collective-permute-start.4 = (f32[256,128]{1,0:T(8,128)S(1)}, f32[256,128]{1,0:T(8,128)S(1)}, u32[]{:S(2)}, u32[]{:S(2)}) collective-permute-start(f32[256,128]{1,0:T(8,128)S(1)} %get-tuple-element.28), channel_id=1, source_target_pairs={{0,1},{1,0},{2,3},{3,2},{4,5},{5,4},{6,7},{7,6},{8,9},{9,8},{10,11... | collective-permute-start | bytes 393224 | tf_op jit(solution)/shard_map/ppermute | solution.py:226
  22.0 6.7 %collective-permute-start.5 = (f32[256,128]{1,0:T(8,128)S(1)}, f32[256,128]{1,0:T(8,128)S(1)}, u32[]{:S(2)}, u32[]{:S(2)}) collective-permute-start(f32[256,128]{1,0:T(8,128)S(1)} %get-tuple-element.29), channel_id=1, source_target_pairs={{0,2},{1,3},{2,0},{3,1},{4,6},{5,7},{6,4},{7,5},{8,10},{9,11},{10,... | collective-permute-start | bytes 393224 | tf_op jit(solution)/shard_map/ppermute | solution.py:226
  22.2 6.6 %collective-permute-start.6 = (f32[256,128]{1,0:T(8,128)S(1)}, f32[256,128]{1,0:T(8,128)S(1)}, u32[]{:S(2)}, u32[]{:S(2)}) collective-permute-start(f32[256,128]{1,0:T(8,128)S(1)} %get-tuple-element.30), channel_id=1, source_target_pairs={{0,3},{1,2},{2,1},{3,0},{4,7},{5,6},{6,5},{7,4},{8,11},{9,10},{10,... | collective-permute-start | bytes 393224 | tf_op jit(solution)/shard_map/ppermute | solution.py:226
  29.5 7.0 %collective-permute-start.8 = (f32[160,128]{1,0:T(8,128)S(1)}, f32[160,128]{1,0:T(8,128)S(1)}, u32[]{:S(2)}, u32[]{:S(2)}) collective-permute-start(f32[160,128]{1,0:T(8,128)S(1)} %get-tuple-element.31), channel_id=1, source_target_pairs={{0,16},{4,20},{8,24},{12,28},{16,0},{20,4},{24,8},{28,12},{1,17},{... | collective-permute-start | bytes 245768 | tf_op jit(solution)/shard_map/ppermute | solution.py:226
  32.2 6.4 %collective-permute-start.9 = (f32[160,128]{1,0:T(8,128)S(1)}, f32[160,128]{1,0:T(8,128)S(1)}, u32[]{:S(2)}, u32[]{:S(2)}) collective-permute-start(f32[160,128]{1,0:T(8,128)S(1)} %get-tuple-element.31), channel_id=1, source_target_pairs={{0,24},{4,28},{8,16},{12,20},{16,8},{20,12},{24,0},{28,4},{1,25},{... | collective-permute-start | bytes 245768 | tf_op jit(solution)/shard_map/ppermute | solution.py:226
  33.5 5.3 %collective-permute-start.7 = (f32[160,128]{1,0:T(8,128)S(1)}, f32[160,128]{1,0:T(8,128)S(1)}, u32[]{:S(2)}, u32[]{:S(2)}) collective-permute-start(f32[160,128]{1,0:T(8,128)S(1)} %get-tuple-element.31), channel_id=1, source_target_pairs={{0,8},{4,12},{8,0},{12,4},{16,24},{20,28},{24,16},{28,20},{1,9},{5... | collective-permute-start | bytes 245768 | tf_op jit(solution)/shard_map/ppermute | solution.py:226
  38.9 4.5 %collective-permute-start.10 = (f32[160,128]{1,0:T(8,128)S(1)}, f32[160,128]{1,0:T(8,128)S(1)}, u32[]{:S(2)}, u32[]{:S(2)}) collective-permute-start(f32[160,128]{1,0:T(8,128)S(1)} %add_add_fusion.refs_0_), channel_id=1, source_target_pairs={{0,1},{1,0},{2,3},{3,2},{4,5},{5,4},{6,7},{7,6},{8,9},{9,8},{10,11... | collective-permute-start | bytes 245768 | tf_op jit(solution)/shard_map/ppermute | solution.py:226
  40.7 4.4 %collective-permute-start.11 = (f32[160,128]{1,0:T(8,128)S(1)}, f32[160,128]{1,0:T(8,128)S(1)}, u32[]{:S(2)}, u32[]{:S(2)}) collective-permute-start(f32[160,128]{1,0:T(8,128)S(1)} %add_add_fusion.refs_0_), channel_id=1, source_target_pairs={{0,2},{1,3},{2,0},{3,1},{4,6},{5,7},{6,4},{7,5},{8,10},{9,11},{10,... | collective-permute-start | bytes 245768 | tf_op jit(solution)/shard_map/ppermute | solution.py:226
  41.8 5.3 %collective-permute-start.12 = (f32[160,128]{1,0:T(8,128)S(1)}, f32[160,128]{1,0:T(8,128)S(1)}, u32[]{:S(2)}, u32[]{:S(2)}) collective-permute-start(f32[160,128]{1,0:T(8,128)S(1)} %add_add_fusion.refs_0_), channel_id=1, source_target_pairs={{0,3},{1,2},{2,1},{3,0},{4,7},{5,6},{6,5},{7,4},{8,11},{9,10},{10,... | collective-permute-start | bytes 245768 | tf_op jit(solution)/shard_map/ppermute | solution.py:226
  42.4 4.7 %collective-permute-start.13 = (f32[160,128]{1,0:T(8,128)S(1)}, f32[160,128]{1,0:T(8,128)S(1)}, u32[]{:S(2)}, u32[]{:S(2)}) collective-permute-start(f32[160,128]{1,0:T(8,128)S(1)} %add_add_fusion.refs_0_), channel_id=1, source_target_pairs={{0,4},{4,0},{8,12},{12,8},{16,20},{20,16},{24,28},{28,24},{1,5},{5... | collective-permute-start | bytes 245768 | tf_op jit(solution)/shard_map/ppermute | solution.py:226
  43.4 3.8 %collective-permute-start.14 = (f32[160,128]{1,0:T(8,128)S(1)}, f32[160,128]{1,0:T(8,128)S(1)}, u32[]{:S(2)}, u32[]{:S(2)}) collective-permute-start(f32[160,128]{1,0:T(8,128)S(1)} %collective-permute-done.10.refs_1_), channel_id=1, source_target_pairs={{0,4},{4,0},{8,12},{12,8},{16,20},{20,16},{24,28},{28,24},{1,5},{5... | collective-permute-start | bytes 245768 | tf_op jit(solution)/shard_map/ppermute | solution.py:226
  45.2 2.0 %collective-permute-start.15 = (f32[160,128]{1,0:T(8,128)S(1)}, f32[160,128]{1,0:T(8,128)S(1)}, u32[]{:S(2)}, u32[]{:S(2)}) collective-permute-start(f32[160,128]{1,0:T(8,128)S(1)} %collective-permute-done.11.refs_2_), channel_id=1, source_target_pairs={{0,4},{4,0},{8,12},{12,8},{16,20},{20,16},{24,28},{28,24},{1,5},{5... | collective-permute-start | bytes 245768 | tf_op jit(solution)/shard_map/ppermute | solution.py:226
  47.1 1.3 %collective-permute-start.16 = (f32[160,128]{1,0:T(8,128)S(1)}, f32[160,128]{1,0:T(8,128)S(1)}, u32[]{:S(2)}, u32[]{:S(2)}) collective-permute-start(f32[160,128]{1,0:T(8,128)S(1)} %collective-permute-done.12.refs_3_), channel_id=1, source_target_pairs={{0,4},{4,0},{8,12},{12,8},{16,20},{20,16},{24,28},{28,24},{1,5},{5... | collective-permute-start | bytes 245768 | tf_op jit(solution)/shard_map/ppermute | solution.py:226
Sparse Core Ops, SparseCore 0:
  47.3 24.1 all-gather.2

commit v4 on v3

--- a/solution.py
+++ b/solution.py
@@ -69,43 +69,18 @@
     return [(i, j) for i in range(count) for j in range(i, count)]
 
 
-def front_kernel(
-    order_ref,
-    columns_ref,
-    factor_ref,
-    border_ref,
-    wait_ref,
-    moved_ref,
-    keep_ref,
-    send_ref,
-    packed_ref,
-    factor_here,
-    border_here,
-    columns_here,
-    sems,
-    *,
-    width,
-):
+def moved_kernel(order_ref, factor_ref, border_ref, moved_ref, factor_here, border_here, sems):
     depth = factor_here.shape[0]
     chunk = depth // 4
     chunks = [slice(k * chunk, (k + 1) * chunk) for k in range(4)]
     loads = [pltpu.make_async_copy(border_ref.at[0], border_here, sems.at[0])]
-    columns_load = pltpu.make_async_copy(columns_ref, columns_here, sems.at[5])
-    columns_load.start()
     for k, at in enumerate(chunks):
         loads.append(
             pltpu.make_async_copy(factor_ref.at[0, at], factor_here.at[at], sems.at[k + 1])
         )
     for load in loads:
         load.start()
-    core = lax.rem(lax.axis_index("scen"), 2)
-    place = lax.axis_index("col")
     order = order_ref[0]
-    columns_load.wait()
-    columns = columns_here[pl.ds(place, 1), :]
-    spread = (
-        lax.broadcasted_iota(jnp.int32, (width, columns.shape[1]), 0) == columns
-    ).astype(jnp.bfloat16)
     loads[0].wait()
     border = border_here[...]
     within = lax.broadcasted_iota(jnp.int32, border.shape, 1) < order
@@ -114,8 +89,40 @@
     for k, at in enumerate(chunks):
         loads[k + 1].wait()
         product = product + matmul(inside[:, at], factor_here[at])
-    moved = jnp.where(within, product, 0.0).astype(jnp.bfloat16)
-    moved_ref[...] = moved
+    moved_ref[0] = jnp.where(within, product, 0.0).astype(jnp.bfloat16)
+    moved_ref[1] = border
+
+
+def transform(order, factor, border):
+    return pl.pallas_call(
+        moved_kernel,
+        out_shape=jax.ShapeDtypeStruct((2,) + border.shape[1:], jnp.bfloat16),
+        in_specs=[SMEM, HBM, HBM],
+        out_specs=VMEM,
+        scratch_shapes=[
+            pltpu.VMEM(factor.shape[1:], factor.dtype),
+            pltpu.VMEM(border.shape[1:], border.dtype),
+            pltpu.SemaphoreType.DMA((5,)),
+        ],
+        compiler_params=PARAMS,
+        cost_estimate=long_cost(20),
+        name="transform",
+    )(order, in_hbm(factor), in_hbm(border))
+
+
+def front_kernel(columns_ref, moved_ref, *refs, width):
+    count = (len(refs) - 3) // 2
+    borders, couplings = refs[:count], refs[count : 2 * count]
+    keep_ref, send_ref, packed_ref = refs[2 * count :]
+    core = lax.rem(lax.axis_index("scen"), 2)
+    place = lax.axis_index("col")
+    columns = columns_ref[pl.ds(place, 1), :]
+    spread = (
+        lax.broadcasted_iota(jnp.int32, (width, columns.shape[1]), 0) == columns
+    ).astype(jnp.bfloat16)
+    moved, border = moved_ref[0], moved_ref[1]
+    for panel_ref, coupling_ref in zip(borders, couplings):
+        coupling_ref[...] = matmul_nt(panel_ref[...], moved)
     terms = 0.5 * (matmul_nt(border, moved) + matmul_nt(moved, border))
     high, low = split_two(terms)
     half_spread = matmul_nt(high, spread) + matmul_nt(low, spread)
@@ -132,25 +139,20 @@
     send_ref[...] = packed_ref[pl.ds(pl.multiple_of((1 - core) * half, 8), half), :]
 
 
-def front(order, columns, factor, border, width, wait):
+def front(columns, moved, width, borders):
     total = len(upper_blocks(width)) * BLOCK
     half = jax.ShapeDtypeStruct((total // 2, BLOCK), jnp.float32)
-    return pl.pallas_call(
+    coupling = jax.ShapeDtypeStruct((borders[0].shape[0], moved.shape[1]), jnp.float32)
+    *couplings, keep, send = pl.pallas_call(
         functools.partial(front_kernel, width=width),
-        out_shape=[jax.ShapeDtypeStruct(border.shape[1:], jnp.bfloat16), half, half],
-        in_specs=[SMEM, HBM, HBM, HBM, VMEM],
-        out_specs=[VMEM, VMEM, VMEM],
-        scratch_shapes=[
-            pltpu.VMEM((total, BLOCK), jnp.float32),
-            pltpu.VMEM(factor.shape[1:], factor.dtype),
-            pltpu.VMEM(border.shape[1:], border.dtype),
-            pltpu.VMEM(columns.shape, columns.dtype),
-            pltpu.SemaphoreType.DMA((6,)),
-        ],
-        compiler_params=PARAMS,
-        cost_estimate=long_cost(20),
+        out_shape=[coupling] * len(borders) + [half, half],
+        in_specs=[VMEM] * (len(borders) + 2),
+        out_specs=[VMEM] * (len(borders) + 2),
+        scratch_shapes=[pltpu.VMEM((total, BLOCK), jnp.float32)],
+        compiler_params=PARAMS,
         name="front",
-    )(order, in_hbm(columns), in_hbm(factor), in_hbm(border), wait)
+    )(columns, moved, *borders)
+    return couplings, keep, send
 
 
 def deal_kernel(border_ref, *refs):
@@ -179,46 +181,36 @@
     )(in_hbm(border))
 
 
-def quarter_kernel(keep_ref, got_ref, moved_ref, *refs):
-    count = (len(refs) - 1) // 2
-    borders, own_ref, out_refs = refs[:count], refs[count], refs[count + 1 :]
+def quarter_kernel(keep_ref, got_ref, *refs):
+    count = (len(refs) + 1) // 2
+    riders, out_refs = refs[: count - 1], refs[count - 1 :]
     place = lax.axis_index("col")
     rows = out_refs[0].shape[0]
-    size, wide = own_ref.shape
-    moved = moved_ref[...]
-    for m, (border_ref, out_ref) in enumerate(zip(borders, out_refs)):
+    for m, out_ref in enumerate(out_refs):
         at = pl.ds(pl.multiple_of((place ^ m) * rows, 8), rows)
+        out_ref[:rows, :] = keep_ref[at, :] + got_ref[at, :]
         if m > 0:
-            rows = out_ref.shape[0] - wide // BLOCK * size
-            at = pl.ds(pl.multiple_of((place ^ m) * rows, 8), rows)
-        coupling = matmul_nt(border_ref[...], moved)
-        out_ref[:rows, :] = keep_ref[at, :] + got_ref[at, :]
-        if m == 0:
-            own_ref[...] = coupling
-            continue
-        for n in range(wide // BLOCK):
-            out_ref[rows + n * size : rows + (n + 1) * size, :] = coupling[
-                :, n * BLOCK : (n + 1) * BLOCK
-            ]
-
-
-def quarters(keep, got, moved, borders):
-    count = len(borders)
+            size, wide = riders[m - 1].shape
+            for n in range(wide // BLOCK):
+                out_ref[rows + n * size : rows + (n + 1) * size, :] = riders[m - 1][
+                    :, n * BLOCK : (n + 1) * BLOCK
+                ]
+
+
+def quarters(keep, got, riders):
+    count = len(riders) + 1
     rows = keep.shape[0] // count
-    size, wide = borders[0].shape[0], moved.shape[0]
-    rider = wide // BLOCK * size
-    out_shape = [jax.ShapeDtypeStruct((size, wide), jnp.float32)]
-    out_shape += [jax.ShapeDtypeStruct((rows, BLOCK), jnp.float32)]
-    out_shape += [jax.ShapeDtypeStruct((rows + rider, BLOCK), jnp.float32)] * (count - 1)
-    own, *parts = pl.pallas_call(
+    extra = riders[0].size // BLOCK
+    out_shape = [jax.ShapeDtypeStruct((rows, BLOCK), jnp.float32)]
+    out_shape += [jax.ShapeDtypeStruct((rows + extra, BLOCK), jnp.float32)] * (count - 1)
+    return pl.pallas_call(
         quarter_kernel,
         out_shape=out_shape,
-        in_specs=[VMEM] * (3 + count),
-        out_specs=[VMEM] * (1 + count),
+        in_specs=[VMEM] * (1 + count),
+        out_specs=[VMEM] * count,
         compiler_params=PARAMS,
         name="quarters",
-    )(keep, got, moved, *borders)
-    return own, parts
+    )(keep, got, *riders)
 
 
 def swap(value, axis, step):
@@ -298,9 +290,9 @@
                 panels[j] = panels[j] - exact_tn(rest[:, at : at + BLOCK], rest[:, at:])
 
 
-def cholesky_kernel(*refs, col_count):
+def early_kernel(*refs, col_count):
     pieces = refs[: 2 * col_count]
-    barrier_ref, upper_ref, inverse_ref, slice_ref, packed_ref, turned_ref = refs[2 * col_count :]
+    barrier_ref, upper_ref, inverse_ref, rest_ref, packed_ref = refs[2 * col_count :]
     width = barrier_ref.shape[1]
     count = width // BLOCK
     rows = pieces[0].shape[0]
@@ -321,34 +313,68 @@
             extra = barrier_ref[:, i * BLOCK : (i + 1) * BLOCK]
             blocks[i, j] = blocks[i, j] + jnp.where(diagonal, extra, 0.0)
     panels = [jnp.concatenate([blocks[i, j] for j in range(i, count)], 1) for i in range(count)]
-    eliminate(panels, 0, count, upper_ref, inverse_ref)
+    done = inverse_ref.shape[0]
+    eliminate(panels, 0, done, upper_ref, inverse_ref)
+    for i in range(done, count):
+        rest_ref[(i - done) * BLOCK : (i - done + 1) * BLOCK, (i - done) * BLOCK :] = panels[i]
+
+
+def early_cholesky(pieces, barrier):
+    width = barrier.shape[0]
+    half = width // 2
+    col_count = len(pieces) // 2
+    return pl.pallas_call(
+        functools.partial(early_kernel, col_count=col_count),
+        out_shape=[
+            jax.ShapeDtypeStruct((half, width), jnp.float32),
+            jax.ShapeDtypeStruct((half // BLOCK, BLOCK, BLOCK), jnp.float32),
+            jax.ShapeDtypeStruct((half, half), jnp.float32),
+        ],
+        in_specs=[VMEM] * (len(pieces) + 1),
+        out_specs=[VMEM] * 3,
+        scratch_shapes=[pltpu.VMEM((len(upper_blocks(width)) * BLOCK, BLOCK), jnp.float32)],
+        compiler_params=PARAMS,
+        cost_estimate=long_cost(20),
+        name="early",
+    )(*pieces, barrier[None])
+
+
+def late_kernel(*refs):
+    early_ref, rest_ref = refs[:2]
+    upper_ref, inverse_ref, slice_ref, turned_ref = refs[-4:]
+    width = early_ref.shape[1]
+    count = width // BLOCK
+    done = count // 2
+    half = done * BLOCK
+    place = lax.axis_index("col")
+    panels = [None] * done + [
+        rest_ref[i * BLOCK : (i + 1) * BLOCK, i * BLOCK :] for i in range(count - done)
+    ]
+    eliminate(panels, done, count, upper_ref, inverse_ref)
     slice_rows = slice_ref.shape[0]
     start = place * slice_rows
     block = pl.ds(pl.multiple_of(start // BLOCK * BLOCK, BLOCK), BLOCK)
-    turned_ref[...] = upper_ref[:, block].T
+    turned_ref[:, :half] = early_ref[:, block].T
+    turned_ref[:, half:] = upper_ref[:, block].T
     slice_ref[...] = turned_ref[pl.ds(pl.multiple_of(lax.rem(start, BLOCK), 8), slice_rows), :]
 
 
-def cholesky(pieces, barrier):
-    width = barrier.shape[0]
-    col_count = len(pieces) // 2
-    return pl.pallas_call(
-        functools.partial(cholesky_kernel, col_count=col_count),
+def late_cholesky(early, rest, col_count, waits):
+    half, width = early.shape
+    return pl.pallas_call(
+        late_kernel,
         out_shape=[
-            jax.ShapeDtypeStruct((width, width), jnp.float32),
-            jax.ShapeDtypeStruct((width // BLOCK, BLOCK, BLOCK), jnp.float32),
+            jax.ShapeDtypeStruct((half, width), jnp.float32),
+            jax.ShapeDtypeStruct((half // BLOCK, BLOCK, BLOCK), jnp.float32),
             jax.ShapeDtypeStruct((width // col_count, width), jnp.float32),
         ],
-        in_specs=[VMEM] * (len(pieces) + 1),
+        in_specs=[VMEM, VMEM] + [HBM] * len(waits),
         out_specs=[VMEM] * 3,
-        scratch_shapes=[
-            pltpu.VMEM((len(upper_blocks(width)) * BLOCK, BLOCK), jnp.float32),
-            pltpu.VMEM((BLOCK, width), jnp.float32),
-        ],
-        compiler_params=PARAMS,
-        cost_estimate=long_cost(40),
-        name="cholesky",
-    )(*pieces, barrier[None])
+        scratch_shapes=[pltpu.VMEM((BLOCK, width), jnp.float32)],
+        compiler_params=PARAMS,
+        cost_estimate=long_cost(20),
+        name="late",
+    )(early, rest, *waits)
 
 
 def assemble_kernel(columns_ref, rows_ref, own_ref, *refs):
@@ -386,65 +412,72 @@
     )(columns, rows, own, *parts)
 
 
-def solve_rows(rows, upper, inverse, out_ref):
-    count = rows.shape[1] // BLOCK
-    here = [slice(k * BLOCK, (k + 1) * BLOCK) for k in range(count)]
-    left = [rows[:, h] for h in here]
-    for k in range(count):
-        solved = exact_nt(left[k], inverse[k])
-        out_ref[:, here[k]] = solved
-        for j in range(k + 1, count):
-            left[j] = left[j] - exact(solved, upper[here[k], here[j]])
-
-
-def panel_kernel(source_ref, upper_ref, inverse_ref, out_ref, groups_ref, sems, *, group):
-    loads = [
-        pltpu.make_async_copy(source_ref.at[s], groups_ref.at[s], sems.at[s])
-        for s in range(source_ref.shape[0])
-    ]
-    for load in loads:
-        load.start()
-    rows_here, width = out_ref.shape
-    first = lax.axis_index("scen") * rows_here
-    total = jnp.zeros((rows_here, width), jnp.float32)
-    size = (groups_ref.shape[1] - 2 * group) // group
-    wide = groups_ref.shape[2]
-    for s in range(groups_ref.shape[0]):
-        loads[s].wait()
-        index = groups_ref[s, group * size :, :]
+def build_kernel(*refs, group):
+    groups = refs[1:-2]
+    keep_ref, send_ref = refs[-2:]
+    rows_here, width = keep_ref.shape
+    place = lax.axis_index("scen")
+    core = lax.rem(place, 2)
+    first = (place - core) * rows_here
+    size = (groups[0].shape[0] - 2 * group) // group
+    wide = groups[0].shape[1]
+    total = jnp.zeros((2 * rows_here, width), jnp.float32)
+    slot = lax.broadcasted_iota(jnp.int32, (2 * rows_here, group * size), 0)
+    for group_ref in groups:
+        index = group_ref[group * size :, :]
         spreads = []
         for i in range(group):
             columns = index[i : i + 1, :].astype(jnp.int32)
             spread = lax.broadcasted_iota(jnp.int32, (width, wide), 0) == columns
-            high, low = split_two(groups_ref[s, i * size : (i + 1) * size, :])
+            high, low = split_two(group_ref[i * size : (i + 1) * size, :])
             both = matmul_nt(jnp.concatenate([high, low], 0), spread.astype(jnp.bfloat16))
             spreads.append(both[:size] + both[size:])
-        widened = jnp.concatenate(spreads, 0)
         row_index = jnp.concatenate(
             [index[group + i : group + i + 1, :size] for i in range(group)], 1
         )
-        row_index = row_index.astype(jnp.int32) - first
-        row_map = (
-            lax.broadcasted_iota(jnp.int32, (rows_here, group * size), 0) == row_index
-        ).astype(jnp.bfloat16)
-        high, low = split_two(widened)
+        row_map = (slot == row_index.astype(jnp.int32) - first).astype(jnp.bfloat16)
+        high, low = split_two(jnp.concatenate(spreads, 0))
         total = total + (matmul(row_map, high) + matmul(row_map, low))
-    solve_rows(total, upper_ref, inverse_ref, out_ref)
-
-
-def panel_rows_of(groups, group, upper, inverse, rows_here):
-    return pl.pallas_call(
-        functools.partial(panel_kernel, group=group),
-        out_shape=jax.ShapeDtypeStruct((rows_here, upper.shape[1]), jnp.float32),
-        in_specs=[HBM, VMEM, VMEM],
+    lower, upper = total[:rows_here], total[rows_here:]
+    keep_ref[...] = jnp.where(core == 0, lower, upper)
+    send_ref[...] = jnp.where(core == 0, upper, lower)
+
+
+def build_rows(groups, group, rows_here, width, wait):
+    half = jax.ShapeDtypeStruct((rows_here, width), jnp.float32)
+    return pl.pallas_call(
+        functools.partial(build_kernel, group=group),
+        out_shape=[half, half],
+        in_specs=[HBM] + [VMEM] * len(groups),
+        out_specs=[VMEM, VMEM],
+        compiler_params=PARAMS,
+        cost_estimate=long_cost(5),
+        name="build",
+    )(wait, *groups)
+
+
+def solve_kernel(keep_ref, got_ref, early_ref, late_ref, first_ref, last_ref, out_ref):
+    uppers, inverses = (early_ref, late_ref), (first_ref, last_ref)
+    count = out_ref.shape[1] // BLOCK
+    done = count // 2
+    here = [slice(k * BLOCK, (k + 1) * BLOCK) for k in range(count)]
+    left = [keep_ref[:, h] + got_ref[:, h] for h in here]
+    for k in range(count):
+        solved = exact_nt(left[k], inverses[k // done][k % done])
+        out_ref[:, here[k]] = solved
+        for j in range(k + 1, count):
+            left[j] = left[j] - exact(solved, uppers[k // done][here[k % done], here[j]])
+
+
+def solve_rows(keep, got, uppers, inverses):
+    return pl.pallas_call(
+        solve_kernel,
+        out_shape=jax.ShapeDtypeStruct(keep.shape, jnp.float32),
+        in_specs=[VMEM] * 6,
         out_specs=VMEM,
-        scratch_shapes=[
-            pltpu.VMEM(groups.shape, groups.dtype),
-            pltpu.SemaphoreType.DMA((groups.shape[0],)),
-        ],
-        compiler_params=PARAMS,
-        name="panel",
-    )(in_hbm(groups), upper, inverse)
+        compiler_params=PARAMS,
+        name="solve",
+    )(keep, got, *uppers, *inverses)
 
 
 def dense_panel(couplings_here, rows, columns, rows_panel, width):
@@ -492,27 +525,34 @@
 
     dealt = deal(panel_border)
     borders = [dealt[0]] + [swap(dealt[m], "col", m) for m in range(1, col_count)]
-    moved, keep, send = front(
-        true_orders, slab_columns, inverse_factor, slab_border, width, dealt[0]
-    )
+    moved = transform(true_orders, inverse_factor, slab_border)
+    couplings, keep, send = front(slab_columns, moved, width, borders)
     got = swap(send, "scen", 1)
-    own, parts = quarters(keep, got, moved, borders)
+    parts = quarters(keep, got, couplings[1:])
     parts = [parts[0]] + [swap(parts[m], "col", m) for m in range(1, col_count)]
-    part, own = sum_and_assemble(parts, own, slab_columns, panel_rows)
+    part, own = sum_and_assemble(parts, couplings[0], slab_columns, panel_rows)
     rows_panel = rows_here * scen_count
     sparse = scen_count * group * size * wide < rows_panel * width
-    if sparse:
-        groups = lax.all_gather(own, "scen")
     part = tree_sum([part] + [swap(part, "scen", 2 * m) for m in range(1, scen_count // 2)])
     pieces = [part] + [swap(part, "col", m) for m in range(1, col_count)]
     pieces = pieces + [swap(piece, "scen", 1) for piece in pieces]
-    upper, inverse, factor_rows = cholesky(pieces, barrier_diag)
+    early, early_inverse, rest = early_cholesky(pieces, barrier_diag)
     if sparse:
-        solved = panel_rows_of(groups, group, upper, inverse, rows_here)
+        groups = [own] + [swap(own, "scen", 2 * m) for m in range(1, scen_count // 2)]
+        rows, other = build_rows(groups, group, rows_here, width, rest)
+        late, late_inverse, factor_rows = late_cholesky(early, rest, col_count, [other])
+        solved = solve_rows(
+            rows, swap(other, "scen", 1), (early, late), (early_inverse, late_inverse)
+        )
     else:
         local = own[: group * size].reshape(group, size, wide)
         rows = dense_panel(local, panel_rows[0], slab_columns, rows_panel, width)
-        solved = dense_solve(rows, upper, inverse)
+        late, late_inverse, factor_rows = late_cholesky(early, rest, col_count, [])
+        solved = dense_solve(
+            rows,
+            jnp.concatenate([early, late], 0),
+            jnp.concatenate([early_inverse, late_inverse], 0),
+        )
     return factor_rows, solved
 
 

time: 87.4 us -> 78.1 us (0.89)
  the two profiles are of different devices: /device:TPU:0 before, /device:TPU:17 now
where the time goes in v4:
time: 78.1 us; the launch traced here: 77.9 us
  Pallas kernels  31.4 us (40%)
  starting transfers between devices  24 us (31%)
  waiting for transfers between devices  21.1 us (27%)
  between operations  1.41 us (2%)
    ppermute x21, starting transfers between devices, swap(): return lax.ppermute(value, axis, [(i, i ^ step) for i in range(count)])  24 us
    ppermute x21, waiting for transfers between devices, swap(): return lax.ppermute(value, axis, [(i, i ^ step) for i in range(count)])  21.1 us
    pallas_call x1, Pallas kernels, early_cholesky(): pl.pallas_call(functools.partial(early_kernel, col_count=col_count), out_...  10.9 us
    pallas_call x1, Pallas kernels, late_cholesky(): pl.pallas_call(late_kernel, out_shape=[jax.ShapeDtypeStruct((half, width)...  10.7 us
    pallas_call x1, Pallas kernels, solve_rows(): pl.pallas_call(solve_kernel, out_shape=jax.ShapeDtypeStruct(keep.shape, j...  2.98 us
    pallas_call x1, Pallas kernels, build_rows(): pl.pallas_call(functools.partial(build_kernel, group=group), out_shape=[h...  2.83 us
  transfers between devices with their start and end apart: 21, of which 7 were waited for; matrix products, arithmetic and copies ran while one was open for 0% of the time, Pallas kernels for 30%

profile of v4, /device:TPU:17, one launch (start us, length us, event | category | flops | bytes accessed | tf_op | source)
XLA Modules:
  0.0 77.9 jit_solution(27472708045590335)
XLA Ops:
  1.6 1.3 %collective-permute-start = (bf16[48,512]{1,0:T(8,128)(2,1)S(1)}, bf16[48,512]{1,0:T(8,128)(2,1)S(1)}, u32[]{:S(2)}, u32[]{:S(2)}) collective-permute-start(bf16[48,512]{1,0:T(8,128)(2,1)S(1)} %get-tuple-element.27), channel_id=1, source_target_pairs={{0,1},{1,0},{2,3},{3,2},{4,5},{5,4},{6,7},{7,6},{8,9},{9,8},{10,11... | collective-permute-start | bytes 147464 | tf_op jit(solution)/shard_map/ppermute | solution.py:218
  2.8 1.2 %collective-permute-start.1 = (bf16[48,512]{1,0:T(8,128)(2,1)S(1)}, bf16[48,512]{1,0:T(8,128)(2,1)S(1)}, u32[]{:S(2)}, u32[]{:S(2)}) collective-permute-start(bf16[48,512]{1,0:T(8,128)(2,1)S(1)} %get-tuple-element.28), channel_id=1, source_target_pairs={{0,2},{1,3},{2,0},{3,1},{4,6},{5,7},{6,4},{7,5},{8,10},{9,11},{10,... | collective-permute-start | bytes 147464 | tf_op jit(solution)/shard_map/ppermute | solution.py:218
  4.9 1.6 %transform.1.moved_ref = bf16[2,256,512]{2,1,0:T(8,128)(2,1)S(1)} custom-call(s32[1]{0:T(128)S(6)} %copy.9.order_ref, bf16[1,512,512]{2,1,0:T(8,128)(2,1)} %factor_ref.1, bf16[1,256,512]{2,1,0:T(8,128)(2,1)} %border_ref.2), custom_call_target="tpu_custom_call" | custom-call | flops 20000000000 | bytes 1048576 | tf_op jit(solution)/shard_map/transform/pallas_call | solution.py:97
  6.5 1.4 %collective-permute-done.2.refs_3_ = bf16[48,512]{1,0:T(8,128)(2,1)S(1)} collective-permute-done((bf16[48,512]{1,0:T(8,128)(2,1)S(1)}, bf16[48,512]{1,0:T(8,128)(2,1)S(1)}, u32[]{:S(2)}, u32[]{:S(2)}) %collective-permute-start.2) | collective-permute-done | bytes 49184 | tf_op jit(solution)/shard_map/ppermute | solution.py:218
  7.9 1.5 %front.1 = (f32[48,256]{1,0:T(8,128)S(1)}, f32[48,256]{1,0:T(8,128)S(1)}, f32[48,256]{1,0:T(8,128)S(1)}, f32[48,256]{1,0:T(8,128)S(1)}, f32[640,128]{1,0:T(8,128)S(1)}, /*index=5*/f32[640,128]{1,0:T(8,128)S(1)}) custom-call(s32[4,256]{1,0:T(4,128)S(1)} %copy-done, bf16[2,256,512]{2,1,0:T(8,128)(2,1)S(1)} %transform.1.moved_ref, ...), custom_call_target="tpu_custom_call" | custom-call | tf_op jit(solution)/shard_map/front/pallas_call | solution.py:146
  9.4 2.5 %collective-permute-start.3 = (f32[640,128]{1,0:T(8,128)S(1)}, f32[640,128]{1,0:T(8,128)S(1)}, u32[]{:S(2)}, u32[]{:S(2)}) collective-permute-start(f32[640,128]{1,0:T(8,128)S(1)} %get-tuple-element.32), channel_id=1, source_target_pairs={{0,4},{4,0},{8,12},{12,8},{16,20},{20,16},{24,28},{28,24},{1,5},{5... | collective-permute-start | bytes 983048 | tf_op jit(solution)/shard_map/ppermute | solution.py:218
  11.8 1.3 %collective-permute-done.3.got_ref = f32[640,128]{1,0:T(8,128)S(1)} collective-permute-done((f32[640,128]{1,0:T(8,128)S(1)}, f32[640,128]{1,0:T(8,128)S(1)}, u32[]{:S(2)}, u32[]{:S(2)}) %collective-permute-start.3) | collective-permute-done | bytes 327712 | tf_op jit(solution)/shard_map/ppermute | solution.py:218
  13.7 2.2 %collective-permute-start.6 = (f32[256,128]{1,0:T(8,128)S(1)}, f32[256,128]{1,0:T(8,128)S(1)}, u32[]{:S(2)}, u32[]{:S(2)}) collective-permute-start(f32[256,128]{1,0:T(8,128)S(1)} %get-tuple-element.39), channel_id=1, source_target_pairs={{0,3},{1,2},{2,1},{3,0},{4,7},{5,6},{6,5},{7,4},{8,11},{9,10},{10,... | collective-permute-start | bytes 393224 | tf_op jit(solution)/shard_map/ppermute | solution.py:218
  15.8 2.1 %collective-permute-done.4.refs_1_ = f32[256,128]{1,0:T(8,128)S(1)} collective-permute-done((f32[256,128]{1,0:T(8,128)S(1)}, f32[256,128]{1,0:T(8,128)S(1)}, u32[]{:S(2)}, u32[]{:S(2)}) %collective-permute-start.4) | collective-permute-done | bytes 131104 | tf_op jit(solution)/shard_map/ppermute | solution.py:218
  17.9 2.8 %collective-permute-done.6.refs_3_ = f32[256,128]{1,0:T(8,128)S(1)} collective-permute-done((f32[256,128]{1,0:T(8,128)S(1)}, f32[256,128]{1,0:T(8,128)S(1)}, u32[]{:S(2)}, u32[]{:S(2)}) %collective-permute-start.6) | collective-permute-done | bytes 131104 | tf_op jit(solution)/shard_map/ppermute | solution.py:218
  20.9 2.4 %collective-permute-start.9 = (f32[160,128]{1,0:T(8,128)S(1)}, f32[160,128]{1,0:T(8,128)S(1)}, u32[]{:S(2)}, u32[]{:S(2)}) collective-permute-start(f32[160,128]{1,0:T(8,128)S(1)} %get-tuple-element.40), channel_id=1, source_target_pairs={{0,24},{4,28},{8,16},{12,20},{16,8},{20,12},{24,0},{28,4},{1,25},{... | collective-permute-start | bytes 245768 | tf_op jit(solution)/shard_map/ppermute | solution.py:218
  23.3 1.1 %collective-permute-start.7 = (f32[160,128]{1,0:T(8,128)S(1)}, f32[160,128]{1,0:T(8,128)S(1)}, u32[]{:S(2)}, u32[]{:S(2)}) collective-permute-start(f32[160,128]{1,0:T(8,128)S(1)} %get-tuple-element.40), channel_id=1, source_target_pairs={{0,8},{4,12},{8,0},{12,4},{16,24},{20,28},{24,16},{28,20},{1,9},{5... | collective-permute-start | bytes 245768 | tf_op jit(solution)/shard_map/ppermute | solution.py:218
  25.1 6.1 %collective-permute-done.9 = f32[160,128]{1,0:T(8,128)S(1)} collective-permute-done((f32[160,128]{1,0:T(8,128)S(1)}, f32[160,128]{1,0:T(8,128)S(1)}, u32[]{:S(2)}, u32[]{:S(2)}) %collective-permute-start.9) | collective-permute-done | bytes 81952 | tf_op jit(solution)/shard_map/ppermute | solution.py:218
  31.2 1.2 %collective-permute-start.10 = (f32[160,128]{1,0:T(8,128)S(1)}, f32[160,128]{1,0:T(8,128)S(1)}, u32[]{:S(2)}, u32[]{:S(2)}) collective-permute-start(f32[160,128]{1,0:T(8,128)S(1)} %add_add_fusion.refs_0_), channel_id=1, source_target_pairs={{0,1},{1,0},{2,3},{3,2},{4,5},{5,4},{6,7},{7,6},{8,9},{9,8},{10,11... | collective-permute-start | bytes 245768 | tf_op jit(solution)/shard_map/ppermute | solution.py:218
  32.6 1.3 %collective-permute-start.12 = (f32[160,128]{1,0:T(8,128)S(1)}, f32[160,128]{1,0:T(8,128)S(1)}, u32[]{:S(2)}, u32[]{:S(2)}) collective-permute-start(f32[160,128]{1,0:T(8,128)S(1)} %add_add_fusion.refs_0_), channel_id=1, source_target_pairs={{0,3},{1,2},{2,1},{3,0},{4,7},{5,6},{6,5},{7,4},{8,11},{9,10},{10,... | collective-permute-start | bytes 245768 | tf_op jit(solution)/shard_map/ppermute | solution.py:218
  34.0 1.5 %collective-permute-start.13 = (f32[160,128]{1,0:T(8,128)S(1)}, f32[160,128]{1,0:T(8,128)S(1)}, u32[]{:S(2)}, u32[]{:S(2)}) collective-permute-start(f32[160,128]{1,0:T(8,128)S(1)} %add_add_fusion.refs_0_), channel_id=1, source_target_pairs={{0,4},{4,0},{8,12},{12,8},{16,20},{20,16},{24,28},{28,24},{1,5},{5... | collective-permute-start | bytes 245768 | tf_op jit(solution)/shard_map/ppermute | solution.py:218
  36.4 3.0 %collective-permute-start.15 = (f32[160,128]{1,0:T(8,128)S(1)}, f32[160,128]{1,0:T(8,128)S(1)}, u32[]{:S(2)}, u32[]{:S(2)}) collective-permute-start(f32[160,128]{1,0:T(8,128)S(1)} %collective-permute-done.11.refs_2_), channel_id=1, source_target_pairs={{0,4},{4,0},{8,12},{12,8},{16,20},{20,16},{24,28},{28,24},{1,5},{5... | collective-permute-start | bytes 245768 | tf_op jit(solution)/shard_map/ppermute | solution.py:218
  39.9 2.1 %collective-permute-start.19 = (f32[200,256]{1,0:T(8,128)S(1)}, f32[200,256]{1,0:T(8,128)S(1)}, u32[]{:S(2)}, u32[]{:S(2)}) collective-permute-start(f32[200,256]{1,0:T(8,128)S(1)} %get-tuple-element.43.refs_1_), channel_id=1, source_target_pairs={{0,24},{4,28},{8,16},{12,20},{16,8},{20,12},{24,0},{28,4},{1,25},{... | collective-permute-start | bytes 614408 | tf_op jit(solution)/shard_map/ppermute | solution.py:218
  42.1 10.9 %early.1 = (f32[256,512]{1,0:T(8,128)S(1)}, f32[2,128,128]{2,1,0:T(8,128)S(1)}, f32[256,256]{1,0:T(8,128)S(1)}) custom-call(f32[160,128]{1,0:T(8,128)S(1)} %add_add_fusion.refs_0_, f32[160,128]{1,0:T(8,128)S(1)} %collective-permute-done.10.refs_1_, f32[160,128]{1,0:T(8,128)S(1)} %collective-permute-done.11.refs_2_, ...), custom_call_target="tpu_custom_call" | custom-call | flops 20000000000 | bytes 1048576 | tf_op jit(solution)/shard_map/early/pallas_call | solution.py:326
  53.0 6.7 %collective-permute-done.19.refs_4_ = f32[200,256]{1,0:T(8,128)S(1)} collective-permute-done((f32[200,256]{1,0:T(8,128)S(1)}, f32[200,256]{1,0:T(8,128)S(1)}, u32[]{:S(2)}, u32[]{:S(2)}) %collective-permute-start.19) | collective-permute-done | bytes 204832 | tf_op jit(solution)/shard_map/ppermute | solution.py:218
  59.7 2.8 %build.1 = (f32[240,512]{1,0:T(8,128)S(1)}, f32[240,512]{1,0:T(8,128)S(1)}) custom-call(f32[256,256]{1,0:T(8,128)S(1)} %get-tuple-element.42.refs_0_.refs_1_, f32[200,256]{1,0:T(8,128)S(1)} %get-tuple-element.43.refs_1_, f32[200,256]{1,0:T(8,128)S(1)} %collective-permute-done.17.refs_2_, f32[200,256]{1,0:T(8,128)S(1)} %collective-permute-done.18.refs_3_, ...), custom_call_target="tpu_custom_call" | custom-call | flops 5000000000 | bytes 1048576 | tf_op jit(solution)/shard_map/build/pallas_call | solution.py:448
  62.5 1.7 %collective-permute-start.20 = (f32[240,512]{1,0:T(8,128)S(1)}, f32[240,512]{1,0:T(8,128)S(1)}, u32[]{:S(2)}, u32[]{:S(2)}) collective-permute-start(f32[240,512]{1,0:T(8,128)S(1)} %get-tuple-element.44.refs_2_), channel_id=1, source_target_pairs={{0,4},{4,0},{8,12},{12,8},{16,20},{20,16},{24,28},{28,24},{1,5},{5... | collective-permute-start | bytes 1474568 | tf_op jit(solution)/shard_map/ppermute | solution.py:218
  64.2 10.7 %late.1 = (f32[256,512]{1,0:T(8,128)S(1)}, f32[2,128,128]{2,1,0:T(8,128)S(1)}, f32[128,512]{1,0:T(8,128)}) custom-call(f32[256,512]{1,0:T(8,128)S(1)} %get-tuple-element.41.refs_0_.early_ref, f32[256,256]{1,0:T(8,128)S(1)} %get-tuple-element.42.refs_0_.refs_1_, f32[240,512]{1,0:T(8,128)S(1)} %get-tuple-element.44.refs_2_), custom_call_target="tpu_custom_call" | custom-call | flops 20000000000 | bytes 1048576 | tf_op jit(solution)/shard_map/late/pallas_call | solution.py:364
  74.9 3.0 %solve.1 = f32[240,512]{1,0:T(8,128)} custom-call(f32[240,512]{1,0:T(8,128)S(1)} %get-tuple-element.46.keep_ref, f32[240,512]{1,0:T(8,128)S(1)} %collective-permute-done.20.got_ref, f32[256,512]{1,0:T(8,128)S(1)} %get-tuple-element.41.refs_0_.early_ref, f32[256,512]{1,0:T(8,128)S(1)} %get-tuple-element.47.late_ref, ...), custom_call_target="tpu_custom_call" | custom-call | tf_op jit(solution)/shard_map/solve/pallas_call | solution.py:473
  (34 shorter events, 4.3 us)
Async XLA Ops:
  1.6 4.9 %collective-permute-start = (bf16[48,512]{1,0:T(8,128)(2,1)S(1)}, bf16[48,512]{1,0:T(8,128)(2,1)S(1)}, u32[]{:S(2)}, u32[]{:S(2)}) collective-permute-start(bf16[48,512]{1,0:T(8,128)(2,1)S(1)} %get-tuple-element.27), channel_id=1, source_target_pairs={{0,1},{1,0},{2,3},{3,2},{4,5},{5,4},{6,7},{7,6},{8,9},{9,8},{10,11... | collective-permute-start | bytes 147464 | tf_op jit(solution)/shard_map/ppermute | solution.py:218
  2.8 3.7 %collective-permute-start.1 = (bf16[48,512]{1,0:T(8,128)(2,1)S(1)}, bf16[48,512]{1,0:T(8,128)(2,1)S(1)}, u32[]{:S(2)}, u32[]{:S(2)}) collective-permute-start(bf16[48,512]{1,0:T(8,128)(2,1)S(1)} %get-tuple-element.28), channel_id=1, source_target_pairs={{0,2},{1,3},{2,0},{3,1},{4,6},{5,7},{6,4},{7,5},{8,10},{9,11},{10,... | collective-permute-start | bytes 147464 | tf_op jit(solution)/shard_map/ppermute | solution.py:218
  4.1 3.8 %collective-permute-start.2 = (bf16[48,512]{1,0:T(8,128)(2,1)S(1)}, bf16[48,512]{1,0:T(8,128)(2,1)S(1)}, u32[]{:S(2)}, u32[]{:S(2)}) collective-permute-start(bf16[48,512]{1,0:T(8,128)(2,1)S(1)} %get-tuple-element.29), channel_id=1, source_target_pairs={{0,3},{1,2},{2,1},{3,0},{4,7},{5,6},{6,5},{7,4},{8,11},{9,10},{10,... | collective-permute-start | bytes 147464 | tf_op jit(solution)/shard_map/ppermute | solution.py:218
  4.9 3.0 %copy-start = (s32[4,256]{1,0:T(4,128)S(1)}, s32[4,256]{1,0:T(4,128)}, u32[]{:S(2)}) copy-start(s32[4,256]{1,0:T(4,128)} %columns_ref.3) | copy-start | bytes 12292
  9.4 3.7 %collective-permute-start.3 = (f32[640,128]{1,0:T(8,128)S(1)}, f32[640,128]{1,0:T(8,128)S(1)}, u32[]{:S(2)}, u32[]{:S(2)}) collective-permute-start(f32[640,128]{1,0:T(8,128)S(1)} %get-tuple-element.32), channel_id=1, source_target_pairs={{0,4},{4,0},{8,12},{12,8},{16,20},{20,16},{24,28},{28,24},{1,5},{5... | collective-permute-start | bytes 983048 | tf_op jit(solution)/shard_map/ppermute | solution.py:218
  13.1 4.8 %collective-permute-start.4 = (f32[256,128]{1,0:T(8,128)S(1)}, f32[256,128]{1,0:T(8,128)S(1)}, u32[]{:S(2)}, u32[]{:S(2)}) collective-permute-start(f32[256,128]{1,0:T(8,128)S(1)} %get-tuple-element.37), channel_id=1, source_target_pairs={{0,1},{1,0},{2,3},{3,2},{4,5},{5,4},{6,7},{7,6},{8,9},{9,8},{10,11... | collective-permute-start | bytes 393224 | tf_op jit(solution)/shard_map/ppermute | solution.py:218
  13.4 4.5 %collective-permute-start.5 = (f32[256,128]{1,0:T(8,128)S(1)}, f32[256,128]{1,0:T(8,128)S(1)}, u32[]{:S(2)}, u32[]{:S(2)}) collective-permute-start(f32[256,128]{1,0:T(8,128)S(1)} %get-tuple-element.38), channel_id=1, source_target_pairs={{0,2},{1,3},{2,0},{3,1},{4,6},{5,7},{6,4},{7,5},{8,10},{9,11},{10,... | collective-permute-start | bytes 393224 | tf_op jit(solution)/shard_map/ppermute | solution.py:218
  13.7 7.0 %copy-start.1 = (s32[1,4,48]{2,1,0:T(4,128)S(1)}, s32[1,4,48]{2,1,0:T(4,128)}, u32[]{:S(2)}) copy-start(s32[1,4,48]{2,1,0:T(4,128)} %rows_ref.1) | copy-start | bytes 2308
  13.7 7.0 %collective-permute-start.6 = (f32[256,128]{1,0:T(8,128)S(1)}, f32[256,128]{1,0:T(8,128)S(1)}, u32[]{:S(2)}, u32[]{:S(2)}) collective-permute-start(f32[256,128]{1,0:T(8,128)S(1)} %get-tuple-element.39), channel_id=1, source_target_pairs={{0,3},{1,2},{2,1},{3,0},{4,7},{5,6},{6,5},{7,4},{8,11},{9,10},{10,... | collective-permute-start | bytes 393224 | tf_op jit(solution)/shard_map/ppermute | solution.py:218
  20.7 4.3 %collective-permute-start.8 = (f32[160,128]{1,0:T(8,128)S(1)}, f32[160,128]{1,0:T(8,128)S(1)}, u32[]{:S(2)}, u32[]{:S(2)}) collective-permute-start(f32[160,128]{1,0:T(8,128)S(1)} %get-tuple-element.40), channel_id=1, source_target_pairs={{0,16},{4,20},{8,24},{12,28},{16,0},{20,4},{24,8},{28,12},{1,17},{... | collective-permute-start | bytes 245768 | tf_op jit(solution)/shard_map/ppermute | solution.py:218
  20.9 10.3 %collective-permute-start.9 = (f32[160,128]{1,0:T(8,128)S(1)}, f32[160,128]{1,0:T(8,128)S(1)}, u32[]{:S(2)}, u32[]{:S(2)}) collective-permute-start(f32[160,128]{1,0:T(8,128)S(1)} %get-tuple-element.40), channel_id=1, source_target_pairs={{0,24},{4,28},{8,16},{12,20},{16,8},{20,12},{24,0},{28,4},{1,25},{... | collective-permute-start | bytes 245768 | tf_op jit(solution)/shard_map/ppermute | solution.py:218
  23.3 7.9 %collective-permute-start.7 = (f32[160,128]{1,0:T(8,128)S(1)}, f32[160,128]{1,0:T(8,128)S(1)}, u32[]{:S(2)}, u32[]{:S(2)}) collective-permute-start(f32[160,128]{1,0:T(8,128)S(1)} %get-tuple-element.40), channel_id=1, source_target_pairs={{0,8},{4,12},{8,0},{12,4},{16,24},{20,28},{24,16},{28,20},{1,9},{5... | collective-permute-start | bytes 245768 | tf_op jit(solution)/shard_map/ppermute | solution.py:218
  31.2 10.9 %copy-start.2 = (f32[512]{0:T(512)S(1)}, f32[512]{0:T(512)}, u32[]{:S(2)}) copy-start(f32[512]{0:T(512)} %param.13) | copy-start | bytes 6148
  31.2 4.2 %collective-permute-start.10 = (f32[160,128]{1,0:T(8,128)S(1)}, f32[160,128]{1,0:T(8,128)S(1)}, u32[]{:S(2)}, u32[]{:S(2)}) collective-permute-start(f32[160,128]{1,0:T(8,128)S(1)} %add_add_fusion.refs_0_), channel_id=1, source_target_pairs={{0,1},{1,0},{2,3},{3,2},{4,5},{5,4},{6,7},{7,6},{8,9},{9,8},{10,11... | collective-permute-start | bytes 245768 | tf_op jit(solution)/shard_map/ppermute | solution.py:218
  32.4 3.9 %collective-permute-start.11 = (f32[160,128]{1,0:T(8,128)S(1)}, f32[160,128]{1,0:T(8,128)S(1)}, u32[]{:S(2)}, u32[]{:S(2)}) collective-permute-start(f32[160,128]{1,0:T(8,128)S(1)} %add_add_fusion.refs_0_), channel_id=1, source_target_pairs={{0,2},{1,3},{2,0},{3,1},{4,6},{5,7},{6,4},{7,5},{8,10},{9,11},{10,... | collective-permute-start | bytes 245768 | tf_op jit(solution)/shard_map/ppermute | solution.py:218
  32.6 6.8 %collective-permute-start.12 = (f32[160,128]{1,0:T(8,128)S(1)}, f32[160,128]{1,0:T(8,128)S(1)}, u32[]{:S(2)}, u32[]{:S(2)}) collective-permute-start(f32[160,128]{1,0:T(8,128)S(1)} %add_add_fusion.refs_0_), channel_id=1, source_target_pairs={{0,3},{1,2},{2,1},{3,0},{4,7},{5,6},{6,5},{7,4},{8,11},{9,10},{10,... | collective-permute-start | bytes 245768 | tf_op jit(solution)/shard_map/ppermute | solution.py:218
  34.0 5.5 %collective-permute-start.13 = (f32[160,128]{1,0:T(8,128)S(1)}, f32[160,128]{1,0:T(8,128)S(1)}, u32[]{:S(2)}, u32[]{:S(2)}) collective-permute-start(f32[160,128]{1,0:T(8,128)S(1)} %add_add_fusion.refs_0_), channel_id=1, source_target_pairs={{0,4},{4,0},{8,12},{12,8},{16,20},{20,16},{24,28},{28,24},{1,5},{5... | collective-permute-start | bytes 245768 | tf_op jit(solution)/shard_map/ppermute | solution.py:218
  35.4 4.5 %collective-permute-start.14 = (f32[160,128]{1,0:T(8,128)S(1)}, f32[160,128]{1,0:T(8,128)S(1)}, u32[]{:S(2)}, u32[]{:S(2)}) collective-permute-start(f32[160,128]{1,0:T(8,128)S(1)} %collective-permute-done.10.refs_1_), channel_id=1, source_target_pairs={{0,4},{4,0},{8,12},{12,8},{16,20},{20,16},{24,28},{28,24},{1,5},{5... | collective-permute-start | bytes 245768 | tf_op jit(solution)/shard_map/ppermute | solution.py:218
  36.4 5.7 %collective-permute-start.15 = (f32[160,128]{1,0:T(8,128)S(1)}, f32[160,128]{1,0:T(8,128)S(1)}, u32[]{:S(2)}, u32[]{:S(2)}) collective-permute-start(f32[160,128]{1,0:T(8,128)S(1)} %collective-permute-done.11.refs_2_), channel_id=1, source_target_pairs={{0,4},{4,0},{8,12},{12,8},{16,20},{20,16},{24,28},{28,24},{1,5},{5... | collective-permute-start | bytes 245768 | tf_op jit(solution)/shard_map/ppermute | solution.py:218
  39.4 2.7 %collective-permute-start.16 = (f32[160,128]{1,0:T(8,128)S(1)}, f32[160,128]{1,0:T(8,128)S(1)}, u32[]{:S(2)}, u32[]{:S(2)}) collective-permute-start(f32[160,128]{1,0:T(8,128)S(1)} %collective-permute-done.12.refs_3_), channel_id=1, source_target_pairs={{0,4},{4,0},{8,12},{12,8},{16,20},{20,16},{24,28},{28,24},{1,5},{5... | collective-permute-start | bytes 245768 | tf_op jit(solution)/shard_map/ppermute | solution.py:218
  39.4 13.6 %collective-permute-start.17 = (f32[200,256]{1,0:T(8,128)S(1)}, f32[200,256]{1,0:T(8,128)S(1)}, u32[]{:S(2)}, u32[]{:S(2)}) collective-permute-start(f32[200,256]{1,0:T(8,128)S(1)} %get-tuple-element.43.refs_1_), channel_id=1, source_target_pairs={{0,8},{4,12},{8,0},{12,4},{16,24},{20,28},{24,16},{28,20},{1,9},{5... | collective-permute-start | bytes 614408 | tf_op jit(solution)/shard_map/ppermute | solution.py:218
  39.4 13.6 %collective-permute-start.18 = (f32[200,256]{1,0:T(8,128)S(1)}, f32[200,256]{1,0:T(8,128)S(1)}, u32[]{:S(2)}, u32[]{:S(2)}) collective-permute-start(f32[200,256]{1,0:T(8,128)S(1)} %get-tuple-element.43.refs_1_), channel_id=1, source_target_pairs={{0,16},{4,20},{8,24},{12,28},{16,0},{20,4},{24,8},{28,12},{1,17},{... | collective-permute-start | bytes 614408 | tf_op jit(solution)/shard_map/ppermute | solution.py:218
  39.9 19.7 %collective-permute-start.19 = (f32[200,256]{1,0:T(8,128)S(1)}, f32[200,256]{1,0:T(8,128)S(1)}, u32[]{:S(2)}, u32[]{:S(2)}) collective-permute-start(f32[200,256]{1,0:T(8,128)S(1)} %get-tuple-element.43.refs_1_), channel_id=1, source_target_pairs={{0,24},{4,28},{8,16},{12,20},{16,8},{20,12},{24,0},{28,4},{1,25},{... | collective-permute-start | bytes 614408 | tf_op jit(solution)/shard_map/ppermute | solution.py:218
  62.5 12.4 %collective-permute-start.20 = (f32[240,512]{1,0:T(8,128)S(1)}, f32[240,512]{1,0:T(8,128)S(1)}, u32[]{:S(2)}, u32[]{:S(2)}) collective-permute-start(f32[240,512]{1,0:T(8,128)S(1)} %get-tuple-element.44.refs_2_), channel_id=1, source_target_pairs={{0,4},{4,0},{8,12},{12,8},{16,20},{20,16},{24,28},{28,24},{1,5},{5... | collective-permute-start | bytes 1474568 | tf_op jit(solution)/shard_map/ppermute | solution.py:218

commit v5 on v4

--- a/solution.py
+++ b/solution.py
@@ -13,6 +13,7 @@
 VMEM = pl.BlockSpec(memory_space=pltpu.VMEM)
 SMEM = pl.BlockSpec(memory_space=pltpu.SMEM)
 HBM = pl.BlockSpec(memory_space=pltpu.HBM)
+ANY = pl.BlockSpec(memory_space=pl.ANY)
 PARAMS = pltpu.CompilerParams(vmem_limit_bytes=40 * 2**20)
 
 
@@ -69,17 +70,34 @@
     return [(i, j) for i in range(count) for j in range(i, count)]
 
 
-def moved_kernel(order_ref, factor_ref, border_ref, moved_ref, factor_here, border_here, sems):
-    depth = factor_here.shape[0]
-    chunk = depth // 4
+def front_kernel(
+    order_ref,
+    columns_ref,
+    factor_ref,
+    border_ref,
+    moved_ref,
+    keep_ref,
+    send_ref,
+    packed_ref,
+    factor_here,
+    border_here,
+    columns_here,
+    sems,
+    *,
+    width,
+):
+    chunk = factor_here.shape[0] // 4
     chunks = [slice(k * chunk, (k + 1) * chunk) for k in range(4)]
     loads = [pltpu.make_async_copy(border_ref.at[0], border_here, sems.at[0])]
     for k, at in enumerate(chunks):
         loads.append(
             pltpu.make_async_copy(factor_ref.at[0, at], factor_here.at[at], sems.at[k + 1])
         )
+    loads.append(pltpu.make_async_copy(columns_ref, columns_here, sems.at[5]))
     for load in loads:
         load.start()
+    core = lax.rem(lax.axis_index("scen"), 2)
+    place = lax.axis_index("col")
     order = order_ref[0]
     loads[0].wait()
     border = border_here[...]
@@ -89,40 +107,13 @@
     for k, at in enumerate(chunks):
         loads[k + 1].wait()
         product = product + matmul(inside[:, at], factor_here[at])
-    moved_ref[0] = jnp.where(within, product, 0.0).astype(jnp.bfloat16)
-    moved_ref[1] = border
-
-
-def transform(order, factor, border):
-    return pl.pallas_call(
-        moved_kernel,
-        out_shape=jax.ShapeDtypeStruct((2,) + border.shape[1:], jnp.bfloat16),
-        in_specs=[SMEM, HBM, HBM],
-        out_specs=VMEM,
-        scratch_shapes=[
-            pltpu.VMEM(factor.shape[1:], factor.dtype),
-            pltpu.VMEM(border.shape[1:], border.dtype),
-            pltpu.SemaphoreType.DMA((5,)),
-        ],
-        compiler_params=PARAMS,
-        cost_estimate=long_cost(20),
-        name="transform",
-    )(order, in_hbm(factor), in_hbm(border))
-
-
-def front_kernel(columns_ref, moved_ref, *refs, width):
-    count = (len(refs) - 3) // 2
-    borders, couplings = refs[:count], refs[count : 2 * count]
-    keep_ref, send_ref, packed_ref = refs[2 * count :]
-    core = lax.rem(lax.axis_index("scen"), 2)
-    place = lax.axis_index("col")
-    columns = columns_ref[pl.ds(place, 1), :]
+    moved = jnp.where(within, product, 0.0).astype(jnp.bfloat16)
+    moved_ref[...] = moved
+    loads[5].wait()
+    columns = columns_here[pl.ds(place, 1), :]
     spread = (
         lax.broadcasted_iota(jnp.int32, (width, columns.shape[1]), 0) == columns
     ).astype(jnp.bfloat16)
-    moved, border = moved_ref[0], moved_ref[1]
-    for panel_ref, coupling_ref in zip(borders, couplings):
-        coupling_ref[...] = matmul_nt(panel_ref[...], moved)
     terms = 0.5 * (matmul_nt(border, moved) + matmul_nt(moved, border))
     high, low = split_two(terms)
     half_spread = matmul_nt(high, spread) + matmul_nt(low, spread)
@@ -139,20 +130,25 @@
     send_ref[...] = packed_ref[pl.ds(pl.multiple_of((1 - core) * half, 8), half), :]
 
 
-def front(columns, moved, width, borders):
+def front(order, columns, factor, border, width):
     total = len(upper_blocks(width)) * BLOCK
     half = jax.ShapeDtypeStruct((total // 2, BLOCK), jnp.float32)
-    coupling = jax.ShapeDtypeStruct((borders[0].shape[0], moved.shape[1]), jnp.float32)
-    *couplings, keep, send = pl.pallas_call(
+    return pl.pallas_call(
         functools.partial(front_kernel, width=width),
-        out_shape=[coupling] * len(borders) + [half, half],
-        in_specs=[VMEM] * (len(borders) + 2),
-        out_specs=[VMEM] * (len(borders) + 2),
-        scratch_shapes=[pltpu.VMEM((total, BLOCK), jnp.float32)],
-        compiler_params=PARAMS,
+        out_shape=[jax.ShapeDtypeStruct(border.shape[1:], jnp.bfloat16), half, half],
+        in_specs=[SMEM, HBM, HBM, HBM],
+        out_specs=[VMEM] * 3,
+        scratch_shapes=[
+            pltpu.VMEM((total, BLOCK), jnp.float32),
+            pltpu.VMEM(factor.shape[1:], factor.dtype),
+            pltpu.VMEM(border.shape[1:], border.dtype),
+            pltpu.VMEM(columns.shape, columns.dtype),
+            pltpu.SemaphoreType.DMA((6,)),
+        ],
+        compiler_params=PARAMS,
+        cost_estimate=long_cost(20),
         name="front",
-    )(columns, moved, *borders)
-    return couplings, keep, send
+    )(order, in_hbm(columns), in_hbm(factor), in_hbm(border))
 
 
 def deal_kernel(border_ref, *refs):
@@ -181,36 +177,43 @@
     )(in_hbm(border))
 
 
-def quarter_kernel(keep_ref, got_ref, *refs):
-    count = (len(refs) + 1) // 2
-    riders, out_refs = refs[: count - 1], refs[count - 1 :]
+def quarter_kernel(keep_ref, got_ref, *out_refs):
     place = lax.axis_index("col")
     rows = out_refs[0].shape[0]
     for m, out_ref in enumerate(out_refs):
         at = pl.ds(pl.multiple_of((place ^ m) * rows, 8), rows)
-        out_ref[:rows, :] = keep_ref[at, :] + got_ref[at, :]
-        if m > 0:
-            size, wide = riders[m - 1].shape
-            for n in range(wide // BLOCK):
-                out_ref[rows + n * size : rows + (n + 1) * size, :] = riders[m - 1][
-                    :, n * BLOCK : (n + 1) * BLOCK
-                ]
-
-
-def quarters(keep, got, riders):
-    count = len(riders) + 1
-    rows = keep.shape[0] // count
-    extra = riders[0].size // BLOCK
-    out_shape = [jax.ShapeDtypeStruct((rows, BLOCK), jnp.float32)]
-    out_shape += [jax.ShapeDtypeStruct((rows + extra, BLOCK), jnp.float32)] * (count - 1)
+        out_ref[...] = keep_ref[at, :] + got_ref[at, :]
+
+
+def quarters(keep, got, col_count):
+    piece = jax.ShapeDtypeStruct((keep.shape[0] // col_count, BLOCK), jnp.float32)
     return pl.pallas_call(
         quarter_kernel,
-        out_shape=out_shape,
-        in_specs=[VMEM] * (1 + count),
-        out_specs=[VMEM] * count,
+        out_shape=[piece] * col_count,
+        in_specs=[VMEM, VMEM],
+        out_specs=[VMEM] * col_count,
         compiler_params=PARAMS,
         name="quarters",
-    )(keep, got, *riders)
+    )(keep, got)
+
+
+def join_kernel(*refs, count):
+    pieces, out_ref = refs[:count], refs[-1]
+    place = lax.axis_index("col")
+    rows = pieces[0].shape[0]
+    for m, piece in enumerate(pieces):
+        out_ref[pl.ds(pl.multiple_of((place ^ m) * rows, 8), rows), :] = piece[...]
+
+
+def join(pieces, waits):
+    return pl.pallas_call(
+        functools.partial(join_kernel, count=len(pieces)),
+        out_shape=jax.ShapeDtypeStruct((len(pieces) * pieces[0].shape[0], BLOCK), jnp.float32),
+        in_specs=[VMEM] * len(pieces) + [ANY] * len(waits),
+        out_specs=VMEM,
+        compiler_params=PARAMS,
+        name="join",
+    )(*pieces, *waits)
 
 
 def swap(value, axis, step):
@@ -290,25 +293,19 @@
                 panels[j] = panels[j] - exact_tn(rest[:, at : at + BLOCK], rest[:, at:])
 
 
-def early_kernel(*refs, col_count):
-    pieces = refs[: 2 * col_count]
-    barrier_ref, upper_ref, inverse_ref, rest_ref, packed_ref = refs[2 * col_count :]
+def early_kernel(mine_ref, other_ref, barrier_ref, upper_ref, inverse_ref, rest_ref):
     width = barrier_ref.shape[1]
     count = width // BLOCK
-    rows = pieces[0].shape[0]
     core = lax.rem(lax.axis_index("scen"), 2)
-    place = lax.axis_index("col")
-    for side in range(2):
-        owner = core if side == 0 else 1 - core
-        for m in range(col_count):
-            at = (owner * col_count + (place ^ m)) * rows
-            packed_ref[pl.ds(pl.multiple_of(at, 8), rows), :] = pieces[side * col_count + m][...]
     diagonal = lax.broadcasted_iota(jnp.int32, (BLOCK, BLOCK), 0) == lax.broadcasted_iota(
         jnp.int32, (BLOCK, BLOCK), 1
     )
     blocks = {}
-    for n, (i, j) in enumerate(upper_blocks(width)):
-        blocks[i, j] = packed_ref[n * BLOCK : (n + 1) * BLOCK, :]
+    names = upper_blocks(width)
+    half = len(names) // 2
+    for n, (i, j) in enumerate(names):
+        at = slice(n % half * BLOCK, (n % half + 1) * BLOCK)
+        blocks[i, j] = jnp.where(core == n // half, mine_ref[at, :], other_ref[at, :])
         if i == j:
             extra = barrier_ref[:, i * BLOCK : (i + 1) * BLOCK]
             blocks[i, j] = blocks[i, j] + jnp.where(diagonal, extra, 0.0)
@@ -319,33 +316,30 @@
         rest_ref[(i - done) * BLOCK : (i - done + 1) * BLOCK, (i - done) * BLOCK :] = panels[i]
 
 
-def early_cholesky(pieces, barrier):
+def early_cholesky(mine, other, barrier, done):
     width = barrier.shape[0]
-    half = width // 2
-    col_count = len(pieces) // 2
-    return pl.pallas_call(
-        functools.partial(early_kernel, col_count=col_count),
+    rows = done * BLOCK
+    return pl.pallas_call(
+        early_kernel,
         out_shape=[
-            jax.ShapeDtypeStruct((half, width), jnp.float32),
-            jax.ShapeDtypeStruct((half // BLOCK, BLOCK, BLOCK), jnp.float32),
-            jax.ShapeDtypeStruct((half, half), jnp.float32),
+            jax.ShapeDtypeStruct((rows, width), jnp.float32),
+            jax.ShapeDtypeStruct((done, BLOCK, BLOCK), jnp.float32),
+            jax.ShapeDtypeStruct((width - rows, width - rows), jnp.float32),
         ],
-        in_specs=[VMEM] * (len(pieces) + 1),
+        in_specs=[VMEM] * 3,
         out_specs=[VMEM] * 3,
-        scratch_shapes=[pltpu.VMEM((len(upper_blocks(width)) * BLOCK, BLOCK), jnp.float32)],
         compiler_params=PARAMS,
         cost_estimate=long_cost(20),
         name="early",
-    )(*pieces, barrier[None])
+    )(mine, other, barrier[None])
 
 
 def late_kernel(*refs):
     early_ref, rest_ref = refs[:2]
     upper_ref, inverse_ref, slice_ref, turned_ref = refs[-4:]
-    width = early_ref.shape[1]
+    rows, width = early_ref.shape
     count = width // BLOCK
-    done = count // 2
-    half = done * BLOCK
+    done = rows // BLOCK
     place = lax.axis_index("col")
     panels = [None] * done + [
         rest_ref[i * BLOCK : (i + 1) * BLOCK, i * BLOCK :] for i in range(count - done)
@@ -354,21 +348,22 @@
     slice_rows = slice_ref.shape[0]
     start = place * slice_rows
     block = pl.ds(pl.multiple_of(start // BLOCK * BLOCK, BLOCK), BLOCK)
-    turned_ref[:, :half] = early_ref[:, block].T
-    turned_ref[:, half:] = upper_ref[:, block].T
+    turned_ref[:, :rows] = early_ref[:, block].T
+    turned_ref[:, rows:] = upper_ref[:, block].T
     slice_ref[...] = turned_ref[pl.ds(pl.multiple_of(lax.rem(start, BLOCK), 8), slice_rows), :]
 
 
 def late_cholesky(early, rest, col_count, waits):
-    half, width = early.shape
+    width = early.shape[1]
+    rest_rows = width - early.shape[0]
     return pl.pallas_call(
         late_kernel,
         out_shape=[
-            jax.ShapeDtypeStruct((half, width), jnp.float32),
-            jax.ShapeDtypeStruct((half // BLOCK, BLOCK, BLOCK), jnp.float32),
+            jax.ShapeDtypeStruct((rest_rows, width), jnp.float32),
+            jax.ShapeDtypeStruct((rest_rows // BLOCK, BLOCK, BLOCK), jnp.float32),
             jax.ShapeDtypeStruct((width // col_count, width), jnp.float32),
         ],
-        in_specs=[VMEM, VMEM] + [HBM] * len(waits),
+        in_specs=[VMEM, VMEM] + [ANY] * len(waits),
         out_specs=[VMEM] * 3,
         scratch_shapes=[pltpu.VMEM((BLOCK, width), jnp.float32)],
         compiler_params=PARAMS,
@@ -377,39 +372,55 @@
     )(early, rest, *waits)
 
 
-def assemble_kernel(columns_ref, rows_ref, own_ref, *refs):
-    parts, total_ref, out_ref = refs[:-2], refs[-2], refs[-1]
-    rows = total_ref.shape[0]
-    total_ref[...] = tree_sum([part[:rows, :] for part in parts])
+def coupling_kernel(moved_ref, *refs, parts):
+    count = (len(refs) - parts - 1) // 2
+    refs[parts + count][...] = tree_sum([ref[...] for ref in refs[:parts]])
+    moved = moved_ref[...]
+    for border_ref, out_ref in zip(refs[parts:], refs[parts + count + 1 :]):
+        out_ref[...] = matmul_nt(border_ref[...], moved)
+
+
+def sum_and_couplings(parts, moved, borders):
+    shape = jax.ShapeDtypeStruct((borders[0].shape[0], moved.shape[0]), jnp.float32)
+    total, *partial = pl.pallas_call(
+        functools.partial(coupling_kernel, parts=len(parts)),
+        out_shape=[jax.ShapeDtypeStruct(parts[0].shape, jnp.float32)] + [shape] * len(borders),
+        in_specs=[VMEM] * (len(parts) + len(borders) + 1),
+        out_specs=[VMEM] * (len(borders) + 1),
+        compiler_params=PARAMS,
+        name="couplings",
+    )(moved, *parts, *borders)
+    return total, partial
+
+
+def assemble_kernel(columns_ref, rows_ref, *refs, parts):
+    refs[-2][...] = tree_sum([ref[...] for ref in refs[:parts]])
+    pieces, out_ref = refs[parts:-2], refs[-1]
     place = lax.axis_index("col")
-    size, wide = own_ref.shape
-    count = len(parts)
-    out_ref[pl.ds(pl.multiple_of(place * size, 8), size), :] = own_ref[...]
-    for m in range(1, count):
-        at = pl.ds(pl.multiple_of((place ^ m) * size, 8), size)
-        for n in range(wide // BLOCK):
-            out_ref[at, n * BLOCK : (n + 1) * BLOCK] = parts[m][
-                rows + n * size : rows + (n + 1) * size, :
-            ]
-    out_ref[count * size :, :] = jnp.zeros((out_ref.shape[0] - count * size, wide), jnp.float32)
-    out_ref[count * size : count * size + count, :] = columns_ref[...].astype(jnp.float32)
-    at = count * size + count
-    out_ref[at : at + count, :size] = rows_ref[0].astype(jnp.float32)
-
-
-def sum_and_assemble(parts, own, columns, rows):
-    size, wide = own.shape
-    return pl.pallas_call(
-        assemble_kernel,
+    size = pieces[0].shape[0]
+    count = len(pieces)
+    for m, piece in enumerate(pieces):
+        out_ref[pl.ds(pl.multiple_of((place ^ m) * size, 8), size), :] = piece[...]
+    at = count * size
+    out_ref[at:, :] = jnp.zeros((out_ref.shape[0] - at, out_ref.shape[1]), jnp.float32)
+    out_ref[at : at + count, :] = columns_ref[...].astype(jnp.float32)
+    out_ref[at + count : at + 2 * count, :size] = rows_ref[0].astype(jnp.float32)
+
+
+def sum_and_assemble(parts, pieces, columns, rows):
+    size, wide = pieces[0].shape
+    count = len(pieces)
+    return pl.pallas_call(
+        functools.partial(assemble_kernel, parts=len(parts)),
         out_shape=[
             jax.ShapeDtypeStruct(parts[0].shape, jnp.float32),
-            jax.ShapeDtypeStruct((len(parts) * size + -(-len(parts) // 4) * 8, wide), jnp.float32),
+            jax.ShapeDtypeStruct((count * size + -(-count // 4) * 8, wide), jnp.float32),
         ],
-        in_specs=[VMEM] * (len(parts) + 3),
+        in_specs=[VMEM] * (len(parts) + count + 2),
         out_specs=[VMEM] * 2,
         compiler_params=PARAMS,
         name="assemble",
-    )(columns, rows, own, *parts)
+    )(columns, rows, *parts, *pieces)
 
 
 def build_kernel(*refs, group):
@@ -448,7 +459,7 @@
     return pl.pallas_call(
         functools.partial(build_kernel, group=group),
         out_shape=[half, half],
-        in_specs=[HBM] + [VMEM] * len(groups),
+        in_specs=[ANY] + [VMEM] * len(groups),
         out_specs=[VMEM, VMEM],
         compiler_params=PARAMS,
         cost_estimate=long_cost(5),
@@ -457,16 +468,18 @@
 
 
 def solve_kernel(keep_ref, got_ref, early_ref, late_ref, first_ref, last_ref, out_ref):
-    uppers, inverses = (early_ref, late_ref), (first_ref, last_ref)
     count = out_ref.shape[1] // BLOCK
-    done = count // 2
+    done = first_ref.shape[0]
     here = [slice(k * BLOCK, (k + 1) * BLOCK) for k in range(count)]
     left = [keep_ref[:, h] + got_ref[:, h] for h in here]
     for k in range(count):
-        solved = exact_nt(left[k], inverses[k // done][k % done])
+        upper_ref, inverse_ref, at = (
+            (early_ref, first_ref, k) if k < done else (late_ref, last_ref, k - done)
+        )
+        solved = exact_nt(left[k], inverse_ref[at])
         out_ref[:, here[k]] = solved
         for j in range(k + 1, count):
-            left[j] = left[j] - exact(solved, uppers[k // done][here[k % done], here[j]])
+            left[j] = left[j] - exact(solved, upper_ref[here[at], here[j]])
 
 
 def solve_rows(keep, got, uppers, inverses):
@@ -523,22 +536,25 @@
     group, size = panel_border.shape[1:3]
     wide = slab_columns.shape[1]
 
+    moved, keep, send = front(true_orders, slab_columns, inverse_factor, slab_border, width)
+    got = swap(send, "scen", 1)
+    parts = quarters(keep, got, col_count)
     dealt = deal(panel_border)
     borders = [dealt[0]] + [swap(dealt[m], "col", m) for m in range(1, col_count)]
-    moved = transform(true_orders, inverse_factor, slab_border)
-    couplings, keep, send = front(slab_columns, moved, width, borders)
-    got = swap(send, "scen", 1)
-    parts = quarters(keep, got, couplings[1:])
     parts = [parts[0]] + [swap(parts[m], "col", m) for m in range(1, col_count)]
-    part, own = sum_and_assemble(parts, couplings[0], slab_columns, panel_rows)
+    part, partial = sum_and_couplings(parts, moved, borders)
+    parts = [part] + [swap(part, "scen", 2 * m) for m in range(1, scen_count // 2)]
+    pieces = [partial[0]] + [swap(partial[m], "col", m) for m in range(1, col_count)]
+    part, own = sum_and_assemble(parts, pieces, slab_columns, panel_rows)
     rows_panel = rows_here * scen_count
     sparse = scen_count * group * size * wide < rows_panel * width
-    part = tree_sum([part] + [swap(part, "scen", 2 * m) for m in range(1, scen_count // 2)])
-    pieces = [part] + [swap(part, "col", m) for m in range(1, col_count)]
-    pieces = pieces + [swap(piece, "scen", 1) for piece in pieces]
-    early, early_inverse, rest = early_cholesky(pieces, barrier_diag)
+    groups = [own]
     if sparse:
-        groups = [own] + [swap(own, "scen", 2 * m) for m in range(1, scen_count // 2)]
+        groups += [swap(own, "scen", 2 * m) for m in range(1, scen_count // 2)]
+    mine = join([part] + [swap(part, "col", m) for m in range(1, col_count)], groups[1:2])
+    done = (width // BLOCK * 3) // 4
+    early, early_inverse, rest = early_cholesky(mine, swap(mine, "scen", 1), barrier_diag, done)
+    if sparse:
         rows, other = build_rows(groups, group, rows_here, width, rest)
         late, late_inverse, factor_rows = late_cholesky(early, rest, col_count, [other])
         solved = solve_rows(

time: 78.1 us -> 70.6 us (0.904)
  the two profiles are of different devices: /device:TPU:17 before, /device:TPU:0 now
where the time goes in v5:
time: 70.6 us; the launch traced here: 70.1 us
  Pallas kernels  31.5 us (45%)
  starting transfers between devices  25.3 us (36%)
  waiting for transfers between devices  11.9 us (17%)
  between operations  1.4 us (2%)
    ppermute x21, starting transfers between devices, swap(): return lax.ppermute(value, axis, [(i, i ^ step) for i in range(count)])  25.3 us
    pallas_call x1, Pallas kernels, early_cholesky(): pl.pallas_call(early_kernel, out_shape=[jax.ShapeDtypeStruct((rows, width...  16.2 us
    ppermute x21, waiting for transfers between devices, swap(): return lax.ppermute(value, axis, [(i, i ^ step) for i in range(count)])  11.9 us
    pallas_call x1, Pallas kernels, late_cholesky(): pl.pallas_call(late_kernel, out_shape=[jax.ShapeDtypeStruct((rest_rows, w...  5.32 us
    pallas_call x1, Pallas kernels, solve_rows(): pl.pallas_call(solve_kernel, out_shape=jax.ShapeDtypeStruct(keep.shape, j...  2.99 us
    pallas_call x1, Pallas kernels, build_rows(): pl.pallas_call(functools.partial(build_kernel, group=group), out_shape=[h...  2.83 us
    pallas_call x1, Pallas kernels, front(): pl.pallas_call(functools.partial(front_kernel, width=width), out_shape=[j...  2.75 us
  transfers between devices with their start and end apart: 21, of which 7 were waited for; matrix products, arithmetic and copies ran while one was open for 0% of the time, Pallas kernels for 32%

profile of v5, /device:TPU:0, one launch (start us, length us, event | category | flops | bytes accessed | tf_op | source)
XLA Modules:
  0.0 70.1 jit_solution(8677508784706621228)
XLA Ops:
  1.3 2.8 %front.1 = (bf16[256,512]{1,0:T(8,128)(2,1)S(1)}, f32[640,128]{1,0:T(8,128)S(1)}, f32[640,128]{1,0:T(8,128)S(1)}) custom-call(s32[1]{0:T(128)S(6)} %copy.9.order_ref, s32[4,256]{1,0:T(4,128)} %columns_ref.3, bf16[1,512,512]{2,1,0:T(8,128)(2,1)} %factor_ref.1, bf16[1,256,512]{2,1,0:T(8,128)(2,1)} %border_ref.2), custom_call_target="tpu_custom_call" | custom-call | flops 20000000000 | bytes 1048576 | tf_op jit(solution)/shard_map/front/pallas_call | solution.py:136
  4.6 0.9 %deal.1 = (bf16[48,512]{1,0:T(8,128)(2,1)S(1)}, bf16[48,512]{1,0:T(8,128)(2,1)S(1)}, bf16[48,512]{1,0:T(8,128)(2,1)S(1)}, bf16[48,512]{1,0:T(8,128)(2,1)S(1)}) custom-call(bf16[1,4,48,512]{3,2,1,0:T(8,128)(2,1)} %border_ref.3), custom_call_target="tpu_custom_call" | custom-call | tf_op jit(solution)/shard_map/deal/pallas_call | solution.py:169
  5.5 2.6 %collective-permute-start.4 = (bf16[48,512]{1,0:T(8,128)(2,1)S(1)}, bf16[48,512]{1,0:T(8,128)(2,1)S(1)}, u32[]{:S(2)}, u32[]{:S(2)}) collective-permute-start(bf16[48,512]{1,0:T(8,128)(2,1)S(1)} %get-tuple-element.36), channel_id=1, source_target_pairs={{0,1},{1,0},{2,3},{3,2},{4,5},{5,4},{6,7},{7,6},{8,9},{9,8},{10,11... | collective-permute-start | bytes 147464 | tf_op jit(solution)/shard_map/ppermute | solution.py:221
  8.8 1.5 %collective-permute-start.2 = (f32[160,128]{1,0:T(8,128)S(1)}, f32[160,128]{1,0:T(8,128)S(1)}, u32[]{:S(2)}, u32[]{:S(2)}) collective-permute-start(f32[160,128]{1,0:T(8,128)S(1)} %get-tuple-element.33), channel_id=1, source_target_pairs={{0,2},{1,3},{2,0},{3,1},{4,6},{5,7},{6,4},{7,5},{8,10},{9,11},{10,... | collective-permute-start | bytes 245768 | tf_op jit(solution)/shard_map/ppermute | solution.py:221
  10.3 1.3 %collective-permute-start.3 = (f32[160,128]{1,0:T(8,128)S(1)}, f32[160,128]{1,0:T(8,128)S(1)}, u32[]{:S(2)}, u32[]{:S(2)}) collective-permute-start(f32[160,128]{1,0:T(8,128)S(1)} %get-tuple-element.34), channel_id=1, source_target_pairs={{0,3},{1,2},{2,1},{3,0},{4,7},{5,6},{6,5},{7,4},{8,11},{9,10},{10,... | collective-permute-start | bytes 245768 | tf_op jit(solution)/shard_map/ppermute | solution.py:221
  11.6 1.5 %collective-permute-start.5 = (bf16[48,512]{1,0:T(8,128)(2,1)S(1)}, bf16[48,512]{1,0:T(8,128)(2,1)S(1)}, u32[]{:S(2)}, u32[]{:S(2)}) collective-permute-start(bf16[48,512]{1,0:T(8,128)(2,1)S(1)} %get-tuple-element.37), channel_id=1, source_target_pairs={{0,2},{1,3},{2,0},{3,1},{4,6},{5,7},{6,4},{7,5},{8,10},{9,11},{10,... | collective-permute-start | bytes 147464 | tf_op jit(solution)/shard_map/ppermute | solution.py:221
  13.7 3.1 %collective-permute-done.5.refs_6_ = bf16[48,512]{1,0:T(8,128)(2,1)S(1)} collective-permute-done((bf16[48,512]{1,0:T(8,128)(2,1)S(1)}, bf16[48,512]{1,0:T(8,128)(2,1)S(1)}, u32[]{:S(2)}, u32[]{:S(2)}) %collective-permute-start.5) | collective-permute-done | bytes 49184 | tf_op jit(solution)/shard_map/ppermute | solution.py:221
  16.8 1.4 %collective-permute-done.6.refs_7_ = bf16[48,512]{1,0:T(8,128)(2,1)S(1)} collective-permute-done((bf16[48,512]{1,0:T(8,128)(2,1)S(1)}, bf16[48,512]{1,0:T(8,128)(2,1)S(1)}, u32[]{:S(2)}, u32[]{:S(2)}) %collective-permute-start.6) | collective-permute-done | bytes 49184 | tf_op jit(solution)/shard_map/ppermute | solution.py:221
  19.3 1.6 %collective-permute-start.7 = (f32[160,128]{1,0:T(8,128)S(1)}, f32[160,128]{1,0:T(8,128)S(1)}, u32[]{:S(2)}, u32[]{:S(2)}) collective-permute-start(f32[160,128]{1,0:T(8,128)S(1)} %get-tuple-element.39.refs_0_), channel_id=1, source_target_pairs={{0,8},{4,12},{8,0},{12,4},{16,24},{20,28},{24,16},{28,20},{1,9},{5... | collective-permute-start | bytes 245768 | tf_op jit(solution)/shard_map/ppermute | solution.py:221
  20.9 2.6 %collective-permute-start.8 = (f32[160,128]{1,0:T(8,128)S(1)}, f32[160,128]{1,0:T(8,128)S(1)}, u32[]{:S(2)}, u32[]{:S(2)}) collective-permute-start(f32[160,128]{1,0:T(8,128)S(1)} %get-tuple-element.39.refs_0_), channel_id=1, source_target_pairs={{0,16},{4,20},{8,24},{12,28},{16,0},{20,4},{24,8},{28,12},{1,17},{... | collective-permute-start | bytes 245768 | tf_op jit(solution)/shard_map/ppermute | solution.py:221
  23.7 1.2 %collective-permute-start.11 = (f32[48,256]{1,0:T(8,128)S(1)}, f32[48,256]{1,0:T(8,128)S(1)}, u32[]{:S(2)}, u32[]{:S(2)}) collective-permute-start(f32[48,256]{1,0:T(8,128)S(1)} %get-tuple-element.42), channel_id=1, source_target_pairs={{0,2},{1,3},{2,0},{3,1},{4,6},{5,7},{6,4},{7,5},{8,10},{9,11},{10,... | collective-permute-start | bytes 147464 | tf_op jit(solution)/shard_map/ppermute | solution.py:221
  24.9 1.6 %collective-permute-start.12 = (f32[48,256]{1,0:T(8,128)S(1)}, f32[48,256]{1,0:T(8,128)S(1)}, u32[]{:S(2)}, u32[]{:S(2)}) collective-permute-start(f32[48,256]{1,0:T(8,128)S(1)} %get-tuple-element.43), channel_id=1, source_target_pairs={{0,3},{1,2},{2,1},{3,0},{4,7},{5,6},{6,5},{7,4},{8,11},{9,10},{10,... | collective-permute-start | bytes 147464 | tf_op jit(solution)/shard_map/ppermute | solution.py:221
  26.5 1.2 %collective-permute-done.11.refs_6_ = f32[48,256]{1,0:T(8,128)S(1)} collective-permute-done((f32[48,256]{1,0:T(8,128)S(1)}, f32[48,256]{1,0:T(8,128)S(1)}, u32[]{:S(2)}, u32[]{:S(2)}) %collective-permute-start.11) | collective-permute-done | bytes 49184 | tf_op jit(solution)/shard_map/ppermute | solution.py:221
  27.8 2.1 %collective-permute-done.12.refs_7_ = f32[48,256]{1,0:T(8,128)S(1)} collective-permute-done((f32[48,256]{1,0:T(8,128)S(1)}, f32[48,256]{1,0:T(8,128)S(1)}, u32[]{:S(2)}, u32[]{:S(2)}) %collective-permute-start.12) | collective-permute-done | bytes 49184 | tf_op jit(solution)/shard_map/ppermute | solution.py:221
  30.0 0.7 %collective-permute-start.16 = (f32[200,256]{1,0:T(8,128)S(1)}, f32[200,256]{1,0:T(8,128)S(1)}, u32[]{:S(2)}, u32[]{:S(2)}) collective-permute-start(f32[200,256]{1,0:T(8,128)S(1)} %get-tuple-element.45.refs_1_), channel_id=1, source_target_pairs={{0,8},{4,12},{8,0},{12,4},{16,24},{20,28},{24,16},{28,20},{1,9},{5... | collective-permute-start | bytes 614408 | tf_op jit(solution)/shard_map/ppermute | solution.py:221
  31.4 1.5 %collective-permute-start.14 = (f32[160,128]{1,0:T(8,128)S(1)}, f32[160,128]{1,0:T(8,128)S(1)}, u32[]{:S(2)}, u32[]{:S(2)}) collective-permute-start(f32[160,128]{1,0:T(8,128)S(1)} %get-tuple-element.44.refs_0_), channel_id=1, source_target_pairs={{0,2},{1,3},{2,0},{3,1},{4,6},{5,7},{6,4},{7,5},{8,10},{9,11},{10,... | collective-permute-start | bytes 245768 | tf_op jit(solution)/shard_map/ppermute | solution.py:221
  32.9 1.3 %collective-permute-start.15 = (f32[160,128]{1,0:T(8,128)S(1)}, f32[160,128]{1,0:T(8,128)S(1)}, u32[]{:S(2)}, u32[]{:S(2)}) collective-permute-start(f32[160,128]{1,0:T(8,128)S(1)} %get-tuple-element.44.refs_0_), channel_id=1, source_target_pairs={{0,3},{1,2},{2,1},{3,0},{4,7},{5,6},{6,5},{7,4},{8,11},{9,10},{10,... | collective-permute-start | bytes 245768 | tf_op jit(solution)/shard_map/ppermute | solution.py:221
  34.2 1.0 %collective-permute-done.13.refs_1_ = f32[160,128]{1,0:T(8,128)S(1)} collective-permute-done((f32[160,128]{1,0:T(8,128)S(1)}, f32[160,128]{1,0:T(8,128)S(1)}, u32[]{:S(2)}, u32[]{:S(2)}) %collective-permute-start.13) | collective-permute-done | bytes 81952 | tf_op jit(solution)/shard_map/ppermute | solution.py:221
  35.8 2.4 %collective-permute-done.15.refs_3_ = f32[160,128]{1,0:T(8,128)S(1)} collective-permute-done((f32[160,128]{1,0:T(8,128)S(1)}, f32[160,128]{1,0:T(8,128)S(1)}, u32[]{:S(2)}, u32[]{:S(2)}) %collective-permute-start.15) | collective-permute-done | bytes 81952 | tf_op jit(solution)/shard_map/ppermute | solution.py:221
  38.4 4.1 %collective-permute-start.18 = (f32[200,256]{1,0:T(8,128)S(1)}, f32[200,256]{1,0:T(8,128)S(1)}, u32[]{:S(2)}, u32[]{:S(2)}) collective-permute-start(f32[200,256]{1,0:T(8,128)S(1)} %get-tuple-element.45.refs_1_), channel_id=1, source_target_pairs={{0,16},{4,20},{8,24},{12,28},{16,0},{20,4},{24,8},{28,12},{1,17},{... | collective-permute-start | bytes 614408 | tf_op jit(solution)/shard_map/ppermute | solution.py:221
  42.5 16.2 %early.1 = (f32[384,512]{1,0:T(8,128)S(1)}, f32[3,128,128]{2,1,0:T(8,128)S(1)}, f32[128,128]{1,0:T(8,128)S(1)}) custom-call(f32[640,128]{1,0:T(8,128)S(1)} %join.1.mine_ref, f32[640,128]{1,0:T(8,128)S(1)} %collective-permute-done.17.other_ref, f32[1,512]{1,0:T(1,128)S(1)} %bitcast.1), custom_call_target="tpu_custom_call" | custom-call | flops 20000000000 | bytes 1048576 | tf_op jit(solution)/shard_map/early/pallas_call | solution.py:322
  58.7 2.8 %build.1 = (f32[240,512]{1,0:T(8,128)S(1)}, f32[240,512]{1,0:T(8,128)S(1)}) custom-call(f32[128,128]{1,0:T(8,128)S(1)} %get-tuple-element.47.refs_0_.refs_1_, f32[200,256]{1,0:T(8,128)S(1)} %get-tuple-element.45.refs_1_, f32[200,256]{1,0:T(8,128)S(1)} %collective-permute-done.16.refs_4_.refs_2_, f32[200,256]{1,0:T(8,128)S(1)} %collective-permute-done.18.refs_3_, ...), custom_call_target="tpu_custom_call" | custom-call | flops 5000000000 | bytes 1048576 | tf_op jit(solution)/shard_map/build/pallas_call | solution.py:459
  61.8 5.3 %late.1 = (f32[128,512]{1,0:T(8,128)S(1)}, f32[1,128,128]{2,1,0:T(8,128)S(1)}, f32[128,512]{1,0:T(8,128)}) custom-call(f32[384,512]{1,0:T(8,128)S(1)} %get-tuple-element.46.refs_0_.early_ref, f32[128,128]{1,0:T(8,128)S(1)} %get-tuple-element.47.refs_0_.refs_1_, f32[240,512]{1,0:T(8,128)S(1)} %get-tuple-element.48.refs_2_), custom_call_target="tpu_custom_call" | custom-call | flops 20000000000 | bytes 1048576 | tf_op jit(solution)/shard_map/late/pallas_call | solution.py:359
  67.1 3.0 %solve.1 = f32[240,512]{1,0:T(8,128)} custom-call(f32[240,512]{1,0:T(8,128)S(1)} %get-tuple-element.50.keep_ref, f32[240,512]{1,0:T(8,128)S(1)} %collective-permute-done.20.got_ref, f32[384,512]{1,0:T(8,128)S(1)} %get-tuple-element.46.refs_0_.early_ref, f32[128,512]{1,0:T(8,128)S(1)} %get-tuple-element.51.late_ref, ...), custom_call_target="tpu_custom_call" | custom-call | tf_op jit(solution)/shard_map/solve/pallas_call | solution.py:486
  (34 shorter events, 4.9 us)
Async XLA Ops:
  4.0 4.0 %collective-permute-start = (f32[640,128]{1,0:T(8,128)S(1)}, f32[640,128]{1,0:T(8,128)S(1)}, u32[]{:S(2)}, u32[]{:S(2)}) collective-permute-start(f32[640,128]{1,0:T(8,128)S(1)} %get-tuple-element.30), channel_id=1, source_target_pairs={{0,4},{4,0},{8,12},{12,8},{16,20},{20,16},{24,28},{28,24},{1,5},{5... | collective-permute-start | bytes 983048 | tf_op jit(solution)/shard_map/ppermute | solution.py:221
  5.5 7.7 %collective-permute-start.4 = (bf16[48,512]{1,0:T(8,128)(2,1)S(1)}, bf16[48,512]{1,0:T(8,128)(2,1)S(1)}, u32[]{:S(2)}, u32[]{:S(2)}) collective-permute-start(bf16[48,512]{1,0:T(8,128)(2,1)S(1)} %get-tuple-element.36), channel_id=1, source_target_pairs={{0,1},{1,0},{2,3},{3,2},{4,5},{5,4},{6,7},{7,6},{8,9},{9,8},{10,11... | collective-permute-start | bytes 147464 | tf_op jit(solution)/shard_map/ppermute | solution.py:221
  8.1 10.1 %collective-permute-start.1 = (f32[160,128]{1,0:T(8,128)S(1)}, f32[160,128]{1,0:T(8,128)S(1)}, u32[]{:S(2)}, u32[]{:S(2)}) collective-permute-start(f32[160,128]{1,0:T(8,128)S(1)} %get-tuple-element.32), channel_id=1, source_target_pairs={{0,1},{1,0},{2,3},{3,2},{4,5},{5,4},{6,7},{7,6},{8,9},{9,8},{10,11... | collective-permute-start | bytes 245768 | tf_op jit(solution)/shard_map/ppermute | solution.py:221
  8.8 9.4 %collective-permute-start.2 = (f32[160,128]{1,0:T(8,128)S(1)}, f32[160,128]{1,0:T(8,128)S(1)}, u32[]{:S(2)}, u32[]{:S(2)}) collective-permute-start(f32[160,128]{1,0:T(8,128)S(1)} %get-tuple-element.33), channel_id=1, source_target_pairs={{0,2},{1,3},{2,0},{3,1},{4,6},{5,7},{6,4},{7,5},{8,10},{9,11},{10,... | collective-permute-start | bytes 245768 | tf_op jit(solution)/shard_map/ppermute | solution.py:221
  10.3 7.9 %collective-permute-start.3 = (f32[160,128]{1,0:T(8,128)S(1)}, f32[160,128]{1,0:T(8,128)S(1)}, u32[]{:S(2)}, u32[]{:S(2)}) collective-permute-start(f32[160,128]{1,0:T(8,128)S(1)} %get-tuple-element.34), channel_id=1, source_target_pairs={{0,3},{1,2},{2,1},{3,0},{4,7},{5,6},{6,5},{7,4},{8,11},{9,10},{10,... | collective-permute-start | bytes 245768 | tf_op jit(solution)/shard_map/ppermute | solution.py:221
  11.6 5.2 %collective-permute-start.5 = (bf16[48,512]{1,0:T(8,128)(2,1)S(1)}, bf16[48,512]{1,0:T(8,128)(2,1)S(1)}, u32[]{:S(2)}, u32[]{:S(2)}) collective-permute-start(bf16[48,512]{1,0:T(8,128)(2,1)S(1)} %get-tuple-element.37), channel_id=1, source_target_pairs={{0,2},{1,3},{2,0},{3,1},{4,6},{5,7},{6,4},{7,5},{8,10},{9,11},{10,... | collective-permute-start | bytes 147464 | tf_op jit(solution)/shard_map/ppermute | solution.py:221
  13.2 5.0 %collective-permute-start.6 = (bf16[48,512]{1,0:T(8,128)(2,1)S(1)}, bf16[48,512]{1,0:T(8,128)(2,1)S(1)}, u32[]{:S(2)}, u32[]{:S(2)}) collective-permute-start(bf16[48,512]{1,0:T(8,128)(2,1)S(1)} %get-tuple-element.38), channel_id=1, source_target_pairs={{0,3},{1,2},{2,1},{3,0},{4,7},{5,6},{6,5},{7,4},{8,11},{9,10},{10,... | collective-permute-start | bytes 147464 | tf_op jit(solution)/shard_map/ppermute | solution.py:221
  18.6 11.3 %copy-start = (s32[4,256]{1,0:T(4,128)S(1)}, s32[4,256]{1,0:T(4,128)}, u32[]{:S(2)}) copy-start(s32[4,256]{1,0:T(4,128)} %columns_ref.3) | copy-start | bytes 12292
  18.6 6.3 %collective-permute-start.10 = (f32[48,256]{1,0:T(8,128)S(1)}, f32[48,256]{1,0:T(8,128)S(1)}, u32[]{:S(2)}, u32[]{:S(2)}) collective-permute-start(f32[48,256]{1,0:T(8,128)S(1)} %get-tuple-element.41), channel_id=1, source_target_pairs={{0,1},{1,0},{2,3},{3,2},{4,5},{5,4},{6,7},{7,6},{8,9},{9,8},{10,11... | collective-permute-start | bytes 147464 | tf_op jit(solution)/shard_map/ppermute | solution.py:221
  19.3 10.6 %collective-permute-start.7 = (f32[160,128]{1,0:T(8,128)S(1)}, f32[160,128]{1,0:T(8,128)S(1)}, u32[]{:S(2)}, u32[]{:S(2)}) collective-permute-start(f32[160,128]{1,0:T(8,128)S(1)} %get-tuple-element.39.refs_0_), channel_id=1, source_target_pairs={{0,8},{4,12},{8,0},{12,4},{16,24},{20,28},{24,16},{28,20},{1,9},{5... | collective-permute-start | bytes 245768 | tf_op jit(solution)/shard_map/ppermute | solution.py:221
  20.9 9.0 %collective-permute-start.8 = (f32[160,128]{1,0:T(8,128)S(1)}, f32[160,128]{1,0:T(8,128)S(1)}, u32[]{:S(2)}, u32[]{:S(2)}) collective-permute-start(f32[160,128]{1,0:T(8,128)S(1)} %get-tuple-element.39.refs_0_), channel_id=1, source_target_pairs={{0,16},{4,20},{8,24},{12,28},{16,0},{20,4},{24,8},{28,12},{1,17},{... | collective-permute-start | bytes 245768 | tf_op jit(solution)/shard_map/ppermute | solution.py:221
  23.4 6.5 %collective-permute-start.9 = (f32[160,128]{1,0:T(8,128)S(1)}, f32[160,128]{1,0:T(8,128)S(1)}, u32[]{:S(2)}, u32[]{:S(2)}) collective-permute-start(f32[160,128]{1,0:T(8,128)S(1)} %get-tuple-element.39.refs_0_), channel_id=1, source_target_pairs={{0,24},{4,28},{8,16},{12,20},{16,8},{20,12},{24,0},{28,4},{1,25},{... | collective-permute-start | bytes 245768 | tf_op jit(solution)/shard_map/ppermute | solution.py:221
  23.7 6.3 %copy-start.1 = (s32[1,4,48]{2,1,0:T(4,128)S(1)}, s32[1,4,48]{2,1,0:T(4,128)}, u32[]{:S(2)}) copy-start(s32[1,4,48]{2,1,0:T(4,128)} %rows_ref.1) | copy-start | bytes 2308
  23.7 4.1 %collective-permute-start.11 = (f32[48,256]{1,0:T(8,128)S(1)}, f32[48,256]{1,0:T(8,128)S(1)}, u32[]{:S(2)}, u32[]{:S(2)}) collective-permute-start(f32[48,256]{1,0:T(8,128)S(1)} %get-tuple-element.42), channel_id=1, source_target_pairs={{0,2},{1,3},{2,0},{3,1},{4,6},{5,7},{6,4},{7,5},{8,10},{9,11},{10,... | collective-permute-start | bytes 147464 | tf_op jit(solution)/shard_map/ppermute | solution.py:221
  24.9 5.0 %collective-permute-start.12 = (f32[48,256]{1,0:T(8,128)S(1)}, f32[48,256]{1,0:T(8,128)S(1)}, u32[]{:S(2)}, u32[]{:S(2)}) collective-permute-start(f32[48,256]{1,0:T(8,128)S(1)} %get-tuple-element.43), channel_id=1, source_target_pairs={{0,3},{1,2},{2,1},{3,0},{4,7},{5,6},{6,5},{7,4},{8,11},{9,10},{10,... | collective-permute-start | bytes 147464 | tf_op jit(solution)/shard_map/ppermute | solution.py:221
  30.0 8.3 %collective-permute-start.16 = (f32[200,256]{1,0:T(8,128)S(1)}, f32[200,256]{1,0:T(8,128)S(1)}, u32[]{:S(2)}, u32[]{:S(2)}) collective-permute-start(f32[200,256]{1,0:T(8,128)S(1)} %get-tuple-element.45.refs_1_), channel_id=1, source_target_pairs={{0,8},{4,12},{8,0},{12,4},{16,24},{20,28},{24,16},{28,20},{1,9},{5... | collective-permute-start | bytes 614408 | tf_op jit(solution)/shard_map/ppermute | solution.py:221
  30.7 11.7 %copy-start.2 = (f32[512]{0:T(512)S(1)}, f32[512]{0:T(512)}, u32[]{:S(2)}) copy-start(f32[512]{0:T(512)} %param.13) | copy-start | bytes 6148
  30.7 4.4 %collective-permute-start.13 = (f32[160,128]{1,0:T(8,128)S(1)}, f32[160,128]{1,0:T(8,128)S(1)}, u32[]{:S(2)}, u32[]{:S(2)}) collective-permute-start(f32[160,128]{1,0:T(8,128)S(1)} %get-tuple-element.44.refs_0_), channel_id=1, source_target_pairs={{0,1},{1,0},{2,3},{3,2},{4,5},{5,4},{6,7},{7,6},{8,9},{9,8},{10,11... | collective-permute-start | bytes 245768 | tf_op jit(solution)/shard_map/ppermute | solution.py:221
  31.4 4.4 %collective-permute-start.14 = (f32[160,128]{1,0:T(8,128)S(1)}, f32[160,128]{1,0:T(8,128)S(1)}, u32[]{:S(2)}, u32[]{:S(2)}) collective-permute-start(f32[160,128]{1,0:T(8,128)S(1)} %get-tuple-element.44.refs_0_), channel_id=1, source_target_pairs={{0,2},{1,3},{2,0},{3,1},{4,6},{5,7},{6,4},{7,5},{8,10},{9,11},{10,... | collective-permute-start | bytes 245768 | tf_op jit(solution)/shard_map/ppermute | solution.py:221
  32.9 5.3 %collective-permute-start.15 = (f32[160,128]{1,0:T(8,128)S(1)}, f32[160,128]{1,0:T(8,128)S(1)}, u32[]{:S(2)}, u32[]{:S(2)}) collective-permute-start(f32[160,128]{1,0:T(8,128)S(1)} %get-tuple-element.44.refs_0_), channel_id=1, source_target_pairs={{0,3},{1,2},{2,1},{3,0},{4,7},{5,6},{6,5},{7,4},{8,11},{9,10},{10,... | collective-permute-start | bytes 245768 | tf_op jit(solution)/shard_map/ppermute | solution.py:221
  38.3 4.2 %collective-permute-start.17 = (f32[640,128]{1,0:T(8,128)S(1)}, f32[640,128]{1,0:T(8,128)S(1)}, u32[]{:S(2)}, u32[]{:S(2)}) collective-permute-start(f32[640,128]{1,0:T(8,128)S(1)} %join.1.mine_ref), channel_id=1, source_target_pairs={{0,4},{4,0},{8,12},{12,8},{16,20},{20,16},{24,28},{28,24},{1,5},{5... | collective-permute-start | bytes 983048 | tf_op jit(solution)/shard_map/ppermute | solution.py:221
  38.4 20.3 %collective-permute-start.18 = (f32[200,256]{1,0:T(8,128)S(1)}, f32[200,256]{1,0:T(8,128)S(1)}, u32[]{:S(2)}, u32[]{:S(2)}) collective-permute-start(f32[200,256]{1,0:T(8,128)S(1)} %get-tuple-element.45.refs_1_), channel_id=1, source_target_pairs={{0,16},{4,20},{8,24},{12,28},{16,0},{20,4},{24,8},{28,12},{1,17},{... | collective-permute-start | bytes 614408 | tf_op jit(solution)/shard_map/ppermute | solution.py:221
  42.5 16.2 %collective-permute-start.19 = (f32[200,256]{1,0:T(8,128)S(1)}, f32[200,256]{1,0:T(8,128)S(1)}, u32[]{:S(2)}, u32[]{:S(2)}) collective-permute-start(f32[200,256]{1,0:T(8,128)S(1)} %get-tuple-element.45.refs_1_), channel_id=1, source_target_pairs={{0,24},{4,28},{8,16},{12,20},{16,8},{20,12},{24,0},{28,4},{1,25},{... | collective-permute-start | bytes 614408 | tf_op jit(solution)/shard_map/ppermute | solution.py:221
  61.5 5.6 %collective-permute-start.20 = (f32[240,512]{1,0:T(8,128)S(1)}, f32[240,512]{1,0:T(8,128)S(1)}, u32[]{:S(2)}, u32[]{:S(2)}) collective-permute-start(f32[240,512]{1,0:T(8,128)S(1)} %get-tuple-element.48.refs_2_), channel_id=1, source_target_pairs={{0,4},{4,0},{8,12},{12,8},{16,20},{20,16},{24,28},{28,24},{1,5},{5... | collective-permute-start | bytes 1474568 | tf_op jit(solution)/shard_map/ppermute | solution.py:221

commit v6 on v5

--- a/solution.py
+++ b/solution.py
@@ -18,7 +18,7 @@
 
 
 def long_cost(micros):
-    return pl.CostEstimate(flops=micros * 10**9, bytes_accessed=2**20, transcendentals=0)
+    return pl.CostEstimate(flops=micros * 10**9, bytes_accessed=2**10, transcendentals=0)
 
 
 def in_hbm(value):
@@ -198,19 +198,25 @@
 
 
 def join_kernel(*refs, count):
-    pieces, out_ref = refs[:count], refs[-1]
+    pieces, first_ref, last_ref, all_ref = refs[:count], refs[-3], refs[-2], refs[-1]
     place = lax.axis_index("col")
     rows = pieces[0].shape[0]
     for m, piece in enumerate(pieces):
-        out_ref[pl.ds(pl.multiple_of((place ^ m) * rows, 8), rows), :] = piece[...]
+        all_ref[pl.ds(pl.multiple_of((place ^ m) * rows, 8), rows), :] = piece[...]
+    half = first_ref.shape[0]
+    first_ref[...] = all_ref[:half, :]
+    last_ref[...] = all_ref[half:, :]
 
 
 def join(pieces, waits):
+    rows = len(pieces) * pieces[0].shape[0]
+    half = jax.ShapeDtypeStruct((rows // 2, BLOCK), jnp.float32)
     return pl.pallas_call(
         functools.partial(join_kernel, count=len(pieces)),
-        out_shape=jax.ShapeDtypeStruct((len(pieces) * pieces[0].shape[0], BLOCK), jnp.float32),
+        out_shape=[half, half],
         in_specs=[VMEM] * len(pieces) + [ANY] * len(waits),
-        out_specs=VMEM,
+        out_specs=[VMEM, VMEM],
+        scratch_shapes=[pltpu.VMEM((rows, BLOCK), jnp.float32)],
         compiler_params=PARAMS,
         name="join",
     )(*pieces, *waits)
@@ -232,144 +238,151 @@
 
 
 def column_of(tile, j):
-    return jnp.broadcast_to(tile[:, j : j + 1], (tile.shape[0], BLOCK))
+    index = jnp.full(tile.shape, j, jnp.int32)
+    return jnp.take_along_axis(tile, index, axis=1, mode="promise_in_bounds")
+
+
+def weighted_rows(weights, rows):
+    total = weights[0] * rows[0]
+    for weight, row in zip(weights[1:], rows[1:]):
+        total = total + weight * row
+    return total
 
 
 def factor_block(block):
     groups = BLOCK // 8
     sub = lax.broadcasted_iota(jnp.int32, (8, BLOCK), 0)
     lane = lax.broadcasted_iota(jnp.int32, (8, BLOCK), 1)
-    left = [block[8 * t : 8 * t + 8, :] for t in range(groups)]
-    right = [(lane == sub + 8 * t).astype(jnp.float32) for t in range(groups)]
+    owner = lax.shift_right_logical(lane, 3)
+    tiles = [block[8 * t : 8 * t + 8, :] for t in range(groups)]
     upper = []
-    inverse = []
-    for g in range(groups):
-        a, b = left[g], right[g]
-        near = [column_of(a, 8 * g + m) for m in range(8)]
-        out_a, out_b = a, b
-        for i in range(8):
-            pivot = row_of(near[i], i)
-            recip = 1.0 / pivot
-            root = lax.rsqrt(pivot)
-            factor = jnp.where(sub == i, 1.0 - recip, near[i] * recip)
-            row_a, row_b = row_of(a, i), row_of(b, i)
-            out_a = jnp.where(sub == i, row_a * root, out_a)
-            out_b = jnp.where(sub == i, row_b * root, out_b)
-            for m in range(i + 1, 8):
-                near[m] = near[m] - factor * row_of(near[m], i)
-            a = a - factor * row_a
-            b = b - factor * row_b
-        upper.append(jnp.where(lane >= sub + 8 * g, out_a, 0.0))
-        inverse.append(out_b)
-        if g + 1 < groups:
-            rows_a = [row_of(a, i) for i in range(8)]
-            rows_b = [row_of(b, i) for i in range(8)]
-            for t in range(g + 1, groups):
-                weights = [column_of(left[t], 8 * g + i) for i in range(8)]
-                sum_a = weights[0] * rows_a[0]
-                sum_b = weights[0] * rows_b[0]
-                for i in range(1, 8):
-                    sum_a = sum_a + weights[i] * rows_a[i]
-                    sum_b = sum_b + weights[i] * rows_b[i]
-                left[t] = left[t] - sum_a
-                right[t] = right[t] - sum_b
-    return jnp.concatenate(upper, 0), jnp.concatenate(inverse, 0)
-
-
-def eliminate(panels, first, last, upper_ref, inverse_ref):
-    count = len(panels)
-    for i in range(first, last):
-        here = slice((i - first) * BLOCK, (i - first + 1) * BLOCK)
+    lower = []
+    ready = None
+    for pair in range(groups // 2):
+        far = min(groups, 2 * pair + 4)
+        swept = []
+        for g in (2 * pair, 2 * pair + 1):
+            more = g + 1 < groups
+            tile = tiles[g]
+            near = ready or [column_of(tile, 8 * g + m) for m in range(8)]
+            if more:
+                near = near + [column_of(tile, 8 * g + 8 + m) for m in range(8)]
+            mixed = jnp.where(owner == g, (lane == sub + 8 * g).astype(jnp.float32), tile)
+            out_tile, out_mixed = tile, mixed
+            pivot = row_of(near[0], 0)
+            for i in range(8):
+                root = lax.rsqrt(pivot)
+                recip = root * root
+                rows = {m: row_of(near[m], i) for m in range(i + 1, len(near))}
+                if i < 7:
+                    pivot = row_of(near[i + 1], i + 1) - row_of(near[i], i + 1) * rows[i + 1] * recip
+                factor = jnp.where(sub == i, 1.0 - recip, near[i] * recip)
+                for m in rows:
+                    near[m] = near[m] - factor * rows[m]
+                row_tile, row_mixed = row_of(tile, i), row_of(mixed, i)
+                out_tile = jnp.where(sub == i, row_tile * root, out_tile)
+                out_mixed = jnp.where(sub == i, row_mixed * root, out_mixed)
+                tile = tile - factor * row_tile
+                mixed = mixed - factor * row_mixed
+            inner = jnp.where((owner == g) & (lane >= sub + 8 * g), out_tile, 0.0)
+            upper.append(jnp.where(owner > g, out_mixed, inner))
+            lower.append(jnp.where(owner <= g, out_mixed, 0.0))
+            rows = [row_of(mixed, i) for i in range(8)]
+            swept.append((mixed, rows))
+            if not more:
+                break
+            following = tiles[g + 1]
+            weights = [column_of(following, 8 * g + i) for i in range(8)]
+            ready = [
+                column_of(following, 8 * g + 8 + m)
+                - weighted_rows(weights, [row_of(near[8 + m], i) for i in range(8)])
+                for m in range(8)
+            ]
+            for t in range(g + 1, far):
+                if t > g + 1:
+                    weights = [column_of(tiles[t], 8 * g + i) for i in range(8)]
+                tiles[t] = jnp.where(owner == g, 0.0, tiles[t]) - weighted_rows(weights, rows)
+        if far < groups:
+            g = 2 * pair
+            first, second = swept[0][0], swept[1][0]
+            weights = [column_of(first, 8 * g + 8 + i) for i in range(8)]
+            first = jnp.where(owner == g + 1, 0.0, first) - weighted_rows(weights, swept[1][1])
+            parts = [first, second, jnp.zeros((BLOCK - 8 * g - 16, BLOCK), jnp.float32)]
+            if g > 0:
+                parts = [jnp.zeros((8 * g, BLOCK), jnp.float32)] + parts
+            update = exact(jnp.concatenate(tiles[far:], 0), jnp.concatenate(parts, 0))
+            for t in range(far, groups):
+                kept = jnp.where((owner == g) | (owner == g + 1), 0.0, tiles[t])
+                tiles[t] = kept - update[8 * (t - far) : 8 * (t - far) + 8]
+    return jnp.concatenate(upper, 0), jnp.concatenate(lower, 0)
+
+
+def cholesky_kernel(
+    mine_first, mine_last, other_first, other_last, barrier_ref, inverse_ref, slice_ref, upper_ref,
+    turned_ref, packed_ref
+):
+    width = barrier_ref.shape[1]
+    count = width // BLOCK
+    core = lax.rem(lax.axis_index("scen"), 2)
+    place = lax.axis_index("col")
+    diagonal = lax.broadcasted_iota(jnp.int32, (BLOCK, BLOCK), 0) == lax.broadcasted_iota(
+        jnp.int32, (BLOCK, BLOCK), 1
+    )
+    blocks = {}
+    rows = mine_first.shape[0]
+    for n, ref in enumerate((mine_first, mine_last, other_first, other_last)):
+        owner = core if n < 2 else 1 - core
+        at = (2 * owner + n % 2) * rows
+        packed_ref[pl.ds(pl.multiple_of(at, 8), rows), :] = ref[...]
+    for n, (i, j) in enumerate(upper_blocks(width)):
+        blocks[i, j] = packed_ref[n * BLOCK : (n + 1) * BLOCK, :]
+        if i == j:
+            extra = barrier_ref[:, i * BLOCK : (i + 1) * BLOCK]
+            blocks[i, j] = blocks[i, j] + jnp.where(diagonal, extra, 0.0)
+    panels = [jnp.concatenate([blocks[i, j] for j in range(i, count)], 1) for i in range(count)]
+    upper_ref[...] = jnp.zeros(upper_ref.shape, jnp.float32)
+    inverse_ref[...] = jnp.zeros(inverse_ref.shape, jnp.float32)
+    for i in range(count):
+        here = slice(i * BLOCK, (i + 1) * BLOCK)
+        before = slice(0, i * BLOCK)
         own, inverse = factor_block(panels[i][:, :BLOCK])
-        if i > 0:
-            upper_ref[here, : i * BLOCK] = jnp.zeros((BLOCK, i * BLOCK), jnp.float32)
-        upper_ref[here, i * BLOCK : (i + 1) * BLOCK] = own
-        inverse_ref[i - first] = inverse
+        upper_ref[here, here] = own
+        inverse_ref[here, here] = inverse
         if i + 1 < count:
             rest = exact(inverse, panels[i][:, BLOCK:])
             upper_ref[here, (i + 1) * BLOCK :] = rest
             for j in range(i + 1, count):
                 at = (j - i - 1) * BLOCK
                 panels[j] = panels[j] - exact_tn(rest[:, at : at + BLOCK], rest[:, at:])
-
-
-def early_kernel(mine_ref, other_ref, barrier_ref, upper_ref, inverse_ref, rest_ref):
-    width = barrier_ref.shape[1]
-    count = width // BLOCK
-    core = lax.rem(lax.axis_index("scen"), 2)
-    diagonal = lax.broadcasted_iota(jnp.int32, (BLOCK, BLOCK), 0) == lax.broadcasted_iota(
-        jnp.int32, (BLOCK, BLOCK), 1
-    )
-    blocks = {}
-    names = upper_blocks(width)
-    half = len(names) // 2
-    for n, (i, j) in enumerate(names):
-        at = slice(n % half * BLOCK, (n % half + 1) * BLOCK)
-        blocks[i, j] = jnp.where(core == n // half, mine_ref[at, :], other_ref[at, :])
-        if i == j:
-            extra = barrier_ref[:, i * BLOCK : (i + 1) * BLOCK]
-            blocks[i, j] = blocks[i, j] + jnp.where(diagonal, extra, 0.0)
-    panels = [jnp.concatenate([blocks[i, j] for j in range(i, count)], 1) for i in range(count)]
-    done = inverse_ref.shape[0]
-    eliminate(panels, 0, done, upper_ref, inverse_ref)
-    for i in range(done, count):
-        rest_ref[(i - done) * BLOCK : (i - done + 1) * BLOCK, (i - done) * BLOCK :] = panels[i]
-
-
-def early_cholesky(mine, other, barrier, done):
-    width = barrier.shape[0]
-    rows = done * BLOCK
-    return pl.pallas_call(
-        early_kernel,
-        out_shape=[
-            jax.ShapeDtypeStruct((rows, width), jnp.float32),
-            jax.ShapeDtypeStruct((done, BLOCK, BLOCK), jnp.float32),
-            jax.ShapeDtypeStruct((width - rows, width - rows), jnp.float32),
-        ],
-        in_specs=[VMEM] * 3,
-        out_specs=[VMEM] * 3,
-        compiler_params=PARAMS,
-        cost_estimate=long_cost(20),
-        name="early",
-    )(mine, other, barrier[None])
-
-
-def late_kernel(*refs):
-    early_ref, rest_ref = refs[:2]
-    upper_ref, inverse_ref, slice_ref, turned_ref = refs[-4:]
-    rows, width = early_ref.shape
-    count = width // BLOCK
-    done = rows // BLOCK
-    place = lax.axis_index("col")
-    panels = [None] * done + [
-        rest_ref[i * BLOCK : (i + 1) * BLOCK, i * BLOCK :] for i in range(count - done)
-    ]
-    eliminate(panels, done, count, upper_ref, inverse_ref)
+        if i > 0:
+            mixed = exact_tn(upper_ref[before, here], inverse_ref[before, before])
+            inverse_ref[here, before] = -exact(inverse, mixed)
     slice_rows = slice_ref.shape[0]
     start = place * slice_rows
     block = pl.ds(pl.multiple_of(start // BLOCK * BLOCK, BLOCK), BLOCK)
-    turned_ref[:, :rows] = early_ref[:, block].T
-    turned_ref[:, rows:] = upper_ref[:, block].T
+    turned_ref[...] = upper_ref[:, block].T
     slice_ref[...] = turned_ref[pl.ds(pl.multiple_of(lax.rem(start, BLOCK), 8), slice_rows), :]
 
 
-def late_cholesky(early, rest, col_count, waits):
-    width = early.shape[1]
-    rest_rows = width - early.shape[0]
-    return pl.pallas_call(
-        late_kernel,
+def cholesky(halves, barrier, col_count):
+    width = barrier.shape[0]
+    return pl.pallas_call(
+        cholesky_kernel,
         out_shape=[
-            jax.ShapeDtypeStruct((rest_rows, width), jnp.float32),
-            jax.ShapeDtypeStruct((rest_rows // BLOCK, BLOCK, BLOCK), jnp.float32),
+            jax.ShapeDtypeStruct((width, width), jnp.float32),
             jax.ShapeDtypeStruct((width // col_count, width), jnp.float32),
         ],
-        in_specs=[VMEM, VMEM] + [ANY] * len(waits),
-        out_specs=[VMEM] * 3,
-        scratch_shapes=[pltpu.VMEM((BLOCK, width), jnp.float32)],
-        compiler_params=PARAMS,
-        cost_estimate=long_cost(20),
-        name="late",
-    )(early, rest, *waits)
+        in_specs=[VMEM] * 5,
+        out_specs=[VMEM] * 2,
+        scratch_shapes=[
+            pltpu.VMEM((width, width), jnp.float32),
+            pltpu.VMEM((BLOCK, width), jnp.float32),
+            pltpu.VMEM((4 * halves[0].shape[0], BLOCK), jnp.float32),
+        ],
+        compiler_params=PARAMS,
+        cost_estimate=long_cost(0),
+        name="cholesky",
+    )(*halves, barrier[None])
 
 
 def coupling_kernel(moved_ref, *refs, parts):
@@ -423,16 +436,12 @@
     )(columns, rows, *parts, *pieces)
 
 
-def build_kernel(*refs, group):
-    groups = refs[1:-2]
-    keep_ref, send_ref = refs[-2:]
-    rows_here, width = keep_ref.shape
+def placed_rows(groups, group, rows_here, width):
     place = lax.axis_index("scen")
-    core = lax.rem(place, 2)
-    first = (place - core) * rows_here
+    first = (place - lax.rem(place, 2)) * rows_here
     size = (groups[0].shape[0] - 2 * group) // group
     wide = groups[0].shape[1]
-    total = jnp.zeros((2 * rows_here, width), jnp.float32)
+    total = None
     slot = lax.broadcasted_iota(jnp.int32, (2 * rows_here, group * size), 0)
     for group_ref in groups:
         index = group_ref[group * size :, :]
@@ -448,49 +457,67 @@
         )
         row_map = (slot == row_index.astype(jnp.int32) - first).astype(jnp.bfloat16)
         high, low = split_two(jnp.concatenate(spreads, 0))
-        total = total + (matmul(row_map, high) + matmul(row_map, low))
+        part = matmul(row_map, high) + matmul(row_map, low)
+        total = part if total is None else total + part
+    return total
+
+
+def near_kernel(*refs, group):
+    groups, out_ref = refs[1:-1], refs[-1]
+    rows, width = out_ref.shape
+    out_ref[...] = placed_rows(groups, group, rows // 2, width)
+
+
+def near_rows(groups, group, rows_here, width, wait):
+    return pl.pallas_call(
+        functools.partial(near_kernel, group=group),
+        out_shape=jax.ShapeDtypeStruct((2 * rows_here, width), jnp.float32),
+        in_specs=[ANY] + [VMEM] * len(groups),
+        out_specs=VMEM,
+        compiler_params=PARAMS,
+        cost_estimate=long_cost(0),
+        name="near",
+    )(wait, *groups)
+
+
+def far_kernel(near_ref, *refs, group):
+    groups = refs[:-2]
+    keep_ref, send_ref = refs[-2:]
+    rows_here, width = keep_ref.shape
+    core = lax.rem(lax.axis_index("scen"), 2)
+    total = near_ref[...] + placed_rows(groups, group, rows_here, width)
     lower, upper = total[:rows_here], total[rows_here:]
     keep_ref[...] = jnp.where(core == 0, lower, upper)
     send_ref[...] = jnp.where(core == 0, upper, lower)
 
 
-def build_rows(groups, group, rows_here, width, wait):
-    half = jax.ShapeDtypeStruct((rows_here, width), jnp.float32)
-    return pl.pallas_call(
-        functools.partial(build_kernel, group=group),
+def far_rows(near, groups, group):
+    rows, width = near.shape
+    half = jax.ShapeDtypeStruct((rows // 2, width), jnp.float32)
+    return pl.pallas_call(
+        functools.partial(far_kernel, group=group),
         out_shape=[half, half],
-        in_specs=[ANY] + [VMEM] * len(groups),
+        in_specs=[VMEM] * (1 + len(groups)),
         out_specs=[VMEM, VMEM],
         compiler_params=PARAMS,
-        cost_estimate=long_cost(5),
-        name="build",
-    )(wait, *groups)
-
-
-def solve_kernel(keep_ref, got_ref, early_ref, late_ref, first_ref, last_ref, out_ref):
-    count = out_ref.shape[1] // BLOCK
-    done = first_ref.shape[0]
-    here = [slice(k * BLOCK, (k + 1) * BLOCK) for k in range(count)]
-    left = [keep_ref[:, h] + got_ref[:, h] for h in here]
-    for k in range(count):
-        upper_ref, inverse_ref, at = (
-            (early_ref, first_ref, k) if k < done else (late_ref, last_ref, k - done)
-        )
-        solved = exact_nt(left[k], inverse_ref[at])
-        out_ref[:, here[k]] = solved
-        for j in range(k + 1, count):
-            left[j] = left[j] - exact(solved, upper_ref[here[at], here[j]])
-
-
-def solve_rows(keep, got, uppers, inverses):
+        cost_estimate=long_cost(0),
+        name="far",
+    )(near, *groups)
+
+
+def solve_kernel(keep_ref, got_ref, inverse_ref, out_ref):
+    out_ref[...] = exact_nt(keep_ref[...] + got_ref[...], inverse_ref[...])
+
+
+def solve_rows(keep, got, inverse):
     return pl.pallas_call(
         solve_kernel,
         out_shape=jax.ShapeDtypeStruct(keep.shape, jnp.float32),
-        in_specs=[VMEM] * 6,
+        in_specs=[VMEM] * 3,
         out_specs=VMEM,
         compiler_params=PARAMS,
         name="solve",
-    )(keep, got, *uppers, *inverses)
+    )(keep, got, inverse)
 
 
 def dense_panel(couplings_here, rows, columns, rows_panel, width):
@@ -504,20 +531,6 @@
     zero = jnp.zeros((rows_panel, width), jnp.float32)
     total, _ = lax.scan(step, zero, (couplings_here, rows, columns))
     return lax.psum_scatter(total, "scen", scatter_dimension=0, tiled=True)
-
-
-def dense_solve(rows, upper, inverse):
-    width = rows.shape[1]
-    solved = []
-    for k in range(width // BLOCK):
-        here = slice(k * BLOCK, (k + 1) * BLOCK)
-        left = rows[:, here]
-        if k > 0:
-            left = left - jnp.dot(
-                jnp.concatenate(solved, 1), upper[: k * BLOCK, here], precision=HIGHEST
-            )
-        solved.append(jnp.dot(left, inverse[k].T, precision=HIGHEST))
-    return jnp.concatenate(solved, 1)
 
 
 def shards(
@@ -551,24 +564,18 @@
     groups = [own]
     if sparse:
         groups += [swap(own, "scen", 2 * m) for m in range(1, scen_count // 2)]
-    mine = join([part] + [swap(part, "col", m) for m in range(1, col_count)], groups[1:2])
-    done = (width // BLOCK * 3) // 4
-    early, early_inverse, rest = early_cholesky(mine, swap(mine, "scen", 1), barrier_diag, done)
+    mine = join([part] + [swap(part, "col", m) for m in range(1, col_count)], [])
+    halves = list(mine) + [swap(half, "scen", 1) for half in mine]
+    inverse, factor_rows = cholesky(halves, barrier_diag, col_count)
     if sparse:
-        rows, other = build_rows(groups, group, rows_here, width, rest)
-        late, late_inverse, factor_rows = late_cholesky(early, rest, col_count, [other])
-        solved = solve_rows(
-            rows, swap(other, "scen", 1), (early, late), (early_inverse, late_inverse)
-        )
+        half = len(groups) // 2
+        near = near_rows(groups[:half], group, rows_here, width, inverse)
+        rows, other = far_rows(near, groups[half:], group)
+        solved = solve_rows(rows, swap(other, "scen", 1), inverse)
     else:
         local = own[: group * size].reshape(group, size, wide)
         rows = dense_panel(local, panel_rows[0], slab_columns, rows_panel, width)
-        late, late_inverse, factor_rows = late_cholesky(early, rest, col_count, [])
-        solved = dense_solve(
-            rows,
-            jnp.concatenate([early, late], 0),
-            jnp.concatenate([early_inverse, late_inverse], 0),
-        )
+        solved = jnp.dot(rows, inverse.T, precision=HIGHEST)
     return factor_rows, solved
 
 

time: 70.6 us -> 58.8 us (0.83)
  Pallas kernels: 31.5 us -> 21.4 us
  waiting for transfers between devices: 11.9 us -> 10.5 us
    pallas_call x3, Pallas kernels: 24.4 us -> 15.3 us  [the longest x1 12.3 us: cholesky(): pl.pallas_call(cholesky_kernel, out_shape=[jax.ShapeDtypeStruct((width, w...]
    ppermute x21 -> x22, waiting for transfers between devices: 11.9 us -> 10.5 us  [swap(): return lax.ppermute(value, axis, [(i, i ^ step) for i in range(count)])]
    pallas_call x1, Pallas kernels: 2.99 us -> 1.84 us  [solve_rows(): pl.pallas_call(solve_kernel, out_shape=jax.ShapeDtypeStruct(keep.shape, j...]
    ppermute x21 -> x22, starting transfers between devices: 25.3 us -> 25.3 us  [swap(): return lax.ppermute(value, axis, [(i, i ^ step) for i in range(count)])]
  transfers between devices with their start and end apart: 21 -> 22, of which waited for: 7 -> 7; matrix products, arithmetic and copies ran while one was open for 0% -> 0% of each run, Pallas kernels for 32% -> 25%
where the time goes in v6:
time: 58.8 us; the launch traced here: 58.6 us
  starting transfers between devices  25.3 us (43%)
  Pallas kernels  21.4 us (36%)
  waiting for transfers between devices  10.5 us (18%)
  between operations  1.4 us (2%)
    ppermute x22, starting transfers between devices, swap(): return lax.ppermute(value, axis, [(i, i ^ step) for i in range(count)])  25.3 us
    pallas_call x1, Pallas kernels, cholesky(): pl.pallas_call(cholesky_kernel, out_shape=[jax.ShapeDtypeStruct((width, w...  12.3 us
    ppermute x22, waiting for transfers between devices, swap(): return lax.ppermute(value, axis, [(i, i ^ step) for i in range(count)])  10.5 us
    pallas_call x1, Pallas kernels, front(): pl.pallas_call(functools.partial(front_kernel, width=width), out_shape=[j...  2.75 us
    pallas_call x1, Pallas kernels, solve_rows(): pl.pallas_call(solve_kernel, out_shape=jax.ShapeDtypeStruct(keep.shape, j...  1.84 us
    pallas_call x1, Pallas kernels, far_rows(): pl.pallas_call(functools.partial(far_kernel, group=group), out_shape=[hal...  1.53 us
    pallas_call x1, Pallas kernels, near_rows(): pl.pallas_call(functools.partial(near_kernel, group=group), out_shape=jax...  1.51 us
  transfers between devices with their start and end apart: 22, of which 7 were waited for; matrix products, arithmetic and copies ran while one was open for 0% of the time, Pallas kernels for 25%

profile of v6, /device:TPU:0, one launch (start us, length us, event | category | flops | bytes accessed | tf_op | source)
XLA Modules:
  0.0 58.6 jit_solution(8140700478743671890)
XLA Ops:
  1.3 2.8 %front.1 = (bf16[256,512]{1,0:T(8,128)(2,1)S(1)}, f32[640,128]{1,0:T(8,128)S(1)}, f32[640,128]{1,0:T(8,128)S(1)}) custom-call(s32[1]{0:T(128)S(6)} %copy.9.order_ref, s32[4,256]{1,0:T(4,128)} %columns_ref.3, bf16[1,512,512]{2,1,0:T(8,128)(2,1)} %factor_ref.1, bf16[1,256,512]{2,1,0:T(8,128)(2,1)} %border_ref.2), custom_call_target="tpu_custom_call" | custom-call | flops 20000000000 | bytes 1024 | tf_op jit(solution)/shard_map/front/pallas_call | solution.py:136
  4.6 0.9 %deal.1 = (bf16[48,512]{1,0:T(8,128)(2,1)S(1)}, bf16[48,512]{1,0:T(8,128)(2,1)S(1)}, bf16[48,512]{1,0:T(8,128)(2,1)S(1)}, bf16[48,512]{1,0:T(8,128)(2,1)S(1)}) custom-call(bf16[1,4,48,512]{3,2,1,0:T(8,128)(2,1)} %border_ref.3), custom_call_target="tpu_custom_call" | custom-call | tf_op jit(solution)/shard_map/deal/pallas_call | solution.py:169
  5.5 2.6 %collective-permute-start.4 = (bf16[48,512]{1,0:T(8,128)(2,1)S(1)}, bf16[48,512]{1,0:T(8,128)(2,1)S(1)}, u32[]{:S(2)}, u32[]{:S(2)}) collective-permute-start(bf16[48,512]{1,0:T(8,128)(2,1)S(1)} %get-tuple-element.34), channel_id=1, source_target_pairs={{0,1},{1,0},{2,3},{3,2},{4,5},{5,4},{6,7},{7,6},{8,9},{9,8},{10,11... | collective-permute-start | bytes 147464 | tf_op jit(solution)/shard_map/ppermute | solution.py:227
  8.8 1.5 %collective-permute-start.2 = (f32[160,128]{1,0:T(8,128)S(1)}, f32[160,128]{1,0:T(8,128)S(1)}, u32[]{:S(2)}, u32[]{:S(2)}) collective-permute-start(f32[160,128]{1,0:T(8,128)S(1)} %get-tuple-element.31), channel_id=1, source_target_pairs={{0,2},{1,3},{2,0},{3,1},{4,6},{5,7},{6,4},{7,5},{8,10},{9,11},{10,... | collective-permute-start | bytes 245768 | tf_op jit(solution)/shard_map/ppermute | solution.py:227
  10.3 1.3 %collective-permute-start.3 = (f32[160,128]{1,0:T(8,128)S(1)}, f32[160,128]{1,0:T(8,128)S(1)}, u32[]{:S(2)}, u32[]{:S(2)}) collective-permute-start(f32[160,128]{1,0:T(8,128)S(1)} %get-tuple-element.32), channel_id=1, source_target_pairs={{0,3},{1,2},{2,1},{3,0},{4,7},{5,6},{6,5},{7,4},{8,11},{9,10},{10,... | collective-permute-start | bytes 245768 | tf_op jit(solution)/shard_map/ppermute | solution.py:227
  11.6 1.5 %collective-permute-start.5 = (bf16[48,512]{1,0:T(8,128)(2,1)S(1)}, bf16[48,512]{1,0:T(8,128)(2,1)S(1)}, u32[]{:S(2)}, u32[]{:S(2)}) collective-permute-start(bf16[48,512]{1,0:T(8,128)(2,1)S(1)} %get-tuple-element.35), channel_id=1, source_target_pairs={{0,2},{1,3},{2,0},{3,1},{4,6},{5,7},{6,4},{7,5},{8,10},{9,11},{10,... | collective-permute-start | bytes 147464 | tf_op jit(solution)/shard_map/ppermute | solution.py:227
  13.7 3.1 %collective-permute-done.5.refs_6_ = bf16[48,512]{1,0:T(8,128)(2,1)S(1)} collective-permute-done((bf16[48,512]{1,0:T(8,128)(2,1)S(1)}, bf16[48,512]{1,0:T(8,128)(2,1)S(1)}, u32[]{:S(2)}, u32[]{:S(2)}) %collective-permute-start.5) | collective-permute-done | bytes 49184 | tf_op jit(solution)/shard_map/ppermute | solution.py:227
  16.8 1.4 %collective-permute-done.6.refs_7_ = bf16[48,512]{1,0:T(8,128)(2,1)S(1)} collective-permute-done((bf16[48,512]{1,0:T(8,128)(2,1)S(1)}, bf16[48,512]{1,0:T(8,128)(2,1)S(1)}, u32[]{:S(2)}, u32[]{:S(2)}) %collective-permute-start.6) | collective-permute-done | bytes 49184 | tf_op jit(solution)/shard_map/ppermute | solution.py:227
  19.3 3.6 %collective-permute-start.9 = (f32[160,128]{1,0:T(8,128)S(1)}, f32[160,128]{1,0:T(8,128)S(1)}, u32[]{:S(2)}, u32[]{:S(2)}) collective-permute-start(f32[160,128]{1,0:T(8,128)S(1)} %get-tuple-element.37.refs_0_), channel_id=1, source_target_pairs={{0,24},{4,28},{8,16},{12,20},{16,8},{20,12},{24,0},{28,4},{1,25},{... | collective-permute-start | bytes 245768 | tf_op jit(solution)/shard_map/ppermute | solution.py:227
  22.9 0.8 %collective-permute-start.7 = (f32[160,128]{1,0:T(8,128)S(1)}, f32[160,128]{1,0:T(8,128)S(1)}, u32[]{:S(2)}, u32[]{:S(2)}) collective-permute-start(f32[160,128]{1,0:T(8,128)S(1)} %get-tuple-element.37.refs_0_), channel_id=1, source_target_pairs={{0,8},{4,12},{8,0},{12,4},{16,24},{20,28},{24,16},{28,20},{1,9},{5... | collective-permute-start | bytes 245768 | tf_op jit(solution)/shard_map/ppermute | solution.py:227
  23.7 1.2 %collective-permute-start.11 = (f32[48,256]{1,0:T(8,128)S(1)}, f32[48,256]{1,0:T(8,128)S(1)}, u32[]{:S(2)}, u32[]{:S(2)}) collective-permute-start(f32[48,256]{1,0:T(8,128)S(1)} %get-tuple-element.40), channel_id=1, source_target_pairs={{0,2},{1,3},{2,0},{3,1},{4,6},{5,7},{6,4},{7,5},{8,10},{9,11},{10,... | collective-permute-start | bytes 147464 | tf_op jit(solution)/shard_map/ppermute | solution.py:227
  24.9 1.6 %collective-permute-start.12 = (f32[48,256]{1,0:T(8,128)S(1)}, f32[48,256]{1,0:T(8,128)S(1)}, u32[]{:S(2)}, u32[]{:S(2)}) collective-permute-start(f32[48,256]{1,0:T(8,128)S(1)} %get-tuple-element.41), channel_id=1, source_target_pairs={{0,3},{1,2},{2,1},{3,0},{4,7},{5,6},{6,5},{7,4},{8,11},{9,10},{10,... | collective-permute-start | bytes 147464 | tf_op jit(solution)/shard_map/ppermute | solution.py:227
  26.5 1.2 %collective-permute-done.11.refs_6_ = f32[48,256]{1,0:T(8,128)S(1)} collective-permute-done((f32[48,256]{1,0:T(8,128)S(1)}, f32[48,256]{1,0:T(8,128)S(1)}, u32[]{:S(2)}, u32[]{:S(2)}) %collective-permute-start.11) | collective-permute-done | bytes 49184 | tf_op jit(solution)/shard_map/ppermute | solution.py:227
  27.8 2.1 %collective-permute-done.12.refs_7_ = f32[48,256]{1,0:T(8,128)S(1)} collective-permute-done((f32[48,256]{1,0:T(8,128)S(1)}, f32[48,256]{1,0:T(8,128)S(1)}, u32[]{:S(2)}, u32[]{:S(2)}) %collective-permute-start.12) | collective-permute-done | bytes 49184 | tf_op jit(solution)/shard_map/ppermute | solution.py:227
  30.0 1.7 %collective-permute-start.15 = (f32[160,128]{1,0:T(8,128)S(1)}, f32[160,128]{1,0:T(8,128)S(1)}, u32[]{:S(2)}, u32[]{:S(2)}) collective-permute-start(f32[160,128]{1,0:T(8,128)S(1)} %get-tuple-element.42.refs_0_), channel_id=1, source_target_pairs={{0,3},{1,2},{2,1},{3,0},{4,7},{5,6},{6,5},{7,4},{8,11},{9,10},{10,... | collective-permute-start | bytes 245768 | tf_op jit(solution)/shard_map/ppermute | solution.py:227
  32.2 1.3 %collective-permute-start.13 = (f32[160,128]{1,0:T(8,128)S(1)}, f32[160,128]{1,0:T(8,128)S(1)}, u32[]{:S(2)}, u32[]{:S(2)}) collective-permute-start(f32[160,128]{1,0:T(8,128)S(1)} %get-tuple-element.42.refs_0_), channel_id=1, source_target_pairs={{0,1},{1,0},{2,3},{3,2},{4,5},{5,4},{6,7},{7,6},{8,9},{9,8},{10,11... | collective-permute-start | bytes 245768 | tf_op jit(solution)/shard_map/ppermute | solution.py:227
  33.5 1.2 %collective-permute-start.18 = (f32[200,256]{1,0:T(8,128)S(1)}, f32[200,256]{1,0:T(8,128)S(1)}, u32[]{:S(2)}, u32[]{:S(2)}) collective-permute-start(f32[200,256]{1,0:T(8,128)S(1)} %get-tuple-element.47.refs_1_), channel_id=1, source_target_pairs={{0,8},{4,12},{8,0},{12,4},{16,24},{20,28},{24,16},{28,20},{1,9},{5... | collective-permute-start | bytes 614408 | tf_op jit(solution)/shard_map/ppermute | solution.py:227
  34.8 2.4 %collective-permute-start.20 = (f32[200,256]{1,0:T(8,128)S(1)}, f32[200,256]{1,0:T(8,128)S(1)}, u32[]{:S(2)}, u32[]{:S(2)}) collective-permute-start(f32[200,256]{1,0:T(8,128)S(1)} %get-tuple-element.47.refs_1_), channel_id=1, source_target_pairs={{0,24},{4,28},{8,16},{12,20},{16,8},{20,12},{24,0},{28,4},{1,25},{... | collective-permute-start | bytes 614408 | tf_op jit(solution)/shard_map/ppermute | solution.py:227
  38.4 0.9 %collective-permute-done.16.other_first = f32[320,128]{1,0:T(8,128)S(1)} collective-permute-done((f32[320,128]{1,0:T(8,128)S(1)}, f32[320,128]{1,0:T(8,128)S(1)}, u32[]{:S(2)}, u32[]{:S(2)}) %collective-permute-start.16) | collective-permute-done | bytes 163872 | tf_op jit(solution)/shard_map/ppermute | solution.py:227
  39.5 12.3 %cholesky.1 = (f32[512,512]{1,0:T(8,128)S(1)}, f32[128,512]{1,0:T(8,128)}) custom-call(f32[320,128]{1,0:T(8,128)S(1)} %get-tuple-element.43.mine_first, f32[320,128]{1,0:T(8,128)S(1)} %get-tuple-element.44.mine_last, f32[320,128]{1,0:T(8,128)S(1)} %collective-permute-done.16.other_first, f32[320,128]{1,0:T(8,128)S(1)} %collective-permute-done.17.other_last, ...), custom_call_target="tpu_custom_call" | custom-call | bytes 1024 | tf_op jit(solution)/shard_map/cholesky/pallas_call | solution.py:369
  51.8 1.5 %near.1.near_ref = f32[480,512]{1,0:T(8,128)S(1)} custom-call(f32[512,512]{1,0:T(8,128)S(1)} %get-tuple-element.46.refs_0_.inverse_ref, f32[200,256]{1,0:T(8,128)S(1)} %get-tuple-element.47.refs_1_, f32[200,256]{1,0:T(8,128)S(1)} %collective-permute-done.18.refs_2_), custom_call_target="tpu_custom_call" | custom-call | bytes 1024 | tf_op jit(solution)/shard_map/near/pallas_call | solution.py:472
  53.3 1.5 %far.1 = (f32[240,512]{1,0:T(8,128)S(1)}, f32[240,512]{1,0:T(8,128)S(1)}) custom-call(f32[480,512]{1,0:T(8,128)S(1)} %near.1.near_ref, f32[200,256]{1,0:T(8,128)S(1)} %collective-permute-done.19.refs_0_, f32[200,256]{1,0:T(8,128)S(1)} %collective-permute-done.20.refs_1_), custom_call_target="tpu_custom_call" | custom-call | bytes 1024 | tf_op jit(solution)/shard_map/far/pallas_call | solution.py:497
  55.2 1.6 %collective-permute-done.21.got_ref = f32[240,512]{1,0:T(8,128)S(1)} collective-permute-done((f32[240,512]{1,0:T(8,128)S(1)}, f32[240,512]{1,0:T(8,128)S(1)}, u32[]{:S(2)}, u32[]{:S(2)}) %collective-permute-start.21) | collective-permute-done | bytes 491552 | tf_op jit(solution)/shard_map/ppermute | solution.py:227
  56.8 1.8 %solve.1 = f32[240,512]{1,0:T(8,128)} custom-call(f32[240,512]{1,0:T(8,128)S(1)} %get-tuple-element.48.keep_ref, f32[240,512]{1,0:T(8,128)S(1)} %collective-permute-done.21.got_ref, f32[512,512]{1,0:T(8,128)S(1)} %get-tuple-element.46.refs_0_.inverse_ref), custom_call_target="tpu_custom_call" | custom-call | tf_op jit(solution)/shard_map/solve/pallas_call | solution.py:513
  (36 shorter events, 5.3 us)
Async XLA Ops:
  4.0 4.0 %collective-permute-start = (f32[640,128]{1,0:T(8,128)S(1)}, f32[640,128]{1,0:T(8,128)S(1)}, u32[]{:S(2)}, u32[]{:S(2)}) collective-permute-start(f32[640,128]{1,0:T(8,128)S(1)} %get-tuple-element.28), channel_id=1, source_target_pairs={{0,4},{4,0},{8,12},{12,8},{16,20},{20,16},{24,28},{28,24},{1,5},{5... | collective-permute-start | bytes 983048 | tf_op jit(solution)/shard_map/ppermute | solution.py:227
  5.5 7.7 %collective-permute-start.4 = (bf16[48,512]{1,0:T(8,128)(2,1)S(1)}, bf16[48,512]{1,0:T(8,128)(2,1)S(1)}, u32[]{:S(2)}, u32[]{:S(2)}) collective-permute-start(bf16[48,512]{1,0:T(8,128)(2,1)S(1)} %get-tuple-element.34), channel_id=1, source_target_pairs={{0,1},{1,0},{2,3},{3,2},{4,5},{5,4},{6,7},{7,6},{8,9},{9,8},{10,11... | collective-permute-start | bytes 147464 | tf_op jit(solution)/shard_map/ppermute | solution.py:227
  8.1 10.1 %collective-permute-start.1 = (f32[160,128]{1,0:T(8,128)S(1)}, f32[160,128]{1,0:T(8,128)S(1)}, u32[]{:S(2)}, u32[]{:S(2)}) collective-permute-start(f32[160,128]{1,0:T(8,128)S(1)} %get-tuple-element.30), channel_id=1, source_target_pairs={{0,1},{1,0},{2,3},{3,2},{4,5},{5,4},{6,7},{7,6},{8,9},{9,8},{10,11... | collective-permute-start | bytes 245768 | tf_op jit(solution)/shard_map/ppermute | solution.py:227
  8.8 9.4 %collective-permute-start.2 = (f32[160,128]{1,0:T(8,128)S(1)}, f32[160,128]{1,0:T(8,128)S(1)}, u32[]{:S(2)}, u32[]{:S(2)}) collective-permute-start(f32[160,128]{1,0:T(8,128)S(1)} %get-tuple-element.31), channel_id=1, source_target_pairs={{0,2},{1,3},{2,0},{3,1},{4,6},{5,7},{6,4},{7,5},{8,10},{9,11},{10,... | collective-permute-start | bytes 245768 | tf_op jit(solution)/shard_map/ppermute | solution.py:227
  10.3 7.9 %collective-permute-start.3 = (f32[160,128]{1,0:T(8,128)S(1)}, f32[160,128]{1,0:T(8,128)S(1)}, u32[]{:S(2)}, u32[]{:S(2)}) collective-permute-start(f32[160,128]{1,0:T(8,128)S(1)} %get-tuple-element.32), channel_id=1, source_target_pairs={{0,3},{1,2},{2,1},{3,0},{4,7},{5,6},{6,5},{7,4},{8,11},{9,10},{10,... | collective-permute-start | bytes 245768 | tf_op jit(solution)/shard_map/ppermute | solution.py:227
  11.6 5.2 %collective-permute-start.5 = (bf16[48,512]{1,0:T(8,128)(2,1)S(1)}, bf16[48,512]{1,0:T(8,128)(2,1)S(1)}, u32[]{:S(2)}, u32[]{:S(2)}) collective-permute-start(bf16[48,512]{1,0:T(8,128)(2,1)S(1)} %get-tuple-element.35), channel_id=1, source_target_pairs={{0,2},{1,3},{2,0},{3,1},{4,6},{5,7},{6,4},{7,5},{8,10},{9,11},{10,... | collective-permute-start | bytes 147464 | tf_op jit(solution)/shard_map/ppermute | solution.py:227
  13.2 5.0 %collective-permute-start.6 = (bf16[48,512]{1,0:T(8,128)(2,1)S(1)}, bf16[48,512]{1,0:T(8,128)(2,1)S(1)}, u32[]{:S(2)}, u32[]{:S(2)}) collective-permute-start(bf16[48,512]{1,0:T(8,128)(2,1)S(1)} %get-tuple-element.36), channel_id=1, source_target_pairs={{0,3},{1,2},{2,1},{3,0},{4,7},{5,6},{6,5},{7,4},{8,11},{9,10},{10,... | collective-permute-start | bytes 147464 | tf_op jit(solution)/shard_map/ppermute | solution.py:227
  18.6 11.3 %copy-start = (s32[4,256]{1,0:T(4,128)S(1)}, s32[4,256]{1,0:T(4,128)}, u32[]{:S(2)}) copy-start(s32[4,256]{1,0:T(4,128)} %columns_ref.3) | copy-start | bytes 12292
  18.6 6.3 %collective-permute-start.10 = (f32[48,256]{1,0:T(8,128)S(1)}, f32[48,256]{1,0:T(8,128)S(1)}, u32[]{:S(2)}, u32[]{:S(2)}) collective-permute-start(f32[48,256]{1,0:T(8,128)S(1)} %get-tuple-element.39), channel_id=1, source_target_pairs={{0,1},{1,0},{2,3},{3,2},{4,5},{5,4},{6,7},{7,6},{8,9},{9,8},{10,11... | collective-permute-start | bytes 147464 | tf_op jit(solution)/shard_map/ppermute | solution.py:227
  19.3 10.6 %collective-permute-start.9 = (f32[160,128]{1,0:T(8,128)S(1)}, f32[160,128]{1,0:T(8,128)S(1)}, u32[]{:S(2)}, u32[]{:S(2)}) collective-permute-start(f32[160,128]{1,0:T(8,128)S(1)} %get-tuple-element.37.refs_0_), channel_id=1, source_target_pairs={{0,24},{4,28},{8,16},{12,20},{16,8},{20,12},{24,0},{28,4},{1,25},{... | collective-permute-start | bytes 245768 | tf_op jit(solution)/shard_map/ppermute | solution.py:227
  22.9 7.0 %collective-permute-start.8 = (f32[160,128]{1,0:T(8,128)S(1)}, f32[160,128]{1,0:T(8,128)S(1)}, u32[]{:S(2)}, u32[]{:S(2)}) collective-permute-start(f32[160,128]{1,0:T(8,128)S(1)} %get-tuple-element.37.refs_0_), channel_id=1, source_target_pairs={{0,16},{4,20},{8,24},{12,28},{16,0},{20,4},{24,8},{28,12},{1,17},{... | collective-permute-start | bytes 245768 | tf_op jit(solution)/shard_map/ppermute | solution.py:227
  22.9 7.0 %collective-permute-start.7 = (f32[160,128]{1,0:T(8,128)S(1)}, f32[160,128]{1,0:T(8,128)S(1)}, u32[]{:S(2)}, u32[]{:S(2)}) collective-permute-start(f32[160,128]{1,0:T(8,128)S(1)} %get-tuple-element.37.refs_0_), channel_id=1, source_target_pairs={{0,8},{4,12},{8,0},{12,4},{16,24},{20,28},{24,16},{28,20},{1,9},{5... | collective-permute-start | bytes 245768 | tf_op jit(solution)/shard_map/ppermute | solution.py:227
  23.7 6.3 %copy-start.1 = (s32[1,4,48]{2,1,0:T(4,128)S(1)}, s32[1,4,48]{2,1,0:T(4,128)}, u32[]{:S(2)}) copy-start(s32[1,4,48]{2,1,0:T(4,128)} %rows_ref.1) | copy-start | bytes 2308
  23.7 4.1 %collective-permute-start.11 = (f32[48,256]{1,0:T(8,128)S(1)}, f32[48,256]{1,0:T(8,128)S(1)}, u32[]{:S(2)}, u32[]{:S(2)}) collective-permute-start(f32[48,256]{1,0:T(8,128)S(1)} %get-tuple-element.40), channel_id=1, source_target_pairs={{0,2},{1,3},{2,0},{3,1},{4,6},{5,7},{6,4},{7,5},{8,10},{9,11},{10,... | collective-permute-start | bytes 147464 | tf_op jit(solution)/shard_map/ppermute | solution.py:227
  24.9 5.0 %collective-permute-start.12 = (f32[48,256]{1,0:T(8,128)S(1)}, f32[48,256]{1,0:T(8,128)S(1)}, u32[]{:S(2)}, u32[]{:S(2)}) collective-permute-start(f32[48,256]{1,0:T(8,128)S(1)} %get-tuple-element.41), channel_id=1, source_target_pairs={{0,3},{1,2},{2,1},{3,0},{4,7},{5,6},{6,5},{7,4},{8,11},{9,10},{10,... | collective-permute-start | bytes 147464 | tf_op jit(solution)/shard_map/ppermute | solution.py:227
  30.0 7.2 %collective-permute-start.15 = (f32[160,128]{1,0:T(8,128)S(1)}, f32[160,128]{1,0:T(8,128)S(1)}, u32[]{:S(2)}, u32[]{:S(2)}) collective-permute-start(f32[160,128]{1,0:T(8,128)S(1)} %get-tuple-element.42.refs_0_), channel_id=1, source_target_pairs={{0,3},{1,2},{2,1},{3,0},{4,7},{5,6},{6,5},{7,4},{8,11},{9,10},{10,... | collective-permute-start | bytes 245768 | tf_op jit(solution)/shard_map/ppermute | solution.py:227
  31.7 6.0 %collective-permute-start.14 = (f32[160,128]{1,0:T(8,128)S(1)}, f32[160,128]{1,0:T(8,128)S(1)}, u32[]{:S(2)}, u32[]{:S(2)}) collective-permute-start(f32[160,128]{1,0:T(8,128)S(1)} %get-tuple-element.42.refs_0_), channel_id=1, source_target_pairs={{0,2},{1,3},{2,0},{3,1},{4,6},{5,7},{6,4},{7,5},{8,10},{9,11},{10,... | collective-permute-start | bytes 245768 | tf_op jit(solution)/shard_map/ppermute | solution.py:227
  32.2 5.5 %collective-permute-start.13 = (f32[160,128]{1,0:T(8,128)S(1)}, f32[160,128]{1,0:T(8,128)S(1)}, u32[]{:S(2)}, u32[]{:S(2)}) collective-permute-start(f32[160,128]{1,0:T(8,128)S(1)} %get-tuple-element.42.refs_0_), channel_id=1, source_target_pairs={{0,1},{1,0},{2,3},{3,2},{4,5},{5,4},{6,7},{7,6},{8,9},{9,8},{10,11... | collective-permute-start | bytes 245768 | tf_op jit(solution)/shard_map/ppermute | solution.py:227
  33.5 18.2 %collective-permute-start.18 = (f32[200,256]{1,0:T(8,128)S(1)}, f32[200,256]{1,0:T(8,128)S(1)}, u32[]{:S(2)}, u32[]{:S(2)}) collective-permute-start(f32[200,256]{1,0:T(8,128)S(1)} %get-tuple-element.47.refs_1_), channel_id=1, source_target_pairs={{0,8},{4,12},{8,0},{12,4},{16,24},{20,28},{24,16},{28,20},{1,9},{5... | collective-permute-start | bytes 614408 | tf_op jit(solution)/shard_map/ppermute | solution.py:227
  34.8 18.5 %collective-permute-start.20 = (f32[200,256]{1,0:T(8,128)S(1)}, f32[200,256]{1,0:T(8,128)S(1)}, u32[]{:S(2)}, u32[]{:S(2)}) collective-permute-start(f32[200,256]{1,0:T(8,128)S(1)} %get-tuple-element.47.refs_1_), channel_id=1, source_target_pairs={{0,24},{4,28},{8,16},{12,20},{16,8},{20,12},{24,0},{28,4},{1,25},{... | collective-permute-start | bytes 614408 | tf_op jit(solution)/shard_map/ppermute | solution.py:227
  37.2 16.1 %collective-permute-start.19 = (f32[200,256]{1,0:T(8,128)S(1)}, f32[200,256]{1,0:T(8,128)S(1)}, u32[]{:S(2)}, u32[]{:S(2)}) collective-permute-start(f32[200,256]{1,0:T(8,128)S(1)} %get-tuple-element.47.refs_1_), channel_id=1, source_target_pairs={{0,16},{4,20},{8,24},{12,28},{16,0},{20,4},{24,8},{28,12},{1,17},{... | collective-permute-start | bytes 614408 | tf_op jit(solution)/shard_map/ppermute | solution.py:227
  37.8 1.5 %collective-permute-start.16 = (f32[320,128]{1,0:T(8,128)S(1)}, f32[320,128]{1,0:T(8,128)S(1)}, u32[]{:S(2)}, u32[]{:S(2)}) collective-permute-start(f32[320,128]{1,0:T(8,128)S(1)} %get-tuple-element.43.mine_first), channel_id=1, source_target_pairs={{0,4},{4,0},{8,12},{12,8},{16,20},{20,16},{24,28},{28,24},{1,5},{5... | collective-permute-start | bytes 491528 | tf_op jit(solution)/shard_map/ppermute | solution.py:227
  37.9 1.6 %collective-permute-start.17 = (f32[320,128]{1,0:T(8,128)S(1)}, f32[320,128]{1,0:T(8,128)S(1)}, u32[]{:S(2)}, u32[]{:S(2)}) collective-permute-start(f32[320,128]{1,0:T(8,128)S(1)} %get-tuple-element.44.mine_last), channel_id=1, source_target_pairs={{0,4},{4,0},{8,12},{12,8},{16,20},{20,16},{24,28},{28,24},{1,5},{5... | collective-permute-start | bytes 491528 | tf_op jit(solution)/shard_map/ppermute | solution.py:227
  54.8 1.9 %collective-permute-start.21 = (f32[240,512]{1,0:T(8,128)S(1)}, f32[240,512]{1,0:T(8,128)S(1)}, u32[]{:S(2)}, u32[]{:S(2)}) collective-permute-start(f32[240,512]{1,0:T(8,128)S(1)} %get-tuple-element.49), channel_id=1, source_target_pairs={{0,4},{4,0},{8,12},{12,8},{16,20},{20,16},{24,28},{28,24},{1,5},{5... | collective-permute-start | bytes 1474568 | tf_op jit(solution)/shard_map/ppermute | solution.py:227
  (1 other events, 1.7 us)

commit v7 on v6

--- a/solution.py
+++ b/solution.py
@@ -65,9 +65,55 @@
     )
 
 
+def packed_rows(width, unit):
+    count = width // BLOCK
+    rows = (count * (count - 1) // 2 + count // 2) * BLOCK + count // 2
+    return -(-rows // unit) * unit
+
+
 def upper_blocks(width):
     count = width // BLOCK
-    return [(i, j) for i in range(count) for j in range(i, count)]
+    return [(i, j) for i in range(count) for j in range(i + 1, count)]
+
+
+def row_and_lane():
+    shape = (BLOCK, BLOCK)
+    return lax.broadcasted_iota(jnp.int32, shape, 0), lax.broadcasted_iota(jnp.int32, shape, 1)
+
+
+def pack(blocks, width, packed_ref):
+    row, lane = row_and_lane()
+    first = 0
+    for name in upper_blocks(width):
+        packed_ref[first : first + BLOCK, :] = blocks[name]
+        first += BLOCK
+    diagonals = []
+    for i in range(0, width // BLOCK, 2):
+        one, two = blocks[i, i], blocks[i + 1, i + 1]
+        packed_ref[first : first + BLOCK, :] = jnp.where(row <= lane, one, two)
+        first += BLOCK
+        diagonals.append(jnp.sum(jnp.where(row == lane, two, 0.0), 0, keepdims=True))
+    spare = packed_ref.shape[0] - first - len(diagonals)
+    diagonals.append(jnp.zeros((spare, BLOCK), jnp.float32))
+    packed_ref[first:, :] = jnp.concatenate(diagonals, 0)
+
+
+def unpack(packed_ref, width):
+    row, lane = row_and_lane()
+    blocks = {}
+    first = 0
+    for name in upper_blocks(width):
+        blocks[name] = packed_ref[first : first + BLOCK, :]
+        first += BLOCK
+    last = first + width // BLOCK // 2 * BLOCK
+    for n in range(width // BLOCK // 2):
+        square = packed_ref[first + n * BLOCK : first + (n + 1) * BLOCK, :]
+        turned = square.T
+        blocks[2 * n, 2 * n] = jnp.where(row <= lane, square, turned)
+        diagonal = packed_ref[last + n : last + n + 1, :]
+        other = jnp.where(row > lane, square, turned)
+        blocks[2 * n + 1, 2 * n + 1] = jnp.where(row == lane, diagonal, other)
+    return blocks
 
 
 def front_kernel(
@@ -75,17 +121,16 @@
     columns_ref,
     factor_ref,
     border_ref,
+    panel_ref,
     moved_ref,
     keep_ref,
     send_ref,
-    packed_ref,
-    factor_here,
-    border_here,
-    columns_here,
-    sems,
-    *,
+    *refs,
     width,
 ):
+    dealt = refs[:-6]
+    packed_ref, factor_here, border_here, columns_here, sems, deal_sems = refs[-6:]
+    place = lax.axis_index("col")
     chunk = factor_here.shape[0] // 4
     chunks = [slice(k * chunk, (k + 1) * chunk) for k in range(4)]
     loads = [pltpu.make_async_copy(border_ref.at[0], border_here, sems.at[0])]
@@ -96,8 +141,13 @@
     loads.append(pltpu.make_async_copy(columns_ref, columns_here, sems.at[5]))
     for load in loads:
         load.start()
+    deals = [
+        pltpu.make_async_copy(panel_ref.at[0, place ^ m], out_ref, deal_sems.at[m])
+        for m, out_ref in enumerate(dealt)
+    ]
+    for load in deals:
+        load.start()
     core = lax.rem(lax.axis_index("scen"), 2)
-    place = lax.axis_index("col")
     order = order_ref[0]
     loads[0].wait()
     border = border_here[...]
@@ -118,83 +168,88 @@
     high, low = split_two(terms)
     half_spread = matmul_nt(high, spread) + matmul_nt(low, spread)
     high, low = split_two(half_spread)
-    row = 0
+    blocks = {}
     for i in range(width // BLOCK):
         rows = spread[i * BLOCK : (i + 1) * BLOCK]
         part = matmul(rows, high[:, i * BLOCK :]) + matmul(rows, low[:, i * BLOCK :])
         for j in range(i, width // BLOCK):
-            packed_ref[row : row + BLOCK, :] = part[:, (j - i) * BLOCK : (j - i + 1) * BLOCK]
-            row += BLOCK
+            blocks[i, j] = part[:, (j - i) * BLOCK : (j - i + 1) * BLOCK]
+    pack(blocks, width, packed_ref)
     half = keep_ref.shape[0]
     keep_ref[...] = packed_ref[pl.ds(pl.multiple_of(core * half, 8), half), :]
     send_ref[...] = packed_ref[pl.ds(pl.multiple_of((1 - core) * half, 8), half), :]
-
-
-def front(order, columns, factor, border, width):
-    total = len(upper_blocks(width)) * BLOCK
+    for load in deals:
+        load.wait()
+
+
+def front(order, columns, factor, border, panel, width):
+    count = panel.shape[1]
+    total = packed_rows(width, 16 * count)
     half = jax.ShapeDtypeStruct((total // 2, BLOCK), jnp.float32)
-    return pl.pallas_call(
+    piece = jax.ShapeDtypeStruct(panel.shape[2:], panel.dtype)
+    moved, keep, send, *dealt = pl.pallas_call(
         functools.partial(front_kernel, width=width),
-        out_shape=[jax.ShapeDtypeStruct(border.shape[1:], jnp.bfloat16), half, half],
-        in_specs=[SMEM, HBM, HBM, HBM],
-        out_specs=[VMEM] * 3,
+        out_shape=[jax.ShapeDtypeStruct(border.shape[1:], jnp.bfloat16), half, half]
+        + [piece] * count,
+        in_specs=[SMEM, HBM, HBM, HBM, HBM],
+        out_specs=[VMEM] * (3 + count),
         scratch_shapes=[
             pltpu.VMEM((total, BLOCK), jnp.float32),
             pltpu.VMEM(factor.shape[1:], factor.dtype),
             pltpu.VMEM(border.shape[1:], border.dtype),
             pltpu.VMEM(columns.shape, columns.dtype),
             pltpu.SemaphoreType.DMA((6,)),
+            pltpu.SemaphoreType.DMA((count,)),
         ],
         compiler_params=PARAMS,
         cost_estimate=long_cost(20),
         name="front",
-    )(order, in_hbm(columns), in_hbm(factor), in_hbm(border))
-
-
-def deal_kernel(border_ref, *refs):
-    out_refs, sems = refs[:-1], refs[-1]
+    )(order, in_hbm(columns), in_hbm(factor), in_hbm(border), in_hbm(panel))
+    return moved, keep, send, dealt
+
+
+def whole_tiles(rows):
+    return -(-rows // 16) * 16
+
+
+def quarter_kernel(keep_ref, got_ref, *refs):
+    count = (len(refs) + 1) // 2
+    dealt, own_ref, out_refs = refs[: count - 1], refs[count - 1], refs[count:]
     place = lax.axis_index("col")
-    loads = [
-        pltpu.make_async_copy(border_ref.at[0, place ^ m], out_ref, sems.at[m])
-        for m, out_ref in enumerate(out_refs)
-    ]
-    for load in loads:
-        load.start()
-    for load in loads:
-        load.wait()
-
-
-def deal(border):
-    count = border.shape[1]
-    return pl.pallas_call(
-        deal_kernel,
-        out_shape=[jax.ShapeDtypeStruct(border.shape[2:], border.dtype)] * count,
-        in_specs=[HBM],
+    rows = own_ref.shape[0]
+    spare = whole_tiles(rows) - rows
+    for m in range(count):
+        at = pl.ds(pl.multiple_of((place ^ m) * rows, 8), rows)
+        value = keep_ref[at, :] + got_ref[at, :]
+        if m == 0:
+            own_ref[...] = value
+            continue
+        if spare > 0:
+            value = jnp.concatenate([value, jnp.zeros((spare, BLOCK), jnp.float32)], 0)
+        border_ref, out_ref = dealt[m - 1], out_refs[m - 1]
+        size, depth = border_ref.shape
+        parts = list(split_two(value))
+        parts += [border_ref[:, n : n + BLOCK] for n in range(0, depth, BLOCK)]
+        first = 0
+        for part in parts:
+            out_ref[first : first + part.shape[0], :] = part
+            first += part.shape[0]
+
+
+def quarters(keep, got, dealt):
+    count = len(dealt) + 1
+    rows = keep.shape[0] // count
+    length = 2 * whole_tiles(rows) + dealt[0].size // BLOCK
+    own, *messages = pl.pallas_call(
+        quarter_kernel,
+        out_shape=[jax.ShapeDtypeStruct((rows, BLOCK), jnp.float32)]
+        + [jax.ShapeDtypeStruct((length, BLOCK), jnp.bfloat16)] * (count - 1),
+        in_specs=[VMEM] * (1 + count),
         out_specs=[VMEM] * count,
-        scratch_shapes=[pltpu.SemaphoreType.DMA((count,))],
-        compiler_params=PARAMS,
-        name="deal",
-    )(in_hbm(border))
-
-
-def quarter_kernel(keep_ref, got_ref, *out_refs):
-    place = lax.axis_index("col")
-    rows = out_refs[0].shape[0]
-    for m, out_ref in enumerate(out_refs):
-        at = pl.ds(pl.multiple_of((place ^ m) * rows, 8), rows)
-        out_ref[...] = keep_ref[at, :] + got_ref[at, :]
-
-
-def quarters(keep, got, col_count):
-    piece = jax.ShapeDtypeStruct((keep.shape[0] // col_count, BLOCK), jnp.float32)
-    return pl.pallas_call(
-        quarter_kernel,
-        out_shape=[piece] * col_count,
-        in_specs=[VMEM, VMEM],
-        out_specs=[VMEM] * col_count,
         compiler_params=PARAMS,
         name="quarters",
-    )(keep, got)
+    )(keep, got, *dealt)
+    return own, messages
 
 
 def join_kernel(*refs, count):
@@ -325,20 +380,17 @@
     count = width // BLOCK
     core = lax.rem(lax.axis_index("scen"), 2)
     place = lax.axis_index("col")
-    diagonal = lax.broadcasted_iota(jnp.int32, (BLOCK, BLOCK), 0) == lax.broadcasted_iota(
-        jnp.int32, (BLOCK, BLOCK), 1
-    )
-    blocks = {}
+    row, lane = row_and_lane()
+    diagonal = row == lane
     rows = mine_first.shape[0]
     for n, ref in enumerate((mine_first, mine_last, other_first, other_last)):
         owner = core if n < 2 else 1 - core
         at = (2 * owner + n % 2) * rows
         packed_ref[pl.ds(pl.multiple_of(at, 8), rows), :] = ref[...]
-    for n, (i, j) in enumerate(upper_blocks(width)):
-        blocks[i, j] = packed_ref[n * BLOCK : (n + 1) * BLOCK, :]
-        if i == j:
-            extra = barrier_ref[:, i * BLOCK : (i + 1) * BLOCK]
-            blocks[i, j] = blocks[i, j] + jnp.where(diagonal, extra, 0.0)
+    blocks = unpack(packed_ref, width)
+    for i in range(count):
+        extra = barrier_ref[:, i * BLOCK : (i + 1) * BLOCK]
+        blocks[i, i] = blocks[i, i] + jnp.where(diagonal, extra, 0.0)
     panels = [jnp.concatenate([blocks[i, j] for j in range(i, count)], 1) for i in range(count)]
     upper_ref[...] = jnp.zeros(upper_ref.shape, jnp.float32)
     inverse_ref[...] = jnp.zeros(inverse_ref.shape, jnp.float32)
@@ -385,24 +437,35 @@
     )(*halves, barrier[None])
 
 
-def coupling_kernel(moved_ref, *refs, parts):
-    count = (len(refs) - parts - 1) // 2
-    refs[parts + count][...] = tree_sum([ref[...] for ref in refs[:parts]])
+def coupling_kernel(moved_ref, own_ref, border_ref, *refs):
+    count = len(refs) // 2
+    messages, total_ref, out_refs = refs[: count - 1], refs[count - 1], refs[count:]
+    rows = own_ref.shape[0]
+    size, depth = border_ref.shape
+    tiles = whole_tiles(rows)
     moved = moved_ref[...]
-    for border_ref, out_ref in zip(refs[parts:], refs[parts + count + 1 :]):
-        out_ref[...] = matmul_nt(border_ref[...], moved)
-
-
-def sum_and_couplings(parts, moved, borders):
-    shape = jax.ShapeDtypeStruct((borders[0].shape[0], moved.shape[0]), jnp.float32)
+    out_refs[0][...] = matmul_nt(border_ref[...], moved)
+    parts = [own_ref[...]]
+    for message, out_ref in zip(messages, out_refs[1:]):
+        high = message[:tiles, :].astype(jnp.float32)
+        low = message[tiles : 2 * tiles, :].astype(jnp.float32)
+        parts.append((high + low)[:rows])
+        first = [2 * tiles + n * size for n in range(depth // BLOCK)]
+        border = jnp.concatenate([message[at : at + size, :] for at in first], 1)
+        out_ref[...] = matmul_nt(border, moved)
+    total_ref[...] = tree_sum(parts)
+
+
+def sum_and_couplings(own, messages, moved, border):
+    shape = jax.ShapeDtypeStruct((border.shape[0], moved.shape[0]), jnp.float32)
     total, *partial = pl.pallas_call(
-        functools.partial(coupling_kernel, parts=len(parts)),
-        out_shape=[jax.ShapeDtypeStruct(parts[0].shape, jnp.float32)] + [shape] * len(borders),
-        in_specs=[VMEM] * (len(parts) + len(borders) + 1),
-        out_specs=[VMEM] * (len(borders) + 1),
+        coupling_kernel,
+        out_shape=[jax.ShapeDtypeStruct(own.shape, jnp.float32)] + [shape] * (len(messages) + 1),
+        in_specs=[VMEM] * (len(messages) + 3),
+        out_specs=[VMEM] * (len(messages) + 2),
         compiler_params=PARAMS,
         name="couplings",
-    )(moved, *parts, *borders)
+    )(moved, own, border, *messages)
     return total, partial
 
 
@@ -463,24 +526,24 @@
 
 
 def near_kernel(*refs, group):
-    groups, out_ref = refs[1:-1], refs[-1]
+    groups, out_ref = refs[:-1], refs[-1]
     rows, width = out_ref.shape
     out_ref[...] = placed_rows(groups, group, rows // 2, width)
 
 
-def near_rows(groups, group, rows_here, width, wait):
+def near_rows(groups, group, rows_here, width):
     return pl.pallas_call(
         functools.partial(near_kernel, group=group),
         out_shape=jax.ShapeDtypeStruct((2 * rows_here, width), jnp.float32),
-        in_specs=[ANY] + [VMEM] * len(groups),
+        in_specs=[VMEM] * len(groups),
         out_specs=VMEM,
         compiler_params=PARAMS,
         cost_estimate=long_cost(0),
         name="near",
-    )(wait, *groups)
-
-
-def far_kernel(near_ref, *refs, group):
+    )(*groups)
+
+
+def far_kernel(wait_ref, near_ref, *refs, group):
     groups = refs[:-2]
     keep_ref, send_ref = refs[-2:]
     rows_here, width = keep_ref.shape
@@ -491,18 +554,18 @@
     send_ref[...] = jnp.where(core == 0, upper, lower)
 
 
-def far_rows(near, groups, group):
+def far_rows(near, groups, group, wait):
     rows, width = near.shape
     half = jax.ShapeDtypeStruct((rows // 2, width), jnp.float32)
     return pl.pallas_call(
         functools.partial(far_kernel, group=group),
         out_shape=[half, half],
-        in_specs=[VMEM] * (1 + len(groups)),
+        in_specs=[ANY] + [VMEM] * (1 + len(groups)),
         out_specs=[VMEM, VMEM],
         compiler_params=PARAMS,
         cost_estimate=long_cost(0),
         name="far",
-    )(near, *groups)
+    )(wait, near, *groups)
 
 
 def solve_kernel(keep_ref, got_ref, inverse_ref, out_ref):
@@ -549,13 +612,13 @@
     group, size = panel_border.shape[1:3]
     wide = slab_columns.shape[1]
 
-    moved, keep, send = front(true_orders, slab_columns, inverse_factor, slab_border, width)
+    moved, keep, send, dealt = front(
+        true_orders, slab_columns, inverse_factor, slab_border, panel_border, width
+    )
     got = swap(send, "scen", 1)
-    parts = quarters(keep, got, col_count)
-    dealt = deal(panel_border)
-    borders = [dealt[0]] + [swap(dealt[m], "col", m) for m in range(1, col_count)]
-    parts = [parts[0]] + [swap(parts[m], "col", m) for m in range(1, col_count)]
-    part, partial = sum_and_couplings(parts, moved, borders)
+    part, messages = quarters(keep, got, dealt[1:])
+    messages = [swap(message, "col", m + 1) for m, message in enumerate(messages)]
+    part, partial = sum_and_couplings(part, messages, moved, dealt[0])
     parts = [part] + [swap(part, "scen", 2 * m) for m in range(1, scen_count // 2)]
     pieces = [partial[0]] + [swap(partial[m], "col", m) for m in range(1, col_count)]
     part, own = sum_and_assemble(parts, pieces, slab_columns, panel_rows)
@@ -564,13 +627,12 @@
     groups = [own]
     if sparse:
         groups += [swap(own, "scen", 2 * m) for m in range(1, scen_count // 2)]
-    mine = join([part] + [swap(part, "col", m) for m in range(1, col_count)], [])
+    near = [near_rows([own], group, rows_here, width)] if sparse else []
+    mine = join([part] + [swap(part, "col", m) for m in range(1, col_count)], near)
     halves = list(mine) + [swap(half, "scen", 1) for half in mine]
     inverse, factor_rows = cholesky(halves, barrier_diag, col_count)
     if sparse:
-        half = len(groups) // 2
-        near = near_rows(groups[:half], group, rows_here, width, inverse)
-        rows, other = far_rows(near, groups[half:], group)
+        rows, other = far_rows(near[0], groups[1:], group, inverse)
         solved = solve_rows(rows, swap(other, "scen", 1), inverse)
     else:
         local = own[: group * size].reshape(group, size, wide)

time: 58.8 us -> 57.6 us (0.980)
  starting transfers between devices: 25.3 us -> 21.8 us
  waiting for transfers between devices: 10.5 us -> 13.6 us
  Pallas kernels: 21.4 us -> 20.7 us
    ppermute x22 -> x19, starting transfers between devices: 25.3 us -> 21.8 us  [swap(): return lax.ppermute(value, axis, [(i, i ^ step) for i in range(count)])]
    ppermute x22 -> x19, waiting for transfers between devices: 10.5 us -> 13.6 us  [swap(): return lax.ppermute(value, axis, [(i, i ^ step) for i in range(count)])]
    pallas_call x3 -> x2, Pallas kernels: 1.35 us -> 0.48 us  [the longest x1 0.41 us: sum_and_couplings(): pl.pallas_call(coupling_kernel, out_shape=[jax.ShapeDtypeStruct(own.shape...]
    pallas_call x1, Pallas kernels: 1.53 us -> 2.2 us  [far_rows(): pl.pallas_call(functools.partial(far_kernel, group=group), out_shape=[hal...]
    pallas_call x1, Pallas kernels: 1.51 us -> 0.84 us  [near_rows(): pl.pallas_call(functools.partial(near_kernel, group=group), out_shape=jax...]
  transfers between devices with their start and end apart: 22 -> 19, of which waited for: 7 -> 9; matrix products, arithmetic and copies ran while one was open for 0% -> 0% of each run, Pallas kernels for 25% -> 23%
where the time goes in v7:
time: 57.6 us; the launch traced here: 57.5 us
  starting transfers between devices  21.8 us (38%)
  Pallas kernels  20.7 us (36%)
  waiting for transfers between devices  13.6 us (24%)
  between operations  1.37 us (2%)
    ppermute x19, starting transfers between devices, swap(): return lax.ppermute(value, axis, [(i, i ^ step) for i in range(count)])  21.8 us
    ppermute x19, waiting for transfers between devices, swap(): return lax.ppermute(value, axis, [(i, i ^ step) for i in range(count)])  13.6 us
    pallas_call x1, Pallas kernels, cholesky(): pl.pallas_call(cholesky_kernel, out_shape=[jax.ShapeDtypeStruct((width, w...  12.4 us
    pallas_call x1, Pallas kernels, front(): pl.pallas_call(functools.partial(front_kernel, width=width), out_shape=[j...  2.8 us
    pallas_call x1, Pallas kernels, far_rows(): pl.pallas_call(functools.partial(far_kernel, group=group), out_shape=[hal...  2.2 us
    pallas_call x1, Pallas kernels, solve_rows(): pl.pallas_call(solve_kernel, out_shape=jax.ShapeDtypeStruct(keep.shape, j...  1.85 us
  transfers between devices with their start and end apart: 19, of which 9 were waited for; matrix products, arithmetic and copies ran while one was open for 0% of the time, Pallas kernels for 23%

profile of v7, /device:TPU:0, one launch (start us, length us, event | category | flops | bytes accessed | tf_op | source)
XLA Modules:
  0.0 57.5 jit_solution(5375531576477891386)
XLA Ops:
  1.3 2.8 %front.1 = (bf16[256,512]{1,0:T(8,128)(2,1)S(1)}, f32[544,128]{1,0:T(8,128)S(1)}, f32[544,128]{1,0:T(8,128)S(1)}, bf16[48,512]{1,0:T(8,128)(2,1)S(1)}, bf16[48,5...) custom-call(s32[1]{0:T(128)S(6)} %copy.9.order_ref, s32[4,256]{1,0:T(4,128)} %columns_ref.3, ...), custom_call_target="tpu_custom_call" | custom-call | flops 20000000000 | bytes 1024 | tf_op jit(solution)/shard_map/front/pallas_call | solution.py:190
  4.6 1.2 %collective-permute-done.got_ref = f32[544,128]{1,0:T(8,128)S(1)} collective-permute-done((f32[544,128]{1,0:T(8,128)S(1)}, f32[544,128]{1,0:T(8,128)S(1)}, u32[]{:S(2)}, u32[]{:S(2)}) %collective-permute-start) | collective-permute-done | bytes 278560 | tf_op jit(solution)/shard_map/ppermute | solution.py:282
  5.9 2.9 %collective-permute-start.1 = (bf16[480,128]{1,0:T(8,128)(2,1)S(1)}, bf16[480,128]{1,0:T(8,128)(2,1)S(1)}, u32[]{:S(2)}, u32[]{:S(2)}) collective-permute-start(bf16[480,128]{1,0:T(8,128)(2,1)S(1)} %get-tuple-element.34), channel_id=1, source_target_pairs={{0,1},{1,0},{2,3},{3,2},{4,5},{5,4},{6,7},{7,6},{8,9},{9,8},{10,11... | collective-permute-start | bytes 368648 | tf_op jit(solution)/shard_map/ppermute | solution.py:282
  8.8 1.5 %collective-permute-start.2 = (bf16[480,128]{1,0:T(8,128)(2,1)S(1)}, bf16[480,128]{1,0:T(8,128)(2,1)S(1)}, u32[]{:S(2)}, u32[]{:S(2)}) collective-permute-start(bf16[480,128]{1,0:T(8,128)(2,1)S(1)} %get-tuple-element.35), channel_id=1, source_target_pairs={{0,2},{1,3},{2,0},{3,1},{4,6},{5,7},{6,4},{7,5},{8,10},{9,11},{10,... | collective-permute-start | bytes 368648 | tf_op jit(solution)/shard_map/ppermute | solution.py:282
  10.3 2.1 %collective-permute-done.1.refs_0_ = bf16[480,128]{1,0:T(8,128)(2,1)S(1)} collective-permute-done((bf16[480,128]{1,0:T(8,128)(2,1)S(1)}, bf16[480,128]{1,0:T(8,128)(2,1)S(1)}, u32[]{:S(2)}, u32[]{:S(2)}) %collective-permute-start.1) | collective-permute-done | bytes 122912 | tf_op jit(solution)/shard_map/ppermute | solution.py:282
  12.5 4.0 %collective-permute-done.2.refs_1_ = bf16[480,128]{1,0:T(8,128)(2,1)S(1)} collective-permute-done((bf16[480,128]{1,0:T(8,128)(2,1)S(1)}, bf16[480,128]{1,0:T(8,128)(2,1)S(1)}, u32[]{:S(2)}, u32[]{:S(2)}) %collective-permute-start.2) | collective-permute-done | bytes 122912 | tf_op jit(solution)/shard_map/ppermute | solution.py:282
  16.9 1.3 %collective-permute-start.7 = (f32[48,256]{1,0:T(8,128)S(1)}, f32[48,256]{1,0:T(8,128)S(1)}, u32[]{:S(2)}, u32[]{:S(2)}) collective-permute-start(f32[48,256]{1,0:T(8,128)S(1)} %get-tuple-element.39), channel_id=1, source_target_pairs={{0,1},{1,0},{2,3},{3,2},{4,5},{5,4},{6,7},{7,6},{8,9},{9,8},{10,11... | collective-permute-start | bytes 147464 | tf_op jit(solution)/shard_map/ppermute | solution.py:282
  18.2 1.6 %collective-permute-start.4 = (f32[136,128]{1,0:T(8,128)S(1)}, f32[136,128]{1,0:T(8,128)S(1)}, u32[]{:S(2)}, u32[]{:S(2)}) collective-permute-start(f32[136,128]{1,0:T(8,128)S(1)} %get-tuple-element.37.refs_0_), channel_id=1, source_target_pairs={{0,8},{4,12},{8,0},{12,4},{16,24},{20,28},{24,16},{28,20},{1,9},{5... | collective-permute-start | bytes 208904 | tf_op jit(solution)/shard_map/ppermute | solution.py:282
  19.8 2.6 %collective-permute-start.5 = (f32[136,128]{1,0:T(8,128)S(1)}, f32[136,128]{1,0:T(8,128)S(1)}, u32[]{:S(2)}, u32[]{:S(2)}) collective-permute-start(f32[136,128]{1,0:T(8,128)S(1)} %get-tuple-element.37.refs_0_), channel_id=1, source_target_pairs={{0,16},{4,20},{8,24},{12,28},{16,0},{20,4},{24,8},{28,12},{1,17},{... | collective-permute-start | bytes 208904 | tf_op jit(solution)/shard_map/ppermute | solution.py:282
  22.6 0.8 %collective-permute-start.8 = (f32[48,256]{1,0:T(8,128)S(1)}, f32[48,256]{1,0:T(8,128)S(1)}, u32[]{:S(2)}, u32[]{:S(2)}) collective-permute-start(f32[48,256]{1,0:T(8,128)S(1)} %get-tuple-element.40), channel_id=1, source_target_pairs={{0,2},{1,3},{2,0},{3,1},{4,6},{5,7},{6,4},{7,5},{8,10},{9,11},{10,... | collective-permute-start | bytes 147464 | tf_op jit(solution)/shard_map/ppermute | solution.py:282
  23.5 1.4 %collective-permute-start.9 = (f32[48,256]{1,0:T(8,128)S(1)}, f32[48,256]{1,0:T(8,128)S(1)}, u32[]{:S(2)}, u32[]{:S(2)}) collective-permute-start(f32[48,256]{1,0:T(8,128)S(1)} %get-tuple-element.41), channel_id=1, source_target_pairs={{0,3},{1,2},{2,1},{3,0},{4,7},{5,6},{6,5},{7,4},{8,11},{9,10},{10,... | collective-permute-start | bytes 147464 | tf_op jit(solution)/shard_map/ppermute | solution.py:282
  24.9 1.8 %collective-permute-done.8.refs_6_ = f32[48,256]{1,0:T(8,128)S(1)} collective-permute-done((f32[48,256]{1,0:T(8,128)S(1)}, f32[48,256]{1,0:T(8,128)S(1)}, u32[]{:S(2)}, u32[]{:S(2)}) %collective-permute-start.8) | collective-permute-done | bytes 49184 | tf_op jit(solution)/shard_map/ppermute | solution.py:282
  26.7 1.7 %collective-permute-done.9.refs_7_ = f32[48,256]{1,0:T(8,128)S(1)} collective-permute-done((f32[48,256]{1,0:T(8,128)S(1)}, f32[48,256]{1,0:T(8,128)S(1)}, u32[]{:S(2)}, u32[]{:S(2)}) %collective-permute-start.9) | collective-permute-done | bytes 49184 | tf_op jit(solution)/shard_map/ppermute | solution.py:282
  28.6 1.5 %collective-permute-start.10 = (f32[136,128]{1,0:T(8,128)S(1)}, f32[136,128]{1,0:T(8,128)S(1)}, u32[]{:S(2)}, u32[]{:S(2)}) collective-permute-start(f32[136,128]{1,0:T(8,128)S(1)} %get-tuple-element.42.refs_0_), channel_id=1, source_target_pairs={{0,1},{1,0},{2,3},{3,2},{4,5},{5,4},{6,7},{7,6},{8,9},{9,8},{10,11... | collective-permute-start | bytes 208904 | tf_op jit(solution)/shard_map/ppermute | solution.py:282
  30.1 0.9 %collective-permute-start.11 = (f32[136,128]{1,0:T(8,128)S(1)}, f32[136,128]{1,0:T(8,128)S(1)}, u32[]{:S(2)}, u32[]{:S(2)}) collective-permute-start(f32[136,128]{1,0:T(8,128)S(1)} %get-tuple-element.42.refs_0_), channel_id=1, source_target_pairs={{0,2},{1,3},{2,0},{3,1},{4,6},{5,7},{6,4},{7,5},{8,10},{9,11},{10,... | collective-permute-start | bytes 208904 | tf_op jit(solution)/shard_map/ppermute | solution.py:282
  30.9 1.2 %collective-permute-start.12 = (f32[136,128]{1,0:T(8,128)S(1)}, f32[136,128]{1,0:T(8,128)S(1)}, u32[]{:S(2)}, u32[]{:S(2)}) collective-permute-start(f32[136,128]{1,0:T(8,128)S(1)} %get-tuple-element.42.refs_0_), channel_id=1, source_target_pairs={{0,3},{1,2},{2,1},{3,0},{4,7},{5,6},{6,5},{7,4},{8,11},{9,10},{10,... | collective-permute-start | bytes 208904 | tf_op jit(solution)/shard_map/ppermute | solution.py:282
  32.1 0.7 %collective-permute-start.15 = (f32[200,256]{1,0:T(8,128)S(1)}, f32[200,256]{1,0:T(8,128)S(1)}, u32[]{:S(2)}, u32[]{:S(2)}) collective-permute-start(f32[200,256]{1,0:T(8,128)S(1)} %get-tuple-element.43.refs_0_), channel_id=1, source_target_pairs={{0,8},{4,12},{8,0},{12,4},{16,24},{20,28},{24,16},{28,20},{1,9},{5... | collective-permute-start | bytes 614408 | tf_op jit(solution)/shard_map/ppermute | solution.py:282
  32.8 3.5 %collective-permute-start.16 = (f32[200,256]{1,0:T(8,128)S(1)}, f32[200,256]{1,0:T(8,128)S(1)}, u32[]{:S(2)}, u32[]{:S(2)}) collective-permute-start(f32[200,256]{1,0:T(8,128)S(1)} %get-tuple-element.43.refs_0_), channel_id=1, source_target_pairs={{0,16},{4,20},{8,24},{12,28},{16,0},{20,4},{24,8},{28,12},{1,17},{... | collective-permute-start | bytes 614408 | tf_op jit(solution)/shard_map/ppermute | solution.py:282
  36.5 0.8 %near.1.refs_4_.near_ref = f32[480,512]{1,0:T(8,128)S(1)} custom-call(f32[200,256]{1,0:T(8,128)S(1)} %get-tuple-element.43.refs_0_), custom_call_target="tpu_custom_call" | custom-call | bytes 1024 | tf_op jit(solution)/shard_map/near/pallas_call | solution.py:535
  38.0 0.8 %collective-permute-done.13.other_first = f32[272,128]{1,0:T(8,128)S(1)} collective-permute-done((f32[272,128]{1,0:T(8,128)S(1)}, f32[272,128]{1,0:T(8,128)S(1)}, u32[]{:S(2)}, u32[]{:S(2)}) %collective-permute-start.13) | collective-permute-done | bytes 139296 | tf_op jit(solution)/shard_map/ppermute | solution.py:282
  39.1 12.4 %cholesky.1 = (f32[512,512]{1,0:T(8,128)S(1)}, f32[128,512]{1,0:T(8,128)}) custom-call(f32[272,128]{1,0:T(8,128)S(1)} %get-tuple-element.44.mine_first, f32[272,128]{1,0:T(8,128)S(1)} %get-tuple-element.45.mine_last, f32[272,128]{1,0:T(8,128)S(1)} %collective-permute-done.13.other_first, f32[272,128]{1,0:T(8,128)S(1)} %collective-permute-done.14.other_last, ...), custom_call_target="tpu_custom_call" | custom-call | bytes 1024 | tf_op jit(solution)/shard_map/cholesky/pallas_call | solution.py:421
  51.5 2.2 %far.1 = (f32[240,512]{1,0:T(8,128)S(1)}, f32[240,512]{1,0:T(8,128)S(1)}) custom-call(f32[512,512]{1,0:T(8,128)S(1)} %get-tuple-element.47.wait_ref.inverse_ref, f32[480,512]{1,0:T(8,128)S(1)} %near.1.refs_4_.near_ref, f32[200,256]{1,0:T(8,128)S(1)} %collective-permute-done.15.refs_0_, f32[200,256]{1,0:T(8,128)S(1)} %collective-permute-done.16.refs_1_, ...), custom_call_target="tpu_custom_call" | custom-call | bytes 1024 | tf_op jit(solution)/shard_map/far/pallas_call | solution.py:560
  54.1 1.5 %collective-permute-done.18.got_ref = f32[240,512]{1,0:T(8,128)S(1)} collective-permute-done((f32[240,512]{1,0:T(8,128)S(1)}, f32[240,512]{1,0:T(8,128)S(1)}, u32[]{:S(2)}, u32[]{:S(2)}) %collective-permute-start.18) | collective-permute-done | bytes 491552 | tf_op jit(solution)/shard_map/ppermute | solution.py:282
  55.6 1.8 %solve.1 = f32[240,512]{1,0:T(8,128)} custom-call(f32[240,512]{1,0:T(8,128)S(1)} %get-tuple-element.48.keep_ref, f32[240,512]{1,0:T(8,128)S(1)} %collective-permute-done.18.got_ref, f32[512,512]{1,0:T(8,128)S(1)} %get-tuple-element.47.wait_ref.inverse_ref), custom_call_target="tpu_custom_call" | custom-call | tf_op jit(solution)/shard_map/solve/pallas_call | solution.py:576
  (29 shorter events, 2.8 us)
Async XLA Ops:
  4.1 1.7 %collective-permute-start = (f32[544,128]{1,0:T(8,128)S(1)}, f32[544,128]{1,0:T(8,128)S(1)}, u32[]{:S(2)}, u32[]{:S(2)}) collective-permute-start(f32[544,128]{1,0:T(8,128)S(1)} %get-tuple-element.28), channel_id=1, source_target_pairs={{0,4},{4,0},{8,12},{12,8},{16,20},{20,16},{24,28},{28,24},{1,5},{5... | collective-permute-start | bytes 835592 | tf_op jit(solution)/shard_map/ppermute | solution.py:282
  5.9 6.6 %collective-permute-start.1 = (bf16[480,128]{1,0:T(8,128)(2,1)S(1)}, bf16[480,128]{1,0:T(8,128)(2,1)S(1)}, u32[]{:S(2)}, u32[]{:S(2)}) collective-permute-start(bf16[480,128]{1,0:T(8,128)(2,1)S(1)} %get-tuple-element.34), channel_id=1, source_target_pairs={{0,1},{1,0},{2,3},{3,2},{4,5},{5,4},{6,7},{7,6},{8,9},{9,8},{10,11... | collective-permute-start | bytes 368648 | tf_op jit(solution)/shard_map/ppermute | solution.py:282
  8.8 7.7 %collective-permute-start.2 = (bf16[480,128]{1,0:T(8,128)(2,1)S(1)}, bf16[480,128]{1,0:T(8,128)(2,1)S(1)}, u32[]{:S(2)}, u32[]{:S(2)}) collective-permute-start(bf16[480,128]{1,0:T(8,128)(2,1)S(1)} %get-tuple-element.35), channel_id=1, source_target_pairs={{0,2},{1,3},{2,0},{3,1},{4,6},{5,7},{6,4},{7,5},{8,10},{9,11},{10,... | collective-permute-start | bytes 368648 | tf_op jit(solution)/shard_map/ppermute | solution.py:282
  10.3 6.2 %collective-permute-start.3 = (bf16[480,128]{1,0:T(8,128)(2,1)S(1)}, bf16[480,128]{1,0:T(8,128)(2,1)S(1)}, u32[]{:S(2)}, u32[]{:S(2)}) collective-permute-start(bf16[480,128]{1,0:T(8,128)(2,1)S(1)} %get-tuple-element.36), channel_id=1, source_target_pairs={{0,3},{1,2},{2,1},{3,0},{4,7},{5,6},{6,5},{7,4},{8,11},{9,10},{10,... | collective-permute-start | bytes 368648 | tf_op jit(solution)/shard_map/ppermute | solution.py:282
  16.9 11.6 %copy-start = (s32[4,256]{1,0:T(4,128)S(1)}, s32[4,256]{1,0:T(4,128)}, u32[]{:S(2)}) copy-start(s32[4,256]{1,0:T(4,128)} %columns_ref.3) | copy-start | bytes 12292
  16.9 6.5 %collective-permute-start.7 = (f32[48,256]{1,0:T(8,128)S(1)}, f32[48,256]{1,0:T(8,128)S(1)}, u32[]{:S(2)}, u32[]{:S(2)}) collective-permute-start(f32[48,256]{1,0:T(8,128)S(1)} %get-tuple-element.39), channel_id=1, source_target_pairs={{0,1},{1,0},{2,3},{3,2},{4,5},{5,4},{6,7},{7,6},{8,9},{9,8},{10,11... | collective-permute-start | bytes 147464 | tf_op jit(solution)/shard_map/ppermute | solution.py:282
  18.2 10.2 %collective-permute-start.4 = (f32[136,128]{1,0:T(8,128)S(1)}, f32[136,128]{1,0:T(8,128)S(1)}, u32[]{:S(2)}, u32[]{:S(2)}) collective-permute-start(f32[136,128]{1,0:T(8,128)S(1)} %get-tuple-element.37.refs_0_), channel_id=1, source_target_pairs={{0,8},{4,12},{8,0},{12,4},{16,24},{20,28},{24,16},{28,20},{1,9},{5... | collective-permute-start | bytes 208904 | tf_op jit(solution)/shard_map/ppermute | solution.py:282
  19.8 8.6 %collective-permute-start.5 = (f32[136,128]{1,0:T(8,128)S(1)}, f32[136,128]{1,0:T(8,128)S(1)}, u32[]{:S(2)}, u32[]{:S(2)}) collective-permute-start(f32[136,128]{1,0:T(8,128)S(1)} %get-tuple-element.37.refs_0_), channel_id=1, source_target_pairs={{0,16},{4,20},{8,24},{12,28},{16,0},{20,4},{24,8},{28,12},{1,17},{... | collective-permute-start | bytes 208904 | tf_op jit(solution)/shard_map/ppermute | solution.py:282
  22.4 6.1 %collective-permute-start.6 = (f32[136,128]{1,0:T(8,128)S(1)}, f32[136,128]{1,0:T(8,128)S(1)}, u32[]{:S(2)}, u32[]{:S(2)}) collective-permute-start(f32[136,128]{1,0:T(8,128)S(1)} %get-tuple-element.37.refs_0_), channel_id=1, source_target_pairs={{0,24},{4,28},{8,16},{12,20},{16,8},{20,12},{24,0},{28,4},{1,25},{... | collective-permute-start | bytes 208904 | tf_op jit(solution)/shard_map/ppermute | solution.py:282
  22.6 5.9 %copy-start.1 = (s32[1,4,48]{2,1,0:T(4,128)S(1)}, s32[1,4,48]{2,1,0:T(4,128)}, u32[]{:S(2)}) copy-start(s32[1,4,48]{2,1,0:T(4,128)} %rows_ref.1) | copy-start | bytes 2308
  22.6 4.1 %collective-permute-start.8 = (f32[48,256]{1,0:T(8,128)S(1)}, f32[48,256]{1,0:T(8,128)S(1)}, u32[]{:S(2)}, u32[]{:S(2)}) collective-permute-start(f32[48,256]{1,0:T(8,128)S(1)} %get-tuple-element.40), channel_id=1, source_target_pairs={{0,2},{1,3},{2,0},{3,1},{4,6},{5,7},{6,4},{7,5},{8,10},{9,11},{10,... | collective-permute-start | bytes 147464 | tf_op jit(solution)/shard_map/ppermute | solution.py:282
  23.5 5.0 %collective-permute-start.9 = (f32[48,256]{1,0:T(8,128)S(1)}, f32[48,256]{1,0:T(8,128)S(1)}, u32[]{:S(2)}, u32[]{:S(2)}) collective-permute-start(f32[48,256]{1,0:T(8,128)S(1)} %get-tuple-element.41), channel_id=1, source_target_pairs={{0,3},{1,2},{2,1},{3,0},{4,7},{5,6},{6,5},{7,4},{8,11},{9,10},{10,... | collective-permute-start | bytes 147464 | tf_op jit(solution)/shard_map/ppermute | solution.py:282
  28.6 7.8 %collective-permute-start.10 = (f32[136,128]{1,0:T(8,128)S(1)}, f32[136,128]{1,0:T(8,128)S(1)}, u32[]{:S(2)}, u32[]{:S(2)}) collective-permute-start(f32[136,128]{1,0:T(8,128)S(1)} %get-tuple-element.42.refs_0_), channel_id=1, source_target_pairs={{0,1},{1,0},{2,3},{3,2},{4,5},{5,4},{6,7},{7,6},{8,9},{9,8},{10,11... | collective-permute-start | bytes 208904 | tf_op jit(solution)/shard_map/ppermute | solution.py:282
  30.1 7.3 %collective-permute-start.11 = (f32[136,128]{1,0:T(8,128)S(1)}, f32[136,128]{1,0:T(8,128)S(1)}, u32[]{:S(2)}, u32[]{:S(2)}) collective-permute-start(f32[136,128]{1,0:T(8,128)S(1)} %get-tuple-element.42.refs_0_), channel_id=1, source_target_pairs={{0,2},{1,3},{2,0},{3,1},{4,6},{5,7},{6,4},{7,5},{8,10},{9,11},{10,... | collective-permute-start | bytes 208904 | tf_op jit(solution)/shard_map/ppermute | solution.py:282
  30.9 6.4 %collective-permute-start.12 = (f32[136,128]{1,0:T(8,128)S(1)}, f32[136,128]{1,0:T(8,128)S(1)}, u32[]{:S(2)}, u32[]{:S(2)}) collective-permute-start(f32[136,128]{1,0:T(8,128)S(1)} %get-tuple-element.42.refs_0_), channel_id=1, source_target_pairs={{0,3},{1,2},{2,1},{3,0},{4,7},{5,6},{6,5},{7,4},{8,11},{9,10},{10,... | collective-permute-start | bytes 208904 | tf_op jit(solution)/shard_map/ppermute | solution.py:282
  32.1 19.4 %collective-permute-start.15 = (f32[200,256]{1,0:T(8,128)S(1)}, f32[200,256]{1,0:T(8,128)S(1)}, u32[]{:S(2)}, u32[]{:S(2)}) collective-permute-start(f32[200,256]{1,0:T(8,128)S(1)} %get-tuple-element.43.refs_0_), channel_id=1, source_target_pairs={{0,8},{4,12},{8,0},{12,4},{16,24},{20,28},{24,16},{28,20},{1,9},{5... | collective-permute-start | bytes 614408 | tf_op jit(solution)/shard_map/ppermute | solution.py:282
  32.8 18.7 %collective-permute-start.16 = (f32[200,256]{1,0:T(8,128)S(1)}, f32[200,256]{1,0:T(8,128)S(1)}, u32[]{:S(2)}, u32[]{:S(2)}) collective-permute-start(f32[200,256]{1,0:T(8,128)S(1)} %get-tuple-element.43.refs_0_), channel_id=1, source_target_pairs={{0,16},{4,20},{8,24},{12,28},{16,0},{20,4},{24,8},{28,12},{1,17},{... | collective-permute-start | bytes 614408 | tf_op jit(solution)/shard_map/ppermute | solution.py:282
  36.3 15.2 %collective-permute-start.17 = (f32[200,256]{1,0:T(8,128)S(1)}, f32[200,256]{1,0:T(8,128)S(1)}, u32[]{:S(2)}, u32[]{:S(2)}) collective-permute-start(f32[200,256]{1,0:T(8,128)S(1)} %get-tuple-element.43.refs_0_), channel_id=1, source_target_pairs={{0,24},{4,28},{8,16},{12,20},{16,8},{20,12},{24,0},{28,4},{1,25},{... | collective-permute-start | bytes 614408 | tf_op jit(solution)/shard_map/ppermute | solution.py:282
  37.4 1.6 %copy-start.2 = (f32[512]{0:T(512)S(1)}, f32[512]{0:T(512)}, u32[]{:S(2)}) copy-start(f32[512]{0:T(512)} %param.13) | copy-start | bytes 6148
  37.4 1.4 %collective-permute-start.13 = (f32[272,128]{1,0:T(8,128)S(1)}, f32[272,128]{1,0:T(8,128)S(1)}, u32[]{:S(2)}, u32[]{:S(2)}) collective-permute-start(f32[272,128]{1,0:T(8,128)S(1)} %get-tuple-element.44.mine_first), channel_id=1, source_target_pairs={{0,4},{4,0},{8,12},{12,8},{16,20},{20,16},{24,28},{28,24},{1,5},{5... | collective-permute-start | bytes 417800 | tf_op jit(solution)/shard_map/ppermute | solution.py:282
  37.5 1.5 %collective-permute-start.14 = (f32[272,128]{1,0:T(8,128)S(1)}, f32[272,128]{1,0:T(8,128)S(1)}, u32[]{:S(2)}, u32[]{:S(2)}) collective-permute-start(f32[272,128]{1,0:T(8,128)S(1)} %get-tuple-element.45.mine_last), channel_id=1, source_target_pairs={{0,4},{4,0},{8,12},{12,8},{16,20},{20,16},{24,28},{28,24},{1,5},{5... | collective-permute-start | bytes 417800 | tf_op jit(solution)/shard_map/ppermute | solution.py:282
  53.7 1.9 %collective-permute-start.18 = (f32[240,512]{1,0:T(8,128)S(1)}, f32[240,512]{1,0:T(8,128)S(1)}, u32[]{:S(2)}, u32[]{:S(2)}) collective-permute-start(f32[240,512]{1,0:T(8,128)S(1)} %get-tuple-element.49), channel_id=1, source_target_pairs={{0,4},{4,0},{8,12},{12,8},{16,20},{20,16},{24,28},{28,24},{1,5},{5... | collective-permute-start | bytes 1474568 | tf_op jit(solution)/shard_map/ppermute | solution.py:282

commit v8 on v7

--- a/solution.py
+++ b/solution.py
@@ -263,18 +263,18 @@
     last_ref[...] = all_ref[half:, :]
 
 
-def join(pieces, waits):
+def join(pieces):
     rows = len(pieces) * pieces[0].shape[0]
     half = jax.ShapeDtypeStruct((rows // 2, BLOCK), jnp.float32)
     return pl.pallas_call(
         functools.partial(join_kernel, count=len(pieces)),
         out_shape=[half, half],
-        in_specs=[VMEM] * len(pieces) + [ANY] * len(waits),
+        in_specs=[VMEM] * len(pieces),
         out_specs=[VMEM, VMEM],
         scratch_shapes=[pltpu.VMEM((rows, BLOCK), jnp.float32)],
         compiler_params=PARAMS,
         name="join",
-    )(*pieces, *waits)
+    )(*pieces)
 
 
 def swap(value, axis, step):
@@ -372,133 +372,6 @@
     return jnp.concatenate(upper, 0), jnp.concatenate(lower, 0)
 
 
-def cholesky_kernel(
-    mine_first, mine_last, other_first, other_last, barrier_ref, inverse_ref, slice_ref, upper_ref,
-    turned_ref, packed_ref
-):
-    width = barrier_ref.shape[1]
-    count = width // BLOCK
-    core = lax.rem(lax.axis_index("scen"), 2)
-    place = lax.axis_index("col")
-    row, lane = row_and_lane()
-    diagonal = row == lane
-    rows = mine_first.shape[0]
-    for n, ref in enumerate((mine_first, mine_last, other_first, other_last)):
-        owner = core if n < 2 else 1 - core
-        at = (2 * owner + n % 2) * rows
-        packed_ref[pl.ds(pl.multiple_of(at, 8), rows), :] = ref[...]
-    blocks = unpack(packed_ref, width)
-    for i in range(count):
-        extra = barrier_ref[:, i * BLOCK : (i + 1) * BLOCK]
-        blocks[i, i] = blocks[i, i] + jnp.where(diagonal, extra, 0.0)
-    panels = [jnp.concatenate([blocks[i, j] for j in range(i, count)], 1) for i in range(count)]
-    upper_ref[...] = jnp.zeros(upper_ref.shape, jnp.float32)
-    inverse_ref[...] = jnp.zeros(inverse_ref.shape, jnp.float32)
-    for i in range(count):
-        here = slice(i * BLOCK, (i + 1) * BLOCK)
-        before = slice(0, i * BLOCK)
-        own, inverse = factor_block(panels[i][:, :BLOCK])
-        upper_ref[here, here] = own
-        inverse_ref[here, here] = inverse
-        if i + 1 < count:
-            rest = exact(inverse, panels[i][:, BLOCK:])
-            upper_ref[here, (i + 1) * BLOCK :] = rest
-            for j in range(i + 1, count):
-                at = (j - i - 1) * BLOCK
-                panels[j] = panels[j] - exact_tn(rest[:, at : at + BLOCK], rest[:, at:])
-        if i > 0:
-            mixed = exact_tn(upper_ref[before, here], inverse_ref[before, before])
-            inverse_ref[here, before] = -exact(inverse, mixed)
-    slice_rows = slice_ref.shape[0]
-    start = place * slice_rows
-    block = pl.ds(pl.multiple_of(start // BLOCK * BLOCK, BLOCK), BLOCK)
-    turned_ref[...] = upper_ref[:, block].T
-    slice_ref[...] = turned_ref[pl.ds(pl.multiple_of(lax.rem(start, BLOCK), 8), slice_rows), :]
-
-
-def cholesky(halves, barrier, col_count):
-    width = barrier.shape[0]
-    return pl.pallas_call(
-        cholesky_kernel,
-        out_shape=[
-            jax.ShapeDtypeStruct((width, width), jnp.float32),
-            jax.ShapeDtypeStruct((width // col_count, width), jnp.float32),
-        ],
-        in_specs=[VMEM] * 5,
-        out_specs=[VMEM] * 2,
-        scratch_shapes=[
-            pltpu.VMEM((width, width), jnp.float32),
-            pltpu.VMEM((BLOCK, width), jnp.float32),
-            pltpu.VMEM((4 * halves[0].shape[0], BLOCK), jnp.float32),
-        ],
-        compiler_params=PARAMS,
-        cost_estimate=long_cost(0),
-        name="cholesky",
-    )(*halves, barrier[None])
-
-
-def coupling_kernel(moved_ref, own_ref, border_ref, *refs):
-    count = len(refs) // 2
-    messages, total_ref, out_refs = refs[: count - 1], refs[count - 1], refs[count:]
-    rows = own_ref.shape[0]
-    size, depth = border_ref.shape
-    tiles = whole_tiles(rows)
-    moved = moved_ref[...]
-    out_refs[0][...] = matmul_nt(border_ref[...], moved)
-    parts = [own_ref[...]]
-    for message, out_ref in zip(messages, out_refs[1:]):
-        high = message[:tiles, :].astype(jnp.float32)
-        low = message[tiles : 2 * tiles, :].astype(jnp.float32)
-        parts.append((high + low)[:rows])
-        first = [2 * tiles + n * size for n in range(depth // BLOCK)]
-        border = jnp.concatenate([message[at : at + size, :] for at in first], 1)
-        out_ref[...] = matmul_nt(border, moved)
-    total_ref[...] = tree_sum(parts)
-
-
-def sum_and_couplings(own, messages, moved, border):
-    shape = jax.ShapeDtypeStruct((border.shape[0], moved.shape[0]), jnp.float32)
-    total, *partial = pl.pallas_call(
-        coupling_kernel,
-        out_shape=[jax.ShapeDtypeStruct(own.shape, jnp.float32)] + [shape] * (len(messages) + 1),
-        in_specs=[VMEM] * (len(messages) + 3),
-        out_specs=[VMEM] * (len(messages) + 2),
-        compiler_params=PARAMS,
-        name="couplings",
-    )(moved, own, border, *messages)
-    return total, partial
-
-
-def assemble_kernel(columns_ref, rows_ref, *refs, parts):
-    refs[-2][...] = tree_sum([ref[...] for ref in refs[:parts]])
-    pieces, out_ref = refs[parts:-2], refs[-1]
-    place = lax.axis_index("col")
-    size = pieces[0].shape[0]
-    count = len(pieces)
-    for m, piece in enumerate(pieces):
-        out_ref[pl.ds(pl.multiple_of((place ^ m) * size, 8), size), :] = piece[...]
-    at = count * size
-    out_ref[at:, :] = jnp.zeros((out_ref.shape[0] - at, out_ref.shape[1]), jnp.float32)
-    out_ref[at : at + count, :] = columns_ref[...].astype(jnp.float32)
-    out_ref[at + count : at + 2 * count, :size] = rows_ref[0].astype(jnp.float32)
-
-
-def sum_and_assemble(parts, pieces, columns, rows):
-    size, wide = pieces[0].shape
-    count = len(pieces)
-    return pl.pallas_call(
-        functools.partial(assemble_kernel, parts=len(parts)),
-        out_shape=[
-            jax.ShapeDtypeStruct(parts[0].shape, jnp.float32),
-            jax.ShapeDtypeStruct((count * size + -(-count // 4) * 8, wide), jnp.float32),
-        ],
-        in_specs=[VMEM] * (len(parts) + count + 2),
-        out_specs=[VMEM] * 2,
-        compiler_params=PARAMS,
-        name="assemble",
-    )(columns, rows, *parts, *pieces)
-
-
 def placed_rows(groups, group, rows_here, width):
     place = lax.axis_index("scen")
     first = (place - lax.rem(place, 2)) * rows_here
@@ -525,22 +398,150 @@
     return total
 
 
-def near_kernel(*refs, group):
-    groups, out_ref = refs[:-1], refs[-1]
-    rows, width = out_ref.shape
-    out_ref[...] = placed_rows(groups, group, rows // 2, width)
-
-
-def near_rows(groups, group, rows_here, width):
+def cholesky_kernel(
+    mine_first, mine_last, other_first, other_last, barrier_ref, *refs, group
+):
+    upper_ref, turned_ref, packed_ref = refs[-3:]
+    near, near_out = (refs[:1], refs[3:4]) if len(refs) == 7 else ((), ())
+    inverse_ref, slice_ref = refs[len(near) : len(near) + 2]
+    width = barrier_ref.shape[1]
+    count = width // BLOCK
+    core = lax.rem(lax.axis_index("scen"), 2)
+    place = lax.axis_index("col")
+    row, lane = row_and_lane()
+    diagonal = row == lane
+    rows = mine_first.shape[0]
+    for n, ref in enumerate((mine_first, mine_last, other_first, other_last)):
+        owner = core if n < 2 else 1 - core
+        at = (2 * owner + n % 2) * rows
+        packed_ref[pl.ds(pl.multiple_of(at, 8), rows), :] = ref[...]
+    blocks = unpack(packed_ref, width)
+    for i in range(count):
+        extra = barrier_ref[:, i * BLOCK : (i + 1) * BLOCK]
+        blocks[i, i] = blocks[i, i] + jnp.where(diagonal, extra, 0.0)
+    panels = [jnp.concatenate([blocks[i, j] for j in range(i, count)], 1) for i in range(count)]
+    slice_rows = slice_ref.shape[0]
+    start = place * slice_rows
+    block = pl.ds(pl.multiple_of(start // BLOCK * BLOCK, BLOCK), BLOCK)
+    upper_ref[...] = jnp.zeros(upper_ref.shape, jnp.float32)
+    inverse_ref[...] = jnp.zeros(inverse_ref.shape, jnp.float32)
+    for i in range(count):
+        here = slice(i * BLOCK, (i + 1) * BLOCK)
+        before = slice(0, i * BLOCK)
+        own, inverse = factor_block(panels[i][:, :BLOCK])
+        if i == 0 and near_out:
+            rows_near = near_out[0].shape[0] // 2
+            near_out[0][...] = placed_rows(near, group, rows_near, width)
+        upper_ref[here, here] = own
+        inverse_ref[here, here] = inverse
+        if i + 1 < count:
+            rest = []
+            for j in range(i + 1, count):
+                at = (j - i) * BLOCK
+                rest.append(exact(inverse, panels[i][:, at : at + BLOCK]))
+                upper_ref[here, j * BLOCK : (j + 1) * BLOCK] = rest[-1]
+                if j == i + 1:
+                    square = panels[j][:, :BLOCK] - exact_tn(rest[0], rest[0])
+            for j in range(i + 1, count):
+                parts = [square] if j == i + 1 else []
+                done = len(parts)
+                if done < count - j:
+                    wide = jnp.concatenate(rest[j - i - 1 + done :], 1)
+                    update = exact_tn(rest[j - i - 1], wide)
+                    parts.append(panels[j][:, done * BLOCK :] - update)
+                panels[j] = jnp.concatenate(parts, 1)
+        if i + 2 == count:
+            turned_ref[:, : (i + 1) * BLOCK] = upper_ref[: (i + 1) * BLOCK, block].T
+        if i > 0:
+            mixed = exact_tn(upper_ref[before, here], inverse_ref[before, before])
+            inverse_ref[here, before] = -exact(inverse, mixed)
+    turned_ref[:, width - BLOCK :] = upper_ref[width - BLOCK :, block].T
+    slice_ref[...] = turned_ref[pl.ds(pl.multiple_of(lax.rem(start, BLOCK), 8), slice_rows), :]
+
+
+def cholesky(halves, barrier, col_count, near, group, rows_here):
+    width = barrier.shape[0]
+    placed = [jax.ShapeDtypeStruct((2 * rows_here, width), jnp.float32)] * len(near)
     return pl.pallas_call(
-        functools.partial(near_kernel, group=group),
-        out_shape=jax.ShapeDtypeStruct((2 * rows_here, width), jnp.float32),
-        in_specs=[VMEM] * len(groups),
-        out_specs=VMEM,
+        functools.partial(cholesky_kernel, group=group),
+        out_shape=[
+            jax.ShapeDtypeStruct((width, width), jnp.float32),
+            jax.ShapeDtypeStruct((width // col_count, width), jnp.float32),
+        ]
+        + placed,
+        in_specs=[VMEM] * (5 + len(near)),
+        out_specs=[VMEM] * (2 + len(near)),
+        scratch_shapes=[
+            pltpu.VMEM((width, width), jnp.float32),
+            pltpu.VMEM((BLOCK, width), jnp.float32),
+            pltpu.VMEM((4 * halves[0].shape[0], BLOCK), jnp.float32),
+        ],
         compiler_params=PARAMS,
         cost_estimate=long_cost(0),
-        name="near",
-    )(*groups)
+        name="cholesky",
+    )(*halves, barrier[None], *near)
+
+
+def coupling_kernel(moved_ref, own_ref, border_ref, *refs):
+    count = len(refs) // 2
+    messages, total_ref, out_refs = refs[: count - 1], refs[count - 1], refs[count:]
+    rows = own_ref.shape[0]
+    size, depth = border_ref.shape
+    tiles = whole_tiles(rows)
+    moved = moved_ref[...]
+    out_refs[0][...] = matmul_nt(border_ref[...], moved)
+    parts = [own_ref[...]]
+    for message, out_ref in zip(messages, out_refs[1:]):
+        high = message[:tiles, :].astype(jnp.float32)
+        low = message[tiles : 2 * tiles, :].astype(jnp.float32)
+        parts.append((high + low)[:rows])
+        first = [2 * tiles + n * size for n in range(depth // BLOCK)]
+        border = jnp.concatenate([message[at : at + size, :] for at in first], 1)
+        out_ref[...] = matmul_nt(border, moved)
+    total_ref[...] = tree_sum(parts)
+
+
+def sum_and_couplings(own, messages, moved, border):
+    shape = jax.ShapeDtypeStruct((border.shape[0], moved.shape[0]), jnp.float32)
+    total, *partial = pl.pallas_call(
+        coupling_kernel,
+        out_shape=[jax.ShapeDtypeStruct(own.shape, jnp.float32)] + [shape] * (len(messages) + 1),
+        in_specs=[VMEM] * (len(messages) + 3),
+        out_specs=[VMEM] * (len(messages) + 2),
+        compiler_params=PARAMS,
+        name="couplings",
+    )(moved, own, border, *messages)
+    return total, partial
+
+
+def assemble_kernel(columns_ref, rows_ref, *refs, parts):
+    refs[-2][...] = tree_sum([ref[...] for ref in refs[:parts]])
+    pieces, out_ref = refs[parts:-2], refs[-1]
+    place = lax.axis_index("col")
+    size = pieces[0].shape[0]
+    count = len(pieces)
+    for m, piece in enumerate(pieces):
+        out_ref[pl.ds(pl.multiple_of((place ^ m) * size, 8), size), :] = piece[...]
+    at = count * size
+    out_ref[at:, :] = jnp.zeros((out_ref.shape[0] - at, out_ref.shape[1]), jnp.float32)
+    out_ref[at : at + count, :] = columns_ref[...].astype(jnp.float32)
+    out_ref[at + count : at + 2 * count, :size] = rows_ref[0].astype(jnp.float32)
+
+
+def sum_and_assemble(parts, pieces, columns, rows):
+    size, wide = pieces[0].shape
+    count = len(pieces)
+    return pl.pallas_call(
+        functools.partial(assemble_kernel, parts=len(parts)),
+        out_shape=[
+            jax.ShapeDtypeStruct(parts[0].shape, jnp.float32),
+            jax.ShapeDtypeStruct((count * size + -(-count // 4) * 8, wide), jnp.float32),
+        ],
+        in_specs=[VMEM] * (len(parts) + count + 2),
+        out_specs=[VMEM] * 2,
+        compiler_params=PARAMS,
+        name="assemble",
+    )(columns, rows, *parts, *pieces)
 
 
 def far_kernel(wait_ref, near_ref, *refs, group):
@@ -568,8 +569,17 @@
     )(wait, near, *groups)
 
 
-def solve_kernel(keep_ref, got_ref, inverse_ref, out_ref):
-    out_ref[...] = exact_nt(keep_ref[...] + got_ref[...], inverse_ref[...])
+def solve_kernel(keep_ref, got_ref, inverse_ref, out_ref, solved_ref, sems):
+    half = out_ref.shape[1] // 2
+    first, last = slice(0, half), slice(half, 2 * half)
+    rows = keep_ref[...] + got_ref[...]
+    stores = []
+    for n, (here, inner) in enumerate(((last, slice(0, 2 * half)), (first, first))):
+        solved_ref[:, here] = exact_nt(rows[:, inner], inverse_ref[here, inner])
+        stores.append(pltpu.make_async_copy(solved_ref.at[:, here], out_ref.at[:, here], sems.at[n]))
+        stores[-1].start()
+    for store in stores:
+        store.wait()
 
 
 def solve_rows(keep, got, inverse):
@@ -577,7 +587,8 @@
         solve_kernel,
         out_shape=jax.ShapeDtypeStruct(keep.shape, jnp.float32),
         in_specs=[VMEM] * 3,
-        out_specs=VMEM,
+        out_specs=HBM,
+        scratch_shapes=[pltpu.VMEM(keep.shape, jnp.float32), pltpu.SemaphoreType.DMA((2,))],
         compiler_params=PARAMS,
         name="solve",
     )(keep, got, inverse)
@@ -627,10 +638,11 @@
     groups = [own]
     if sparse:
         groups += [swap(own, "scen", 2 * m) for m in range(1, scen_count // 2)]
-    near = [near_rows([own], group, rows_here, width)] if sparse else []
-    mine = join([part] + [swap(part, "col", m) for m in range(1, col_count)], near)
+    mine = join([part] + [swap(part, "col", m) for m in range(1, col_count)])
     halves = list(mine) + [swap(half, "scen", 1) for half in mine]
-    inverse, factor_rows = cholesky(halves, barrier_diag, col_count)
+    inverse, factor_rows, *near = cholesky(
+        halves, barrier_diag, col_count, groups[:1] if sparse else [], group, rows_here
+    )
     if sparse:
         rows, other = far_rows(near[0], groups[1:], group, inverse)
         solved = solve_rows(rows, swap(other, "scen", 1), inverse)

time: 57.6 us -> 56.6 us (0.983)
  Pallas kernels: 20.7 us -> 19.5 us
    pallas_call x2 -> x1, Pallas kernels: 13.3 us -> 12.3 us  [cholesky(): pl.pallas_call(functools.partial(cholesky_kernel, group=group), out_shape...]
  transfers between devices with their start and end apart: 19 -> 19, of which waited for: 9 -> 8; matrix products, arithmetic and copies ran while one was open for 0% -> 0% of each run, Pallas kernels for 23% -> 22%
where the time goes in v8:
time: 56.6 us; the launch traced here: 56.4 us
  starting transfers between devices  21.8 us (39%)
  Pallas kernels  19.5 us (34%)
  waiting for transfers between devices  13.5 us (24%)
  between operations  1.53 us (3%)
    ppermute x19, starting transfers between devices, swap(): return lax.ppermute(value, axis, [(i, i ^ step) for i in range(count)])  21.8 us
    ppermute x19, waiting for transfers between devices, swap(): return lax.ppermute(value, axis, [(i, i ^ step) for i in range(count)])  13.5 us
    pallas_call x1, Pallas kernels, cholesky(): pl.pallas_call(functools.partial(cholesky_kernel, group=group), out_shape...  12.3 us
    pallas_call x1, Pallas kernels, front(): pl.pallas_call(functools.partial(front_kernel, width=width), out_shape=[j...  2.8 us
    pallas_call x1, Pallas kernels, far_rows(): pl.pallas_call(functools.partial(far_kernel, group=group), out_shape=[hal...  2.19 us
    pallas_call x1, Pallas kernels, solve_rows(): pl.pallas_call(solve_kernel, out_shape=jax.ShapeDtypeStruct(keep.shape, j...  1.67 us
  transfers between devices with their start and end apart: 19, of which 8 were waited for; matrix products, arithmetic and copies ran while one was open for 0% of the time, Pallas kernels for 22%

profile of v8, /device:TPU:0, one launch (start us, length us, event | category | flops | bytes accessed | tf_op | source)
XLA Modules:
  0.0 56.4 jit_solution(1031952492366937747)
XLA Ops:
  1.3 2.8 %front.1 = (bf16[256,512]{1,0:T(8,128)(2,1)S(1)}, f32[544,128]{1,0:T(8,128)S(1)}, f32[544,128]{1,0:T(8,128)S(1)}, bf16[48,512]{1,0:T(8,128)(2,1)S(1)}, bf16[48,5...) custom-call(s32[1]{0:T(128)S(6)} %copy.9.order_ref, s32[4,256]{1,0:T(4,128)} %columns_ref.3, ...), custom_call_target="tpu_custom_call" | custom-call | flops 20000000000 | bytes 1024 | tf_op jit(solution)/shard_map/front/pallas_call | solution.py:190
  4.1 0.5 collective-permute-start
  4.6 1.2 %collective-permute-done.got_ref = f32[544,128]{1,0:T(8,128)S(1)} collective-permute-done((f32[544,128]{1,0:T(8,128)S(1)}, f32[544,128]{1,0:T(8,128)S(1)}, u32[]{:S(2)}, u32[]{:S(2)}) %collective-permute-start) | collective-permute-done | bytes 278560 | tf_op jit(solution)/shard_map/ppermute | solution.py:282
  5.9 2.9 %collective-permute-start.1 = (bf16[480,128]{1,0:T(8,128)(2,1)S(1)}, bf16[480,128]{1,0:T(8,128)(2,1)S(1)}, u32[]{:S(2)}, u32[]{:S(2)}) collective-permute-start(bf16[480,128]{1,0:T(8,128)(2,1)S(1)} %get-tuple-element.35), channel_id=1, source_target_pairs={{0,1},{1,0},{2,3},{3,2},{4,5},{5,4},{6,7},{7,6},{8,9},{9,8},{10,11... | collective-permute-start | bytes 368648 | tf_op jit(solution)/shard_map/ppermute | solution.py:282
  8.8 1.5 %collective-permute-start.2 = (bf16[480,128]{1,0:T(8,128)(2,1)S(1)}, bf16[480,128]{1,0:T(8,128)(2,1)S(1)}, u32[]{:S(2)}, u32[]{:S(2)}) collective-permute-start(bf16[480,128]{1,0:T(8,128)(2,1)S(1)} %get-tuple-element.36), channel_id=1, source_target_pairs={{0,2},{1,3},{2,0},{3,1},{4,6},{5,7},{6,4},{7,5},{8,10},{9,11},{10,... | collective-permute-start | bytes 368648 | tf_op jit(solution)/shard_map/ppermute | solution.py:282
  10.3 2.1 %collective-permute-done.1.refs_0_ = bf16[480,128]{1,0:T(8,128)(2,1)S(1)} collective-permute-done((bf16[480,128]{1,0:T(8,128)(2,1)S(1)}, bf16[480,128]{1,0:T(8,128)(2,1)S(1)}, u32[]{:S(2)}, u32[]{:S(2)}) %collective-permute-start.1) | collective-permute-done | bytes 122912 | tf_op jit(solution)/shard_map/ppermute | solution.py:282
  12.5 4.0 %collective-permute-done.2.refs_1_ = bf16[480,128]{1,0:T(8,128)(2,1)S(1)} collective-permute-done((bf16[480,128]{1,0:T(8,128)(2,1)S(1)}, bf16[480,128]{1,0:T(8,128)(2,1)S(1)}, u32[]{:S(2)}, u32[]{:S(2)}) %collective-permute-start.2) | collective-permute-done | bytes 122912 | tf_op jit(solution)/shard_map/ppermute | solution.py:282
  16.9 1.3 %collective-permute-start.7 = (f32[48,256]{1,0:T(8,128)S(1)}, f32[48,256]{1,0:T(8,128)S(1)}, u32[]{:S(2)}, u32[]{:S(2)}) collective-permute-start(f32[48,256]{1,0:T(8,128)S(1)} %get-tuple-element.40), channel_id=1, source_target_pairs={{0,1},{1,0},{2,3},{3,2},{4,5},{5,4},{6,7},{7,6},{8,9},{9,8},{10,11... | collective-permute-start | bytes 147464 | tf_op jit(solution)/shard_map/ppermute | solution.py:282
  18.2 3.6 %collective-permute-start.6 = (f32[136,128]{1,0:T(8,128)S(1)}, f32[136,128]{1,0:T(8,128)S(1)}, u32[]{:S(2)}, u32[]{:S(2)}) collective-permute-start(f32[136,128]{1,0:T(8,128)S(1)} %get-tuple-element.38.refs_0_), channel_id=1, source_target_pairs={{0,24},{4,28},{8,16},{12,20},{16,8},{20,12},{24,0},{28,4},{1,25},{... | collective-permute-start | bytes 208904 | tf_op jit(solution)/shard_map/ppermute | solution.py:282
  21.8 0.8 %collective-permute-start.4 = (f32[136,128]{1,0:T(8,128)S(1)}, f32[136,128]{1,0:T(8,128)S(1)}, u32[]{:S(2)}, u32[]{:S(2)}) collective-permute-start(f32[136,128]{1,0:T(8,128)S(1)} %get-tuple-element.38.refs_0_), channel_id=1, source_target_pairs={{0,8},{4,12},{8,0},{12,4},{16,24},{20,28},{24,16},{28,20},{1,9},{5... | collective-permute-start | bytes 208904 | tf_op jit(solution)/shard_map/ppermute | solution.py:282
  22.6 0.8 %collective-permute-start.8 = (f32[48,256]{1,0:T(8,128)S(1)}, f32[48,256]{1,0:T(8,128)S(1)}, u32[]{:S(2)}, u32[]{:S(2)}) collective-permute-start(f32[48,256]{1,0:T(8,128)S(1)} %get-tuple-element.41), channel_id=1, source_target_pairs={{0,2},{1,3},{2,0},{3,1},{4,6},{5,7},{6,4},{7,5},{8,10},{9,11},{10,... | collective-permute-start | bytes 147464 | tf_op jit(solution)/shard_map/ppermute | solution.py:282
  23.5 1.4 %collective-permute-start.9 = (f32[48,256]{1,0:T(8,128)S(1)}, f32[48,256]{1,0:T(8,128)S(1)}, u32[]{:S(2)}, u32[]{:S(2)}) collective-permute-start(f32[48,256]{1,0:T(8,128)S(1)} %get-tuple-element.42), channel_id=1, source_target_pairs={{0,3},{1,2},{2,1},{3,0},{4,7},{5,6},{6,5},{7,4},{8,11},{9,10},{10,... | collective-permute-start | bytes 147464 | tf_op jit(solution)/shard_map/ppermute | solution.py:282
  24.9 1.8 %collective-permute-done.8.refs_6_ = f32[48,256]{1,0:T(8,128)S(1)} collective-permute-done((f32[48,256]{1,0:T(8,128)S(1)}, f32[48,256]{1,0:T(8,128)S(1)}, u32[]{:S(2)}, u32[]{:S(2)}) %collective-permute-start.8) | collective-permute-done | bytes 49184 | tf_op jit(solution)/shard_map/ppermute | solution.py:282
  26.7 1.7 %collective-permute-done.9.refs_7_ = f32[48,256]{1,0:T(8,128)S(1)} collective-permute-done((f32[48,256]{1,0:T(8,128)S(1)}, f32[48,256]{1,0:T(8,128)S(1)}, u32[]{:S(2)}, u32[]{:S(2)}) %collective-permute-start.9) | collective-permute-done | bytes 49184 | tf_op jit(solution)/shard_map/ppermute | solution.py:282
  28.5 1.5 %collective-permute-start.12 = (f32[136,128]{1,0:T(8,128)S(1)}, f32[136,128]{1,0:T(8,128)S(1)}, u32[]{:S(2)}, u32[]{:S(2)}) collective-permute-start(f32[136,128]{1,0:T(8,128)S(1)} %get-tuple-element.43.refs_0_), channel_id=1, source_target_pairs={{0,3},{1,2},{2,1},{3,0},{4,7},{5,6},{6,5},{7,4},{8,11},{9,10},{10,... | collective-permute-start | bytes 208904 | tf_op jit(solution)/shard_map/ppermute | solution.py:282
  30.0 1.5 %collective-permute-start.11 = (f32[136,128]{1,0:T(8,128)S(1)}, f32[136,128]{1,0:T(8,128)S(1)}, u32[]{:S(2)}, u32[]{:S(2)}) collective-permute-start(f32[136,128]{1,0:T(8,128)S(1)} %get-tuple-element.43.refs_0_), channel_id=1, source_target_pairs={{0,2},{1,3},{2,0},{3,1},{4,6},{5,7},{6,4},{7,5},{8,10},{9,11},{10,... | collective-permute-start | bytes 208904 | tf_op jit(solution)/shard_map/ppermute | solution.py:282
  31.5 0.5 collective-permute-start.10
  32.1 3.6 %collective-permute-start.17 = (f32[200,256]{1,0:T(8,128)S(1)}, f32[200,256]{1,0:T(8,128)S(1)}, u32[]{:S(2)}, u32[]{:S(2)}) collective-permute-start(f32[200,256]{1,0:T(8,128)S(1)} %get-tuple-element.46.refs_0_), channel_id=1, source_target_pairs={{0,24},{4,28},{8,16},{12,20},{16,8},{20,12},{24,0},{28,4},{1,25},{... | collective-permute-start | bytes 614408 | tf_op jit(solution)/shard_map/ppermute | solution.py:282
  35.7 0.8 %collective-permute-start.15 = (f32[200,256]{1,0:T(8,128)S(1)}, f32[200,256]{1,0:T(8,128)S(1)}, u32[]{:S(2)}, u32[]{:S(2)}) collective-permute-start(f32[200,256]{1,0:T(8,128)S(1)} %get-tuple-element.46.refs_0_), channel_id=1, source_target_pairs={{0,8},{4,12},{8,0},{12,4},{16,24},{20,28},{24,16},{28,20},{1,9},{5... | collective-permute-start | bytes 614408 | tf_op jit(solution)/shard_map/ppermute | solution.py:282
  37.1 0.8 %collective-permute-done.13.other_first = f32[272,128]{1,0:T(8,128)S(1)} collective-permute-done((f32[272,128]{1,0:T(8,128)S(1)}, f32[272,128]{1,0:T(8,128)S(1)}, u32[]{:S(2)}, u32[]{:S(2)}) %collective-permute-start.13) | collective-permute-done | bytes 139296 | tf_op jit(solution)/shard_map/ppermute | solution.py:282
  38.2 12.3 %cholesky.1 = (f32[512,512]{1,0:T(8,128)S(1)}, f32[128,512]{1,0:T(8,128)}, f32[480,512]{1,0:T(8,128)S(1)}) custom-call(f32[272,128]{1,0:T(8,128)S(1)} %get-tuple-element.44.mine_first, f32[272,128]{1,0:T(8,128)S(1)} %get-tuple-element.45.mine_last, f32[272,128]{1,0:T(8,128)S(1)} %collective-permute-done.13.other_first, ...), custom_call_target="tpu_custom_call" | custom-call | bytes 1024 | tf_op jit(solution)/shard_map/cholesky/pallas_call | solution.py:465
  50.5 2.2 %far.1 = (f32[240,512]{1,0:T(8,128)S(1)}, f32[240,512]{1,0:T(8,128)S(1)}) custom-call(f32[512,512]{1,0:T(8,128)S(1)} %get-tuple-element.48.wait_ref.inverse_ref, f32[480,512]{1,0:T(8,128)S(1)} %get-tuple-element.49.near_ref, f32[200,256]{1,0:T(8,128)S(1)} %collective-permute-done.15.refs_0_, f32[200,256]{1,0:T(8,128)S(1)} %collective-permute-done.16.refs_1_, ...), custom_call_target="tpu_custom_call" | custom-call | bytes 1024 | tf_op jit(solution)/shard_map/far/pallas_call | solution.py:561
  53.1 1.5 %collective-permute-done.18.got_ref = f32[240,512]{1,0:T(8,128)S(1)} collective-permute-done((f32[240,512]{1,0:T(8,128)S(1)}, f32[240,512]{1,0:T(8,128)S(1)}, u32[]{:S(2)}, u32[]{:S(2)}) %collective-permute-start.18) | collective-permute-done | bytes 491552 | tf_op jit(solution)/shard_map/ppermute | solution.py:282
  54.6 1.7 %solve.1 = f32[240,512]{1,0:T(8,128)} custom-call(f32[240,512]{1,0:T(8,128)S(1)} %get-tuple-element.50.keep_ref, f32[240,512]{1,0:T(8,128)S(1)} %collective-permute-done.18.got_ref, f32[512,512]{1,0:T(8,128)S(1)} %get-tuple-element.48.wait_ref.inverse_ref), custom_call_target="tpu_custom_call" | custom-call | tf_op jit(solution)/shard_map/solve/pallas_call | solution.py:586
  (28 shorter events, 1.8 us)
Async XLA Ops:
  4.1 1.7 %collective-permute-start = (f32[544,128]{1,0:T(8,128)S(1)}, f32[544,128]{1,0:T(8,128)S(1)}, u32[]{:S(2)}, u32[]{:S(2)}) collective-permute-start(f32[544,128]{1,0:T(8,128)S(1)} %get-tuple-element.29), channel_id=1, source_target_pairs={{0,4},{4,0},{8,12},{12,8},{16,20},{20,16},{24,28},{28,24},{1,5},{5... | collective-permute-start | bytes 835592 | tf_op jit(solution)/shard_map/ppermute | solution.py:282
  5.9 6.6 %collective-permute-start.1 = (bf16[480,128]{1,0:T(8,128)(2,1)S(1)}, bf16[480,128]{1,0:T(8,128)(2,1)S(1)}, u32[]{:S(2)}, u32[]{:S(2)}) collective-permute-start(bf16[480,128]{1,0:T(8,128)(2,1)S(1)} %get-tuple-element.35), channel_id=1, source_target_pairs={{0,1},{1,0},{2,3},{3,2},{4,5},{5,4},{6,7},{7,6},{8,9},{9,8},{10,11... | collective-permute-start | bytes 368648 | tf_op jit(solution)/shard_map/ppermute | solution.py:282
  8.8 7.7 %collective-permute-start.2 = (bf16[480,128]{1,0:T(8,128)(2,1)S(1)}, bf16[480,128]{1,0:T(8,128)(2,1)S(1)}, u32[]{:S(2)}, u32[]{:S(2)}) collective-permute-start(bf16[480,128]{1,0:T(8,128)(2,1)S(1)} %get-tuple-element.36), channel_id=1, source_target_pairs={{0,2},{1,3},{2,0},{3,1},{4,6},{5,7},{6,4},{7,5},{8,10},{9,11},{10,... | collective-permute-start | bytes 368648 | tf_op jit(solution)/shard_map/ppermute | solution.py:282
  10.3 6.2 %collective-permute-start.3 = (bf16[480,128]{1,0:T(8,128)(2,1)S(1)}, bf16[480,128]{1,0:T(8,128)(2,1)S(1)}, u32[]{:S(2)}, u32[]{:S(2)}) collective-permute-start(bf16[480,128]{1,0:T(8,128)(2,1)S(1)} %get-tuple-element.37), channel_id=1, source_target_pairs={{0,3},{1,2},{2,1},{3,0},{4,7},{5,6},{6,5},{7,4},{8,11},{9,10},{10,... | collective-permute-start | bytes 368648 | tf_op jit(solution)/shard_map/ppermute | solution.py:282
  16.9 11.5 %copy-start = (s32[4,256]{1,0:T(4,128)S(1)}, s32[4,256]{1,0:T(4,128)}, u32[]{:S(2)}) copy-start(s32[4,256]{1,0:T(4,128)} %columns_ref.3) | copy-start | bytes 12292
  16.9 6.5 %collective-permute-start.7 = (f32[48,256]{1,0:T(8,128)S(1)}, f32[48,256]{1,0:T(8,128)S(1)}, u32[]{:S(2)}, u32[]{:S(2)}) collective-permute-start(f32[48,256]{1,0:T(8,128)S(1)} %get-tuple-element.40), channel_id=1, source_target_pairs={{0,1},{1,0},{2,3},{3,2},{4,5},{5,4},{6,7},{7,6},{8,9},{9,8},{10,11... | collective-permute-start | bytes 147464 | tf_op jit(solution)/shard_map/ppermute | solution.py:282
  18.2 10.2 %collective-permute-start.6 = (f32[136,128]{1,0:T(8,128)S(1)}, f32[136,128]{1,0:T(8,128)S(1)}, u32[]{:S(2)}, u32[]{:S(2)}) collective-permute-start(f32[136,128]{1,0:T(8,128)S(1)} %get-tuple-element.38.refs_0_), channel_id=1, source_target_pairs={{0,24},{4,28},{8,16},{12,20},{16,8},{20,12},{24,0},{28,4},{1,25},{... | collective-permute-start | bytes 208904 | tf_op jit(solution)/shard_map/ppermute | solution.py:282
  21.8 6.6 %collective-permute-start.5 = (f32[136,128]{1,0:T(8,128)S(1)}, f32[136,128]{1,0:T(8,128)S(1)}, u32[]{:S(2)}, u32[]{:S(2)}) collective-permute-start(f32[136,128]{1,0:T(8,128)S(1)} %get-tuple-element.38.refs_0_), channel_id=1, source_target_pairs={{0,16},{4,20},{8,24},{12,28},{16,0},{20,4},{24,8},{28,12},{1,17},{... | collective-permute-start | bytes 208904 | tf_op jit(solution)/shard_map/ppermute | solution.py:282
  21.8 6.6 %collective-permute-start.4 = (f32[136,128]{1,0:T(8,128)S(1)}, f32[136,128]{1,0:T(8,128)S(1)}, u32[]{:S(2)}, u32[]{:S(2)}) collective-permute-start(f32[136,128]{1,0:T(8,128)S(1)} %get-tuple-element.38.refs_0_), channel_id=1, source_target_pairs={{0,8},{4,12},{8,0},{12,4},{16,24},{20,28},{24,16},{28,20},{1,9},{5... | collective-permute-start | bytes 208904 | tf_op jit(solution)/shard_map/ppermute | solution.py:282
  22.6 5.8 %copy-start.1 = (s32[1,4,48]{2,1,0:T(4,128)S(1)}, s32[1,4,48]{2,1,0:T(4,128)}, u32[]{:S(2)}) copy-start(s32[1,4,48]{2,1,0:T(4,128)} %rows_ref.1) | copy-start | bytes 2308
  22.6 4.1 %collective-permute-start.8 = (f32[48,256]{1,0:T(8,128)S(1)}, f32[48,256]{1,0:T(8,128)S(1)}, u32[]{:S(2)}, u32[]{:S(2)}) collective-permute-start(f32[48,256]{1,0:T(8,128)S(1)} %get-tuple-element.41), channel_id=1, source_target_pairs={{0,2},{1,3},{2,0},{3,1},{4,6},{5,7},{6,4},{7,5},{8,10},{9,11},{10,... | collective-permute-start | bytes 147464 | tf_op jit(solution)/shard_map/ppermute | solution.py:282
  23.5 5.0 %collective-permute-start.9 = (f32[48,256]{1,0:T(8,128)S(1)}, f32[48,256]{1,0:T(8,128)S(1)}, u32[]{:S(2)}, u32[]{:S(2)}) collective-permute-start(f32[48,256]{1,0:T(8,128)S(1)} %get-tuple-element.42), channel_id=1, source_target_pairs={{0,3},{1,2},{2,1},{3,0},{4,7},{5,6},{6,5},{7,4},{8,11},{9,10},{10,... | collective-permute-start | bytes 147464 | tf_op jit(solution)/shard_map/ppermute | solution.py:282
  28.5 7.1 %collective-permute-start.12 = (f32[136,128]{1,0:T(8,128)S(1)}, f32[136,128]{1,0:T(8,128)S(1)}, u32[]{:S(2)}, u32[]{:S(2)}) collective-permute-start(f32[136,128]{1,0:T(8,128)S(1)} %get-tuple-element.43.refs_0_), channel_id=1, source_target_pairs={{0,3},{1,2},{2,1},{3,0},{4,7},{5,6},{6,5},{7,4},{8,11},{9,10},{10,... | collective-permute-start | bytes 208904 | tf_op jit(solution)/shard_map/ppermute | solution.py:282
  30.0 6.5 %collective-permute-start.11 = (f32[136,128]{1,0:T(8,128)S(1)}, f32[136,128]{1,0:T(8,128)S(1)}, u32[]{:S(2)}, u32[]{:S(2)}) collective-permute-start(f32[136,128]{1,0:T(8,128)S(1)} %get-tuple-element.43.refs_0_), channel_id=1, source_target_pairs={{0,2},{1,3},{2,0},{3,1},{4,6},{5,7},{6,4},{7,5},{8,10},{9,11},{10,... | collective-permute-start | bytes 208904 | tf_op jit(solution)/shard_map/ppermute | solution.py:282
  31.5 4.9 %collective-permute-start.10 = (f32[136,128]{1,0:T(8,128)S(1)}, f32[136,128]{1,0:T(8,128)S(1)}, u32[]{:S(2)}, u32[]{:S(2)}) collective-permute-start(f32[136,128]{1,0:T(8,128)S(1)} %get-tuple-element.43.refs_0_), channel_id=1, source_target_pairs={{0,1},{1,0},{2,3},{3,2},{4,5},{5,4},{6,7},{7,6},{8,9},{9,8},{10,11... | collective-permute-start | bytes 208904 | tf_op jit(solution)/shard_map/ppermute | solution.py:282
  32.1 18.4 %collective-permute-start.17 = (f32[200,256]{1,0:T(8,128)S(1)}, f32[200,256]{1,0:T(8,128)S(1)}, u32[]{:S(2)}, u32[]{:S(2)}) collective-permute-start(f32[200,256]{1,0:T(8,128)S(1)} %get-tuple-element.46.refs_0_), channel_id=1, source_target_pairs={{0,24},{4,28},{8,16},{12,20},{16,8},{20,12},{24,0},{28,4},{1,25},{... | collective-permute-start | bytes 614408 | tf_op jit(solution)/shard_map/ppermute | solution.py:282
  35.7 14.8 %collective-permute-start.16 = (f32[200,256]{1,0:T(8,128)S(1)}, f32[200,256]{1,0:T(8,128)S(1)}, u32[]{:S(2)}, u32[]{:S(2)}) collective-permute-start(f32[200,256]{1,0:T(8,128)S(1)} %get-tuple-element.46.refs_0_), channel_id=1, source_target_pairs={{0,16},{4,20},{8,24},{12,28},{16,0},{20,4},{24,8},{28,12},{1,17},{... | collective-permute-start | bytes 614408 | tf_op jit(solution)/shard_map/ppermute | solution.py:282
  35.7 14.8 %collective-permute-start.15 = (f32[200,256]{1,0:T(8,128)S(1)}, f32[200,256]{1,0:T(8,128)S(1)}, u32[]{:S(2)}, u32[]{:S(2)}) collective-permute-start(f32[200,256]{1,0:T(8,128)S(1)} %get-tuple-element.46.refs_0_), channel_id=1, source_target_pairs={{0,8},{4,12},{8,0},{12,4},{16,24},{20,28},{24,16},{28,20},{1,9},{5... | collective-permute-start | bytes 614408 | tf_op jit(solution)/shard_map/ppermute | solution.py:282
  36.5 1.6 %copy-start.2 = (f32[512]{0:T(512)S(1)}, f32[512]{0:T(512)}, u32[]{:S(2)}) copy-start(f32[512]{0:T(512)} %param.13) | copy-start | bytes 6148
  36.5 1.4 %collective-permute-start.13 = (f32[272,128]{1,0:T(8,128)S(1)}, f32[272,128]{1,0:T(8,128)S(1)}, u32[]{:S(2)}, u32[]{:S(2)}) collective-permute-start(f32[272,128]{1,0:T(8,128)S(1)} %get-tuple-element.44.mine_first), channel_id=1, source_target_pairs={{0,4},{4,0},{8,12},{12,8},{16,20},{20,16},{24,28},{28,24},{1,5},{5... | collective-permute-start | bytes 417800 | tf_op jit(solution)/shard_map/ppermute | solution.py:282
  36.6 1.5 %collective-permute-start.14 = (f32[272,128]{1,0:T(8,128)S(1)}, f32[272,128]{1,0:T(8,128)S(1)}, u32[]{:S(2)}, u32[]{:S(2)}) collective-permute-start(f32[272,128]{1,0:T(8,128)S(1)} %get-tuple-element.45.mine_last), channel_id=1, source_target_pairs={{0,4},{4,0},{8,12},{12,8},{16,20},{20,16},{24,28},{28,24},{1,5},{5... | collective-permute-start | bytes 417800 | tf_op jit(solution)/shard_map/ppermute | solution.py:282
  52.7 1.9 %collective-permute-start.18 = (f32[240,512]{1,0:T(8,128)S(1)}, f32[240,512]{1,0:T(8,128)S(1)}, u32[]{:S(2)}, u32[]{:S(2)}) collective-permute-start(f32[240,512]{1,0:T(8,128)S(1)} %get-tuple-element.51), channel_id=1, source_target_pairs={{0,4},{4,0},{8,12},{12,8},{16,20},{20,16},{24,28},{28,24},{1,5},{5... | collective-permute-start | bytes 1474568 | tf_op jit(solution)/shard_map/ppermute | solution.py:282

commit v9 on v8

--- a/solution.py
+++ b/solution.py
@@ -10,6 +10,7 @@
 NF = 8192
 BLOCK = 128
 HIGHEST = lax.Precision.HIGHEST
+HIGH = lax.Precision.HIGH
 VMEM = pl.BlockSpec(memory_space=pltpu.VMEM)
 SMEM = pl.BlockSpec(memory_space=pltpu.SMEM)
 HBM = pl.BlockSpec(memory_space=pltpu.HBM)
@@ -41,26 +42,26 @@
     )
 
 
-def exact_tn(left, right):
+def close_tn(left, right):
     return lax.dot_general(
         left,
         right,
         (((0,), (0,)), ((), ())),
-        precision=HIGHEST,
+        precision=HIGH,
         preferred_element_type=jnp.float32,
     )
 
 
-def exact(left, right):
-    return jnp.dot(left, right, precision=HIGHEST, preferred_element_type=jnp.float32)
-
-
-def exact_nt(left, right):
+def close(left, right):
+    return jnp.dot(left, right, precision=HIGH, preferred_element_type=jnp.float32)
+
+
+def close_nt(left, right):
     return lax.dot_general(
         left,
         right,
         (((1,), (1,)), ((), ())),
-        precision=HIGHEST,
+        precision=HIGH,
         preferred_element_type=jnp.float32,
     )
 
@@ -365,7 +366,7 @@
             parts = [first, second, jnp.zeros((BLOCK - 8 * g - 16, BLOCK), jnp.float32)]
             if g > 0:
                 parts = [jnp.zeros((8 * g, BLOCK), jnp.float32)] + parts
-            update = exact(jnp.concatenate(tiles[far:], 0), jnp.concatenate(parts, 0))
+            update = close(jnp.concatenate(tiles[far:], 0), jnp.concatenate(parts, 0))
             for t in range(far, groups):
                 kept = jnp.where((owner == g) | (owner == g + 1), 0.0, tiles[t])
                 tiles[t] = kept - update[8 * (t - far) : 8 * (t - far) + 8]
@@ -438,23 +439,23 @@
             rest = []
             for j in range(i + 1, count):
                 at = (j - i) * BLOCK
-                rest.append(exact(inverse, panels[i][:, at : at + BLOCK]))
+                rest.append(close(inverse, panels[i][:, at : at + BLOCK]))
                 upper_ref[here, j * BLOCK : (j + 1) * BLOCK] = rest[-1]
                 if j == i + 1:
-                    square = panels[j][:, :BLOCK] - exact_tn(rest[0], rest[0])
+                    square = panels[j][:, :BLOCK] - close_tn(rest[0], rest[0])
             for j in range(i + 1, count):
                 parts = [square] if j == i + 1 else []
                 done = len(parts)
                 if done < count - j:
                     wide = jnp.concatenate(rest[j - i - 1 + done :], 1)
-                    update = exact_tn(rest[j - i - 1], wide)
+                    update = close_tn(rest[j - i - 1], wide)
                     parts.append(panels[j][:, done * BLOCK :] - update)
                 panels[j] = jnp.concatenate(parts, 1)
         if i + 2 == count:
             turned_ref[:, : (i + 1) * BLOCK] = upper_ref[: (i + 1) * BLOCK, block].T
         if i > 0:
-            mixed = exact_tn(upper_ref[before, here], inverse_ref[before, before])
-            inverse_ref[here, before] = -exact(inverse, mixed)
+            mixed = close_tn(upper_ref[before, here], inverse_ref[before, before])
+            inverse_ref[here, before] = -close(inverse, mixed)
     turned_ref[:, width - BLOCK :] = upper_ref[width - BLOCK :, block].T
     slice_ref[...] = turned_ref[pl.ds(pl.multiple_of(lax.rem(start, BLOCK), 8), slice_rows), :]
 
@@ -575,7 +576,7 @@
     rows = keep_ref[...] + got_ref[...]
     stores = []
     for n, (here, inner) in enumerate(((last, slice(0, 2 * half)), (first, first))):
-        solved_ref[:, here] = exact_nt(rows[:, inner], inverse_ref[here, inner])
+        solved_ref[:, here] = close_nt(rows[:, inner], inverse_ref[here, inner])
         stores.append(pltpu.make_async_copy(solved_ref.at[:, here], out_ref.at[:, here], sems.at[n]))
         stores[-1].start()
     for store in stores:

time: 56.6 us -> 55.5 us (0.981)
  Pallas kernels: 19.5 us -> 18.4 us
    pallas_call x1, Pallas kernels: 12.3 us -> 11.5 us  [cholesky(): pl.pallas_call(functools.partial(cholesky_kernel, group=group), out_shape...]
  transfers between devices with their start and end apart: 19 -> 19, of which waited for: 8 -> 8; matrix products, arithmetic and copies ran while one was open for 0% -> 0% of each run, Pallas kernels for 22% -> 21%
where the time goes in v9:
time: 55.5 us; the launch traced here: 55.3 us
  starting transfers between devices  21.8 us (39%)
  Pallas kernels  18.4 us (33%)
  waiting for transfers between devices  13.5 us (24%)
  between operations  1.53 us (3%)
    ppermute x19, starting transfers between devices, swap(): return lax.ppermute(value, axis, [(i, i ^ step) for i in range(count)])  21.8 us
    ppermute x19, waiting for transfers between devices, swap(): return lax.ppermute(value, axis, [(i, i ^ step) for i in range(count)])  13.5 us
    pallas_call x1, Pallas kernels, cholesky(): pl.pallas_call(functools.partial(cholesky_kernel, group=group), out_shape...  11.5 us
    pallas_call x1, Pallas kernels, front(): pl.pallas_call(functools.partial(front_kernel, width=width), out_shape=[j...  2.8 us
    pallas_call x1, Pallas kernels, far_rows(): pl.pallas_call(functools.partial(far_kernel, group=group), out_shape=[hal...  2.2 us
    pallas_call x1, Pallas kernels, solve_rows(): pl.pallas_call(solve_kernel, out_shape=jax.ShapeDtypeStruct(keep.shape, j...  1.37 us
  transfers between devices with their start and end apart: 19, of which 8 were waited for; matrix products, arithmetic and copies ran while one was open for 0% of the time, Pallas kernels for 21%

profile of v9, /device:TPU:0, one launch (start us, length us, event | category | flops | bytes accessed | tf_op | source)
XLA Modules:
  0.0 55.3 jit_solution(10863190886198454281)
XLA Ops:
  1.3 2.8 %front.1 = (bf16[256,512]{1,0:T(8,128)(2,1)S(1)}, f32[544,128]{1,0:T(8,128)S(1)}, f32[544,128]{1,0:T(8,128)S(1)}, bf16[48,512]{1,0:T(8,128)(2,1)S(1)}, bf16[48,5...) custom-call(s32[1]{0:T(128)S(6)} %copy.9.order_ref, s32[4,256]{1,0:T(4,128)} %columns_ref.3, ...), custom_call_target="tpu_custom_call" | custom-call | flops 20000000000 | bytes 1024 | tf_op jit(solution)/shard_map/front/pallas_call | solution.py:191
  4.1 0.5 collective-permute-start
  4.6 1.2 %collective-permute-done.got_ref = f32[544,128]{1,0:T(8,128)S(1)} collective-permute-done((f32[544,128]{1,0:T(8,128)S(1)}, f32[544,128]{1,0:T(8,128)S(1)}, u32[]{:S(2)}, u32[]{:S(2)}) %collective-permute-start) | collective-permute-done | bytes 278560 | tf_op jit(solution)/shard_map/ppermute | solution.py:283
  5.9 2.9 %collective-permute-start.1 = (bf16[480,128]{1,0:T(8,128)(2,1)S(1)}, bf16[480,128]{1,0:T(8,128)(2,1)S(1)}, u32[]{:S(2)}, u32[]{:S(2)}) collective-permute-start(bf16[480,128]{1,0:T(8,128)(2,1)S(1)} %get-tuple-element.35), channel_id=1, source_target_pairs={{0,1},{1,0},{2,3},{3,2},{4,5},{5,4},{6,7},{7,6},{8,9},{9,8},{10,11... | collective-permute-start | bytes 368648 | tf_op jit(solution)/shard_map/ppermute | solution.py:283
  8.8 1.5 %collective-permute-start.2 = (bf16[480,128]{1,0:T(8,128)(2,1)S(1)}, bf16[480,128]{1,0:T(8,128)(2,1)S(1)}, u32[]{:S(2)}, u32[]{:S(2)}) collective-permute-start(bf16[480,128]{1,0:T(8,128)(2,1)S(1)} %get-tuple-element.36), channel_id=1, source_target_pairs={{0,2},{1,3},{2,0},{3,1},{4,6},{5,7},{6,4},{7,5},{8,10},{9,11},{10,... | collective-permute-start | bytes 368648 | tf_op jit(solution)/shard_map/ppermute | solution.py:283
  10.3 2.1 %collective-permute-done.1.refs_0_ = bf16[480,128]{1,0:T(8,128)(2,1)S(1)} collective-permute-done((bf16[480,128]{1,0:T(8,128)(2,1)S(1)}, bf16[480,128]{1,0:T(8,128)(2,1)S(1)}, u32[]{:S(2)}, u32[]{:S(2)}) %collective-permute-start.1) | collective-permute-done | bytes 122912 | tf_op jit(solution)/shard_map/ppermute | solution.py:283
  12.5 4.0 %collective-permute-done.2.refs_1_ = bf16[480,128]{1,0:T(8,128)(2,1)S(1)} collective-permute-done((bf16[480,128]{1,0:T(8,128)(2,1)S(1)}, bf16[480,128]{1,0:T(8,128)(2,1)S(1)}, u32[]{:S(2)}, u32[]{:S(2)}) %collective-permute-start.2) | collective-permute-done | bytes 122912 | tf_op jit(solution)/shard_map/ppermute | solution.py:283
  16.9 1.3 %collective-permute-start.7 = (f32[48,256]{1,0:T(8,128)S(1)}, f32[48,256]{1,0:T(8,128)S(1)}, u32[]{:S(2)}, u32[]{:S(2)}) collective-permute-start(f32[48,256]{1,0:T(8,128)S(1)} %get-tuple-element.40), channel_id=1, source_target_pairs={{0,1},{1,0},{2,3},{3,2},{4,5},{5,4},{6,7},{7,6},{8,9},{9,8},{10,11... | collective-permute-start | bytes 147464 | tf_op jit(solution)/shard_map/ppermute | solution.py:283
  18.2 3.6 %collective-permute-start.6 = (f32[136,128]{1,0:T(8,128)S(1)}, f32[136,128]{1,0:T(8,128)S(1)}, u32[]{:S(2)}, u32[]{:S(2)}) collective-permute-start(f32[136,128]{1,0:T(8,128)S(1)} %get-tuple-element.38.refs_0_), channel_id=1, source_target_pairs={{0,24},{4,28},{8,16},{12,20},{16,8},{20,12},{24,0},{28,4},{1,25},{... | collective-permute-start | bytes 208904 | tf_op jit(solution)/shard_map/ppermute | solution.py:283
  21.8 0.8 %collective-permute-start.4 = (f32[136,128]{1,0:T(8,128)S(1)}, f32[136,128]{1,0:T(8,128)S(1)}, u32[]{:S(2)}, u32[]{:S(2)}) collective-permute-start(f32[136,128]{1,0:T(8,128)S(1)} %get-tuple-element.38.refs_0_), channel_id=1, source_target_pairs={{0,8},{4,12},{8,0},{12,4},{16,24},{20,28},{24,16},{28,20},{1,9},{5... | collective-permute-start | bytes 208904 | tf_op jit(solution)/shard_map/ppermute | solution.py:283
  22.6 0.8 %collective-permute-start.8 = (f32[48,256]{1,0:T(8,128)S(1)}, f32[48,256]{1,0:T(8,128)S(1)}, u32[]{:S(2)}, u32[]{:S(2)}) collective-permute-start(f32[48,256]{1,0:T(8,128)S(1)} %get-tuple-element.41), channel_id=1, source_target_pairs={{0,2},{1,3},{2,0},{3,1},{4,6},{5,7},{6,4},{7,5},{8,10},{9,11},{10,... | collective-permute-start | bytes 147464 | tf_op jit(solution)/shard_map/ppermute | solution.py:283
  23.5 1.4 %collective-permute-start.9 = (f32[48,256]{1,0:T(8,128)S(1)}, f32[48,256]{1,0:T(8,128)S(1)}, u32[]{:S(2)}, u32[]{:S(2)}) collective-permute-start(f32[48,256]{1,0:T(8,128)S(1)} %get-tuple-element.42), channel_id=1, source_target_pairs={{0,3},{1,2},{2,1},{3,0},{4,7},{5,6},{6,5},{7,4},{8,11},{9,10},{10,... | collective-permute-start | bytes 147464 | tf_op jit(solution)/shard_map/ppermute | solution.py:283
  24.9 1.8 %collective-permute-done.8.refs_6_ = f32[48,256]{1,0:T(8,128)S(1)} collective-permute-done((f32[48,256]{1,0:T(8,128)S(1)}, f32[48,256]{1,0:T(8,128)S(1)}, u32[]{:S(2)}, u32[]{:S(2)}) %collective-permute-start.8) | collective-permute-done | bytes 49184 | tf_op jit(solution)/shard_map/ppermute | solution.py:283
  26.7 1.7 %collective-permute-done.9.refs_7_ = f32[48,256]{1,0:T(8,128)S(1)} collective-permute-done((f32[48,256]{1,0:T(8,128)S(1)}, f32[48,256]{1,0:T(8,128)S(1)}, u32[]{:S(2)}, u32[]{:S(2)}) %collective-permute-start.9) | collective-permute-done | bytes 49184 | tf_op jit(solution)/shard_map/ppermute | solution.py:283
  28.5 1.5 %collective-permute-start.12 = (f32[136,128]{1,0:T(8,128)S(1)}, f32[136,128]{1,0:T(8,128)S(1)}, u32[]{:S(2)}, u32[]{:S(2)}) collective-permute-start(f32[136,128]{1,0:T(8,128)S(1)} %get-tuple-element.43.refs_0_), channel_id=1, source_target_pairs={{0,3},{1,2},{2,1},{3,0},{4,7},{5,6},{6,5},{7,4},{8,11},{9,10},{10,... | collective-permute-start | bytes 208904 | tf_op jit(solution)/shard_map/ppermute | solution.py:283
  30.0 1.5 %collective-permute-start.11 = (f32[136,128]{1,0:T(8,128)S(1)}, f32[136,128]{1,0:T(8,128)S(1)}, u32[]{:S(2)}, u32[]{:S(2)}) collective-permute-start(f32[136,128]{1,0:T(8,128)S(1)} %get-tuple-element.43.refs_0_), channel_id=1, source_target_pairs={{0,2},{1,3},{2,0},{3,1},{4,6},{5,7},{6,4},{7,5},{8,10},{9,11},{10,... | collective-permute-start | bytes 208904 | tf_op jit(solution)/shard_map/ppermute | solution.py:283
  31.5 0.5 collective-permute-start.10
  32.1 3.6 %collective-permute-start.17 = (f32[200,256]{1,0:T(8,128)S(1)}, f32[200,256]{1,0:T(8,128)S(1)}, u32[]{:S(2)}, u32[]{:S(2)}) collective-permute-start(f32[200,256]{1,0:T(8,128)S(1)} %get-tuple-element.46.refs_0_), channel_id=1, source_target_pairs={{0,24},{4,28},{8,16},{12,20},{16,8},{20,12},{24,0},{28,4},{1,25},{... | collective-permute-start | bytes 614408 | tf_op jit(solution)/shard_map/ppermute | solution.py:283
  35.7 0.8 %collective-permute-start.15 = (f32[200,256]{1,0:T(8,128)S(1)}, f32[200,256]{1,0:T(8,128)S(1)}, u32[]{:S(2)}, u32[]{:S(2)}) collective-permute-start(f32[200,256]{1,0:T(8,128)S(1)} %get-tuple-element.46.refs_0_), channel_id=1, source_target_pairs={{0,8},{4,12},{8,0},{12,4},{16,24},{20,28},{24,16},{28,20},{1,9},{5... | collective-permute-start | bytes 614408 | tf_op jit(solution)/shard_map/ppermute | solution.py:283
  37.1 0.8 %collective-permute-done.13.other_first = f32[272,128]{1,0:T(8,128)S(1)} collective-permute-done((f32[272,128]{1,0:T(8,128)S(1)}, f32[272,128]{1,0:T(8,128)S(1)}, u32[]{:S(2)}, u32[]{:S(2)}) %collective-permute-start.13) | collective-permute-done | bytes 139296 | tf_op jit(solution)/shard_map/ppermute | solution.py:283
  38.2 11.5 %cholesky.1 = (f32[512,512]{1,0:T(8,128)S(1)}, f32[128,512]{1,0:T(8,128)}, f32[480,512]{1,0:T(8,128)S(1)}) custom-call(f32[272,128]{1,0:T(8,128)S(1)} %get-tuple-element.44.mine_first, f32[272,128]{1,0:T(8,128)S(1)} %get-tuple-element.45.mine_last, f32[272,128]{1,0:T(8,128)S(1)} %collective-permute-done.13.other_first, ...), custom_call_target="tpu_custom_call" | custom-call | bytes 1024 | tf_op jit(solution)/shard_map/cholesky/pallas_call | solution.py:466
  49.7 2.2 %far.1 = (f32[240,512]{1,0:T(8,128)S(1)}, f32[240,512]{1,0:T(8,128)S(1)}) custom-call(f32[512,512]{1,0:T(8,128)S(1)} %get-tuple-element.48.wait_ref.inverse_ref, f32[480,512]{1,0:T(8,128)S(1)} %get-tuple-element.49.near_ref, f32[200,256]{1,0:T(8,128)S(1)} %collective-permute-done.15.refs_0_, f32[200,256]{1,0:T(8,128)S(1)} %collective-permute-done.16.refs_1_, ...), custom_call_target="tpu_custom_call" | custom-call | bytes 1024 | tf_op jit(solution)/shard_map/far/pallas_call | solution.py:562
  52.2 1.6 %collective-permute-done.18.got_ref = f32[240,512]{1,0:T(8,128)S(1)} collective-permute-done((f32[240,512]{1,0:T(8,128)S(1)}, f32[240,512]{1,0:T(8,128)S(1)}, u32[]{:S(2)}, u32[]{:S(2)}) %collective-permute-start.18) | collective-permute-done | bytes 491552 | tf_op jit(solution)/shard_map/ppermute | solution.py:283
  53.8 1.4 %solve.1 = f32[240,512]{1,0:T(8,128)} custom-call(f32[240,512]{1,0:T(8,128)S(1)} %get-tuple-element.50.keep_ref, f32[240,512]{1,0:T(8,128)S(1)} %collective-permute-done.18.got_ref, f32[512,512]{1,0:T(8,128)S(1)} %get-tuple-element.48.wait_ref.inverse_ref), custom_call_target="tpu_custom_call" | custom-call | tf_op jit(solution)/shard_map/solve/pallas_call | solution.py:587
  (28 shorter events, 1.8 us)
Async XLA Ops:
  4.1 1.7 %collective-permute-start = (f32[544,128]{1,0:T(8,128)S(1)}, f32[544,128]{1,0:T(8,128)S(1)}, u32[]{:S(2)}, u32[]{:S(2)}) collective-permute-start(f32[544,128]{1,0:T(8,128)S(1)} %get-tuple-element.29), channel_id=1, source_target_pairs={{0,4},{4,0},{8,12},{12,8},{16,20},{20,16},{24,28},{28,24},{1,5},{5... | collective-permute-start | bytes 835592 | tf_op jit(solution)/shard_map/ppermute | solution.py:283
  5.9 6.6 %collective-permute-start.1 = (bf16[480,128]{1,0:T(8,128)(2,1)S(1)}, bf16[480,128]{1,0:T(8,128)(2,1)S(1)}, u32[]{:S(2)}, u32[]{:S(2)}) collective-permute-start(bf16[480,128]{1,0:T(8,128)(2,1)S(1)} %get-tuple-element.35), channel_id=1, source_target_pairs={{0,1},{1,0},{2,3},{3,2},{4,5},{5,4},{6,7},{7,6},{8,9},{9,8},{10,11... | collective-permute-start | bytes 368648 | tf_op jit(solution)/shard_map/ppermute | solution.py:283
  8.8 7.7 %collective-permute-start.2 = (bf16[480,128]{1,0:T(8,128)(2,1)S(1)}, bf16[480,128]{1,0:T(8,128)(2,1)S(1)}, u32[]{:S(2)}, u32[]{:S(2)}) collective-permute-start(bf16[480,128]{1,0:T(8,128)(2,1)S(1)} %get-tuple-element.36), channel_id=1, source_target_pairs={{0,2},{1,3},{2,0},{3,1},{4,6},{5,7},{6,4},{7,5},{8,10},{9,11},{10,... | collective-permute-start | bytes 368648 | tf_op jit(solution)/shard_map/ppermute | solution.py:283
  10.3 6.2 %collective-permute-start.3 = (bf16[480,128]{1,0:T(8,128)(2,1)S(1)}, bf16[480,128]{1,0:T(8,128)(2,1)S(1)}, u32[]{:S(2)}, u32[]{:S(2)}) collective-permute-start(bf16[480,128]{1,0:T(8,128)(2,1)S(1)} %get-tuple-element.37), channel_id=1, source_target_pairs={{0,3},{1,2},{2,1},{3,0},{4,7},{5,6},{6,5},{7,4},{8,11},{9,10},{10,... | collective-permute-start | bytes 368648 | tf_op jit(solution)/shard_map/ppermute | solution.py:283
  16.9 11.5 %copy-start = (s32[4,256]{1,0:T(4,128)S(1)}, s32[4,256]{1,0:T(4,128)}, u32[]{:S(2)}) copy-start(s32[4,256]{1,0:T(4,128)} %columns_ref.3) | copy-start | bytes 12292
  16.9 6.5 %collective-permute-start.7 = (f32[48,256]{1,0:T(8,128)S(1)}, f32[48,256]{1,0:T(8,128)S(1)}, u32[]{:S(2)}, u32[]{:S(2)}) collective-permute-start(f32[48,256]{1,0:T(8,128)S(1)} %get-tuple-element.40), channel_id=1, source_target_pairs={{0,1},{1,0},{2,3},{3,2},{4,5},{5,4},{6,7},{7,6},{8,9},{9,8},{10,11... | collective-permute-start | bytes 147464 | tf_op jit(solution)/shard_map/ppermute | solution.py:283
  18.2 10.2 %collective-permute-start.6 = (f32[136,128]{1,0:T(8,128)S(1)}, f32[136,128]{1,0:T(8,128)S(1)}, u32[]{:S(2)}, u32[]{:S(2)}) collective-permute-start(f32[136,128]{1,0:T(8,128)S(1)} %get-tuple-element.38.refs_0_), channel_id=1, source_target_pairs={{0,24},{4,28},{8,16},{12,20},{16,8},{20,12},{24,0},{28,4},{1,25},{... | collective-permute-start | bytes 208904 | tf_op jit(solution)/shard_map/ppermute | solution.py:283
  21.8 6.6 %collective-permute-start.5 = (f32[136,128]{1,0:T(8,128)S(1)}, f32[136,128]{1,0:T(8,128)S(1)}, u32[]{:S(2)}, u32[]{:S(2)}) collective-permute-start(f32[136,128]{1,0:T(8,128)S(1)} %get-tuple-element.38.refs_0_), channel_id=1, source_target_pairs={{0,16},{4,20},{8,24},{12,28},{16,0},{20,4},{24,8},{28,12},{1,17},{... | collective-permute-start | bytes 208904 | tf_op jit(solution)/shard_map/ppermute | solution.py:283
  21.8 6.6 %collective-permute-start.4 = (f32[136,128]{1,0:T(8,128)S(1)}, f32[136,128]{1,0:T(8,128)S(1)}, u32[]{:S(2)}, u32[]{:S(2)}) collective-permute-start(f32[136,128]{1,0:T(8,128)S(1)} %get-tuple-element.38.refs_0_), channel_id=1, source_target_pairs={{0,8},{4,12},{8,0},{12,4},{16,24},{20,28},{24,16},{28,20},{1,9},{5... | collective-permute-start | bytes 208904 | tf_op jit(solution)/shard_map/ppermute | solution.py:283
  22.6 5.8 %copy-start.1 = (s32[1,4,48]{2,1,0:T(4,128)S(1)}, s32[1,4,48]{2,1,0:T(4,128)}, u32[]{:S(2)}) copy-start(s32[1,4,48]{2,1,0:T(4,128)} %rows_ref.1) | copy-start | bytes 2308
  22.6 4.1 %collective-permute-start.8 = (f32[48,256]{1,0:T(8,128)S(1)}, f32[48,256]{1,0:T(8,128)S(1)}, u32[]{:S(2)}, u32[]{:S(2)}) collective-permute-start(f32[48,256]{1,0:T(8,128)S(1)} %get-tuple-element.41), channel_id=1, source_target_pairs={{0,2},{1,3},{2,0},{3,1},{4,6},{5,7},{6,4},{7,5},{8,10},{9,11},{10,... | collective-permute-start | bytes 147464 | tf_op jit(solution)/shard_map/ppermute | solution.py:283
  23.5 5.0 %collective-permute-start.9 = (f32[48,256]{1,0:T(8,128)S(1)}, f32[48,256]{1,0:T(8,128)S(1)}, u32[]{:S(2)}, u32[]{:S(2)}) collective-permute-start(f32[48,256]{1,0:T(8,128)S(1)} %get-tuple-element.42), channel_id=1, source_target_pairs={{0,3},{1,2},{2,1},{3,0},{4,7},{5,6},{6,5},{7,4},{8,11},{9,10},{10,... | collective-permute-start | bytes 147464 | tf_op jit(solution)/shard_map/ppermute | solution.py:283
  28.5 7.1 %collective-permute-start.12 = (f32[136,128]{1,0:T(8,128)S(1)}, f32[136,128]{1,0:T(8,128)S(1)}, u32[]{:S(2)}, u32[]{:S(2)}) collective-permute-start(f32[136,128]{1,0:T(8,128)S(1)} %get-tuple-element.43.refs_0_), channel_id=1, source_target_pairs={{0,3},{1,2},{2,1},{3,0},{4,7},{5,6},{6,5},{7,4},{8,11},{9,10},{10,... | collective-permute-start | bytes 208904 | tf_op jit(solution)/shard_map/ppermute | solution.py:283
  30.0 6.5 %collective-permute-start.11 = (f32[136,128]{1,0:T(8,128)S(1)}, f32[136,128]{1,0:T(8,128)S(1)}, u32[]{:S(2)}, u32[]{:S(2)}) collective-permute-start(f32[136,128]{1,0:T(8,128)S(1)} %get-tuple-element.43.refs_0_), channel_id=1, source_target_pairs={{0,2},{1,3},{2,0},{3,1},{4,6},{5,7},{6,4},{7,5},{8,10},{9,11},{10,... | collective-permute-start | bytes 208904 | tf_op jit(solution)/shard_map/ppermute | solution.py:283
  31.5 4.9 %collective-permute-start.10 = (f32[136,128]{1,0:T(8,128)S(1)}, f32[136,128]{1,0:T(8,128)S(1)}, u32[]{:S(2)}, u32[]{:S(2)}) collective-permute-start(f32[136,128]{1,0:T(8,128)S(1)} %get-tuple-element.43.refs_0_), channel_id=1, source_target_pairs={{0,1},{1,0},{2,3},{3,2},{4,5},{5,4},{6,7},{7,6},{8,9},{9,8},{10,11... | collective-permute-start | bytes 208904 | tf_op jit(solution)/shard_map/ppermute | solution.py:283
  32.1 17.6 %collective-permute-start.17 = (f32[200,256]{1,0:T(8,128)S(1)}, f32[200,256]{1,0:T(8,128)S(1)}, u32[]{:S(2)}, u32[]{:S(2)}) collective-permute-start(f32[200,256]{1,0:T(8,128)S(1)} %get-tuple-element.46.refs_0_), channel_id=1, source_target_pairs={{0,24},{4,28},{8,16},{12,20},{16,8},{20,12},{24,0},{28,4},{1,25},{... | collective-permute-start | bytes 614408 | tf_op jit(solution)/shard_map/ppermute | solution.py:283
  35.7 14.0 %collective-permute-start.16 = (f32[200,256]{1,0:T(8,128)S(1)}, f32[200,256]{1,0:T(8,128)S(1)}, u32[]{:S(2)}, u32[]{:S(2)}) collective-permute-start(f32[200,256]{1,0:T(8,128)S(1)} %get-tuple-element.46.refs_0_), channel_id=1, source_target_pairs={{0,16},{4,20},{8,24},{12,28},{16,0},{20,4},{24,8},{28,12},{1,17},{... | collective-permute-start | bytes 614408 | tf_op jit(solution)/shard_map/ppermute | solution.py:283
  35.7 14.0 %collective-permute-start.15 = (f32[200,256]{1,0:T(8,128)S(1)}, f32[200,256]{1,0:T(8,128)S(1)}, u32[]{:S(2)}, u32[]{:S(2)}) collective-permute-start(f32[200,256]{1,0:T(8,128)S(1)} %get-tuple-element.46.refs_0_), channel_id=1, source_target_pairs={{0,8},{4,12},{8,0},{12,4},{16,24},{20,28},{24,16},{28,20},{1,9},{5... | collective-permute-start | bytes 614408 | tf_op jit(solution)/shard_map/ppermute | solution.py:283
  36.5 1.6 %copy-start.2 = (f32[512]{0:T(512)S(1)}, f32[512]{0:T(512)}, u32[]{:S(2)}) copy-start(f32[512]{0:T(512)} %param.13) | copy-start | bytes 6148
  36.5 1.4 %collective-permute-start.13 = (f32[272,128]{1,0:T(8,128)S(1)}, f32[272,128]{1,0:T(8,128)S(1)}, u32[]{:S(2)}, u32[]{:S(2)}) collective-permute-start(f32[272,128]{1,0:T(8,128)S(1)} %get-tuple-element.44.mine_first), channel_id=1, source_target_pairs={{0,4},{4,0},{8,12},{12,8},{16,20},{20,16},{24,28},{28,24},{1,5},{5... | collective-permute-start | bytes 417800 | tf_op jit(solution)/shard_map/ppermute | solution.py:283
  36.6 1.5 %collective-permute-start.14 = (f32[272,128]{1,0:T(8,128)S(1)}, f32[272,128]{1,0:T(8,128)S(1)}, u32[]{:S(2)}, u32[]{:S(2)}) collective-permute-start(f32[272,128]{1,0:T(8,128)S(1)} %get-tuple-element.45.mine_last), channel_id=1, source_target_pairs={{0,4},{4,0},{8,12},{12,8},{16,20},{20,16},{24,28},{28,24},{1,5},{5... | collective-permute-start | bytes 417800 | tf_op jit(solution)/shard_map/ppermute | solution.py:283
  51.9 1.9 %collective-permute-start.18 = (f32[240,512]{1,0:T(8,128)S(1)}, f32[240,512]{1,0:T(8,128)S(1)}, u32[]{:S(2)}, u32[]{:S(2)}) collective-permute-start(f32[240,512]{1,0:T(8,128)S(1)} %get-tuple-element.51), channel_id=1, source_target_pairs={{0,4},{4,0},{8,12},{12,8},{16,20},{20,16},{24,28},{28,24},{1,5},{5... | collective-permute-start | bytes 1474568 | tf_op jit(solution)/shard_map/ppermute | solution.py:283

commit v10 on v9

--- a/solution.py
+++ b/solution.py
@@ -378,25 +378,22 @@
     first = (place - lax.rem(place, 2)) * rows_here
     size = (groups[0].shape[0] - 2 * group) // group
     wide = groups[0].shape[1]
-    total = None
-    slot = lax.broadcasted_iota(jnp.int32, (2 * rows_here, group * size), 0)
+    spreads = []
+    rows = []
     for group_ref in groups:
         index = group_ref[group * size :, :]
-        spreads = []
         for i in range(group):
             columns = index[i : i + 1, :].astype(jnp.int32)
             spread = lax.broadcasted_iota(jnp.int32, (width, wide), 0) == columns
             high, low = split_two(group_ref[i * size : (i + 1) * size, :])
             both = matmul_nt(jnp.concatenate([high, low], 0), spread.astype(jnp.bfloat16))
             spreads.append(both[:size] + both[size:])
-        row_index = jnp.concatenate(
-            [index[group + i : group + i + 1, :size] for i in range(group)], 1
-        )
-        row_map = (slot == row_index.astype(jnp.int32) - first).astype(jnp.bfloat16)
-        high, low = split_two(jnp.concatenate(spreads, 0))
-        part = matmul(row_map, high) + matmul(row_map, low)
-        total = part if total is None else total + part
-    return total
+            rows.append(index[group + i : group + i + 1, :size])
+    row_index = jnp.concatenate(rows, 1).astype(jnp.int32) - first
+    slot = lax.broadcasted_iota(jnp.int32, (2 * rows_here, row_index.shape[1]), 0)
+    row_map = (slot == row_index).astype(jnp.bfloat16)
+    high, low = split_two(jnp.concatenate(spreads, 0))
+    return matmul(row_map, high) + matmul(row_map, low)
 
 
 def cholesky_kernel(

time: 55.5 us -> 54.9 us (0.989)
  no operation moved by 1% of the time
where the time goes in v10:
time: 54.9 us; the launch traced here: 54.7 us
  starting transfers between devices  21.8 us (40%)
  Pallas kernels  18 us (33%)
  waiting for transfers between devices  13.5 us (25%)
  between operations  1.37 us (2%)
    ppermute x19, starting transfers between devices, swap(): return lax.ppermute(value, axis, [(i, i ^ step) for i in range(count)])  21.8 us
    ppermute x19, waiting for transfers between devices, swap(): return lax.ppermute(value, axis, [(i, i ^ step) for i in range(count)])  13.5 us
    pallas_call x1, Pallas kernels, cholesky(): pl.pallas_call(functools.partial(cholesky_kernel, group=group), out_shape...  11.3 us
    pallas_call x1, Pallas kernels, front(): pl.pallas_call(functools.partial(front_kernel, width=width), out_shape=[j...  2.8 us
    pallas_call x1, Pallas kernels, far_rows(): pl.pallas_call(functools.partial(far_kernel, group=group), out_shape=[hal...  1.94 us
    pallas_call x1, Pallas kernels, solve_rows(): pl.pallas_call(solve_kernel, out_shape=jax.ShapeDtypeStruct(keep.shape, j...  1.37 us
  transfers between devices with their start and end apart: 19, of which 8 were waited for; matrix products, arithmetic and copies ran while one was open for 0% of the time, Pallas kernels for 21%

profile of v10, /device:TPU:0, one launch (start us, length us, event | category | flops | bytes accessed | tf_op | source)
XLA Modules:
  0.0 54.7 jit_solution(6164406609661491879)
XLA Ops:
  1.3 2.8 %front.1 = (bf16[256,512]{1,0:T(8,128)(2,1)S(1)}, f32[544,128]{1,0:T(8,128)S(1)}, f32[544,128]{1,0:T(8,128)S(1)}, bf16[48,512]{1,0:T(8,128)(2,1)S(1)}, bf16[48,5...) custom-call(s32[1]{0:T(128)S(6)} %copy.9.order_ref, s32[4,256]{1,0:T(4,128)} %columns_ref.3, ...), custom_call_target="tpu_custom_call" | custom-call | flops 20000000000 | bytes 1024 | tf_op jit(solution)/shard_map/front/pallas_call | solution.py:191
  4.1 0.5 collective-permute-start
  4.6 1.2 %collective-permute-done.got_ref = f32[544,128]{1,0:T(8,128)S(1)} collective-permute-done((f32[544,128]{1,0:T(8,128)S(1)}, f32[544,128]{1,0:T(8,128)S(1)}, u32[]{:S(2)}, u32[]{:S(2)}) %collective-permute-start) | collective-permute-done | bytes 278560 | tf_op jit(solution)/shard_map/ppermute | solution.py:283
  5.9 2.9 %collective-permute-start.1 = (bf16[480,128]{1,0:T(8,128)(2,1)S(1)}, bf16[480,128]{1,0:T(8,128)(2,1)S(1)}, u32[]{:S(2)}, u32[]{:S(2)}) collective-permute-start(bf16[480,128]{1,0:T(8,128)(2,1)S(1)} %get-tuple-element.35), channel_id=1, source_target_pairs={{0,1},{1,0},{2,3},{3,2},{4,5},{5,4},{6,7},{7,6},{8,9},{9,8},{10,11... | collective-permute-start | bytes 368648 | tf_op jit(solution)/shard_map/ppermute | solution.py:283
  8.8 1.5 %collective-permute-start.2 = (bf16[480,128]{1,0:T(8,128)(2,1)S(1)}, bf16[480,128]{1,0:T(8,128)(2,1)S(1)}, u32[]{:S(2)}, u32[]{:S(2)}) collective-permute-start(bf16[480,128]{1,0:T(8,128)(2,1)S(1)} %get-tuple-element.36), channel_id=1, source_target_pairs={{0,2},{1,3},{2,0},{3,1},{4,6},{5,7},{6,4},{7,5},{8,10},{9,11},{10,... | collective-permute-start | bytes 368648 | tf_op jit(solution)/shard_map/ppermute | solution.py:283
  10.3 2.1 %collective-permute-done.1.refs_0_ = bf16[480,128]{1,0:T(8,128)(2,1)S(1)} collective-permute-done((bf16[480,128]{1,0:T(8,128)(2,1)S(1)}, bf16[480,128]{1,0:T(8,128)(2,1)S(1)}, u32[]{:S(2)}, u32[]{:S(2)}) %collective-permute-start.1) | collective-permute-done | bytes 122912 | tf_op jit(solution)/shard_map/ppermute | solution.py:283
  12.5 4.0 %collective-permute-done.2.refs_1_ = bf16[480,128]{1,0:T(8,128)(2,1)S(1)} collective-permute-done((bf16[480,128]{1,0:T(8,128)(2,1)S(1)}, bf16[480,128]{1,0:T(8,128)(2,1)S(1)}, u32[]{:S(2)}, u32[]{:S(2)}) %collective-permute-start.2) | collective-permute-done | bytes 122912 | tf_op jit(solution)/shard_map/ppermute | solution.py:283
  16.9 1.3 %collective-permute-start.7 = (f32[48,256]{1,0:T(8,128)S(1)}, f32[48,256]{1,0:T(8,128)S(1)}, u32[]{:S(2)}, u32[]{:S(2)}) collective-permute-start(f32[48,256]{1,0:T(8,128)S(1)} %get-tuple-element.40), channel_id=1, source_target_pairs={{0,1},{1,0},{2,3},{3,2},{4,5},{5,4},{6,7},{7,6},{8,9},{9,8},{10,11... | collective-permute-start | bytes 147464 | tf_op jit(solution)/shard_map/ppermute | solution.py:283
  18.2 3.6 %collective-permute-start.6 = (f32[136,128]{1,0:T(8,128)S(1)}, f32[136,128]{1,0:T(8,128)S(1)}, u32[]{:S(2)}, u32[]{:S(2)}) collective-permute-start(f32[136,128]{1,0:T(8,128)S(1)} %get-tuple-element.38.refs_0_), channel_id=1, source_target_pairs={{0,24},{4,28},{8,16},{12,20},{16,8},{20,12},{24,0},{28,4},{1,25},{... | collective-permute-start | bytes 208904 | tf_op jit(solution)/shard_map/ppermute | solution.py:283
  21.8 0.8 %collective-permute-start.4 = (f32[136,128]{1,0:T(8,128)S(1)}, f32[136,128]{1,0:T(8,128)S(1)}, u32[]{:S(2)}, u32[]{:S(2)}) collective-permute-start(f32[136,128]{1,0:T(8,128)S(1)} %get-tuple-element.38.refs_0_), channel_id=1, source_target_pairs={{0,8},{4,12},{8,0},{12,4},{16,24},{20,28},{24,16},{28,20},{1,9},{5... | collective-permute-start | bytes 208904 | tf_op jit(solution)/shard_map/ppermute | solution.py:283
  22.6 0.8 %collective-permute-start.8 = (f32[48,256]{1,0:T(8,128)S(1)}, f32[48,256]{1,0:T(8,128)S(1)}, u32[]{:S(2)}, u32[]{:S(2)}) collective-permute-start(f32[48,256]{1,0:T(8,128)S(1)} %get-tuple-element.41), channel_id=1, source_target_pairs={{0,2},{1,3},{2,0},{3,1},{4,6},{5,7},{6,4},{7,5},{8,10},{9,11},{10,... | collective-permute-start | bytes 147464 | tf_op jit(solution)/shard_map/ppermute | solution.py:283
  23.5 1.4 %collective-permute-start.9 = (f32[48,256]{1,0:T(8,128)S(1)}, f32[48,256]{1,0:T(8,128)S(1)}, u32[]{:S(2)}, u32[]{:S(2)}) collective-permute-start(f32[48,256]{1,0:T(8,128)S(1)} %get-tuple-element.42), channel_id=1, source_target_pairs={{0,3},{1,2},{2,1},{3,0},{4,7},{5,6},{6,5},{7,4},{8,11},{9,10},{10,... | collective-permute-start | bytes 147464 | tf_op jit(solution)/shard_map/ppermute | solution.py:283
  24.9 1.8 %collective-permute-done.8.refs_6_ = f32[48,256]{1,0:T(8,128)S(1)} collective-permute-done((f32[48,256]{1,0:T(8,128)S(1)}, f32[48,256]{1,0:T(8,128)S(1)}, u32[]{:S(2)}, u32[]{:S(2)}) %collective-permute-start.8) | collective-permute-done | bytes 49184 | tf_op jit(solution)/shard_map/ppermute | solution.py:283
  26.7 1.7 %collective-permute-done.9.refs_7_ = f32[48,256]{1,0:T(8,128)S(1)} collective-permute-done((f32[48,256]{1,0:T(8,128)S(1)}, f32[48,256]{1,0:T(8,128)S(1)}, u32[]{:S(2)}, u32[]{:S(2)}) %collective-permute-start.9) | collective-permute-done | bytes 49184 | tf_op jit(solution)/shard_map/ppermute | solution.py:283
  28.5 1.5 %collective-permute-start.12 = (f32[136,128]{1,0:T(8,128)S(1)}, f32[136,128]{1,0:T(8,128)S(1)}, u32[]{:S(2)}, u32[]{:S(2)}) collective-permute-start(f32[136,128]{1,0:T(8,128)S(1)} %get-tuple-element.43.refs_0_), channel_id=1, source_target_pairs={{0,3},{1,2},{2,1},{3,0},{4,7},{5,6},{6,5},{7,4},{8,11},{9,10},{10,... | collective-permute-start | bytes 208904 | tf_op jit(solution)/shard_map/ppermute | solution.py:283
  30.0 1.5 %collective-permute-start.11 = (f32[136,128]{1,0:T(8,128)S(1)}, f32[136,128]{1,0:T(8,128)S(1)}, u32[]{:S(2)}, u32[]{:S(2)}) collective-permute-start(f32[136,128]{1,0:T(8,128)S(1)} %get-tuple-element.43.refs_0_), channel_id=1, source_target_pairs={{0,2},{1,3},{2,0},{3,1},{4,6},{5,7},{6,4},{7,5},{8,10},{9,11},{10,... | collective-permute-start | bytes 208904 | tf_op jit(solution)/shard_map/ppermute | solution.py:283
  31.5 0.5 collective-permute-start.10
  32.1 3.6 %collective-permute-start.17 = (f32[200,256]{1,0:T(8,128)S(1)}, f32[200,256]{1,0:T(8,128)S(1)}, u32[]{:S(2)}, u32[]{:S(2)}) collective-permute-start(f32[200,256]{1,0:T(8,128)S(1)} %get-tuple-element.46.refs_0_), channel_id=1, source_target_pairs={{0,24},{4,28},{8,16},{12,20},{16,8},{20,12},{24,0},{28,4},{1,25},{... | collective-permute-start | bytes 614408 | tf_op jit(solution)/shard_map/ppermute | solution.py:283
  35.7 0.8 %collective-permute-start.15 = (f32[200,256]{1,0:T(8,128)S(1)}, f32[200,256]{1,0:T(8,128)S(1)}, u32[]{:S(2)}, u32[]{:S(2)}) collective-permute-start(f32[200,256]{1,0:T(8,128)S(1)} %get-tuple-element.46.refs_0_), channel_id=1, source_target_pairs={{0,8},{4,12},{8,0},{12,4},{16,24},{20,28},{24,16},{28,20},{1,9},{5... | collective-permute-start | bytes 614408 | tf_op jit(solution)/shard_map/ppermute | solution.py:283
  37.1 0.8 %collective-permute-done.13.other_first = f32[272,128]{1,0:T(8,128)S(1)} collective-permute-done((f32[272,128]{1,0:T(8,128)S(1)}, f32[272,128]{1,0:T(8,128)S(1)}, u32[]{:S(2)}, u32[]{:S(2)}) %collective-permute-start.13) | collective-permute-done | bytes 139296 | tf_op jit(solution)/shard_map/ppermute | solution.py:283
  38.2 11.3 %cholesky.1 = (f32[512,512]{1,0:T(8,128)S(1)}, f32[128,512]{1,0:T(8,128)}, f32[480,512]{1,0:T(8,128)S(1)}) custom-call(f32[272,128]{1,0:T(8,128)S(1)} %get-tuple-element.44.mine_first, f32[272,128]{1,0:T(8,128)S(1)} %get-tuple-element.45.mine_last, f32[272,128]{1,0:T(8,128)S(1)} %collective-permute-done.13.other_first, ...), custom_call_target="tpu_custom_call" | custom-call | bytes 1024 | tf_op jit(solution)/shard_map/cholesky/pallas_call | solution.py:463
  49.5 1.9 %far.1 = (f32[240,512]{1,0:T(8,128)S(1)}, f32[240,512]{1,0:T(8,128)S(1)}) custom-call(f32[512,512]{1,0:T(8,128)S(1)} %get-tuple-element.48.wait_ref.inverse_ref, f32[480,512]{1,0:T(8,128)S(1)} %get-tuple-element.49.near_ref, f32[200,256]{1,0:T(8,128)S(1)} %collective-permute-done.15.refs_0_, f32[200,256]{1,0:T(8,128)S(1)} %collective-permute-done.16.refs_1_, ...), custom_call_target="tpu_custom_call" | custom-call | bytes 1024 | tf_op jit(solution)/shard_map/far/pallas_call | solution.py:559
  51.8 1.6 %collective-permute-done.18.got_ref = f32[240,512]{1,0:T(8,128)S(1)} collective-permute-done((f32[240,512]{1,0:T(8,128)S(1)}, f32[240,512]{1,0:T(8,128)S(1)}, u32[]{:S(2)}, u32[]{:S(2)}) %collective-permute-start.18) | collective-permute-done | bytes 491552 | tf_op jit(solution)/shard_map/ppermute | solution.py:283
  53.3 1.4 %solve.1 = f32[240,512]{1,0:T(8,128)} custom-call(f32[240,512]{1,0:T(8,128)S(1)} %get-tuple-element.50.keep_ref, f32[240,512]{1,0:T(8,128)S(1)} %collective-permute-done.18.got_ref, f32[512,512]{1,0:T(8,128)S(1)} %get-tuple-element.48.wait_ref.inverse_ref), custom_call_target="tpu_custom_call" | custom-call | tf_op jit(solution)/shard_map/solve/pallas_call | solution.py:584
  (28 shorter events, 1.8 us)
Async XLA Ops:
  4.1 1.7 %collective-permute-start = (f32[544,128]{1,0:T(8,128)S(1)}, f32[544,128]{1,0:T(8,128)S(1)}, u32[]{:S(2)}, u32[]{:S(2)}) collective-permute-start(f32[544,128]{1,0:T(8,128)S(1)} %get-tuple-element.29), channel_id=1, source_target_pairs={{0,4},{4,0},{8,12},{12,8},{16,20},{20,16},{24,28},{28,24},{1,5},{5... | collective-permute-start | bytes 835592 | tf_op jit(solution)/shard_map/ppermute | solution.py:283
  5.9 6.6 %collective-permute-start.1 = (bf16[480,128]{1,0:T(8,128)(2,1)S(1)}, bf16[480,128]{1,0:T(8,128)(2,1)S(1)}, u32[]{:S(2)}, u32[]{:S(2)}) collective-permute-start(bf16[480,128]{1,0:T(8,128)(2,1)S(1)} %get-tuple-element.35), channel_id=1, source_target_pairs={{0,1},{1,0},{2,3},{3,2},{4,5},{5,4},{6,7},{7,6},{8,9},{9,8},{10,11... | collective-permute-start | bytes 368648 | tf_op jit(solution)/shard_map/ppermute | solution.py:283
  8.8 7.7 %collective-permute-start.2 = (bf16[480,128]{1,0:T(8,128)(2,1)S(1)}, bf16[480,128]{1,0:T(8,128)(2,1)S(1)}, u32[]{:S(2)}, u32[]{:S(2)}) collective-permute-start(bf16[480,128]{1,0:T(8,128)(2,1)S(1)} %get-tuple-element.36), channel_id=1, source_target_pairs={{0,2},{1,3},{2,0},{3,1},{4,6},{5,7},{6,4},{7,5},{8,10},{9,11},{10,... | collective-permute-start | bytes 368648 | tf_op jit(solution)/shard_map/ppermute | solution.py:283
  10.3 6.2 %collective-permute-start.3 = (bf16[480,128]{1,0:T(8,128)(2,1)S(1)}, bf16[480,128]{1,0:T(8,128)(2,1)S(1)}, u32[]{:S(2)}, u32[]{:S(2)}) collective-permute-start(bf16[480,128]{1,0:T(8,128)(2,1)S(1)} %get-tuple-element.37), channel_id=1, source_target_pairs={{0,3},{1,2},{2,1},{3,0},{4,7},{5,6},{6,5},{7,4},{8,11},{9,10},{10,... | collective-permute-start | bytes 368648 | tf_op jit(solution)/shard_map/ppermute | solution.py:283
  16.9 11.5 %copy-start = (s32[4,256]{1,0:T(4,128)S(1)}, s32[4,256]{1,0:T(4,128)}, u32[]{:S(2)}) copy-start(s32[4,256]{1,0:T(4,128)} %columns_ref.3) | copy-start | bytes 12292
  16.9 6.5 %collective-permute-start.7 = (f32[48,256]{1,0:T(8,128)S(1)}, f32[48,256]{1,0:T(8,128)S(1)}, u32[]{:S(2)}, u32[]{:S(2)}) collective-permute-start(f32[48,256]{1,0:T(8,128)S(1)} %get-tuple-element.40), channel_id=1, source_target_pairs={{0,1},{1,0},{2,3},{3,2},{4,5},{5,4},{6,7},{7,6},{8,9},{9,8},{10,11... | collective-permute-start | bytes 147464 | tf_op jit(solution)/shard_map/ppermute | solution.py:283
  18.2 10.2 %collective-permute-start.6 = (f32[136,128]{1,0:T(8,128)S(1)}, f32[136,128]{1,0:T(8,128)S(1)}, u32[]{:S(2)}, u32[]{:S(2)}) collective-permute-start(f32[136,128]{1,0:T(8,128)S(1)} %get-tuple-element.38.refs_0_), channel_id=1, source_target_pairs={{0,24},{4,28},{8,16},{12,20},{16,8},{20,12},{24,0},{28,4},{1,25},{... | collective-permute-start | bytes 208904 | tf_op jit(solution)/shard_map/ppermute | solution.py:283
  21.8 6.6 %collective-permute-start.5 = (f32[136,128]{1,0:T(8,128)S(1)}, f32[136,128]{1,0:T(8,128)S(1)}, u32[]{:S(2)}, u32[]{:S(2)}) collective-permute-start(f32[136,128]{1,0:T(8,128)S(1)} %get-tuple-element.38.refs_0_), channel_id=1, source_target_pairs={{0,16},{4,20},{8,24},{12,28},{16,0},{20,4},{24,8},{28,12},{1,17},{... | collective-permute-start | bytes 208904 | tf_op jit(solution)/shard_map/ppermute | solution.py:283
  21.8 6.6 %collective-permute-start.4 = (f32[136,128]{1,0:T(8,128)S(1)}, f32[136,128]{1,0:T(8,128)S(1)}, u32[]{:S(2)}, u32[]{:S(2)}) collective-permute-start(f32[136,128]{1,0:T(8,128)S(1)} %get-tuple-element.38.refs_0_), channel_id=1, source_target_pairs={{0,8},{4,12},{8,0},{12,4},{16,24},{20,28},{24,16},{28,20},{1,9},{5... | collective-permute-start | bytes 208904 | tf_op jit(solution)/shard_map/ppermute | solution.py:283
  22.6 5.8 %copy-start.1 = (s32[1,4,48]{2,1,0:T(4,128)S(1)}, s32[1,4,48]{2,1,0:T(4,128)}, u32[]{:S(2)}) copy-start(s32[1,4,48]{2,1,0:T(4,128)} %rows_ref.1) | copy-start | bytes 2308
  22.6 4.1 %collective-permute-start.8 = (f32[48,256]{1,0:T(8,128)S(1)}, f32[48,256]{1,0:T(8,128)S(1)}, u32[]{:S(2)}, u32[]{:S(2)}) collective-permute-start(f32[48,256]{1,0:T(8,128)S(1)} %get-tuple-element.41), channel_id=1, source_target_pairs={{0,2},{1,3},{2,0},{3,1},{4,6},{5,7},{6,4},{7,5},{8,10},{9,11},{10,... | collective-permute-start | bytes 147464 | tf_op jit(solution)/shard_map/ppermute | solution.py:283
  23.5 5.0 %collective-permute-start.9 = (f32[48,256]{1,0:T(8,128)S(1)}, f32[48,256]{1,0:T(8,128)S(1)}, u32[]{:S(2)}, u32[]{:S(2)}) collective-permute-start(f32[48,256]{1,0:T(8,128)S(1)} %get-tuple-element.42), channel_id=1, source_target_pairs={{0,3},{1,2},{2,1},{3,0},{4,7},{5,6},{6,5},{7,4},{8,11},{9,10},{10,... | collective-permute-start | bytes 147464 | tf_op jit(solution)/shard_map/ppermute | solution.py:283
  28.5 7.2 %collective-permute-start.12 = (f32[136,128]{1,0:T(8,128)S(1)}, f32[136,128]{1,0:T(8,128)S(1)}, u32[]{:S(2)}, u32[]{:S(2)}) collective-permute-start(f32[136,128]{1,0:T(8,128)S(1)} %get-tuple-element.43.refs_0_), channel_id=1, source_target_pairs={{0,3},{1,2},{2,1},{3,0},{4,7},{5,6},{6,5},{7,4},{8,11},{9,10},{10,... | collective-permute-start | bytes 208904 | tf_op jit(solution)/shard_map/ppermute | solution.py:283
  30.0 6.5 %collective-permute-start.11 = (f32[136,128]{1,0:T(8,128)S(1)}, f32[136,128]{1,0:T(8,128)S(1)}, u32[]{:S(2)}, u32[]{:S(2)}) collective-permute-start(f32[136,128]{1,0:T(8,128)S(1)} %get-tuple-element.43.refs_0_), channel_id=1, source_target_pairs={{0,2},{1,3},{2,0},{3,1},{4,6},{5,7},{6,4},{7,5},{8,10},{9,11},{10,... | collective-permute-start | bytes 208904 | tf_op jit(solution)/shard_map/ppermute | solution.py:283
  31.5 4.9 %collective-permute-start.10 = (f32[136,128]{1,0:T(8,128)S(1)}, f32[136,128]{1,0:T(8,128)S(1)}, u32[]{:S(2)}, u32[]{:S(2)}) collective-permute-start(f32[136,128]{1,0:T(8,128)S(1)} %get-tuple-element.43.refs_0_), channel_id=1, source_target_pairs={{0,1},{1,0},{2,3},{3,2},{4,5},{5,4},{6,7},{7,6},{8,9},{9,8},{10,11... | collective-permute-start | bytes 208904 | tf_op jit(solution)/shard_map/ppermute | solution.py:283
  32.1 17.4 %collective-permute-start.17 = (f32[200,256]{1,0:T(8,128)S(1)}, f32[200,256]{1,0:T(8,128)S(1)}, u32[]{:S(2)}, u32[]{:S(2)}) collective-permute-start(f32[200,256]{1,0:T(8,128)S(1)} %get-tuple-element.46.refs_0_), channel_id=1, source_target_pairs={{0,24},{4,28},{8,16},{12,20},{16,8},{20,12},{24,0},{28,4},{1,25},{... | collective-permute-start | bytes 614408 | tf_op jit(solution)/shard_map/ppermute | solution.py:283
  35.7 13.8 %collective-permute-start.16 = (f32[200,256]{1,0:T(8,128)S(1)}, f32[200,256]{1,0:T(8,128)S(1)}, u32[]{:S(2)}, u32[]{:S(2)}) collective-permute-start(f32[200,256]{1,0:T(8,128)S(1)} %get-tuple-element.46.refs_0_), channel_id=1, source_target_pairs={{0,16},{4,20},{8,24},{12,28},{16,0},{20,4},{24,8},{28,12},{1,17},{... | collective-permute-start | bytes 614408 | tf_op jit(solution)/shard_map/ppermute | solution.py:283
  35.7 13.8 %collective-permute-start.15 = (f32[200,256]{1,0:T(8,128)S(1)}, f32[200,256]{1,0:T(8,128)S(1)}, u32[]{:S(2)}, u32[]{:S(2)}) collective-permute-start(f32[200,256]{1,0:T(8,128)S(1)} %get-tuple-element.46.refs_0_), channel_id=1, source_target_pairs={{0,8},{4,12},{8,0},{12,4},{16,24},{20,28},{24,16},{28,20},{1,9},{5... | collective-permute-start | bytes 614408 | tf_op jit(solution)/shard_map/ppermute | solution.py:283
  36.5 1.6 %copy-start.2 = (f32[512]{0:T(512)S(1)}, f32[512]{0:T(512)}, u32[]{:S(2)}) copy-start(f32[512]{0:T(512)} %param.13) | copy-start | bytes 6148
  36.5 1.4 %collective-permute-start.13 = (f32[272,128]{1,0:T(8,128)S(1)}, f32[272,128]{1,0:T(8,128)S(1)}, u32[]{:S(2)}, u32[]{:S(2)}) collective-permute-start(f32[272,128]{1,0:T(8,128)S(1)} %get-tuple-element.44.mine_first), channel_id=1, source_target_pairs={{0,4},{4,0},{8,12},{12,8},{16,20},{20,16},{24,28},{28,24},{1,5},{5... | collective-permute-start | bytes 417800 | tf_op jit(solution)/shard_map/ppermute | solution.py:283
  36.6 1.5 %collective-permute-start.14 = (f32[272,128]{1,0:T(8,128)S(1)}, f32[272,128]{1,0:T(8,128)S(1)}, u32[]{:S(2)}, u32[]{:S(2)}) collective-permute-start(f32[272,128]{1,0:T(8,128)S(1)} %get-tuple-element.45.mine_last), channel_id=1, source_target_pairs={{0,4},{4,0},{8,12},{12,8},{16,20},{20,16},{24,28},{28,24},{1,5},{5... | collective-permute-start | bytes 417800 | tf_op jit(solution)/shard_map/ppermute | solution.py:283
  51.4 1.9 %collective-permute-start.18 = (f32[240,512]{1,0:T(8,128)S(1)}, f32[240,512]{1,0:T(8,128)S(1)}, u32[]{:S(2)}, u32[]{:S(2)}) collective-permute-start(f32[240,512]{1,0:T(8,128)S(1)} %get-tuple-element.51), channel_id=1, source_target_pairs={{0,4},{4,0},{8,12},{12,8},{16,20},{20,16},{24,28},{28,24},{1,5},{5... | collective-permute-start | bytes 1474568 | tf_op jit(solution)/shard_map/ppermute | solution.py:283
